TPU v7x, 32 devices: a whole 2x2x4 slice. The times are simulated.
32 devices in a mesh: groups: 2 (over x), row: 8 (over z, y), col: 2 (over core).
Axes of the slice: x: 2, y: 2, z: 4, core: 2. Of those that a mesh axis runs over, the one named last changes fastest.
Arguments:
- pair: bfloat16 [192, 96, 128], P(('groups', 'row'), 'col'), parts along dimension 0, may hold values from -6 to 6
- token_mask: int32 [192], P('groups'), parts along dimension 0, may hold values 0 or 1
- gain_in: float32 [128], replicated, may hold values from 0.1 to 1.9
- bias_in: float32 [128], replicated, may hold values from -3 to 3
- w_in: bfloat16 [128, 512], replicated, may hold values from -0.5 to 0.5
- w_gate: bfloat16 [128, 128], replicated, may hold values from -0.5 to 0.5
- gain_out: float32 [128], replicated, may hold values from 0.1 to 1.9
- bias_out: float32 [128], replicated, may hold values from -3 to 3
- w_out: bfloat16 [128, 128], replicated, may hold values from -0.5 to 0.5
Outputs:
- update: bfloat16 [192, 96, 128], P(('groups', 'row'), 'col'), parts along dimension 0
There are 2 independent parts, one for each index of `groups`. A program takes and returns all parts, laid end to end along the dimension named above; an argument that names none is the same for every part. Nothing has to cross between parts.
All inputs are finite; a program needn't handle non-finite values.
Results may differ from a plain program's by a relative error of at most 0.0059.
Values may be sent and summed in bfloat16 or wider, within the bound.
No kernel may reach another device: no remote copies, remote signals or barrier semaphores. Data moves between devices by JAX's collectives and lax.ppermute only.
A program may use at most 128 MiB of HBM per device.

v0:
```python
import jax
import jax.numpy as jnp
from jax import lax
from jax.sharding import PartitionSpec as P

epsilon = 1e-05


def layer_norm(values, gain, bias):
    mean = jnp.mean(values, axis=-1, keepdims=True)
    centred = values - mean
    variance = jnp.mean(centred * centred, axis=-1, keepdims=True)
    return centred * lax.rsqrt(variance + epsilon) * gain + bias


def per_device(pair, token_mask, gain_in, bias_in, w_in, w_gate, gain_out, bias_out, w_out):
    row_count, col_count, channels = pair.shape
    hidden = w_out.shape[0]
    row_start = lax.axis_index("row") * row_count
    col_start = lax.axis_index("col") * col_count
    mask_float = token_mask.astype(jnp.float32)
    mask_rows = lax.dynamic_slice_in_dim(mask_float, row_start, row_count)
    mask_cols = lax.dynamic_slice_in_dim(mask_float, col_start, col_count)
    pair_mask = (mask_rows[:, None] * mask_cols[None, :])[:, :, None]
    normed = layer_norm(pair.astype(jnp.float32), gain_in, bias_in).astype(jnp.bfloat16)
    flat = normed.reshape(row_count * col_count, channels)
    projected = jnp.dot(flat, w_in, preferred_element_type=jnp.float32).reshape(
        row_count, col_count, 4 * hidden
    )
    left = (
        pair_mask * jax.nn.sigmoid(projected[:, :, 0:hidden]) * projected[:, :, hidden : 2 * hidden]
    ).astype(jnp.bfloat16)
    right = (
        pair_mask
        * jax.nn.sigmoid(projected[:, :, 2 * hidden : 3 * hidden])
        * projected[:, :, 3 * hidden : 4 * hidden]
    ).astype(jnp.bfloat16)
    gate = jax.nn.sigmoid(jnp.dot(flat, w_gate, preferred_element_type=jnp.float32)).reshape(
        row_count, col_count, channels
    )
    left_rows = lax.all_gather(left, "col", axis=1, tiled=True)
    panel = lax.all_to_all(left_rows, "row", split_axis=1, concat_axis=0, tiled=True)
    total = jnp.einsum(
        "kic,kjc->ijc",
        panel,
        lax.all_gather(right, "row", axis=0, tiled=True),
        preferred_element_type=jnp.float32,
    )
    summed_norm = layer_norm(total, gain_out, bias_out).astype(jnp.bfloat16)
    output = jnp.dot(
        summed_norm.reshape(row_count * col_count, hidden),
        w_out,
        preferred_element_type=jnp.float32,
    ).reshape(row_count, col_count, channels)
    return (gate * output).astype(jnp.bfloat16)


def solution(mesh):
    in_specs = (P(("groups", "row"), "col", None), P("groups"), P(), P(), P(), P(), P(), P(), P())
    out_specs = P(("groups", "row"), "col", None)
    return jax.shard_map(
        per_device, mesh=mesh, in_specs=in_specs, out_specs=out_specs, check_vma=False
    )
```

profile of v0, /device:TPU:0, one launch (start us, length us, event | category | flops | bytes accessed | tf_op | source)
XLA Modules:
  0.0 78.5 jit_solution(6771143080119905370)
XLA Ops:
  6.5 0.7 convert_element_type.23
  7.2 0.1 dynamic_slice.6
  7.3 0.1 dynamic_slice.7
  7.4 1.1 %convert_reduce_fusion = f32[12,48]{1,0:T(8,128)S(1)} fusion(bf16[12,48,128]{2,1,0:T(8,128)(2,1)} %param.9), kind=kLoop, calls=%fused_computation.7 | loop fusion | flops 146880 | bytes 149760 | tf_op jit(solution)/shard_map/reduce_sum | solution.py:10
  8.5 1.2 %fusion.6 = f32[12,48]{1,0:T(8,128)S(1)} fusion(bf16[12,48,128]{2,1,0:T(8,128)(2,1)} %param.9, f32[12,48]{1,0:T(8,128)S(1)} %broadcast_multiply_fusion.2), kind=kLoop, calls=%fused_computation.10 | loop fusion | flops 294336 | bytes 152064 | tf_op jit(solution)/shard_map/reduce_sum | solution.py:12
  9.7 0.1 broadcast_multiply_fusion
  9.7 1.1 %fusion.9 = bf16[12,48,128]{2,1,0:T(8,128)(2,1)S(1)} fusion(bf16[12,48,128]{2,1,0:T(8,128)(2,1)} %param.9, f32[128]{0:T(128)} %param.12, f32[128]{0:T(128)} %param.11, f32[12,48]{1,0:T(8,128)S(1)} %add_rsqrt_fusion.1, f32[12,48]{1,0:T(8,128)S(1)} %broadcast_multiply_fusion.2), kind=kLoop, calls=%fused_computation.13 | loop fusion | flops 442368 | bytes 300544 | tf_op jit(solution)/shard_map/convert_element_type | solution.py:25
  10.9 0.3 fusion.24
  11.2 0.9 %fusion.10 = (bf16[12,48,128]{2,1,0:T(8,128)(2,1)S(1)}, bf16[12,48,128]{2,1,0:T(8,128)(2,1)}) fusion(f32[12,48,512]{2,1,0:T(8,128)S(1)} %fusion.24, f32[12,48]{1,0:T(8,128)S(1)} %broadcast_multiply_fusion), kind=kLoop, calls=%fused_computation.15 | loop fusion | flops 884736 | bytes 1476864 | tf_op jit(solution)/shard_map/convert_element_type | solution.py:32
  12.1 0.0 all-gather.2.cloned.1.call-update
  12.1 2.1 %all_gather.7 = bf16[12,96,128]{2,1,0:T(8,128)(2,1)S(1)} all-gather(bf16[12,48,128]{2,1,0:T(8,128)(2,1)S(1)} %get-tuple-element.5), channel_id=1, replica_groups=mesh['groups'=2,'row'=8,'col'=2] {'col'}, dimensions={1}, use_global_device_ids=true | all-gather | bytes 442368 | tf_op jit(solution)/shard_map/all_gather | solution.py:41
  14.2 0.9 %copy.23 = bf16[12,96,128]{2,0,1:T(8,128)(2,1)} copy(bf16[12,96,128]{2,1,0:T(8,128)(2,1)S(1)} %all_gather.7) | data formatting | bytes 589824 | tf_op jit(solution)/shard_map/all_gather | solution.py:41
  15.1 7.2 %all-to-all-start = ((bf16[12,96,128]{2,0,1:T(8,128)(2,1)}), bf16[12,96,128]{2,0,1:T(8,128)(2,1)S(1)}, u32[]{:S(2)}, u32[]{:S(2)}) async-start(bf16[12,96,128]{2,0,1:T(8,128)(2,1)} %copy.23), calls=%async_computation | async-start | bytes 786432 | tf_op jit(solution)/shard_map/all_to_all | solution.py:42
  22.3 0.9 %fusion.2 = f32[576,128]{1,0:T(8,128)} fusion(bf16[576,128]{1,0:T(8,128)(2,1)S(1)} %bitcast.28, bf16[128,128]{1,0:T(8,128)(2,1)S(1)} %copy-done.4), kind=kOutput, calls=%fused_computation.4 | convolution fusion | flops 19095552 | bytes 475136 | tf_op jit(solution)/shard_map/dot_general | solution.py:38
  23.2 15.7 %all-to-all-done = bf16[12,96,128]{2,0,1:T(8,128)(2,1)S(1)} async-done(((bf16[12,96,128]{2,0,1:T(8,128)(2,1)}), bf16[12,96,128]{2,0,1:T(8,128)(2,1)S(1)}, u32[]{:S(2)}, u32[]{:S(2)}) %all-to-all-start) | async-done | bytes 294944 | tf_op jit(solution)/shard_map/all_to_all | solution.py:42
  38.9 0.1 all_to_all.16
  39.0 1.2 %copy.27 = bf16[96,12,128]{0,1,2:T(8,128)(2,1)} copy(bf16[96,12,128]{2,0,1:T(8,128)(2,1)S(1)} %all_to_all.16) | data formatting | bytes 589824 | tf_op jit(solution)/shard_map/all_to_all | solution.py:42
  40.2 19.2 %all-gather.2.cloned.1.call-done = bf16[96,48,128]{2,1,0:T(8,128)(2,1)} async-done(((bf16[12,48,128]{2,1,0:T(8,128)(2,1)}), bf16[96,48,128]{2,1,0:T(8,128)(2,1)}) %all-gather.2.cloned.1.call-update) | async-done | bytes 1179664 | tf_op jit(solution)/shard_map/all_gather | solution.py:46
  59.4 5.3 %copy.26 = bf16[96,48,128]{1,0,2:T(8,128)(2,1)S(1)} copy(bf16[96,48,128]{2,1,0:T(8,128)(2,1)} %all-gather.2.cloned.1.call-done) | data formatting | bytes 2359296 | tf_op jit(solution)/shard_map/all_gather | solution.py:46
  64.7 3.0 %fusion.27 = f32[128,48,12]{1,2,0:T(8,128)} fusion(bf16[96,48,128]{1,0,2:T(8,128)(2,1)S(1)} %copy.26, bf16[96,12,128]{0,1,2:T(8,128)(2,1)} %copy.27), kind=kOutput, calls=%fused_computation.44 | convolution fusion | flops 14155776 | bytes 1769472 | tf_op jit(solution)/shard_map/kic,kjc->ijc/dot_general | solution.py:43
  67.7 1.5 %copy.28 = f32[128,48,12]{0,1,2:T(8,128)S(1)} copy(f32[128,48,12]{1,2,0:T(8,128)} %fusion.27) | data formatting | bytes 589824 | tf_op jit(solution)/shard_map/kic,kjc->ijc/dot_general | solution.py:43
  69.2 0.1 bitcast_reduce_fusion
  69.4 0.3 multiply_reduce_fusion
  69.7 2.0 %fusion.3 = bf16[12,48,128]{2,1,0:T(8,128)(2,1)} fusion(f32[12,48,128]{2,1,0:T(8,128)} %bitcast.29, f32[128,48,12]{0,1,2:T(8,128)S(1)} %copy.28, f32[128]{0:T(128)S(1)} %copy-done.2, f32[128]{0:T(128)S(1)} %copy-done.3, f32[12,48]{1,0:T(8,128)S(1)} %add_rsqrt_fusion, f32[12,48]{1,0:T(8,128)S(1)} %broadcast_multiply_fusion.1, bf16[128,128]{1,0:T(8,128)(2,1)S(1)} %copy-done.1), kind=kOutput, calls=%fused_computation.5 | convolution fusion | flops 19390464 | bytes 775680 | tf_op jit(solution)/shard_map/dot_general | solution.py:50
  (16 shorter events, 0.1 us)
Async XLA Ops:
  6.5 4.4 %copy-start = (bf16[128,512]{1,0:T(8,128)(2,1)S(1)}, bf16[128,512]{1,0:T(8,128)(2,1)}, u32[]{:S(2)}) copy-start(bf16[128,512]{1,0:T(8,128)(2,1)} %param.13) | copy-start | bytes 393220
  6.5 15.7 %copy-start.4 = (bf16[128,128]{1,0:T(8,128)(2,1)S(1)}, bf16[128,128]{1,0:T(8,128)(2,1)}, u32[]{:S(2)}) copy-start(bf16[128,128]{1,0:T(8,128)(2,1)} %param.14) | copy-start | bytes 98308
  6.5 52.9 %all-gather.2.cloned.1.call-start = ((), (), s32[]{:S(2)}) async-start(), calls=%async_computation.1 | async-start | bytes 1327104 | tf_op jit(solution)/shard_map/all_gather | solution.py:46
  15.1 23.8 %all-to-all-start = ((bf16[12,96,128]{2,0,1:T(8,128)(2,1)}), bf16[12,96,128]{2,0,1:T(8,128)(2,1)S(1)}, u32[]{:S(2)}, u32[]{:S(2)}) async-start(bf16[12,96,128]{2,0,1:T(8,128)(2,1)} %copy.23), calls=%async_computation | async-start | bytes 786432 | tf_op jit(solution)/shard_map/all_to_all | solution.py:42
  64.7 5.0 %copy-start.1 = (bf16[128,128]{1,0:T(8,128)(2,1)S(1)}, bf16[128,128]{1,0:T(8,128)(2,1)}, u32[]{:S(2)}) copy-start(bf16[128,128]{1,0:T(8,128)(2,1)} %param.17) | copy-start | bytes 98308
  64.7 5.0 %copy-start.2 = (f32[128]{0:T(128)S(1)}, f32[128]{0:T(128)}, u32[]{:S(2)}) copy-start(f32[128]{0:T(128)} %param.16) | copy-start | bytes 1540
  64.7 5.0 %copy-start.3 = (f32[128]{0:T(128)S(1)}, f32[128]{0:T(128)}, u32[]{:S(2)}) copy-start(f32[128]{0:T(128)} %param.15) | copy-start | bytes 1540
Sparse Core Ops, SparseCore 0:
  12.2 47.1 all-gather.1
where the time goes:
time: 78.9 us; the launch traced here: 78.5 us
  waiting for transfers between devices  34.9 us (44%)
  between operations  13.5 us (17%)
  local copies, waits for them, and re-layouts  9.2 us (12%)
  starting transfers between devices  7.19 us (9%)
  matrix products  6.16 us (8%)
  other arithmetic  5.46 us (7%)
  blocking collectives  2.11 us (3%)
    all_gather x1, waiting for transfers between devices, per_device(): lax.all_gather(right, 'row', axis=0, tiled=True)  19.2 us
    all_to_all x1, waiting for transfers between devices, per_device(): lax.all_to_all(left_rows, 'row', split_axis=1, concat_axis=0, tiled=True)  15.7 us
    all_to_all x1, starting transfers between devices, per_device(): lax.all_to_all(left_rows, 'row', split_axis=1, concat_axis=0, tiled=True)  7.19 us
    all_gather x1, local copies, waits for them, and re-layouts, per_device(): lax.all_gather(right, 'row', axis=0, tiled=True)  5.29 us
    dot_general x1, matrix products, per_device(): jnp.einsum('kic,kjc->ijc', panel, lax.all_gather(right, 'row', axis=0, ti...  2.97 us
    all_gather x1, blocking collectives, per_device(): left_rows = lax.all_gather(left, 'col', axis=1, tiled=True)  2.11 us
    dot_general x1, matrix products, per_device(): jnp.dot(summed_norm.reshape(row_count * col_count, hidden), w_out, prefer...  1.97 us
  transfers between devices with their start and end apart: 2, of which 2 were waited for; matrix products, arithmetic and copies ran while one was open for 4% of the time, Pallas kernels for 0%

commit v1 on v0

v1 whole, which is shorter than its diff:
```python
import jax
import jax.numpy as jnp
from jax import lax
from jax.sharding import PartitionSpec as P

epsilon = 1e-05
AXES = ("row", "col")


def layer_norm(values, gain, bias, axis):
    mean = jnp.mean(values, axis=axis, keepdims=True)
    centred = values - mean
    variance = jnp.mean(centred * centred, axis=axis, keepdims=True)
    return centred * lax.rsqrt(variance + epsilon) * gain + bias


def exchange(pieces, me, devices):
    got = [lax.dynamic_index_in_dim(pieces, me, 0, False)]
    for step in range(1, devices):
        piece = lax.dynamic_index_in_dim(pieces, me ^ step, 0, False)
        got.append(lax.ppermute(piece, AXES, [(i, i ^ step) for i in range(devices)]))
    return got


def per_device(rows, cols, pair, token_mask, gain_in, bias_in, w_in, w_gate, gain_out, bias_out, w_out):
    row_count, col_count, channels = pair.shape
    hidden = w_out.shape[0]
    devices = rows * cols
    share = hidden // devices
    tokens = row_count * col_count
    row_start = lax.axis_index("row") * row_count
    col_start = lax.axis_index("col") * col_count
    mask_float = token_mask.astype(jnp.float32)
    mask_rows = lax.dynamic_slice_in_dim(mask_float, row_start, row_count)
    mask_cols = lax.dynamic_slice_in_dim(mask_float, col_start, col_count)
    pair_mask = (mask_rows[:, None] * mask_cols[None, :]).reshape(1, tokens)
    flat = pair.reshape(tokens, channels).astype(jnp.float32)
    normed = layer_norm(flat, gain_in, bias_in, -1).astype(jnp.bfloat16)
    projected = lax.dot_general(w_in, normed, (((0,), (1,)), ((), ())), preferred_element_type=jnp.float32)
    projected = projected.reshape(2, 2, hidden, tokens)
    sides = (pair_mask * jax.nn.sigmoid(projected[:, 0]) * projected[:, 1]).astype(jnp.bfloat16)
    sides = sides.reshape(2, devices, share, tokens).transpose(1, 0, 2, 3)
    gate = jax.nn.sigmoid(jnp.dot(normed, w_gate, preferred_element_type=jnp.float32))
    me = lax.axis_index("row") * cols + lax.axis_index("col")
    got = exchange(sides, me, devices)
    got = jnp.stack(got).reshape(rows, cols, 2, share, row_count, col_count).transpose(2, 3, 0, 4, 1, 5)
    got = jnp.where(lax.axis_index("col") == 0, got, got[:, :, :, :, ::-1])
    got = got.reshape(2, share, rows * row_count, cols * col_count)
    total = jnp.einsum("cki,ckj->cij", got[0], got[1], preferred_element_type=jnp.float32).astype(jnp.bfloat16)
    total = total.reshape(share, rows, row_count, cols, col_count).transpose(1, 3, 0, 2, 4)
    total = total.reshape(devices, share, tokens)
    total = jnp.stack(exchange(total, me, devices))
    order = jnp.arange(devices) ^ me
    gain_out = gain_out.reshape(devices, share)[order].reshape(hidden)
    bias_out = bias_out.reshape(devices, share)[order].reshape(hidden)
    w_out = w_out.reshape(devices, share, channels)[order].reshape(hidden, channels)
    total = total.reshape(hidden, tokens).astype(jnp.float32)
    summed_norm = layer_norm(total, gain_out[:, None], bias_out[:, None], 0).astype(jnp.bfloat16)
    output = lax.dot_general(summed_norm, w_out, (((0,), (0,)), ((), ())), preferred_element_type=jnp.float32)
    return (gate * output).astype(jnp.bfloat16).reshape(row_count, col_count, channels)


def solution(mesh):
    import functools

    in_specs = (P(("groups", "row"), "col", None), P("groups"), P(), P(), P(), P(), P(), P(), P())
    out_specs = P(("groups", "row"), "col", None)
    body = functools.partial(per_device, mesh.shape["row"], mesh.shape["col"])
    return jax.shard_map(body, mesh=mesh, in_specs=in_specs, out_specs=out_specs, check_vma=False)
```

time: 78.9 us -> 66.8 us (0.85)
  starting transfers between devices: 7.19 us -> 42.7 us
  waiting for transfers between devices: 34.9 us -> 7.8 us
  between operations: 13.5 us -> 0.46 us
  matrix products: 6.16 us -> 1.75 us
  blocking collectives: 2.11 us -> 0 us
    ppermute x0 -> x30, starting transfers between devices: none -> 42.7 us  [exchange(): lax.ppermute(piece, AXES, [(i, i ^ step) for i in range(devices)])]
    all_gather x1 -> x0, waiting for transfers between devices: 19.2 us -> none  [per_device(): lax.all_gather(right, 'row', axis=0, tiled=True)]
    all_to_all x1 -> x0, waiting for transfers between devices: 15.7 us -> none  [per_device(): lax.all_to_all(left_rows, 'row', split_axis=1, concat_axis=0, tiled=True)]
    ppermute x0 -> x30, waiting for transfers between devices: none -> 7.8 us  [exchange(): lax.ppermute(piece, AXES, [(i, i ^ step) for i in range(devices)])]
    all_to_all x1 -> x0, starting transfers between devices: 7.19 us -> none  [per_device(): lax.all_to_all(left_rows, 'row', split_axis=1, concat_axis=0, tiled=True)]
    all_gather x2 -> x0, local copies, waits for them, and re-layouts: 6.19 us -> none  [the longest x1 5.29 us: per_device(): lax.all_gather(right, 'row', axis=0, tiled=True)]
    dot_general x4, matrix products: 6.16 us -> 1.75 us  [the longest x1 0.98 us: per_device(): lax.dot_general(summed_norm, w_out, (((0,), (0,)), ((), ())), preferred_e...]
    reshape x0 -> x7, local copies, waits for them, and re-layouts: none -> 2.57 us  [the longest x1 1.02 us: per_device(): jnp.stack(got).reshape(rows, cols, 2, share, row_count, col_count)]
  transfers between devices with their start and end apart: 2 -> 30, of which waited for: 2 -> 4; matrix products, arithmetic and copies ran while one was open for 4% -> 4% of each run, Pallas kernels for 0% -> 0%
where the time goes in v1:
time: 66.8 us; the launch traced here: 66.6 us
  starting transfers between devices  42.7 us (64%)
  local copies, waits for them, and re-layouts  9.06 us (14%)
  waiting for transfers between devices  7.8 us (12%)
  other arithmetic  4.8 us (7%)
  matrix products  1.75 us (3%)
    ppermute x30, starting transfers between devices, exchange(): lax.ppermute(piece, AXES, [(i, i ^ step) for i in range(devices)])  42.7 us
    ppermute x30, waiting for transfers between devices, exchange(): lax.ppermute(piece, AXES, [(i, i ^ step) for i in range(devices)])  7.8 us
    unnamed x41, local copies, waits for them, and re-layouts  1.82 us
  transfers between devices with their start and end apart: 30, of which 4 were waited for; matrix products, arithmetic and copies ran while one was open for 4% of the time, Pallas kernels for 0%

profile of v1, /device:TPU:0, one launch (start us, length us, event | category | flops | bytes accessed | tf_op | source)
XLA Modules:
  0.0 66.6 jit_solution(3404464517378949916)
XLA Ops:
  0.0 1.1 %convert_reduce_fusion.1 = f32[12,48]{1,0:T(8,128)S(1)} fusion(bf16[12,48,128]{2,1,0:T(8,128)(2,1)} %param.9), kind=kLoop, calls=%fused_computation.35 | loop fusion | flops 146880 | bytes 149760 | tf_op jit(solution)/shard_map/reduce_sum | solution.py:11
  1.1 1.2 %multiply_reduce_fusion = f32[12,48]{1,0:T(8,128)S(1)} fusion(bf16[12,48,128]{2,1,0:T(8,128)(2,1)} %param.9, f32[12,48]{1,0:T(8,128)S(1)} %broadcast_multiply_fusion.1), kind=kLoop, calls=%fused_computation.30 | loop fusion | flops 294336 | bytes 152064 | tf_op jit(solution)/shard_map/reduce_sum | solution.py:13
  3.4 1.2 %fusion.15 = bf16[576,128]{1,0:T(8,128)(2,1)S(1)} fusion(bf16[12,48,128]{2,1,0:T(8,128)(2,1)} %param.9, f32[128]{0:T(128)} %param.12, f32[128]{0:T(128)} %param.11, f32[576]{0:T(1024)S(1)} %rsqrt.20, f32[576]{0:T(1024)S(1)} %div.25), kind=kLoop, calls=%fused_computation.29 | loop fusion | flops 442368 | bytes 300544 | tf_op jit(solution)/shard_map/convert_element_type | solution.py:38
  5.7 0.9 %fusion.22 = (f32[2,1,128,576]{2,1,0,3:T(1,128)S(1)}, f32[2,1,128,576]{2,1,0,3:T(1,128)S(1)}) fusion(f32[2,2,128,576]{2,1,0,3:T(2,128)S(1)} %reshape.180), kind=kLoop, calls=%fused_computation.106 | loop fusion | bytes 2359296 | tf_op jit(solution)/shard_map/slice | solution.py:41
  6.6 0.8 %copy.25 = f32[2,1,128,576]{3,2,0,1:T(8,128)S(1)} copy(f32[2,1,128,576]{2,1,0,3:T(1,128)S(1)} %get-tuple-element.5) | data formatting | bytes 1179648
  9.0 2.6 %collective-permute-start.1 = (bf16[2,8,576]{2,1,0:T(8,128)(2,1)S(1)}, bf16[2,8,576]{2,1,0:T(8,128)(2,1)S(1)}, u32[]{:S(2)}, u32[]{:S(2)}) collective-permute-start(bf16[2,8,576]{2,1,0:T(8,128)(2,1)S(1)} %get-tuple-element.22), channel_id=1, source_target_pairs={{0,2},{1,3},{2,0},{3,1},{4,6},{5,7},{6,4},{7,5},{8,10},{9,11},{10,... | collective-permute-start | bytes 55304 | tf_op jit(solution)/shard_map/ppermute | solution.py:21
  11.7 1.8 %collective-permute-start.3 = (bf16[2,8,576]{2,1,0:T(8,128)(2,1)S(1)}, bf16[2,8,576]{2,1,0:T(8,128)(2,1)S(1)}, u32[]{:S(2)}, u32[]{:S(2)}) collective-permute-start(bf16[2,8,576]{2,1,0:T(8,128)(2,1)S(1)} %get-tuple-element.20), channel_id=1, source_target_pairs={{0,4},{1,5},{2,6},{3,7},{4,0},{5,1},{6,2},{7,3},{8,12},{9,13},{10,... | collective-permute-start | bytes 55304 | tf_op jit(solution)/shard_map/ppermute | solution.py:21
  13.8 2.7 %collective-permute-start.5 = (bf16[2,8,576]{2,1,0:T(8,128)(2,1)S(1)}, bf16[2,8,576]{2,1,0:T(8,128)(2,1)S(1)}, u32[]{:S(2)}, u32[]{:S(2)}) collective-permute-start(bf16[2,8,576]{2,1,0:T(8,128)(2,1)S(1)} %get-tuple-element.18), channel_id=1, source_target_pairs={{0,6},{1,7},{2,4},{3,5},{4,2},{5,3},{6,0},{7,1},{8,14},{9,15},{10,... | collective-permute-start | bytes 55304 | tf_op jit(solution)/shard_map/ppermute | solution.py:21
  16.6 2.7 %collective-permute-start.7 = (bf16[2,8,576]{2,1,0:T(8,128)(2,1)S(1)}, bf16[2,8,576]{2,1,0:T(8,128)(2,1)S(1)}, u32[]{:S(2)}, u32[]{:S(2)}) collective-permute-start(bf16[2,8,576]{2,1,0:T(8,128)(2,1)S(1)} %get-tuple-element.16), channel_id=1, source_target_pairs={{0,8},{1,9},{2,10},{3,11},{4,12},{5,13},{6,14},{7,15},{8,0},{9,1},... | collective-permute-start | bytes 55304 | tf_op jit(solution)/shard_map/ppermute | solution.py:21
  19.4 3.5 %collective-permute-start.9 = (bf16[2,8,576]{2,1,0:T(8,128)(2,1)S(1)}, bf16[2,8,576]{2,1,0:T(8,128)(2,1)S(1)}, u32[]{:S(2)}, u32[]{:S(2)}) collective-permute-start(bf16[2,8,576]{2,1,0:T(8,128)(2,1)S(1)} %get-tuple-element.14), channel_id=1, source_target_pairs={{0,10},{1,11},{2,8},{3,9},{4,14},{5,15},{6,12},{7,13},{8,2},{9,3},... | collective-permute-start | bytes 55304 | tf_op jit(solution)/shard_map/ppermute | solution.py:21
  23.0 3.5 %collective-permute-start.11 = (bf16[2,8,576]{2,1,0:T(8,128)(2,1)S(1)}, bf16[2,8,576]{2,1,0:T(8,128)(2,1)S(1)}, u32[]{:S(2)}, u32[]{:S(2)}) collective-permute-start(bf16[2,8,576]{2,1,0:T(8,128)(2,1)S(1)} %get-tuple-element.12), channel_id=1, source_target_pairs={{0,12},{1,13},{2,14},{3,15},{4,8},{5,9},{6,10},{7,11},{8,4},{9,5},... | collective-permute-start | bytes 55304 | tf_op jit(solution)/shard_map/ppermute | solution.py:21
  26.6 4.4 %collective-permute-start.13 = (bf16[2,8,576]{2,1,0:T(8,128)(2,1)S(1)}, bf16[2,8,576]{2,1,0:T(8,128)(2,1)S(1)}, u32[]{:S(2)}, u32[]{:S(2)}) collective-permute-start(bf16[2,8,576]{2,1,0:T(8,128)(2,1)S(1)} %get-tuple-element.10), channel_id=1, source_target_pairs={{0,14},{1,15},{2,12},{3,13},{4,10},{5,11},{6,8},{7,9},{8,6},{9,7},... | collective-permute-start | bytes 55304 | tf_op jit(solution)/shard_map/ppermute | solution.py:21
  31.6 1.7 %collective-permute-done.13 = bf16[2,8,576]{2,1,0:T(8,128)(2,1)S(1)} collective-permute-done((bf16[2,8,576]{2,1,0:T(8,128)(2,1)S(1)}, bf16[2,8,576]{2,1,0:T(8,128)(2,1)S(1)}, u32[]{:S(2)}, u32[]{:S(2)}) %collective-permute-start.13) | collective-permute-done | bytes 18464 | tf_op jit(solution)/shard_map/ppermute | solution.py:21
  33.3 3.7 %collective-permute-done.14 = bf16[2,8,576]{2,1,0:T(8,128)(2,1)S(1)} collective-permute-done((bf16[2,8,576]{2,1,0:T(8,128)(2,1)S(1)}, bf16[2,8,576]{2,1,0:T(8,128)(2,1)S(1)}, u32[]{:S(2)}, u32[]{:S(2)}) %collective-permute-start.14) | collective-permute-done | bytes 18464 | tf_op jit(solution)/shard_map/ppermute | solution.py:21
  36.9 1.0 %reshape.181 = bf16[8,2,2,8,12,48]{5,4,3,2,1,0:T(8,128)(2,1)S(1)} reshape(bf16[16,2,8,576]{3,2,1,0:T(8,128)(2,1)S(1)} %constant_dynamic-update-slice_fusion) | data formatting | bytes 589824 | tf_op jit(solution)/shard_map/reshape | solution.py:46
  43.5 1.2 %collective-permute-start.17 = (bf16[8,576]{1,0:T(8,128)(2,1)S(1)}, bf16[8,576]{1,0:T(8,128)(2,1)S(1)}, u32[]{:S(2)}, u32[]{:S(2)}) collective-permute-start(bf16[8,576]{1,0:T(8,128)(2,1)S(1)} %get-tuple-element.36), channel_id=1, source_target_pairs={{0,3},{1,2},{2,1},{3,0},{4,7},{5,6},{6,5},{7,4},{8,11},{9,10},{10,... | collective-permute-start | bytes 27656 | tf_op jit(solution)/shard_map/ppermute | solution.py:21
  44.7 1.8 %collective-permute-start.19 = (bf16[8,576]{1,0:T(8,128)(2,1)S(1)}, bf16[8,576]{1,0:T(8,128)(2,1)S(1)}, u32[]{:S(2)}, u32[]{:S(2)}) collective-permute-start(bf16[8,576]{1,0:T(8,128)(2,1)S(1)} %get-tuple-element.34), channel_id=1, source_target_pairs={{0,5},{1,4},{2,7},{3,6},{4,1},{5,0},{6,3},{7,2},{8,13},{9,12},{10,... | collective-permute-start | bytes 27656 | tf_op jit(solution)/shard_map/ppermute | solution.py:21
  46.8 2.3 %collective-permute-start.21 = (bf16[8,576]{1,0:T(8,128)(2,1)S(1)}, bf16[8,576]{1,0:T(8,128)(2,1)S(1)}, u32[]{:S(2)}, u32[]{:S(2)}) collective-permute-start(bf16[8,576]{1,0:T(8,128)(2,1)S(1)} %get-tuple-element.32), channel_id=1, source_target_pairs={{0,7},{1,6},{2,5},{3,4},{4,3},{5,2},{6,1},{7,0},{8,15},{9,14},{10,... | collective-permute-start | bytes 27656 | tf_op jit(solution)/shard_map/ppermute | solution.py:21
  49.2 2.7 %collective-permute-start.23 = (bf16[8,576]{1,0:T(8,128)(2,1)S(1)}, bf16[8,576]{1,0:T(8,128)(2,1)S(1)}, u32[]{:S(2)}, u32[]{:S(2)}) collective-permute-start(bf16[8,576]{1,0:T(8,128)(2,1)S(1)} %get-tuple-element.30), channel_id=1, source_target_pairs={{0,9},{1,8},{2,11},{3,10},{4,13},{5,12},{6,15},{7,14},{8,1},{9,0},... | collective-permute-start | bytes 27656 | tf_op jit(solution)/shard_map/ppermute | solution.py:21
  52.2 3.2 %collective-permute-start.25 = (bf16[8,576]{1,0:T(8,128)(2,1)S(1)}, bf16[8,576]{1,0:T(8,128)(2,1)S(1)}, u32[]{:S(2)}, u32[]{:S(2)}) collective-permute-start(bf16[8,576]{1,0:T(8,128)(2,1)S(1)} %get-tuple-element.28), channel_id=1, source_target_pairs={{0,11},{1,10},{2,9},{3,8},{4,15},{5,14},{6,13},{7,12},{8,3},{9,2},... | collective-permute-start | bytes 27656 | tf_op jit(solution)/shard_map/ppermute | solution.py:21
  55.9 3.1 %collective-permute-start.27 = (bf16[8,576]{1,0:T(8,128)(2,1)S(1)}, bf16[8,576]{1,0:T(8,128)(2,1)S(1)}, u32[]{:S(2)}, u32[]{:S(2)}) collective-permute-start(bf16[8,576]{1,0:T(8,128)(2,1)S(1)} %get-tuple-element.26), channel_id=1, source_target_pairs={{0,13},{1,12},{2,15},{3,14},{4,9},{5,8},{6,11},{7,10},{8,5},{9,4},... | collective-permute-start | bytes 27656 | tf_op jit(solution)/shard_map/ppermute | solution.py:21
  59.6 3.8 %collective-permute-start.29 = (bf16[8,576]{1,0:T(8,128)(2,1)S(1)}, bf16[8,576]{1,0:T(8,128)(2,1)S(1)}, u32[]{:S(2)}, u32[]{:S(2)}) collective-permute-start(bf16[8,576]{1,0:T(8,128)(2,1)S(1)} %get-tuple-element.24), channel_id=1, source_target_pairs={{0,15},{1,14},{2,13},{3,12},{4,11},{5,10},{6,9},{7,8},{8,7},{9,6},... | collective-permute-start | bytes 27656 | tf_op jit(solution)/shard_map/ppermute | solution.py:21
  63.5 2.0 %collective-permute-done.28 = bf16[8,576]{1,0:T(8,128)(2,1)S(1)} collective-permute-done((bf16[8,576]{1,0:T(8,128)(2,1)S(1)}, bf16[8,576]{1,0:T(8,128)(2,1)S(1)}, u32[]{:S(2)}, u32[]{:S(2)}) %collective-permute-start.28) | collective-permute-done | bytes 9248 | tf_op jit(solution)/shard_map/ppermute | solution.py:21
  65.6 1.0 %fusion.4 = bf16[576,128]{1,0:T(8,128)(2,1)} fusion(f32[576,128]{1,0:T(8,128)S(1)} %fusion.3, bf16[16,8,128]{2,1,0:T(8,128)(2,1)S(1)} %gather_fusion.2, bf16[16,8,576]{2,1,0:T(8,128)(2,1)S(1)} %constant_dynamic-update-slice_fusion.16, f32[16,8]{1,0:T(8,128)S(1)} %gather_fusion.1, f32[16,8]{1,0:T(8,128)S(1)} %gather_fusion, f32[576]{0:T(1024)S(1)} %add_rsqrt_fusion.1, ...), kind=kOutput, calls=%fused_computation.12 | convolution fusion | flops 19464192 | bytes 628224 | tf_op jit(solution)/shard_map/dot_general | solution.py:59
  (121 shorter events, 12.4 us)
Async XLA Ops:
  9.0 7.5 %collective-permute-start.1 = (bf16[2,8,576]{2,1,0:T(8,128)(2,1)S(1)}, bf16[2,8,576]{2,1,0:T(8,128)(2,1)S(1)}, u32[]{:S(2)}, u32[]{:S(2)}) collective-permute-start(bf16[2,8,576]{2,1,0:T(8,128)(2,1)S(1)} %get-tuple-element.22), channel_id=1, source_target_pairs={{0,2},{1,3},{2,0},{3,1},{4,6},{5,7},{6,4},{7,5},{8,10},{9,11},{10,... | collective-permute-start | bytes 55304 | tf_op jit(solution)/shard_map/ppermute | solution.py:21
  11.7 7.6 %collective-permute-start.3 = (bf16[2,8,576]{2,1,0:T(8,128)(2,1)S(1)}, bf16[2,8,576]{2,1,0:T(8,128)(2,1)S(1)}, u32[]{:S(2)}, u32[]{:S(2)}) collective-permute-start(bf16[2,8,576]{2,1,0:T(8,128)(2,1)S(1)} %get-tuple-element.20), channel_id=1, source_target_pairs={{0,4},{1,5},{2,6},{3,7},{4,0},{5,1},{6,2},{7,3},{8,12},{9,13},{10,... | collective-permute-start | bytes 55304 | tf_op jit(solution)/shard_map/ppermute | solution.py:21
  13.5 5.8 %collective-permute-start.4 = (bf16[2,8,576]{2,1,0:T(8,128)(2,1)S(1)}, bf16[2,8,576]{2,1,0:T(8,128)(2,1)S(1)}, u32[]{:S(2)}, u32[]{:S(2)}) collective-permute-start(bf16[2,8,576]{2,1,0:T(8,128)(2,1)S(1)} %get-tuple-element.19), channel_id=1, source_target_pairs={{0,5},{1,4},{2,7},{3,6},{4,1},{5,0},{6,3},{7,2},{8,13},{9,12},{10,... | collective-permute-start | bytes 55304 | tf_op jit(solution)/shard_map/ppermute | solution.py:21
  13.8 9.1 %collective-permute-start.5 = (bf16[2,8,576]{2,1,0:T(8,128)(2,1)S(1)}, bf16[2,8,576]{2,1,0:T(8,128)(2,1)S(1)}, u32[]{:S(2)}, u32[]{:S(2)}) collective-permute-start(bf16[2,8,576]{2,1,0:T(8,128)(2,1)S(1)} %get-tuple-element.18), channel_id=1, source_target_pairs={{0,6},{1,7},{2,4},{3,5},{4,2},{5,3},{6,0},{7,1},{8,14},{9,15},{10,... | collective-permute-start | bytes 55304 | tf_op jit(solution)/shard_map/ppermute | solution.py:21
  16.5 6.5 %collective-permute-start.6 = (bf16[2,8,576]{2,1,0:T(8,128)(2,1)S(1)}, bf16[2,8,576]{2,1,0:T(8,128)(2,1)S(1)}, u32[]{:S(2)}, u32[]{:S(2)}) collective-permute-start(bf16[2,8,576]{2,1,0:T(8,128)(2,1)S(1)} %get-tuple-element.17), channel_id=1, source_target_pairs={{0,7},{1,6},{2,5},{3,4},{4,3},{5,2},{6,1},{7,0},{8,15},{9,14},{10,... | collective-permute-start | bytes 55304 | tf_op jit(solution)/shard_map/ppermute | solution.py:21
  16.6 9.9 %collective-permute-start.7 = (bf16[2,8,576]{2,1,0:T(8,128)(2,1)S(1)}, bf16[2,8,576]{2,1,0:T(8,128)(2,1)S(1)}, u32[]{:S(2)}, u32[]{:S(2)}) collective-permute-start(bf16[2,8,576]{2,1,0:T(8,128)(2,1)S(1)} %get-tuple-element.16), channel_id=1, source_target_pairs={{0,8},{1,9},{2,10},{3,11},{4,12},{5,13},{6,14},{7,15},{8,0},{9,1},... | collective-permute-start | bytes 55304 | tf_op jit(solution)/shard_map/ppermute | solution.py:21
  19.3 7.3 %collective-permute-start.8 = (bf16[2,8,576]{2,1,0:T(8,128)(2,1)S(1)}, bf16[2,8,576]{2,1,0:T(8,128)(2,1)S(1)}, u32[]{:S(2)}, u32[]{:S(2)}) collective-permute-start(bf16[2,8,576]{2,1,0:T(8,128)(2,1)S(1)} %get-tuple-element.15), channel_id=1, source_target_pairs={{0,9},{1,8},{2,11},{3,10},{4,13},{5,12},{6,15},{7,14},{8,1},{9,0},... | collective-permute-start | bytes 55304 | tf_op jit(solution)/shard_map/ppermute | solution.py:21
  19.4 11.6 %collective-permute-start.9 = (bf16[2,8,576]{2,1,0:T(8,128)(2,1)S(1)}, bf16[2,8,576]{2,1,0:T(8,128)(2,1)S(1)}, u32[]{:S(2)}, u32[]{:S(2)}) collective-permute-start(bf16[2,8,576]{2,1,0:T(8,128)(2,1)S(1)} %get-tuple-element.14), channel_id=1, source_target_pairs={{0,10},{1,11},{2,8},{3,9},{4,14},{5,15},{6,12},{7,13},{8,2},{9,3},... | collective-permute-start | bytes 55304 | tf_op jit(solution)/shard_map/ppermute | solution.py:21
  22.8 8.3 %collective-permute-start.10 = (bf16[2,8,576]{2,1,0:T(8,128)(2,1)S(1)}, bf16[2,8,576]{2,1,0:T(8,128)(2,1)S(1)}, u32[]{:S(2)}, u32[]{:S(2)}) collective-permute-start(bf16[2,8,576]{2,1,0:T(8,128)(2,1)S(1)} %get-tuple-element.13), channel_id=1, source_target_pairs={{0,11},{1,10},{2,9},{3,8},{4,15},{5,14},{6,13},{7,12},{8,3},{9,2},... | collective-permute-start | bytes 55304 | tf_op jit(solution)/shard_map/ppermute | solution.py:21
  23.0 8.2 %collective-permute-start.11 = (bf16[2,8,576]{2,1,0:T(8,128)(2,1)S(1)}, bf16[2,8,576]{2,1,0:T(8,128)(2,1)S(1)}, u32[]{:S(2)}, u32[]{:S(2)}) collective-permute-start(bf16[2,8,576]{2,1,0:T(8,128)(2,1)S(1)} %get-tuple-element.12), channel_id=1, source_target_pairs={{0,12},{1,13},{2,14},{3,15},{4,8},{5,9},{6,10},{7,11},{8,4},{9,5},... | collective-permute-start | bytes 55304 | tf_op jit(solution)/shard_map/ppermute | solution.py:21
  26.6 6.6 %collective-permute-start.13 = (bf16[2,8,576]{2,1,0:T(8,128)(2,1)S(1)}, bf16[2,8,576]{2,1,0:T(8,128)(2,1)S(1)}, u32[]{:S(2)}, u32[]{:S(2)}) collective-permute-start(bf16[2,8,576]{2,1,0:T(8,128)(2,1)S(1)} %get-tuple-element.10), channel_id=1, source_target_pairs={{0,14},{1,15},{2,12},{3,13},{4,10},{5,11},{6,8},{7,9},{8,6},{9,7},... | collective-permute-start | bytes 55304 | tf_op jit(solution)/shard_map/ppermute | solution.py:21
  31.0 5.9 %collective-permute-start.14 = (bf16[2,8,576]{2,1,0:T(8,128)(2,1)S(1)}, bf16[2,8,576]{2,1,0:T(8,128)(2,1)S(1)}, u32[]{:S(2)}, u32[]{:S(2)}) collective-permute-start(bf16[2,8,576]{2,1,0:T(8,128)(2,1)S(1)} %get-tuple-element.9), channel_id=1, source_target_pairs={{0,15},{1,14},{2,13},{3,12},{4,11},{5,10},{6,9},{7,8},{8,7},{9,6},... | collective-permute-start | bytes 55304 | tf_op jit(solution)/shard_map/ppermute | solution.py:21
  40.8 5.7 %collective-permute-start.15 = (bf16[8,576]{1,0:T(8,128)(2,1)S(1)}, bf16[8,576]{1,0:T(8,128)(2,1)S(1)}, u32[]{:S(2)}, u32[]{:S(2)}) collective-permute-start(bf16[8,576]{1,0:T(8,128)(2,1)S(1)} %get-tuple-element.38), channel_id=1, source_target_pairs={{0,1},{1,0},{2,3},{3,2},{4,5},{5,4},{6,7},{7,6},{8,9},{9,8},{10,11... | collective-permute-start | bytes 27656 | tf_op jit(solution)/shard_map/ppermute | solution.py:21
  44.7 7.2 %collective-permute-start.19 = (bf16[8,576]{1,0:T(8,128)(2,1)S(1)}, bf16[8,576]{1,0:T(8,128)(2,1)S(1)}, u32[]{:S(2)}, u32[]{:S(2)}) collective-permute-start(bf16[8,576]{1,0:T(8,128)(2,1)S(1)} %get-tuple-element.34), channel_id=1, source_target_pairs={{0,5},{1,4},{2,7},{3,6},{4,1},{5,0},{6,3},{7,2},{8,13},{9,12},{10,... | collective-permute-start | bytes 27656 | tf_op jit(solution)/shard_map/ppermute | solution.py:21
  46.5 5.7 %collective-permute-start.20 = (bf16[8,576]{1,0:T(8,128)(2,1)S(1)}, bf16[8,576]{1,0:T(8,128)(2,1)S(1)}, u32[]{:S(2)}, u32[]{:S(2)}) collective-permute-start(bf16[8,576]{1,0:T(8,128)(2,1)S(1)} %get-tuple-element.33), channel_id=1, source_target_pairs={{0,6},{1,7},{2,4},{3,5},{4,2},{5,3},{6,0},{7,1},{8,14},{9,15},{10,... | collective-permute-start | bytes 27656 | tf_op jit(solution)/shard_map/ppermute | solution.py:21
  46.8 8.6 %collective-permute-start.21 = (bf16[8,576]{1,0:T(8,128)(2,1)S(1)}, bf16[8,576]{1,0:T(8,128)(2,1)S(1)}, u32[]{:S(2)}, u32[]{:S(2)}) collective-permute-start(bf16[8,576]{1,0:T(8,128)(2,1)S(1)} %get-tuple-element.32), channel_id=1, source_target_pairs={{0,7},{1,6},{2,5},{3,4},{4,3},{5,2},{6,1},{7,0},{8,15},{9,14},{10,... | collective-permute-start | bytes 27656 | tf_op jit(solution)/shard_map/ppermute | solution.py:21
  49.1 6.8 %collective-permute-start.22 = (bf16[8,576]{1,0:T(8,128)(2,1)S(1)}, bf16[8,576]{1,0:T(8,128)(2,1)S(1)}, u32[]{:S(2)}, u32[]{:S(2)}) collective-permute-start(bf16[8,576]{1,0:T(8,128)(2,1)S(1)} %get-tuple-element.31), channel_id=1, source_target_pairs={{0,8},{1,9},{2,10},{3,11},{4,12},{5,13},{6,14},{7,15},{8,0},{9,1},... | collective-permute-start | bytes 27656 | tf_op jit(solution)/shard_map/ppermute | solution.py:21
  49.2 9.8 %collective-permute-start.23 = (bf16[8,576]{1,0:T(8,128)(2,1)S(1)}, bf16[8,576]{1,0:T(8,128)(2,1)S(1)}, u32[]{:S(2)}, u32[]{:S(2)}) collective-permute-start(bf16[8,576]{1,0:T(8,128)(2,1)S(1)} %get-tuple-element.30), channel_id=1, source_target_pairs={{0,9},{1,8},{2,11},{3,10},{4,13},{5,12},{6,15},{7,14},{8,1},{9,0},... | collective-permute-start | bytes 27656 | tf_op jit(solution)/shard_map/ppermute | solution.py:21
  51.9 7.7 %collective-permute-start.24 = (bf16[8,576]{1,0:T(8,128)(2,1)S(1)}, bf16[8,576]{1,0:T(8,128)(2,1)S(1)}, u32[]{:S(2)}, u32[]{:S(2)}) collective-permute-start(bf16[8,576]{1,0:T(8,128)(2,1)S(1)} %get-tuple-element.29), channel_id=1, source_target_pairs={{0,10},{1,11},{2,8},{3,9},{4,14},{5,15},{6,12},{7,13},{8,2},{9,3},... | collective-permute-start | bytes 27656 | tf_op jit(solution)/shard_map/ppermute | solution.py:21
  52.2 11.2 %collective-permute-start.25 = (bf16[8,576]{1,0:T(8,128)(2,1)S(1)}, bf16[8,576]{1,0:T(8,128)(2,1)S(1)}, u32[]{:S(2)}, u32[]{:S(2)}) collective-permute-start(bf16[8,576]{1,0:T(8,128)(2,1)S(1)} %get-tuple-element.28), channel_id=1, source_target_pairs={{0,11},{1,10},{2,9},{3,8},{4,15},{5,14},{6,13},{7,12},{8,3},{9,2},... | collective-permute-start | bytes 27656 | tf_op jit(solution)/shard_map/ppermute | solution.py:21
  55.4 8.0 %collective-permute-start.26 = (bf16[8,576]{1,0:T(8,128)(2,1)S(1)}, bf16[8,576]{1,0:T(8,128)(2,1)S(1)}, u32[]{:S(2)}, u32[]{:S(2)}) collective-permute-start(bf16[8,576]{1,0:T(8,128)(2,1)S(1)} %get-tuple-element.27), channel_id=1, source_target_pairs={{0,12},{1,13},{2,14},{3,15},{4,8},{5,9},{6,10},{7,11},{8,4},{9,5},... | collective-permute-start | bytes 27656 | tf_op jit(solution)/shard_map/ppermute | solution.py:21
  55.9 7.5 %collective-permute-start.27 = (bf16[8,576]{1,0:T(8,128)(2,1)S(1)}, bf16[8,576]{1,0:T(8,128)(2,1)S(1)}, u32[]{:S(2)}, u32[]{:S(2)}) collective-permute-start(bf16[8,576]{1,0:T(8,128)(2,1)S(1)} %get-tuple-element.26), channel_id=1, source_target_pairs={{0,13},{1,12},{2,15},{3,14},{4,9},{5,8},{6,11},{7,10},{8,5},{9,4},... | collective-permute-start | bytes 27656 | tf_op jit(solution)/shard_map/ppermute | solution.py:21
  59.0 6.5 %collective-permute-start.28 = (bf16[8,576]{1,0:T(8,128)(2,1)S(1)}, bf16[8,576]{1,0:T(8,128)(2,1)S(1)}, u32[]{:S(2)}, u32[]{:S(2)}) collective-permute-start(bf16[8,576]{1,0:T(8,128)(2,1)S(1)} %get-tuple-element.25), channel_id=1, source_target_pairs={{0,14},{1,15},{2,12},{3,13},{4,10},{5,11},{6,8},{7,9},{8,6},{9,7},... | collective-permute-start | bytes 27656 | tf_op jit(solution)/shard_map/ppermute | solution.py:21
  59.6 5.9 %collective-permute-start.29 = (bf16[8,576]{1,0:T(8,128)(2,1)S(1)}, bf16[8,576]{1,0:T(8,128)(2,1)S(1)}, u32[]{:S(2)}, u32[]{:S(2)}) collective-permute-start(bf16[8,576]{1,0:T(8,128)(2,1)S(1)} %get-tuple-element.24), channel_id=1, source_target_pairs={{0,15},{1,14},{2,13},{3,12},{4,11},{5,10},{6,9},{7,8},{8,7},{9,6},... | collective-permute-start | bytes 27656 | tf_op jit(solution)/shard_map/ppermute | solution.py:21
  (11 other events, 43.3 us)

commit v2 on v1

v2 whole, which is shorter than its diff:
```python
import jax
import jax.numpy as jnp
from jax import lax
from jax.sharding import PartitionSpec as P

epsilon = 1e-05


def layer_norm(values, gain, bias, axis):
    mean = jnp.mean(values, axis=axis, keepdims=True)
    centred = values - mean
    variance = jnp.mean(centred * centred, axis=axis, keepdims=True)
    return centred * lax.rsqrt(variance + epsilon) * gain + bias


def per_device(rows, cols, pair, token_mask, gain_in, bias_in, w_in, w_gate, gain_out, bias_out, w_out):
    row_count, col_count, channels = pair.shape
    hidden = w_out.shape[0]
    share = hidden // rows
    tokens = row_count * col_count
    row_start = lax.axis_index("row") * row_count
    col_start = lax.axis_index("col") * col_count
    mask_float = token_mask.astype(jnp.float32)
    mask_rows = lax.dynamic_slice_in_dim(mask_float, row_start, row_count)
    mask_cols = lax.dynamic_slice_in_dim(mask_float, col_start, col_count)
    pair_mask = (mask_rows[:, None] * mask_cols[None, :]).reshape(1, tokens)
    flat = pair.reshape(tokens, channels).astype(jnp.float32)
    normed = layer_norm(flat, gain_in, bias_in, -1).astype(jnp.bfloat16)
    projected = lax.dot_general(w_in, normed, (((0,), (1,)), ((), ())), preferred_element_type=jnp.float32)
    projected = projected.reshape(2, 2, hidden, tokens)
    sides = (pair_mask * jax.nn.sigmoid(projected[:, 0]) * projected[:, 1]).astype(jnp.bfloat16)
    sides = sides.reshape(2, rows, share, tokens).transpose(1, 0, 2, 3)
    gate = jax.nn.sigmoid(jnp.dot(normed, w_gate, preferred_element_type=jnp.float32))
    got = lax.all_to_all(sides, "row", split_axis=0, concat_axis=0, tiled=True)
    left = lax.all_gather(got[:, 0], "col")
    left = left.reshape(cols, rows, share, row_count, col_count).transpose(2, 1, 3, 0, 4)
    left = left.reshape(share, rows * row_count, cols * col_count)
    right = got[:, 1].reshape(rows, share, row_count, col_count).transpose(1, 0, 2, 3)
    right = right.reshape(share, rows * row_count, col_count)
    total = jnp.einsum("cki,ckj->cij", left, right, preferred_element_type=jnp.float32).astype(jnp.bfloat16)
    total = total.reshape(share, rows, row_count, col_count).transpose(1, 0, 2, 3)
    total = total.reshape(rows, share, tokens)
    total = lax.all_to_all(total, "row", split_axis=0, concat_axis=0, tiled=True)
    total = total.reshape(hidden, tokens).astype(jnp.float32)
    summed_norm = layer_norm(total, gain_out[:, None], bias_out[:, None], 0).astype(jnp.bfloat16)
    output = lax.dot_general(summed_norm, w_out, (((0,), (0,)), ((), ())), preferred_element_type=jnp.float32)
    return (gate * output).astype(jnp.bfloat16).reshape(row_count, col_count, channels)


def solution(mesh):
    import functools

    in_specs = (P(("groups", "row"), "col", None), P("groups"), P(), P(), P(), P(), P(), P(), P())
    out_specs = P(("groups", "row"), "col", None)
    body = functools.partial(per_device, mesh.shape["row"], mesh.shape["col"])
    return jax.shard_map(body, mesh=mesh, in_specs=in_specs, out_specs=out_specs, check_vma=False)
```

time: 66.8 us -> 46.6 us (0.70)
  starting transfers between devices: 42.7 us -> 3.51 us
  blocking collectives: 0 us -> 20 us
  local copies, waits for them, and re-layouts: 9.06 us -> 8.34 us
    ppermute x30 -> x0, starting transfers between devices: 42.7 us -> none  [exchange(): lax.ppermute(piece, AXES, [(i, i ^ step) for i in range(devices)])]
    all_to_all x0 -> x1, blocking collectives: none -> 18 us  [per_device(): got = lax.all_to_all(sides, 'row', split_axis=0, concat_axis=0, tiled=True)]
    ppermute x30 -> x0, waiting for transfers between devices: 7.8 us -> none  [exchange(): lax.ppermute(piece, AXES, [(i, i ^ step) for i in range(devices)])]
    all_to_all x0 -> x1, waiting for transfers between devices: none -> 7.75 us  [per_device(): lax.all_to_all(total, 'row', split_axis=0, concat_axis=0, tiled=True)]
    all_to_all x0 -> x1, starting transfers between devices: none -> 3.51 us  [per_device(): lax.all_to_all(total, 'row', split_axis=0, concat_axis=0, tiled=True)]
    all_gather x0 -> x1, blocking collectives: none -> 2.04 us  [per_device(): left = lax.all_gather(got[:, 0], 'col')]
    gather x3 -> x0, local copies, waits for them, and re-layouts: 1.71 us -> none  [the longest x1 0.58 us: per_device(): w_out.reshape(devices, share, channels)[order].reshape(hidden, channels)]
    transpose x0 -> x4, local copies, waits for them, and re-layouts: none -> 1.47 us  [the longest x1 1.22 us: per_device(): left.reshape(cols, rows, share, row_count, col_count)]
  transfers between devices with their start and end apart: 30 -> 1, of which waited for: 4 -> 1; matrix products, arithmetic and copies ran while one was open for 4% -> 0% of each run, Pallas kernels for 0% -> 0%
where the time goes in v2:
time: 46.6 us; the launch traced here: 46.2 us
  blocking collectives  20 us (43%)
  local copies, waits for them, and re-layouts  8.34 us (18%)
  waiting for transfers between devices  7.75 us (17%)
  other arithmetic  4.67 us (10%)
  starting transfers between devices  3.51 us (8%)
  matrix products  1.69 us (4%)
    all_to_all x1, blocking collectives, per_device(): got = lax.all_to_all(sides, 'row', split_axis=0, concat_axis=0, tiled=True)  18 us
    all_to_all x1, waiting for transfers between devices, per_device(): lax.all_to_all(total, 'row', split_axis=0, concat_axis=0, tiled=True)  7.75 us
    all_to_all x1, starting transfers between devices, per_device(): lax.all_to_all(total, 'row', split_axis=0, concat_axis=0, tiled=True)  3.51 us
    all_gather x1, blocking collectives, per_device(): left = lax.all_gather(got[:, 0], 'col')  2.04 us
    unnamed x12, local copies, waits for them, and re-layouts  1.58 us
    reduce_sum x2, other arithmetic, layer_norm(): variance = jnp.mean(centred * centred, axis=axis, keepdims=True)  1.25 us
    transpose x1, local copies, waits for them, and re-layouts, per_device(): left.reshape(cols, rows, share, row_count, col_count)  1.22 us
    convert_element_type x1, other arithmetic, per_device(): normed = layer_norm(flat, gain_in, bias_in, -1).astype(jnp.bfloat16)  1.16 us
  transfers between devices with their start and end apart: 1, of which 1 were waited for; matrix products, arithmetic and copies ran while one was open for 0% of the time, Pallas kernels for 0%

profile of v2, /device:TPU:0, one launch (start us, length us, event | category | flops | bytes accessed | tf_op | source)
XLA Modules:
  0.0 46.2 jit_solution(4150408870790071334)
XLA Ops:
  0.0 1.1 %convert_reduce_fusion.1 = f32[12,48]{1,0:T(8,128)S(1)} fusion(bf16[12,48,128]{2,1,0:T(8,128)(2,1)} %param.9), kind=kLoop, calls=%fused_computation.25 | loop fusion | flops 146880 | bytes 149760 | tf_op jit(solution)/shard_map/reduce_sum | solution.py:10
  1.1 1.2 %multiply_reduce_fusion.1 = f32[12,48]{1,0:T(8,128)S(1)} fusion(bf16[12,48,128]{2,1,0:T(8,128)(2,1)} %param.9, f32[12,48]{1,0:T(8,128)S(1)} %broadcast_multiply_fusion.1), kind=kLoop, calls=%fused_computation.23 | loop fusion | flops 294336 | bytes 152064 | tf_op jit(solution)/shard_map/reduce_sum | solution.py:12
  2.4 0.7 %convert_element_type.43 = f32[96]{0:T(128)S(1)} convert(s32[96]{0:T(128)} %param.10) | non-fusion elementwise | flops 96 | bytes 768 | tf_op jit(solution)/shard_map/convert_element_type | solution.py:23
  3.4 1.2 %fusion.13 = bf16[576,128]{1,0:T(8,128)(2,1)S(1)} fusion(bf16[12,48,128]{2,1,0:T(8,128)(2,1)} %param.9, f32[128]{0:T(128)} %param.12, f32[128]{0:T(128)} %param.11, f32[576]{0:T(1024)S(1)} %rsqrt.20, f32[576]{0:T(1024)S(1)} %div.25), kind=kLoop, calls=%fused_computation.22 | loop fusion | flops 442368 | bytes 300544 | tf_op jit(solution)/shard_map/convert_element_type | solution.py:28
  4.6 0.3 convolution_bitcast_fusion
  4.9 0.8 %reshape.105 = f32[2,2,128,576]{2,1,0,3:T(2,128)S(1)} reshape(f32[512,576]{0,1:T(8,128)S(1)} %convolution_bitcast_fusion) | data formatting | bytes 2359296 | tf_op jit(solution)/shard_map/reshape | solution.py:30
  5.7 0.9 %fusion.14 = (f32[2,1,128,576]{2,1,0,3:T(1,128)S(1)}, f32[2,1,128,576]{2,1,0,3:T(1,128)S(1)}) fusion(f32[2,2,128,576]{2,1,0,3:T(2,128)S(1)} %reshape.105), kind=kLoop, calls=%fused_computation.31 | loop fusion | bytes 2359296 | tf_op jit(solution)/shard_map/slice | solution.py:31
  6.6 0.8 %copy.25 = f32[2,1,128,576]{3,2,0,1:T(8,128)S(1)} copy(f32[2,1,128,576]{2,1,0,3:T(1,128)S(1)} %get-tuple-element.5) | data formatting | bytes 1179648
  7.4 0.2 add_divide_fusion
  7.6 0.8 %copy.26 = f32[2,1,128,576]{3,2,0,1:T(8,128)S(1)} copy(f32[2,1,128,576]{2,1,0,3:T(1,128)S(1)} %get-tuple-element.6) | data formatting | bytes 1179648
  8.5 18.0 %all_to_all.10 = bf16[8,2,16,576]{3,2,1,0:T(8,128)(2,1)S(1)} all-to-all(bf16[8,2,16,576]{3,2,1,0:T(8,128)(2,1)S(1)} %copy.19), channel_id=1, replica_groups=mesh['groups'=2,'row'=8,'col'=2] {'row'}, dimensions={0} | all-to-all | bytes 589824 | tf_op jit(solution)/shard_map/all_to_all | solution.py:34
  26.5 2.0 %all-gather = bf16[16,1,16,576]{3,2,1,0:T(8,128)(2,1)S(1)} all-gather(bf16[8,1,16,576]{3,2,1,0:T(8,128)(2,1)S(1)} %get-tuple-element.8), channel_id=2, replica_groups=mesh['groups'=2,'row'=8,'col'=2] {'col'}, dimensions={0}, use_global_device_ids=true | all-gather | bytes 442368 | tf_op jit(solution)/shard_map/all_gather | solution.py:35
  28.5 1.0 %reshape.106 = bf16[2,8,16,12,48]{4,3,2,1,0:T(8,128)(2,1)S(1)} reshape(bf16[16,1,16,576]{3,2,1,0:T(8,128)(2,1)S(1)} %all-gather) | data formatting | bytes 589824 | tf_op jit(solution)/shard_map/reshape | solution.py:36
  29.5 1.2 %copy.20 = bf16[16,8,12,2,48]{4,3,2,1,0:T(2,128)(2,1)S(1)} copy(bf16[16,8,12,2,48]{4,2,0,1,3:T(8,128)(2,1)S(1)} %bitcast.46) | data formatting | bytes 589824 | tf_op jit(solution)/shard_map/transpose | solution.py:36
  30.8 0.3 reshape.107
  31.1 0.5 %reshape_squeeze.3 = bf16[8,16,12,48]{3,2,1,0:T(8,128)(2,1)S(1)} reshape(bf16[8,1,16,576]{3,2,1,0:T(8,128)(2,1)S(1)} %get-tuple-element.7) | data formatting | bytes 294912 | tf_op jit(solution)/shard_map/reshape;squeeze | solution.py:38
  31.7 0.3 convolution_convert_fusion
  32.0 0.3 copy.23
  32.5 1.0 %reshape.110 = bf16[8,16,576]{2,1,0:T(8,128)(2,1)} reshape(bf16[8,16,12,48]{3,2,1,0:T(8,128)(2,1)S(1)} %copy.24) | data formatting | bytes 294912 | tf_op jit(solution)/shard_map/reshape | solution.py:42
  33.6 3.5 %all-to-all-start.1 = ((bf16[8,16,576]{2,1,0:T(8,128)(2,1)}), bf16[8,16,576]{2,1,0:T(8,128)(2,1)S(1)}, u32[]{:S(2)}, u32[]{:S(2)}) async-start(bf16[8,16,576]{2,1,0:T(8,128)(2,1)} %reshape.110), calls=%async_computation.1 | async-start | bytes 327680 | tf_op jit(solution)/shard_map/all_to_all | solution.py:43
  37.1 0.2 fusion.2
  37.3 7.7 %all-to-all-done.1 = bf16[8,16,576]{2,1,0:T(8,128)(2,1)S(1)} async-done(((bf16[8,16,576]{2,1,0:T(8,128)(2,1)}), bf16[8,16,576]{2,1,0:T(8,128)(2,1)S(1)}, u32[]{:S(2)}, u32[]{:S(2)}) %all-to-all-start.1) | async-done | bytes 147488 | tf_op jit(solution)/shard_map/all_to_all | solution.py:43
  45.2 0.1 fusion.9
  45.3 0.9 %fusion.3 = bf16[576,128]{1,0:T(8,128)(2,1)} fusion(f32[576,128]{1,0:T(8,128)S(1)} %fusion.2, bf16[128,576]{1,0:T(8,128)(2,1)S(1)} %fusion.9, bf16[128,128]{1,0:T(8,128)(2,1)S(1)} %copy-done.1), kind=kOutput, calls=%fused_computation.7 | convolution fusion | flops 19021824 | bytes 622592 | tf_op jit(solution)/shard_map/dot_general | solution.py:46
  (27 shorter events, 1.0 us)
Async XLA Ops:
  0.0 4.6 %copy-start = (bf16[128,512]{1,0:T(8,128)(2,1)S(1)}, bf16[128,512]{1,0:T(8,128)(2,1)}, u32[]{:S(2)}) copy-start(bf16[128,512]{1,0:T(8,128)(2,1)} %param.13) | copy-start | bytes 393220
  32.0 5.1 %copy-start.4 = (bf16[128,128]{1,0:T(8,128)(2,1)S(1)}, bf16[128,128]{1,0:T(8,128)(2,1)}, u32[]{:S(2)}) copy-start(bf16[128,128]{1,0:T(8,128)(2,1)} %param.14) | copy-start | bytes 98308
  32.5 12.7 %copy-start.2 = (f32[128]{0:T(128)S(1)}, f32[128]{0:T(128)}, u32[]{:S(2)}) copy-start(f32[128]{0:T(128)} %param.16) | copy-start | bytes 1540
  32.5 12.7 %copy-start.3 = (f32[128]{0:T(128)S(1)}, f32[128]{0:T(128)}, u32[]{:S(2)}) copy-start(f32[128]{0:T(128)} %param.15) | copy-start | bytes 1540
  33.5 11.8 %copy-start.1 = (bf16[128,128]{1,0:T(8,128)(2,1)S(1)}, bf16[128,128]{1,0:T(8,128)(2,1)}, u32[]{:S(2)}) copy-start(bf16[128,128]{1,0:T(8,128)(2,1)} %param.17) | copy-start | bytes 98308
  33.6 11.5 %all-to-all-start.1 = ((bf16[8,16,576]{2,1,0:T(8,128)(2,1)}), bf16[8,16,576]{2,1,0:T(8,128)(2,1)S(1)}, u32[]{:S(2)}, u32[]{:S(2)}) async-start(bf16[8,16,576]{2,1,0:T(8,128)(2,1)} %reshape.110), calls=%async_computation.1 | async-start | bytes 327680 | tf_op jit(solution)/shard_map/all_to_all | solution.py:43

commit v3 on v1

v3 whole, which is shorter than its diff:
```python
import functools

import jax
import jax.numpy as jnp
from jax import lax
from jax.experimental import pallas as pl
from jax.experimental.pallas import tpu as pltpu
from jax.sharding import PartitionSpec as P

epsilon = 1e-05
AXES = ("row", "col")
VMEM = pl.BlockSpec(memory_space=pltpu.VMEM)
LIMIT = pltpu.CompilerParams(vmem_limit_bytes=32 * 1024 * 1024)


def sigmoid(x):
    return 0.5 * jnp.tanh(0.5 * x) + 0.5


def layer_norm(values, gain, bias, axis):
    mean = jnp.mean(values, axis=axis, keepdims=True)
    centred = values - mean
    variance = jnp.mean(centred * centred, axis=axis, keepdims=True)
    return centred * lax.rsqrt(variance + epsilon) * gain + bias


def column(row):
    n = row.shape[1]
    eye = lax.broadcasted_iota(jnp.int32, (n, n), 0) == lax.broadcasted_iota(jnp.int32, (n, n), 1)
    return jnp.sum(jnp.where(eye, row, 0.0), axis=1, keepdims=True)


def project_kernel(pair_ref, gain_ref, bias_ref, w_ref, sides_ref, normed_ref):
    devices, both, tokens = sides_ref.shape
    channels = pair_ref.shape[2]
    hidden = w_ref.shape[1] // 4
    share = both // 2
    flat = pair_ref[...].reshape(tokens, channels).astype(jnp.float32)
    normed = layer_norm(flat, gain_ref[...], bias_ref[...], -1).astype(jnp.bfloat16)
    normed_ref[...] = normed
    projected = lax.dot_general(w_ref[...], normed, (((0,), (1,)), ((), ())), preferred_element_type=jnp.float32)
    left = sigmoid(projected[:hidden]) * projected[hidden : 2 * hidden]
    right = sigmoid(projected[2 * hidden : 3 * hidden]) * projected[3 * hidden :]
    sides = jnp.concatenate([left.reshape(devices, share, tokens), right.reshape(devices, share, tokens)], axis=1)
    sides_ref[...] = sides.astype(jnp.bfloat16)


def triangle_kernel(rows, cols, row_count, col_count, got_ref, mask_ref, total_ref, wide_ref, sum_ref, flat_ref):
    both = got_ref.shape[1]
    share = both // 2
    length = rows * row_count
    for source in range(rows * cols):
        row, col = divmod(source, cols)
        piece = got_ref[source].astype(jnp.float32)
        for k in range(row_count):
            at = (row * row_count + k) * both
            wide_ref[at : at + both, col * col_count : (col + 1) * col_count] = piece[:, k * col_count : (k + 1) * col_count]
    mask_row = mask_ref[...].astype(jnp.float32)
    mask = column(mask_row) * mask_row
    for c in range(share):
        left = (wide_ref[pl.ds(c, length, stride=both), 0:length] * mask).astype(jnp.bfloat16)
        right = (wide_ref[pl.ds(share + c, length, stride=both), 0:length] * mask).astype(jnp.bfloat16)
        sum_ref[pl.ds(c, length, stride=share), 0:length] = lax.dot_general(
            left, right, (((0,), (0,)), ((), ())), preferred_element_type=jnp.float32
        )
    for target in range(rows * cols):
        row, col = divmod(target, cols)
        for i in range(row_count):
            at = (row * row_count + i) * share
            flat_ref[target * share : (target + 1) * share, i * col_count : (i + 1) * col_count] = sum_ref[
                at : at + share, col * col_count : (col + 1) * col_count
            ]
        total_ref[target] = flat_ref[target * share : (target + 1) * share, :].astype(jnp.bfloat16)


def output_kernel(total_ref, gate_ref, gain_ref, bias_ref, w_ref, out_ref):
    devices, share, tokens = total_ref.shape
    total = total_ref[...].astype(jnp.float32).reshape(devices * share, tokens)
    normed = layer_norm(total, column(gain_ref[...]), column(bias_ref[...]), 0).astype(jnp.bfloat16)
    output = lax.dot_general(normed, w_ref[...], (((0,), (0,)), ((), ())), preferred_element_type=jnp.float32)
    out_ref[...] = (sigmoid(gate_ref[...]) * output).astype(jnp.bfloat16).reshape(out_ref.shape)


def per_device(rows, cols, pair, token_mask, gain_in, bias_in, w_in, w_gate, gain_out, bias_out, w_out):
    row_count, col_count, channels = pair.shape
    hidden = w_out.shape[0]
    devices = rows * cols
    share = hidden // devices
    tokens = row_count * col_count
    length = rows * row_count
    sides, normed = pl.pallas_call(
        project_kernel,
        out_shape=(
            jax.ShapeDtypeStruct((devices, 2 * share, tokens), jnp.bfloat16),
            jax.ShapeDtypeStruct((tokens, channels), jnp.bfloat16),
        ),
        in_specs=[VMEM] * 4,
        out_specs=(VMEM, VMEM),
        compiler_params=LIMIT,
    )(pair, gain_in.reshape(1, channels), bias_in.reshape(1, channels), w_in)
    got = lax.all_to_all(sides, AXES, split_axis=0, concat_axis=0, tiled=True)
    total = pl.pallas_call(
        functools.partial(triangle_kernel, rows, cols, row_count, col_count),
        out_shape=jax.ShapeDtypeStruct((devices, share, tokens), jnp.bfloat16),
        in_specs=[VMEM] * 2,
        out_specs=VMEM,
        scratch_shapes=[
            pltpu.VMEM((length * 2 * share, 128), jnp.float32),
            pltpu.VMEM((length * share, 128), jnp.float32),
            pltpu.VMEM((hidden, tokens), jnp.float32),
        ],
        compiler_params=LIMIT,
    )(got, token_mask.reshape(1, length))
    gate = jnp.dot(normed, w_gate, preferred_element_type=jnp.float32)
    total = lax.all_to_all(total, AXES, split_axis=0, concat_axis=0, tiled=True)
    return pl.pallas_call(
        output_kernel,
        out_shape=jax.ShapeDtypeStruct(pair.shape, jnp.bfloat16),
        in_specs=[VMEM] * 5,
        out_specs=VMEM,
        compiler_params=LIMIT,
    )(total, gate, gain_out.reshape(1, hidden), bias_out.reshape(1, hidden), w_out)


def plain_per_device(rows, cols, pair, token_mask, gain_in, bias_in, w_in, w_gate, gain_out, bias_out, w_out):
    row_count, col_count, channels = pair.shape
    hidden = w_out.shape[0]
    devices = rows * cols
    share = hidden // devices
    tokens = row_count * col_count
    row_start = lax.axis_index("row") * row_count
    col_start = lax.axis_index("col") * col_count
    mask_float = token_mask.astype(jnp.float32)
    mask_rows = lax.dynamic_slice_in_dim(mask_float, row_start, row_count)
    mask_cols = lax.dynamic_slice_in_dim(mask_float, col_start, col_count)
    pair_mask = (mask_rows[:, None] * mask_cols[None, :]).reshape(1, tokens)
    flat = pair.reshape(tokens, channels).astype(jnp.float32)
    normed = layer_norm(flat, gain_in, bias_in, -1).astype(jnp.bfloat16)
    projected = lax.dot_general(w_in, normed, (((0,), (1,)), ((), ())), preferred_element_type=jnp.float32)
    projected = projected.reshape(2, 2, hidden, tokens)
    sides = (pair_mask * jax.nn.sigmoid(projected[:, 0]) * projected[:, 1]).astype(jnp.bfloat16)
    sides = sides.reshape(2, devices, share, tokens).transpose(1, 0, 2, 3)
    gate = jax.nn.sigmoid(jnp.dot(normed, w_gate, preferred_element_type=jnp.float32))
    got = lax.all_to_all(sides, AXES, split_axis=0, concat_axis=0, tiled=True)
    got = got.reshape(rows, cols, 2, share, row_count, col_count).transpose(2, 3, 0, 4, 1, 5)
    got = got.reshape(2, share, rows * row_count, cols * col_count)
    total = jnp.einsum("cki,ckj->cij", got[0], got[1], preferred_element_type=jnp.float32).astype(jnp.bfloat16)
    total = total.reshape(share, rows, row_count, cols, col_count).transpose(1, 3, 0, 2, 4)
    total = total.reshape(devices, share, tokens)
    total = lax.all_to_all(total, AXES, split_axis=0, concat_axis=0, tiled=True)
    total = total.reshape(hidden, tokens).astype(jnp.float32)
    summed_norm = layer_norm(total, gain_out[:, None], bias_out[:, None], 0).astype(jnp.bfloat16)
    output = lax.dot_general(summed_norm, w_out, (((0,), (0,)), ((), ())), preferred_element_type=jnp.float32)
    return (gate * output).astype(jnp.bfloat16).reshape(row_count, col_count, channels)


def solution(mesh):
    in_specs = (P(("groups", "row"), "col", None), P("groups"), P(), P(), P(), P(), P(), P(), P())
    out_specs = P(("groups", "row"), "col", None)
    rows, cols = mesh.shape["row"], mesh.shape["col"]

    def per_shard(*args):
        hidden = args[-1].shape[0]
        length = args[1].shape[0]
        fits = hidden % (8 * rows * cols) == 0 and length <= 128
        return (per_device if fits else plain_per_device)(rows, cols, *args)

    return jax.shard_map(per_shard, mesh=mesh, in_specs=in_specs, out_specs=out_specs, check_vma=False)
```

time: 66.8 us -> 37.8 us (0.57)
  starting transfers between devices: 42.7 us -> 3.52 us
  blocking collectives: 0 us -> 18.3 us
  local copies, waits for them, and re-layouts: 9.06 us -> 3.82 us
  other arithmetic: 4.8 us -> 0 us
  Pallas kernels: 0 us -> 3.35 us
  matrix products: 1.75 us -> 0.17 us
    ppermute x30 -> x0, starting transfers between devices: 42.7 us -> none  [exchange(): lax.ppermute(piece, AXES, [(i, i ^ step) for i in range(devices)])]
    all_to_all x0 -> x1, blocking collectives: none -> 18.3 us  [per_device(): got = lax.all_to_all(sides, AXES, split_axis=0, concat_axis=0, tiled=True)]
    all_to_all x0 -> x1, waiting for transfers between devices: none -> 8.23 us  [per_device(): total = lax.all_to_all(total, AXES, split_axis=0, concat_axis=0, tiled=True)]
    ppermute x30 -> x0, waiting for transfers between devices: 7.8 us -> none  [exchange(): lax.ppermute(piece, AXES, [(i, i ^ step) for i in range(devices)])]
    all_to_all x0 -> x1, starting transfers between devices: none -> 3.52 us  [per_device(): total = lax.all_to_all(total, AXES, split_axis=0, concat_axis=0, tiled=True)]
    pallas_call x0 -> x3, Pallas kernels: none -> 3.35 us  [the longest x1 1.67 us: per_device(): pl.pallas_call(functools.partial(triangle_kernel, rows, cols, row_count,...]
    reshape x7 -> x0, local copies, waits for them, and re-layouts: 2.57 us -> none  [the longest x1 1.02 us: per_device(): jnp.stack(got).reshape(rows, cols, 2, share, row_count, col_count)]
    reduce_sum x4 -> x0, other arithmetic: 2.38 us -> none  [the longest x2 1.25 us: layer_norm(): variance = jnp.mean(centred * centred, axis=axis, keepdims=True)]
  transfers between devices with their start and end apart: 30 -> 1, of which waited for: 4 -> 1; matrix products, arithmetic and copies ran while one was open for 4% -> 0% of each run, Pallas kernels for 0% -> 0%
where the time goes in v3:
time: 37.8 us; the launch traced here: 37.4 us
  blocking collectives  18.3 us (48%)
  waiting for transfers between devices  8.23 us (22%)
  local copies, waits for them, and re-layouts  3.82 us (10%)
  starting transfers between devices  3.52 us (9%)
  Pallas kernels  3.35 us (9%)
    all_to_all x1, blocking collectives, per_device(): got = lax.all_to_all(sides, AXES, split_axis=0, concat_axis=0, tiled=True)  18.3 us
    all_to_all x1, waiting for transfers between devices, per_device(): total = lax.all_to_all(total, AXES, split_axis=0, concat_axis=0, tiled=True)  8.23 us
    unnamed x18, local copies, waits for them, and re-layouts  3.82 us
    all_to_all x1, starting transfers between devices, per_device(): total = lax.all_to_all(total, AXES, split_axis=0, concat_axis=0, tiled=True)  3.52 us
    pallas_call x1, Pallas kernels, per_device(): pl.pallas_call(functools.partial(triangle_kernel, rows, cols, row_count,...  1.67 us
    pallas_call x1, Pallas kernels, per_device(): pl.pallas_call(output_kernel, out_shape=jax.ShapeDtypeStruct(pair.shape,...  1 us
  transfers between devices with their start and end apart: 1, of which 1 were waited for; matrix products, arithmetic and copies ran while one was open for 0% of the time, Pallas kernels for 0%

profile of v3, /device:TPU:0, one launch (start us, length us, event | category | flops | bytes accessed | tf_op | source)
XLA Modules:
  0.0 37.4 jit_solution(10609361789575735478)
XLA Ops:
  0.0 0.0 copy-start
  0.0 0.0 copy-start.4
  0.0 0.0 copy-start.5
  0.0 0.7 %copy-done.4 = f32[128]{0:T(128)S(1)} copy-done((f32[128]{0:T(128)S(1)}, f32[128]{0:T(128)}, u32[]{:S(2)}) %copy-start.4) | copy-done | bytes 536
  0.7 0.0 copy-done.5
  0.7 0.0 copy-start.1
  0.7 0.9 %copy-done.1 = bf16[12,48,128]{2,1,0:T(8,128)(2,1)S(1)} copy-done((bf16[12,48,128]{2,1,0:T(8,128)(2,1)S(1)}, bf16[12,48,128]{2,1,0:T(8,128)(2,1)}, u32[]{:S(2)}) %copy-start.1) | copy-done | bytes 147480
  1.6 0.0 copy-start.2
  1.6 0.9 %copy-done.2 = bf16[128,512]{1,0:T(8,128)(2,1)S(1)} copy-done((bf16[128,512]{1,0:T(8,128)(2,1)S(1)}, bf16[128,512]{1,0:T(8,128)(2,1)}, u32[]{:S(2)}) %copy-start.2) | copy-done | bytes 131096
  2.5 0.7 %shard_map.91 = (bf16[16,16,576]{2,1,0:T(8,128)(2,1)S(1)}, bf16[576,128]{1,0:T(8,128)(2,1)S(1)}) custom-call(bf16[12,48,128]{2,1,0:T(8,128)(2,1)S(1)} %copy-done.1, f32[1,128]{1,0:T(1,128)S(1)} %bitcast.7, f32[1,128]{1,0:T(1,128)S(1)} %bitcast.8, bf16[128,512]{1,0:T(8,128)(2,1)S(1)} %copy-done.2), custom_call_target="tpu_custom_call" | custom-call | tf_op jit(solution)/shard_map/pallas_call | solution.py:91
  3.2 18.3 %all_to_all.10.got_ref = bf16[16,16,576]{2,1,0:T(8,128)(2,1)S(1)} all-to-all(bf16[16,16,576]{2,1,0:T(8,128)(2,1)S(1)} %get-tuple-element.7), channel_id=1, replica_groups=mesh['groups'=2,'row'=8,'col'=2] {'row','col'}, dimensions={0} | all-to-all | bytes 589824 | tf_op jit(solution)/shard_map/all_to_all | solution.py:101
  21.5 0.0 copy-start.6
  21.5 0.7 %copy-done.6 = s32[96]{0:T(128)S(1)} copy-done((s32[96]{0:T(128)S(1)}, s32[96]{0:T(128)}, u32[]{:S(2)}) %copy-start.6) | copy-done | bytes 408
  22.1 1.7 %shard_map.92 = bf16[16,8,576]{2,1,0:T(8,128)(2,1)} custom-call(bf16[16,16,576]{2,1,0:T(8,128)(2,1)S(1)} %all_to_all.10.got_ref, s32[1,96]{1,0:T(1,128)S(1)} %bitcast.9), custom_call_target="tpu_custom_call" | custom-call | tf_op jit(solution)/shard_map/pallas_call | solution.py:102
  23.8 3.5 %all-to-all-start.1 = ((bf16[16,8,576]{2,1,0:T(8,128)(2,1)}), bf16[16,8,576]{2,1,0:T(8,128)(2,1)S(1)}, u32[]{:S(2)}, u32[]{:S(2)}) async-start(bf16[16,8,576]{2,1,0:T(8,128)(2,1)} %shard_map.92), calls=%async_computation.1 | async-start | bytes 327680 | tf_op jit(solution)/shard_map/all_to_all | solution.py:115
  27.3 0.0 copy-done
  27.3 0.0 copy-start.3
  27.4 0.2 fusion.gate_ref
  27.5 8.2 %all-to-all-done.1.total_ref = bf16[16,8,576]{2,1,0:T(8,128)(2,1)S(1)} async-done(((bf16[16,8,576]{2,1,0:T(8,128)(2,1)}), bf16[16,8,576]{2,1,0:T(8,128)(2,1)S(1)}, u32[]{:S(2)}, u32[]{:S(2)}) %all-to-all-start.1) | async-done | bytes 147488 | tf_op jit(solution)/shard_map/all_to_all | solution.py:115
  35.8 0.0 copy-start.7
  35.8 0.0 copy-done.3
  35.8 0.6 %copy-done.7 = f32[128]{0:T(128)S(1)} copy-done((f32[128]{0:T(128)S(1)}, f32[128]{0:T(128)}, u32[]{:S(2)}) %copy-start.7) | copy-done | bytes 536
  36.4 0.0 copy-done.8
  36.4 1.0 %shard_map.93 = bf16[12,48,128]{2,1,0:T(8,128)(2,1)} custom-call(bf16[16,8,576]{2,1,0:T(8,128)(2,1)S(1)} %all-to-all-done.1.total_ref, f32[576,128]{1,0:T(8,128)S(1)} %fusion.gate_ref, f32[1,128]{1,0:T(1,128)S(1)} %bitcast.10, f32[1,128]{1,0:T(1,128)S(1)} %bitcast.11, bf16[128,128]{1,0:T(8,128)(2,1)S(1)} %copy-done.3), custom_call_target="tpu_custom_call" | custom-call | tf_op jit(solution)/shard_map/pallas_call | solution.py:116
  (1 shorter events, 0.0 us)
Async XLA Ops:
  0.0 27.3 %copy-start = (bf16[128,128]{1,0:T(8,128)(2,1)S(1)}, bf16[128,128]{1,0:T(8,128)(2,1)}, u32[]{:S(2)}) copy-start(bf16[128,128]{1,0:T(8,128)(2,1)} %param.14) | copy-start | bytes 98308
  0.0 0.7 %copy-start.4 = (f32[128]{0:T(128)S(1)}, f32[128]{0:T(128)}, u32[]{:S(2)}) copy-start(f32[128]{0:T(128)} %param.11) | copy-start | bytes 1540
  0.0 0.7 %copy-start.5 = (f32[128]{0:T(128)S(1)}, f32[128]{0:T(128)}, u32[]{:S(2)}) copy-start(f32[128]{0:T(128)} %param.12) | copy-start | bytes 1540
  0.7 0.9 %copy-start.1 = (bf16[12,48,128]{2,1,0:T(8,128)(2,1)S(1)}, bf16[12,48,128]{2,1,0:T(8,128)(2,1)}, u32[]{:S(2)}) copy-start(bf16[12,48,128]{2,1,0:T(8,128)(2,1)} %pair_ref.1) | copy-start | bytes 442372
  1.6 0.9 %copy-start.2 = (bf16[128,512]{1,0:T(8,128)(2,1)S(1)}, bf16[128,512]{1,0:T(8,128)(2,1)}, u32[]{:S(2)}) copy-start(bf16[128,512]{1,0:T(8,128)(2,1)} %w_ref.2) | copy-start | bytes 393220
  21.5 0.7 %copy-start.6 = (s32[96]{0:T(128)S(1)}, s32[96]{0:T(128)}, u32[]{:S(2)}) copy-start(s32[96]{0:T(128)} %param.10) | copy-start | bytes 1156
  23.8 11.9 %all-to-all-start.1 = ((bf16[16,8,576]{2,1,0:T(8,128)(2,1)}), bf16[16,8,576]{2,1,0:T(8,128)(2,1)S(1)}, u32[]{:S(2)}, u32[]{:S(2)}) async-start(bf16[16,8,576]{2,1,0:T(8,128)(2,1)} %shard_map.92), calls=%async_computation.1 | async-start | bytes 327680 | tf_op jit(solution)/shard_map/all_to_all | solution.py:115
  27.3 8.4 %copy-start.3 = (bf16[128,128]{1,0:T(8,128)(2,1)S(1)}, bf16[128,128]{1,0:T(8,128)(2,1)}, u32[]{:S(2)}) copy-start(bf16[128,128]{1,0:T(8,128)(2,1)} %w_ref.3) | copy-start | bytes 98308
  35.8 0.7 %copy-start.7 = (f32[128]{0:T(128)S(1)}, f32[128]{0:T(128)}, u32[]{:S(2)}) copy-start(f32[128]{0:T(128)} %param.15) | copy-start | bytes 1540
  35.8 0.7 %copy-start.8 = (f32[128]{0:T(128)S(1)}, f32[128]{0:T(128)}, u32[]{:S(2)}) copy-start(f32[128]{0:T(128)} %param.16) | copy-start | bytes 1540

commit v4 on v3

--- a/solution.py
+++ b/solution.py
@@ -8,8 +8,9 @@
 from jax.sharding import PartitionSpec as P
 
 epsilon = 1e-05
-AXES = ("row", "col")
+AXES = ("half", "quad", "col")
 VMEM = pl.BlockSpec(memory_space=pltpu.VMEM)
+HBM = pl.BlockSpec(memory_space=pltpu.HBM)
 LIMIT = pltpu.CompilerParams(vmem_limit_bytes=32 * 1024 * 1024)
 
 
@@ -30,14 +31,31 @@
     return jnp.sum(jnp.where(eye, row, 0.0), axis=1, keepdims=True)
 
 
-def project_kernel(pair_ref, gain_ref, bias_ref, w_ref, sides_ref, normed_ref):
+def project_kernel(pair_hbm, gain_hbm, bias_hbm, w_hbm, mask_hbm, sides_ref, normed_ref, left_mask_ref, pair_ref, gain_ref, bias_ref, w_ref, mask_ref, column_ref, sems):
+    copies = [
+        pltpu.make_async_copy(source, target, sems.at[n])
+        for n, (source, target) in enumerate(
+            [(mask_hbm, mask_ref), (pair_hbm, pair_ref), (gain_hbm, gain_ref), (bias_hbm, bias_ref), (w_hbm, w_ref)]
+        )
+    ]
+    for copy in copies:
+        copy.start()
     devices, both, tokens = sides_ref.shape
     channels = pair_ref.shape[2]
     hidden = w_ref.shape[1] // 4
     share = both // 2
+    depth, length = left_mask_ref.shape
+    copies[0].wait()
+    mask_row = mask_ref[...].astype(jnp.float32)
+    column_ref[...] = jnp.broadcast_to(column(mask_row), column_ref.shape)
+    start = pl.multiple_of(lax.axis_index("half") * depth, depth)
+    left_mask_ref[...] = column_ref[pl.ds(start, depth), 0:length] * mask_row
+    for copy in copies[1:4]:
+        copy.wait()
     flat = pair_ref[...].reshape(tokens, channels).astype(jnp.float32)
     normed = layer_norm(flat, gain_ref[...], bias_ref[...], -1).astype(jnp.bfloat16)
     normed_ref[...] = normed
+    copies[4].wait()
     projected = lax.dot_general(w_ref[...], normed, (((0,), (1,)), ((), ())), preferred_element_type=jnp.float32)
     left = sigmoid(projected[:hidden]) * projected[hidden : 2 * hidden]
     right = sigmoid(projected[2 * hidden : 3 * hidden]) * projected[3 * hidden :]
@@ -45,21 +63,21 @@
     sides_ref[...] = sides.astype(jnp.bfloat16)
 
 
-def triangle_kernel(rows, cols, row_count, col_count, got_ref, mask_ref, total_ref, wide_ref, sum_ref, flat_ref):
-    both = got_ref.shape[1]
+def triangle_kernel(rows, cols, row_count, col_count, got_ref, left_mask_ref, mask_ref, total_ref, wide_ref, sum_ref, flat_ref):
+    sources, both, _ = got_ref.shape
     share = both // 2
-    length = rows * row_count
-    for source in range(rows * cols):
+    depth, length = left_mask_ref.shape
+    for source in range(sources):
         row, col = divmod(source, cols)
         piece = got_ref[source].astype(jnp.float32)
         for k in range(row_count):
             at = (row * row_count + k) * both
             wide_ref[at : at + both, col * col_count : (col + 1) * col_count] = piece[:, k * col_count : (k + 1) * col_count]
-    mask_row = mask_ref[...].astype(jnp.float32)
-    mask = column(mask_row) * mask_row
+    left_mask = left_mask_ref[...]
+    right_mask = mask_ref[...].astype(jnp.float32)
     for c in range(share):
-        left = (wide_ref[pl.ds(c, length, stride=both), 0:length] * mask).astype(jnp.bfloat16)
-        right = (wide_ref[pl.ds(share + c, length, stride=both), 0:length] * mask).astype(jnp.bfloat16)
+        left = (wide_ref[pl.ds(c, depth, stride=both), 0:length] * left_mask).astype(jnp.bfloat16)
+        right = (wide_ref[pl.ds(share + c, depth, stride=both), 0:length] * right_mask).astype(jnp.bfloat16)
         sum_ref[pl.ds(c, length, stride=share), 0:length] = lax.dot_general(
             left, right, (((0,), (0,)), ((), ())), preferred_element_type=jnp.float32
         )
@@ -73,53 +91,85 @@
         total_ref[target] = flat_ref[target * share : (target + 1) * share, :].astype(jnp.bfloat16)
 
 
+def gate_kernel(normed_ref, w_ref, gain_ref, bias_ref, gate_ref, gain_out_ref, bias_out_ref):
+    gate_ref[...] = sigmoid(jnp.dot(normed_ref[...], w_ref[...], preferred_element_type=jnp.float32))
+    gain_out_ref[...] = column(gain_ref[...])
+    bias_out_ref[...] = column(bias_ref[...])
+
+
 def output_kernel(total_ref, gate_ref, gain_ref, bias_ref, w_ref, out_ref):
-    devices, share, tokens = total_ref.shape
-    total = total_ref[...].astype(jnp.float32).reshape(devices * share, tokens)
-    normed = layer_norm(total, column(gain_ref[...]), column(bias_ref[...]), 0).astype(jnp.bfloat16)
+    sources, share, tokens = total_ref.shape
+    hidden = w_ref.shape[0]
+    parts = total_ref[...].astype(jnp.float32).reshape(sources * share // hidden, hidden, tokens)
+    total = jnp.sum(parts, axis=0)
+    normed = layer_norm(total, gain_ref[...], bias_ref[...], 0).astype(jnp.bfloat16)
     output = lax.dot_general(normed, w_ref[...], (((0,), (0,)), ((), ())), preferred_element_type=jnp.float32)
-    out_ref[...] = (sigmoid(gate_ref[...]) * output).astype(jnp.bfloat16).reshape(out_ref.shape)
-
-
-def per_device(rows, cols, pair, token_mask, gain_in, bias_in, w_in, w_gate, gain_out, bias_out, w_out):
+    out_ref[...] = (gate_ref[...] * output).astype(jnp.bfloat16).reshape(out_ref.shape)
+
+
+def per_device(rows, cols, halves, pair, token_mask, gain_in, bias_in, w_in, w_gate, gain_out, bias_out, w_out):
     row_count, col_count, channels = pair.shape
     hidden = w_out.shape[0]
     devices = rows * cols
-    share = hidden // devices
+    near = devices // halves
+    share = hidden // near
     tokens = row_count * col_count
     length = rows * row_count
-    sides, normed = pl.pallas_call(
+    depth = length // halves
+    token_mask = token_mask.reshape(1, length)
+    sides, normed, left_mask = pl.pallas_call(
         project_kernel,
         out_shape=(
-            jax.ShapeDtypeStruct((devices, 2 * share, tokens), jnp.bfloat16),
+            jax.ShapeDtypeStruct((near, 2 * share, tokens), jnp.bfloat16),
             jax.ShapeDtypeStruct((tokens, channels), jnp.bfloat16),
+            jax.ShapeDtypeStruct((depth, length), jnp.float32),
         ),
-        in_specs=[VMEM] * 4,
-        out_specs=(VMEM, VMEM),
-        compiler_params=LIMIT,
-    )(pair, gain_in.reshape(1, channels), bias_in.reshape(1, channels), w_in)
-    got = lax.all_to_all(sides, AXES, split_axis=0, concat_axis=0, tiled=True)
+        in_specs=[HBM] * 5,
+        out_specs=(VMEM, VMEM, VMEM),
+        scratch_shapes=[
+            pltpu.VMEM(pair.shape, pair.dtype),
+            pltpu.VMEM((1, channels), jnp.float32),
+            pltpu.VMEM((1, channels), jnp.float32),
+            pltpu.VMEM(w_in.shape, w_in.dtype),
+            pltpu.VMEM((1, length), jnp.int32),
+            pltpu.VMEM((length, 128), jnp.float32),
+            pltpu.SemaphoreType.DMA((5,)),
+        ],
+        compiler_params=LIMIT,
+    )(pair, gain_in.reshape(1, channels), bias_in.reshape(1, channels), w_in, token_mask)
+    got = lax.all_to_all(sides, ("quad", "col"), split_axis=0, concat_axis=0, tiled=True)
     total = pl.pallas_call(
         functools.partial(triangle_kernel, rows, cols, row_count, col_count),
         out_shape=jax.ShapeDtypeStruct((devices, share, tokens), jnp.bfloat16),
-        in_specs=[VMEM] * 2,
+        in_specs=[VMEM] * 3,
         out_specs=VMEM,
         scratch_shapes=[
-            pltpu.VMEM((length * 2 * share, 128), jnp.float32),
+            pltpu.VMEM((depth * 2 * share, 128), jnp.float32),
             pltpu.VMEM((length * share, 128), jnp.float32),
-            pltpu.VMEM((hidden, tokens), jnp.float32),
+            pltpu.VMEM((devices * share, tokens), jnp.float32),
         ],
         compiler_params=LIMIT,
-    )(got, token_mask.reshape(1, length))
-    gate = jnp.dot(normed, w_gate, preferred_element_type=jnp.float32)
-    total = lax.all_to_all(total, AXES, split_axis=0, concat_axis=0, tiled=True)
+    )(got, left_mask, token_mask)
+    gate, gain_out, bias_out = pl.pallas_call(
+        gate_kernel,
+        out_shape=(
+            jax.ShapeDtypeStruct((tokens, channels), jnp.float32),
+            jax.ShapeDtypeStruct((hidden, 1), jnp.float32),
+            jax.ShapeDtypeStruct((hidden, 1), jnp.float32),
+        ),
+        in_specs=[VMEM] * 4,
+        out_specs=(VMEM, VMEM, VMEM),
+        compiler_params=LIMIT,
+        cost_estimate=pl.CostEstimate(flops=2 * tokens * channels * channels, bytes_accessed=4 * tokens * channels, transcendentals=0),
+    )(normed, w_gate, gain_out.reshape(1, hidden), bias_out.reshape(1, hidden))
+    total = lax.all_to_all(total, ("half", "quad", "col"), split_axis=0, concat_axis=0, tiled=True)
     return pl.pallas_call(
         output_kernel,
         out_shape=jax.ShapeDtypeStruct(pair.shape, jnp.bfloat16),
         in_specs=[VMEM] * 5,
         out_specs=VMEM,
         compiler_params=LIMIT,
-    )(total, gate, gain_out.reshape(1, hidden), bias_out.reshape(1, hidden), w_out)
+    )(total, gate, gain_out, bias_out, w_out)
 
 
 def plain_per_device(rows, cols, pair, token_mask, gain_in, bias_in, w_in, w_gate, gain_out, bias_out, w_out):
@@ -128,7 +178,7 @@
     devices = rows * cols
     share = hidden // devices
     tokens = row_count * col_count
-    row_start = lax.axis_index("row") * row_count
+    row_start = lax.axis_index(("half", "quad")) * row_count
     col_start = lax.axis_index("col") * col_count
     mask_float = token_mask.astype(jnp.float32)
     mask_rows = lax.dynamic_slice_in_dim(mask_float, row_start, row_count)
@@ -155,14 +205,17 @@
 
 
 def solution(mesh):
-    in_specs = (P(("groups", "row"), "col", None), P("groups"), P(), P(), P(), P(), P(), P(), P())
-    out_specs = P(("groups", "row"), "col", None)
     rows, cols = mesh.shape["row"], mesh.shape["col"]
+    halves = 2
+    parts = (mesh.shape["groups"], halves, rows // halves, cols)
+    finer = jax.sharding.Mesh(mesh.devices.reshape(parts), ("groups", "half", "quad", "col"))
 
     def per_shard(*args):
-        hidden = args[-1].shape[0]
-        length = args[1].shape[0]
-        fits = hidden % (8 * rows * cols) == 0 and length <= 128
-        return (per_device if fits else plain_per_device)(rows, cols, *args)
-
-    return jax.shard_map(per_shard, mesh=mesh, in_specs=in_specs, out_specs=out_specs, check_vma=False)
+        near, hidden, length = rows * cols // halves, args[-1].shape[0], args[1].shape[0]
+        if hidden % (16 * near) == 0 and length <= 128:
+            return per_device(rows, cols, halves, *args)
+        return plain_per_device(rows, cols, *args)
+
+    tokens = P(("groups", "half", "quad"), "col", None)
+    in_specs = (tokens, P("groups"), P(), P(), P(), P(), P(), P(), P())
+    return jax.shard_map(per_shard, mesh=finer, in_specs=in_specs, out_specs=tokens, check_vma=False)

time: 37.8 us -> 35.1 us (0.929)
  blocking collectives: 18.3 us -> 12.6 us
  waiting for transfers between devices: 8.23 us -> 10.2 us
  Pallas kernels: 3.35 us -> 4.5 us
  starting transfers between devices: 3.52 us -> 4.28 us
  local copies, waits for them, and re-layouts: 3.82 us -> 3.15 us
    all_to_all x1, blocking collectives: 18.3 us -> 12.6 us  [per_device(): lax.all_to_all(sides, ('quad', 'col'), split_axis=0, concat_axis=0, tiled...]
    all_to_all x1, waiting for transfers between devices: 8.23 us -> 10.2 us  [per_device(): lax.all_to_all(total, ('half', 'quad', 'col'), split_axis=0, concat_axis=...]
    all_to_all x1, starting transfers between devices: 3.52 us -> 4.28 us  [per_device(): lax.all_to_all(total, ('half', 'quad', 'col'), split_axis=0, concat_axis=...]
    unnamed x18, local copies, waits for them, and re-layouts: 3.82 us -> 3.15 us
    pallas_call x1 -> x2, Pallas kernels: 0.68 us -> 1.27 us  [the longest x1 1.08 us: per_device(): pl.pallas_call(project_kernel, out_shape=(jax.ShapeDtypeStruct((near, 2 *...]
    pallas_call x1, Pallas kernels: 1.67 us -> 2.21 us  [per_device(): pl.pallas_call(functools.partial(triangle_kernel, rows, cols, row_count,...]
  transfers between devices with their start and end apart: 1 -> 1, of which waited for: 1 -> 1; matrix products, arithmetic and copies ran while one was open for 0% -> 0% of each run, Pallas kernels for 0% -> 1%
where the time goes in v4:
time: 35.1 us; the launch traced here: 34.8 us
  blocking collectives  12.6 us (36%)
  waiting for transfers between devices  10.2 us (29%)
  Pallas kernels  4.5 us (13%)
  starting transfers between devices  4.28 us (12%)
  local copies, waits for them, and re-layouts  3.15 us (9%)
    all_to_all x1, blocking collectives, per_device(): lax.all_to_all(sides, ('quad', 'col'), split_axis=0, concat_axis=0, tiled...  12.6 us
    all_to_all x1, waiting for transfers between devices, per_device(): lax.all_to_all(total, ('half', 'quad', 'col'), split_axis=0, concat_axis=...  10.2 us
    all_to_all x1, starting transfers between devices, per_device(): lax.all_to_all(total, ('half', 'quad', 'col'), split_axis=0, concat_axis=...  4.28 us
    unnamed x18, local copies, waits for them, and re-layouts  3.15 us
    pallas_call x1, Pallas kernels, per_device(): pl.pallas_call(functools.partial(triangle_kernel, rows, cols, row_count,...  2.21 us
    pallas_call x1, Pallas kernels, per_device(): pl.pallas_call(project_kernel, out_shape=(jax.ShapeDtypeStruct((near, 2 *...  1.08 us
    pallas_call x1, Pallas kernels, per_device(): pl.pallas_call(output_kernel, out_shape=jax.ShapeDtypeStruct(pair.shape,...  1.03 us
  transfers between devices with their start and end apart: 1, of which 1 were waited for; matrix products, arithmetic and copies ran while one was open for 0% of the time, Pallas kernels for 1%

profile of v4, /device:TPU:0, one launch (start us, length us, event | category | flops | bytes accessed | tf_op | source)
XLA Modules:
  0.0 34.8 jit_solution(17736378606579144868)
XLA Ops:
  0.0 0.0 copy-start.4
  0.0 0.0 copy-start.5
  0.0 0.0 copy-start.6
  0.0 0.6 %copy-done.4 = s32[96]{0:T(128)S(1)} copy-done((s32[96]{0:T(128)S(1)}, s32[96]{0:T(128)}, u32[]{:S(2)}) %copy-start.4) | copy-done | bytes 408
  0.7 0.0 copy-done.5
  0.7 0.0 copy-done.6
  0.7 0.0 copy-start
  0.7 0.9 %copy-done = bf16[12,48,128]{2,1,0:T(8,128)(2,1)S(1)} copy-done((bf16[12,48,128]{2,1,0:T(8,128)(2,1)S(1)}, bf16[12,48,128]{2,1,0:T(8,128)(2,1)}, u32[]{:S(2)}) %copy-start) | copy-done | bytes 147480
  1.6 0.0 copy-start.1
  1.6 0.9 %copy-done.1 = bf16[128,512]{1,0:T(8,128)(2,1)S(1)} copy-done((bf16[128,512]{1,0:T(8,128)(2,1)S(1)}, bf16[128,512]{1,0:T(8,128)(2,1)}, u32[]{:S(2)}) %copy-start.1) | copy-done | bytes 131096
  2.5 1.1 %shard_map.91 = (bf16[8,32,576]{2,1,0:T(8,128)(2,1)S(1)}, bf16[576,128]{1,0:T(8,128)(2,1)S(1)}, f32[48,96]{1,0:T(8,128)S(1)}) custom-call(bf16[12,48,128]{2,1,0:T(8,128)(2,1)S(1)} %copy-done, f32[1,128]{1,0:T(1,128)S(1)} %bitcast.7, f32[1,128]{1,0:T(1,128)S(1)} %bitcast.8, bf16[128,512]{1,0:T(8,128)(2,1)S(1)} %copy-done.1, s32[1,96]{1,0:T(1,128)S(1)} %bitcast.5), custom_call_target="tpu_custom_call" | custom-call | tf_op jit(solution)/shard_map/pallas_call | solution.py:120
  3.6 12.6 %all_to_all.10.got_ref = bf16[8,32,576]{2,1,0:T(8,128)(2,1)S(1)} all-to-all(bf16[8,32,576]{2,1,0:T(8,128)(2,1)S(1)} %get-tuple-element.11), channel_id=1, replica_groups=mesh['groups'=2,'half'=2,'quad'=4,'col'=2] {'quad','col'}, dimensions={0} | all-to-all | bytes 589824 | tf_op jit(solution)/shard_map/all_to_all | solution.py:140
  16.2 2.2 %shard_map.92 = bf16[16,16,576]{2,1,0:T(8,128)(2,1)} custom-call(bf16[8,32,576]{2,1,0:T(8,128)(2,1)S(1)} %all_to_all.10.got_ref, f32[48,96]{1,0:T(8,128)S(1)} %get-tuple-element.12.left_mask_ref, s32[1,96]{1,0:T(1,128)S(1)} %bitcast.6), custom_call_target="tpu_custom_call" | custom-call | tf_op jit(solution)/shard_map/pallas_call | solution.py:141
  18.4 0.0 copy-start.3
  18.4 4.3 %all-to-all-start.1 = ((bf16[16,16,576]{2,1,0:T(8,128)(2,1)}), bf16[16,16,576]{2,1,0:T(8,128)(2,1)S(1)}, u32[]{:S(2)}, u32[]{:S(2)}) async-start(bf16[16,16,576]{2,1,0:T(8,128)(2,1)} %shard_map.92), calls=%async_computation.1 | async-start | bytes 655360 | tf_op jit(solution)/shard_map/all_to_all | solution.py:165
  22.7 0.0 copy-start.7
  22.7 0.0 copy-start.8
  22.7 0.0 copy-done.3
  22.7 0.6 %copy-done.7 = f32[128]{0:T(128)S(1)} copy-done((f32[128]{0:T(128)S(1)}, f32[128]{0:T(128)}, u32[]{:S(2)}) %copy-start.7) | copy-done | bytes 536
  23.3 0.0 copy-done.8
  23.3 0.2 shard_map.93
  23.5 10.2 %all-to-all-done.1.total_ref = bf16[16,16,576]{2,1,0:T(8,128)(2,1)S(1)} async-done(((bf16[16,16,576]{2,1,0:T(8,128)(2,1)}), bf16[16,16,576]{2,1,0:T(8,128)(2,1)S(1)}, u32[]{:S(2)}, u32[]{:S(2)}) %all-to-all-start.1) | async-done | bytes 294944 | tf_op jit(solution)/shard_map/all_to_all | solution.py:165
  33.8 0.0 copy-done.2
  33.8 1.0 %shard_map.94 = bf16[12,48,128]{2,1,0:T(8,128)(2,1)} custom-call(bf16[16,16,576]{2,1,0:T(8,128)(2,1)S(1)} %all-to-all-done.1.total_ref, f32[576,128]{1,0:T(8,128)S(1)} %get-tuple-element.14.gate_ref, f32[128,1]{1,0:T(8,128)S(1)} %get-tuple-element.15.gain_ref, f32[128,1]{1,0:T(8,128)S(1)} %get-tuple-element.16.bias_ref, bf16[128,128]{1,0:T(8,128)(2,1)S(1)} %copy-done.2), custom_call_target="tpu_custom_call" | custom-call | tf_op jit(solution)/shard_map/pallas_call | solution.py:166
  (1 shorter events, 0.0 us)
Async XLA Ops:
  0.0 0.7 %copy-start.4 = (s32[96]{0:T(128)S(1)}, s32[96]{0:T(128)}, u32[]{:S(2)}) copy-start(s32[96]{0:T(128)} %param.10) | copy-start | bytes 1156
  0.0 0.7 %copy-start.5 = (f32[128]{0:T(128)S(1)}, f32[128]{0:T(128)}, u32[]{:S(2)}) copy-start(f32[128]{0:T(128)} %param.11) | copy-start | bytes 1540
  0.0 0.7 %copy-start.6 = (f32[128]{0:T(128)S(1)}, f32[128]{0:T(128)}, u32[]{:S(2)}) copy-start(f32[128]{0:T(128)} %param.12) | copy-start | bytes 1540
  0.7 0.9 %copy-start = (bf16[12,48,128]{2,1,0:T(8,128)(2,1)S(1)}, bf16[12,48,128]{2,1,0:T(8,128)(2,1)}, u32[]{:S(2)}) copy-start(bf16[12,48,128]{2,1,0:T(8,128)(2,1)} %pair_hbm.1) | copy-start | bytes 442372
  1.6 0.9 %copy-start.1 = (bf16[128,512]{1,0:T(8,128)(2,1)S(1)}, bf16[128,512]{1,0:T(8,128)(2,1)}, u32[]{:S(2)}) copy-start(bf16[128,512]{1,0:T(8,128)(2,1)} %w_hbm.1) | copy-start | bytes 393220
  18.4 4.3 %copy-start.3 = (bf16[128,128]{1,0:T(8,128)(2,1)S(1)}, bf16[128,128]{1,0:T(8,128)(2,1)}, u32[]{:S(2)}) copy-start(bf16[128,128]{1,0:T(8,128)(2,1)} %w_ref.2) | copy-start | bytes 98308
  18.4 15.4 %all-to-all-start.1 = ((bf16[16,16,576]{2,1,0:T(8,128)(2,1)}), bf16[16,16,576]{2,1,0:T(8,128)(2,1)S(1)}, u32[]{:S(2)}, u32[]{:S(2)}) async-start(bf16[16,16,576]{2,1,0:T(8,128)(2,1)} %shard_map.92), calls=%async_computation.1 | async-start | bytes 655360 | tf_op jit(solution)/shard_map/all_to_all | solution.py:165
  22.7 0.7 %copy-start.7 = (f32[128]{0:T(128)S(1)}, f32[128]{0:T(128)}, u32[]{:S(2)}) copy-start(f32[128]{0:T(128)} %param.15) | copy-start | bytes 1540
  22.7 0.7 %copy-start.8 = (f32[128]{0:T(128)S(1)}, f32[128]{0:T(128)}, u32[]{:S(2)}) copy-start(f32[128]{0:T(128)} %param.16) | copy-start | bytes 1540
  23.3 10.4 %copy-start.2 = (bf16[128,128]{1,0:T(8,128)(2,1)S(1)}, bf16[128,128]{1,0:T(8,128)(2,1)}, u32[]{:S(2)}) copy-start(bf16[128,128]{1,0:T(8,128)(2,1)} %w_ref.3) | copy-start | bytes 98308

commit v5 on v4

--- a/solution.py
+++ b/solution.py
@@ -63,12 +63,13 @@
     sides_ref[...] = sides.astype(jnp.bfloat16)
 
 
-def triangle_kernel(rows, cols, row_count, col_count, got_ref, left_mask_ref, mask_ref, total_ref, wide_ref, sum_ref, flat_ref):
+def triangle_kernel(halves, cols, row_count, col_count, got_ref, left_mask_ref, mask_ref, total_ref, wide_ref, sum_ref, flat_ref):
     sources, both, _ = got_ref.shape
     share = both // 2
     depth, length = left_mask_ref.shape
+    quads = sources // cols
     for source in range(sources):
-        row, col = divmod(source, cols)
+        col, row = divmod(source, quads)
         piece = got_ref[source].astype(jnp.float32)
         for k in range(row_count):
             at = (row * row_count + k) * both
@@ -81,8 +82,9 @@
         sum_ref[pl.ds(c, length, stride=share), 0:length] = lax.dot_general(
             left, right, (((0,), (0,)), ((), ())), preferred_element_type=jnp.float32
         )
-    for target in range(rows * cols):
-        row, col = divmod(target, cols)
+    for target in range(sources * halves):
+        col, row = divmod(target // halves, quads)
+        row += target % halves * quads
         for i in range(row_count):
             at = (row * row_count + i) * share
             flat_ref[target * share : (target + 1) * share, i * col_count : (i + 1) * col_count] = sum_ref[
@@ -100,8 +102,9 @@
 def output_kernel(total_ref, gate_ref, gain_ref, bias_ref, w_ref, out_ref):
     sources, share, tokens = total_ref.shape
     hidden = w_ref.shape[0]
-    parts = total_ref[...].astype(jnp.float32).reshape(sources * share // hidden, hidden, tokens)
-    total = jnp.sum(parts, axis=0)
+    halves = sources * share // hidden
+    parts = total_ref[...].astype(jnp.float32).reshape(sources // halves, halves, share, tokens)
+    total = jnp.sum(parts, axis=1).reshape(hidden, tokens)
     normed = layer_norm(total, gain_ref[...], bias_ref[...], 0).astype(jnp.bfloat16)
     output = lax.dot_general(normed, w_ref[...], (((0,), (0,)), ((), ())), preferred_element_type=jnp.float32)
     out_ref[...] = (gate_ref[...] * output).astype(jnp.bfloat16).reshape(out_ref.shape)
@@ -117,6 +120,7 @@
     length = rows * row_count
     depth = length // halves
     token_mask = token_mask.reshape(1, length)
+    arguments = (pair, gain_in.reshape(1, channels), bias_in.reshape(1, channels), w_in, token_mask)
     sides, normed, left_mask = pl.pallas_call(
         project_kernel,
         out_shape=(
@@ -136,10 +140,10 @@
             pltpu.SemaphoreType.DMA((5,)),
         ],
         compiler_params=LIMIT,
-    )(pair, gain_in.reshape(1, channels), bias_in.reshape(1, channels), w_in, token_mask)
-    got = lax.all_to_all(sides, ("quad", "col"), split_axis=0, concat_axis=0, tiled=True)
+    )(*(pltpu.with_memory_space_constraint(x, pltpu.HBM) for x in arguments))
+    got = lax.all_to_all(sides, ("col", "quad"), split_axis=0, concat_axis=0, tiled=True)
     total = pl.pallas_call(
-        functools.partial(triangle_kernel, rows, cols, row_count, col_count),
+        functools.partial(triangle_kernel, halves, cols, row_count, col_count),
         out_shape=jax.ShapeDtypeStruct((devices, share, tokens), jnp.bfloat16),
         in_specs=[VMEM] * 3,
         out_specs=VMEM,
@@ -162,7 +166,7 @@
         compiler_params=LIMIT,
         cost_estimate=pl.CostEstimate(flops=2 * tokens * channels * channels, bytes_accessed=4 * tokens * channels, transcendentals=0),
     )(normed, w_gate, gain_out.reshape(1, hidden), bias_out.reshape(1, hidden))
-    total = lax.all_to_all(total, ("half", "quad", "col"), split_axis=0, concat_axis=0, tiled=True)
+    total = lax.all_to_all(total, ("col", "quad", "half"), split_axis=0, concat_axis=0, tiled=True)
     return pl.pallas_call(
         output_kernel,
         out_shape=jax.ShapeDtypeStruct(pair.shape, jnp.bfloat16),

time: 35.1 us -> 34.4 us (0.980)
  local copies, waits for them, and re-layouts: 3.15 us -> 1.31 us
  waiting for transfers between devices: 10.2 us -> 10.9 us
  Pallas kernels: 4.5 us -> 5.03 us
    unnamed x18 -> x10, local copies, waits for them, and re-layouts: 3.15 us -> 1.31 us
    all_to_all x1, waiting for transfers between devices: 10.2 us -> 10.9 us  [per_device(): lax.all_to_all(total, ('col', 'quad', 'half'), split_axis=0, concat_axis=...]
    pallas_call x1, Pallas kernels: 1.08 us -> 1.58 us  [per_device(): pl.pallas_call(project_kernel, out_shape=(jax.ShapeDtypeStruct((near, 2 *...]
where the time goes in v5:
time: 34.4 us; the launch traced here: 34.1 us
  blocking collectives  12.6 us (37%)
  waiting for transfers between devices  10.9 us (32%)
  Pallas kernels  5.03 us (15%)
  starting transfers between devices  4.19 us (12%)
  local copies, waits for them, and re-layouts  1.31 us (4%)
    all_to_all x1, blocking collectives, per_device(): lax.all_to_all(sides, ('col', 'quad'), split_axis=0, concat_axis=0, tiled...  12.6 us
    all_to_all x1, waiting for transfers between devices, per_device(): lax.all_to_all(total, ('col', 'quad', 'half'), split_axis=0, concat_axis=...  10.9 us
    all_to_all x1, starting transfers between devices, per_device(): lax.all_to_all(total, ('col', 'quad', 'half'), split_axis=0, concat_axis=...  4.19 us
    pallas_call x1, Pallas kernels, per_device(): pl.pallas_call(functools.partial(triangle_kernel, halves, cols, row_count...  2.25 us
    pallas_call x1, Pallas kernels, per_device(): pl.pallas_call(project_kernel, out_shape=(jax.ShapeDtypeStruct((near, 2 *...  1.58 us
    unnamed x10, local copies, waits for them, and re-layouts  1.31 us
    pallas_call x1, Pallas kernels, per_device(): pl.pallas_call(output_kernel, out_shape=jax.ShapeDtypeStruct(pair.shape,...  1.03 us
  transfers between devices with their start and end apart: 1, of which 1 were waited for; matrix products, arithmetic and copies ran while one was open for 0% of the time, Pallas kernels for 1%

profile of v5, /device:TPU:0, one launch (start us, length us, event | category | flops | bytes accessed | tf_op | source)
XLA Modules:
  0.0 34.1 jit_solution(355051770064755846)
XLA Ops:
  0.0 1.6 %shard_map.91 = (bf16[8,32,576]{2,1,0:T(8,128)(2,1)S(1)}, bf16[576,128]{1,0:T(8,128)(2,1)S(1)}, f32[48,96]{1,0:T(8,128)S(1)}) custom-call(bf16[12,48,128]{2,1,0:T(8,128)(2,1)} %pair_hbm.1, f32[1,128]{1,0:T(1,128)} %bitcast.9, f32[1,128]{1,0:T(1,128)} %bitcast.10, bf16[128,512]{1,0:T(8,128)(2,1)} %w_hbm.1, s32[1,96]{1,0:T(1,128)} %bitcast.5), custom_call_target="tpu_custom_call" | custom-call | tf_op jit(solution)/shard_map/pallas_call | solution.py:124
  1.6 12.6 %all_to_all.10.got_ref = bf16[8,32,576]{2,1,0:T(8,128)(2,1)S(1)} all-to-all(bf16[8,32,576]{2,1,0:T(8,128)(2,1)S(1)} %get-tuple-element.11), channel_id=1, replica_groups=mesh['groups'=2,'half'=2,'quad'=4,'col'=2] {'col','quad'}, dimensions={0} | all-to-all | bytes 589824 | tf_op jit(solution)/shard_map/all_to_all | solution.py:144
  14.2 0.0 copy-start.2
  14.2 0.7 %copy-done.2 = s32[96]{0:T(128)S(1)} copy-done((s32[96]{0:T(128)S(1)}, s32[96]{0:T(128)}, u32[]{:S(2)}) %copy-start.2) | copy-done | bytes 408
  14.8 2.2 %shard_map.92 = bf16[16,16,576]{2,1,0:T(8,128)(2,1)} custom-call(bf16[8,32,576]{2,1,0:T(8,128)(2,1)S(1)} %all_to_all.10.got_ref, f32[48,96]{1,0:T(8,128)S(1)} %get-tuple-element.12.left_mask_ref, s32[1,96]{1,0:T(1,128)S(1)} %bitcast.6), custom_call_target="tpu_custom_call" | custom-call | tf_op jit(solution)/shard_map/pallas_call | solution.py:145
  17.1 0.0 copy-start.1
  17.1 4.2 %all-to-all-start.1 = ((bf16[16,16,576]{2,1,0:T(8,128)(2,1)}), bf16[16,16,576]{2,1,0:T(8,128)(2,1)S(1)}, u32[]{:S(2)}, u32[]{:S(2)}) async-start(bf16[16,16,576]{2,1,0:T(8,128)(2,1)} %shard_map.92), calls=%async_computation.1 | async-start | bytes 655360 | tf_op jit(solution)/shard_map/all_to_all | solution.py:169
  21.3 0.0 copy-start.3
  21.3 0.0 copy-start.4
  21.3 0.0 copy-done.1
  21.3 0.6 %copy-done.3 = f32[128]{0:T(128)S(1)} copy-done((f32[128]{0:T(128)S(1)}, f32[128]{0:T(128)}, u32[]{:S(2)}) %copy-start.3) | copy-done | bytes 536
  21.9 0.0 copy-done.4
  22.0 0.0 copy-start
  22.0 0.2 shard_map.93
  22.2 10.9 %all-to-all-done.1.total_ref = bf16[16,16,576]{2,1,0:T(8,128)(2,1)S(1)} async-done(((bf16[16,16,576]{2,1,0:T(8,128)(2,1)}), bf16[16,16,576]{2,1,0:T(8,128)(2,1)S(1)}, u32[]{:S(2)}, u32[]{:S(2)}) %all-to-all-start.1) | async-done | bytes 294944 | tf_op jit(solution)/shard_map/all_to_all | solution.py:169
  33.0 0.0 copy-done
  33.0 1.0 %shard_map.94 = bf16[12,48,128]{2,1,0:T(8,128)(2,1)} custom-call(bf16[16,16,576]{2,1,0:T(8,128)(2,1)S(1)} %all-to-all-done.1.total_ref, f32[576,128]{1,0:T(8,128)S(1)} %get-tuple-element.14.gate_ref, f32[128,1]{1,0:T(8,128)S(1)} %get-tuple-element.15.gain_ref, f32[128,1]{1,0:T(8,128)S(1)} %get-tuple-element.16.bias_ref, bf16[128,128]{1,0:T(8,128)(2,1)S(1)} %copy-done), custom_call_target="tpu_custom_call" | custom-call | tf_op jit(solution)/shard_map/pallas_call | solution.py:170
Async XLA Ops:
  14.2 0.7 %copy-start.2 = (s32[96]{0:T(128)S(1)}, s32[96]{0:T(128)}, u32[]{:S(2)}) copy-start(s32[96]{0:T(128)} %param.10) | copy-start | bytes 1156
  17.1 4.2 %copy-start.1 = (bf16[128,128]{1,0:T(8,128)(2,1)S(1)}, bf16[128,128]{1,0:T(8,128)(2,1)}, u32[]{:S(2)}) copy-start(bf16[128,128]{1,0:T(8,128)(2,1)} %w_ref.2) | copy-start | bytes 98308
  17.1 15.9 %all-to-all-start.1 = ((bf16[16,16,576]{2,1,0:T(8,128)(2,1)}), bf16[16,16,576]{2,1,0:T(8,128)(2,1)S(1)}, u32[]{:S(2)}, u32[]{:S(2)}) async-start(bf16[16,16,576]{2,1,0:T(8,128)(2,1)} %shard_map.92), calls=%async_computation.1 | async-start | bytes 655360 | tf_op jit(solution)/shard_map/all_to_all | solution.py:169
  21.3 0.7 %copy-start.3 = (f32[128]{0:T(128)S(1)}, f32[128]{0:T(128)}, u32[]{:S(2)}) copy-start(f32[128]{0:T(128)} %param.15) | copy-start | bytes 1540
  21.3 0.7 %copy-start.4 = (f32[128]{0:T(128)S(1)}, f32[128]{0:T(128)}, u32[]{:S(2)}) copy-start(f32[128]{0:T(128)} %param.16) | copy-start | bytes 1540
  22.0 11.1 %copy-start = (bf16[128,128]{1,0:T(8,128)(2,1)S(1)}, bf16[128,128]{1,0:T(8,128)(2,1)}, u32[]{:S(2)}) copy-start(bf16[128,128]{1,0:T(8,128)(2,1)} %w_ref.3) | copy-start | bytes 98308

commit v6 on v5

--- a/solution.py
+++ b/solution.py
@@ -31,7 +31,7 @@
     return jnp.sum(jnp.where(eye, row, 0.0), axis=1, keepdims=True)
 
 
-def project_kernel(pair_hbm, gain_hbm, bias_hbm, w_hbm, mask_hbm, sides_ref, normed_ref, left_mask_ref, pair_ref, gain_ref, bias_ref, w_ref, mask_ref, column_ref, sems):
+def project_kernel(pair_hbm, gain_hbm, bias_hbm, w_hbm, mask_hbm, sides_ref, normed_ref, left_mask_ref, right_mask_ref, pair_ref, gain_ref, bias_ref, w_ref, mask_ref, column_ref, sems):
     copies = [
         pltpu.make_async_copy(source, target, sems.at[n])
         for n, (source, target) in enumerate(
@@ -47,6 +47,7 @@
     depth, length = left_mask_ref.shape
     copies[0].wait()
     mask_row = mask_ref[...].astype(jnp.float32)
+    right_mask_ref[...] = mask_row
     column_ref[...] = jnp.broadcast_to(column(mask_row), column_ref.shape)
     start = pl.multiple_of(lax.axis_index("half") * depth, depth)
     left_mask_ref[...] = column_ref[pl.ds(start, depth), 0:length] * mask_row
@@ -63,7 +64,7 @@
     sides_ref[...] = sides.astype(jnp.bfloat16)
 
 
-def triangle_kernel(halves, cols, row_count, col_count, got_ref, left_mask_ref, mask_ref, total_ref, wide_ref, sum_ref, flat_ref):
+def triangle_kernel(halves, cols, row_count, col_count, got_ref, left_mask_ref, right_mask_ref, total_ref, wide_ref, sum_ref, flat_ref):
     sources, both, _ = got_ref.shape
     share = both // 2
     depth, length = left_mask_ref.shape
@@ -75,7 +76,7 @@
             at = (row * row_count + k) * both
             wide_ref[at : at + both, col * col_count : (col + 1) * col_count] = piece[:, k * col_count : (k + 1) * col_count]
     left_mask = left_mask_ref[...]
-    right_mask = mask_ref[...].astype(jnp.float32)
+    right_mask = right_mask_ref[...]
     for c in range(share):
         left = (wide_ref[pl.ds(c, depth, stride=both), 0:length] * left_mask).astype(jnp.bfloat16)
         right = (wide_ref[pl.ds(share + c, depth, stride=both), 0:length] * right_mask).astype(jnp.bfloat16)
@@ -84,7 +85,7 @@
         )
     for target in range(sources * halves):
         col, row = divmod(target // halves, quads)
-        row += target % halves * quads
+        row += (halves - 1 - target % halves) * quads
         for i in range(row_count):
             at = (row * row_count + i) * share
             flat_ref[target * share : (target + 1) * share, i * col_count : (i + 1) * col_count] = sum_ref[
@@ -115,21 +116,24 @@
     hidden = w_out.shape[0]
     devices = rows * cols
     near = devices // halves
+    quads = rows // halves
+    far_order = [half * near + quad * cols + col for col in range(cols) for quad in range(quads) for half in reversed(range(halves))]
     share = hidden // near
     tokens = row_count * col_count
     length = rows * row_count
     depth = length // halves
     token_mask = token_mask.reshape(1, length)
     arguments = (pair, gain_in.reshape(1, channels), bias_in.reshape(1, channels), w_in, token_mask)
-    sides, normed, left_mask = pl.pallas_call(
+    sides, normed, left_mask, right_mask = pl.pallas_call(
         project_kernel,
         out_shape=(
             jax.ShapeDtypeStruct((near, 2 * share, tokens), jnp.bfloat16),
             jax.ShapeDtypeStruct((tokens, channels), jnp.bfloat16),
             jax.ShapeDtypeStruct((depth, length), jnp.float32),
+            jax.ShapeDtypeStruct((1, length), jnp.float32),
         ),
         in_specs=[HBM] * 5,
-        out_specs=(VMEM, VMEM, VMEM),
+        out_specs=(VMEM, VMEM, VMEM, VMEM),
         scratch_shapes=[
             pltpu.VMEM(pair.shape, pair.dtype),
             pltpu.VMEM((1, channels), jnp.float32),
@@ -153,7 +157,7 @@
             pltpu.VMEM((devices * share, tokens), jnp.float32),
         ],
         compiler_params=LIMIT,
-    )(got, left_mask, token_mask)
+    )(got, left_mask, right_mask)
     gate, gain_out, bias_out = pl.pallas_call(
         gate_kernel,
         out_shape=(
@@ -166,7 +170,7 @@
         compiler_params=LIMIT,
         cost_estimate=pl.CostEstimate(flops=2 * tokens * channels * channels, bytes_accessed=4 * tokens * channels, transcendentals=0),
     )(normed, w_gate, gain_out.reshape(1, hidden), bias_out.reshape(1, hidden))
-    total = lax.all_to_all(total, ("col", "quad", "half"), split_axis=0, concat_axis=0, tiled=True)
+    total = lax.all_to_all(total, ("half", "quad", "col"), split_axis=0, concat_axis=0, tiled=True, axis_index_groups=[far_order])
     return pl.pallas_call(
         output_kernel,
         out_shape=jax.ShapeDtypeStruct(pair.shape, jnp.bfloat16),

time: 34.4 us -> 33.6 us (0.977)
  waiting for transfers between devices: 10.9 us -> 8.84 us
  starting transfers between devices: 4.19 us -> 6.05 us
  local copies, waits for them, and re-layouts: 1.31 us -> 0.65 us
    all_to_all x1, waiting for transfers between devices: 10.9 us -> 8.84 us  [per_device(): lax.all_to_all(total, ('half', 'quad', 'col'), split_axis=0, concat_axis=...]
    all_to_all x1, starting transfers between devices: 4.19 us -> 6.05 us  [per_device(): lax.all_to_all(total, ('half', 'quad', 'col'), split_axis=0, concat_axis=...]
    unnamed x10 -> x8, local copies, waits for them, and re-layouts: 1.31 us -> 0.65 us
where the time goes in v6:
time: 33.6 us; the launch traced here: 33.2 us
  blocking collectives  12.6 us (38%)
  waiting for transfers between devices  8.84 us (26%)
  starting transfers between devices  6.05 us (18%)
  Pallas kernels  5.05 us (15%)
  local copies, waits for them, and re-layouts  0.65 us (2%)
    all_to_all x1, blocking collectives, per_device(): lax.all_to_all(sides, ('col', 'quad'), split_axis=0, concat_axis=0, tiled...  12.6 us
    all_to_all x1, waiting for transfers between devices, per_device(): lax.all_to_all(total, ('half', 'quad', 'col'), split_axis=0, concat_axis=...  8.84 us
    all_to_all x1, starting transfers between devices, per_device(): lax.all_to_all(total, ('half', 'quad', 'col'), split_axis=0, concat_axis=...  6.05 us
    pallas_call x1, Pallas kernels, per_device(): pl.pallas_call(functools.partial(triangle_kernel, halves, cols, row_count...  2.26 us
    pallas_call x1, Pallas kernels, per_device(): pl.pallas_call(project_kernel, out_shape=(jax.ShapeDtypeStruct((near, 2 *...  1.58 us
    pallas_call x1, Pallas kernels, per_device(): pl.pallas_call(output_kernel, out_shape=jax.ShapeDtypeStruct(pair.shape,...  1.03 us
  transfers between devices with their start and end apart: 1, of which 1 were waited for; matrix products, arithmetic and copies ran while one was open for 0% of the time, Pallas kernels for 1%

profile of v6, /device:TPU:0, one launch (start us, length us, event | category | flops | bytes accessed | tf_op | source)
XLA Modules:
  0.0 33.2 jit_solution(12987895390093686169)
XLA Ops:
  0.0 1.6 %shard_map.91 = (bf16[8,32,576]{2,1,0:T(8,128)(2,1)S(1)}, bf16[576,128]{1,0:T(8,128)(2,1)S(1)}, f32[48,96]{1,0:T(8,128)S(1)}, f32[1,96]{1,0:T(1,128)S(1)}) custom-call(bf16[12,48,128]{2,1,0:T(8,128)(2,1)} %pair_hbm.1, f32[1,128]{1,0:T(1,128)} %bitcast.7, f32[1,128]{1,0:T(1,128)} %bitcast.8, bf16[128,512]{1,0:T(8,128)(2,1)} %w_hbm.1, s32[1,96]{1,0:T(1,128)} %bitcast.9), custom_call_target="tpu_custom_call" | custom-call | tf_op jit(solution)/shard_map/pallas_call | solution.py:127
  1.6 12.6 %all_to_all.10.got_ref = bf16[8,32,576]{2,1,0:T(8,128)(2,1)S(1)} all-to-all(bf16[8,32,576]{2,1,0:T(8,128)(2,1)S(1)} %get-tuple-element.12), channel_id=1, replica_groups=mesh['groups'=2,'half'=2,'quad'=4,'col'=2] {'col','quad'}, dimensions={0} | all-to-all | bytes 589824 | tf_op jit(solution)/shard_map/all_to_all | solution.py:148
  14.2 2.3 %shard_map.92 = bf16[16,16,576]{2,1,0:T(8,128)(2,1)} custom-call(bf16[8,32,576]{2,1,0:T(8,128)(2,1)S(1)} %all_to_all.10.got_ref, f32[48,96]{1,0:T(8,128)S(1)} %get-tuple-element.13.left_mask_ref, f32[1,96]{1,0:T(1,128)S(1)} %get-tuple-element.14.right_mask_ref), custom_call_target="tpu_custom_call" | custom-call | tf_op jit(solution)/shard_map/pallas_call | solution.py:149
  16.4 0.0 copy-start.1
  16.4 6.1 %all-to-all-start.1 = ((bf16[16,16,576]{2,1,0:T(8,128)(2,1)}), bf16[16,16,576]{2,1,0:T(8,128)(2,1)S(1)}, u32[]{:S(2)}, u32[]{:S(2)}) async-start(bf16[16,16,576]{2,1,0:T(8,128)(2,1)} %shard_map.92), calls=%async_computation.1 | async-start | bytes 655360 | tf_op jit(solution)/shard_map/all_to_all | solution.py:173
  22.5 0.0 copy-start.2
  22.5 0.0 copy-start.3
  22.5 0.0 copy-done.1
  22.5 0.6 %copy-done.2 = f32[128]{0:T(128)S(1)} copy-done((f32[128]{0:T(128)S(1)}, f32[128]{0:T(128)}, u32[]{:S(2)}) %copy-start.2) | copy-done | bytes 536
  23.2 0.0 copy-done.3
  23.2 0.0 copy-start
  23.2 0.2 shard_map.93
  23.4 8.8 %all-to-all-done.1.total_ref = bf16[16,16,576]{2,1,0:T(8,128)(2,1)S(1)} async-done(((bf16[16,16,576]{2,1,0:T(8,128)(2,1)}), bf16[16,16,576]{2,1,0:T(8,128)(2,1)S(1)}, u32[]{:S(2)}, u32[]{:S(2)}) %all-to-all-start.1) | async-done | bytes 294944 | tf_op jit(solution)/shard_map/all_to_all | solution.py:173
  32.2 0.0 copy-done
  32.2 1.0 %shard_map.94 = bf16[12,48,128]{2,1,0:T(8,128)(2,1)} custom-call(bf16[16,16,576]{2,1,0:T(8,128)(2,1)S(1)} %all-to-all-done.1.total_ref, f32[576,128]{1,0:T(8,128)S(1)} %get-tuple-element.16.gate_ref, f32[128,1]{1,0:T(8,128)S(1)} %get-tuple-element.17.gain_ref, f32[128,1]{1,0:T(8,128)S(1)} %get-tuple-element.18.bias_ref, bf16[128,128]{1,0:T(8,128)(2,1)S(1)} %copy-done), custom_call_target="tpu_custom_call" | custom-call | tf_op jit(solution)/shard_map/pallas_call | solution.py:174
Async XLA Ops:
  16.4 6.1 %copy-start.1 = (bf16[128,128]{1,0:T(8,128)(2,1)S(1)}, bf16[128,128]{1,0:T(8,128)(2,1)}, u32[]{:S(2)}) copy-start(bf16[128,128]{1,0:T(8,128)(2,1)} %w_ref.2) | copy-start | bytes 98308
  16.4 15.8 %all-to-all-start.1 = ((bf16[16,16,576]{2,1,0:T(8,128)(2,1)}), bf16[16,16,576]{2,1,0:T(8,128)(2,1)S(1)}, u32[]{:S(2)}, u32[]{:S(2)}) async-start(bf16[16,16,576]{2,1,0:T(8,128)(2,1)} %shard_map.92), calls=%async_computation.1 | async-start | bytes 655360 | tf_op jit(solution)/shard_map/all_to_all | solution.py:173
  22.5 0.7 %copy-start.2 = (f32[128]{0:T(128)S(1)}, f32[128]{0:T(128)}, u32[]{:S(2)}) copy-start(f32[128]{0:T(128)} %param.15) | copy-start | bytes 1540
  22.5 0.7 %copy-start.3 = (f32[128]{0:T(128)S(1)}, f32[128]{0:T(128)}, u32[]{:S(2)}) copy-start(f32[128]{0:T(128)} %param.16) | copy-start | bytes 1540
  23.2 9.0 %copy-start = (bf16[128,128]{1,0:T(8,128)(2,1)S(1)}, bf16[128,128]{1,0:T(8,128)(2,1)}, u32[]{:S(2)}) copy-start(bf16[128,128]{1,0:T(8,128)(2,1)} %w_ref.3) | copy-start | bytes 98308

commit v7 on v6

--- a/solution.py
+++ b/solution.py
@@ -70,7 +70,7 @@
     depth, length = left_mask_ref.shape
     quads = sources // cols
     for source in range(sources):
-        col, row = divmod(source, quads)
+        col, row = divmod(sources - 1 - source, quads)
         piece = got_ref[source].astype(jnp.float32)
         for k in range(row_count):
             at = (row * row_count + k) * both
@@ -84,7 +84,7 @@
             left, right, (((0,), (0,)), ((), ())), preferred_element_type=jnp.float32
         )
     for target in range(sources * halves):
-        col, row = divmod(target // halves, quads)
+        col, row = divmod(sources - 1 - target // halves, quads)
         row += (halves - 1 - target % halves) * quads
         for i in range(row_count):
             at = (row * row_count + i) * share
@@ -117,7 +117,8 @@
     devices = rows * cols
     near = devices // halves
     quads = rows // halves
-    far_order = [half * near + quad * cols + col for col in range(cols) for quad in range(quads) for half in reversed(range(halves))]
+    near_order = [quad * cols + col for col in reversed(range(cols)) for quad in reversed(range(quads))]
+    far_order = [half * near + index for index in near_order for half in reversed(range(halves))]
     share = hidden // near
     tokens = row_count * col_count
     length = rows * row_count
@@ -145,7 +146,7 @@
         ],
         compiler_params=LIMIT,
     )(*(pltpu.with_memory_space_constraint(x, pltpu.HBM) for x in arguments))
-    got = lax.all_to_all(sides, ("col", "quad"), split_axis=0, concat_axis=0, tiled=True)
+    got = lax.all_to_all(sides, ("quad", "col"), split_axis=0, concat_axis=0, tiled=True, axis_index_groups=[near_order])
     total = pl.pallas_call(
         functools.partial(triangle_kernel, halves, cols, row_count, col_count),
         out_shape=jax.ShapeDtypeStruct((devices, share, tokens), jnp.bfloat16),

time: 33.6 us -> 31.4 us (0.935)
  the two profiles are of different devices: /device:TPU:0 before, /device:TPU:1 now
where the time goes in v7:
time: 31.4 us; the launch traced here: 31.1 us
  blocking collectives  10.4 us (33%)
  starting transfers between devices  7.79 us (25%)
  waiting for transfers between devices  7.13 us (23%)
  Pallas kernels  5.06 us (16%)
  local copies, waits for them, and re-layouts  0.65 us (2%)
    all_to_all x1, blocking collectives, per_device(): lax.all_to_all(sides, ('quad', 'col'), split_axis=0, concat_axis=0, tiled...  10.4 us
    all_to_all x1, starting transfers between devices, per_device(): lax.all_to_all(total, ('half', 'quad', 'col'), split_axis=0, concat_axis=...  7.79 us
    all_to_all x1, waiting for transfers between devices, per_device(): lax.all_to_all(total, ('half', 'quad', 'col'), split_axis=0, concat_axis=...  7.13 us
    pallas_call x1, Pallas kernels, per_device(): pl.pallas_call(functools.partial(triangle_kernel, halves, cols, row_count...  2.27 us
    pallas_call x1, Pallas kernels, per_device(): pl.pallas_call(project_kernel, out_shape=(jax.ShapeDtypeStruct((near, 2 *...  1.57 us
    pallas_call x1, Pallas kernels, per_device(): pl.pallas_call(output_kernel, out_shape=jax.ShapeDtypeStruct(pair.shape,...  1.03 us
    unnamed x8, local copies, waits for them, and re-layouts  0.65 us
  transfers between devices with their start and end apart: 1, of which 1 were waited for; matrix products, arithmetic and copies ran while one was open for 0% of the time, Pallas kernels for 1%

profile of v7, /device:TPU:1, one launch (start us, length us, event | category | flops | bytes accessed | tf_op | source)
XLA Modules:
  0.0 31.1 jit_solution(9011045128746001343)
XLA Ops:
  0.0 1.6 %shard_map.91 = (bf16[8,32,576]{2,1,0:T(8,128)(2,1)S(1)}, bf16[576,128]{1,0:T(8,128)(2,1)S(1)}, f32[48,96]{1,0:T(8,128)S(1)}, f32[1,96]{1,0:T(1,128)S(1)}) custom-call(bf16[12,48,128]{2,1,0:T(8,128)(2,1)} %pair_hbm.1, f32[1,128]{1,0:T(1,128)} %bitcast.7, f32[1,128]{1,0:T(1,128)} %bitcast.8, bf16[128,512]{1,0:T(8,128)(2,1)} %w_hbm.1, s32[1,96]{1,0:T(1,128)} %bitcast.9), custom_call_target="tpu_custom_call" | custom-call | tf_op jit(solution)/shard_map/pallas_call | solution.py:128
  1.6 10.4 %all_to_all.10.got_ref = bf16[8,32,576]{2,1,0:T(8,128)(2,1)S(1)} all-to-all(bf16[8,32,576]{2,1,0:T(8,128)(2,1)S(1)} %get-tuple-element.12), channel_id=1, replica_groups={{7,5,3,1,6,4,2,0},{15,13,11,9,14,12,10,8},{23,21,19,17,22,20,18,16},{31..., dimensions={0} | all-to-all | bytes 589824 | tf_op jit(solution)/shard_map/all_to_all | solution.py:149
  12.0 2.3 %shard_map.92 = bf16[16,16,576]{2,1,0:T(8,128)(2,1)} custom-call(bf16[8,32,576]{2,1,0:T(8,128)(2,1)S(1)} %all_to_all.10.got_ref, f32[48,96]{1,0:T(8,128)S(1)} %get-tuple-element.13.left_mask_ref, f32[1,96]{1,0:T(1,128)S(1)} %get-tuple-element.14.right_mask_ref), custom_call_target="tpu_custom_call" | custom-call | tf_op jit(solution)/shard_map/pallas_call | solution.py:150
  14.3 0.0 copy-start.1
  14.3 7.8 %all-to-all-start.1 = ((bf16[16,16,576]{2,1,0:T(8,128)(2,1)}), bf16[16,16,576]{2,1,0:T(8,128)(2,1)S(1)}, u32[]{:S(2)}, u32[]{:S(2)}) async-start(bf16[16,16,576]{2,1,0:T(8,128)(2,1)} %shard_map.92), calls=%async_computation.1 | async-start | bytes 655360 | tf_op jit(solution)/shard_map/all_to_all | solution.py:174
  22.1 0.0 copy-start.2
  22.1 0.0 copy-start.3
  22.1 0.0 copy-done.1
  22.1 0.6 %copy-done.2 = f32[128]{0:T(128)S(1)} copy-done((f32[128]{0:T(128)S(1)}, f32[128]{0:T(128)}, u32[]{:S(2)}) %copy-start.2) | copy-done | bytes 536
  22.7 0.0 copy-done.3
  22.7 0.0 copy-start
  22.7 0.2 shard_map.93
  22.9 7.1 %all-to-all-done.1.total_ref = bf16[16,16,576]{2,1,0:T(8,128)(2,1)S(1)} async-done(((bf16[16,16,576]{2,1,0:T(8,128)(2,1)}), bf16[16,16,576]{2,1,0:T(8,128)(2,1)S(1)}, u32[]{:S(2)}, u32[]{:S(2)}) %all-to-all-start.1) | async-done | bytes 294944 | tf_op jit(solution)/shard_map/all_to_all | solution.py:174
  30.1 0.0 copy-done
  30.1 1.0 %shard_map.94 = bf16[12,48,128]{2,1,0:T(8,128)(2,1)} custom-call(bf16[16,16,576]{2,1,0:T(8,128)(2,1)S(1)} %all-to-all-done.1.total_ref, f32[576,128]{1,0:T(8,128)S(1)} %get-tuple-element.16.gate_ref, f32[128,1]{1,0:T(8,128)S(1)} %get-tuple-element.17.gain_ref, f32[128,1]{1,0:T(8,128)S(1)} %get-tuple-element.18.bias_ref, bf16[128,128]{1,0:T(8,128)(2,1)S(1)} %copy-done), custom_call_target="tpu_custom_call" | custom-call | tf_op jit(solution)/shard_map/pallas_call | solution.py:175
Async XLA Ops:
  14.3 7.8 %copy-start.1 = (bf16[128,128]{1,0:T(8,128)(2,1)S(1)}, bf16[128,128]{1,0:T(8,128)(2,1)}, u32[]{:S(2)}) copy-start(bf16[128,128]{1,0:T(8,128)(2,1)} %w_ref.2) | copy-start | bytes 98308
  14.3 15.8 %all-to-all-start.1 = ((bf16[16,16,576]{2,1,0:T(8,128)(2,1)}), bf16[16,16,576]{2,1,0:T(8,128)(2,1)S(1)}, u32[]{:S(2)}, u32[]{:S(2)}) async-start(bf16[16,16,576]{2,1,0:T(8,128)(2,1)} %shard_map.92), calls=%async_computation.1 | async-start | bytes 655360 | tf_op jit(solution)/shard_map/all_to_all | solution.py:174
  22.1 0.7 %copy-start.2 = (f32[128]{0:T(128)S(1)}, f32[128]{0:T(128)}, u32[]{:S(2)}) copy-start(f32[128]{0:T(128)} %param.15) | copy-start | bytes 1540
  22.1 0.7 %copy-start.3 = (f32[128]{0:T(128)S(1)}, f32[128]{0:T(128)}, u32[]{:S(2)}) copy-start(f32[128]{0:T(128)} %param.16) | copy-start | bytes 1540
  22.7 7.3 %copy-start = (bf16[128,128]{1,0:T(8,128)(2,1)S(1)}, bf16[128,128]{1,0:T(8,128)(2,1)}, u32[]{:S(2)}) copy-start(bf16[128,128]{1,0:T(8,128)(2,1)} %w_ref.3) | copy-start | bytes 98308

commit v8 on v7

--- a/solution.py
+++ b/solution.py
@@ -8,6 +8,7 @@
 from jax.sharding import PartitionSpec as P
 
 epsilon = 1e-05
+LANES = 128
 AXES = ("half", "quad", "col")
 VMEM = pl.BlockSpec(memory_space=pltpu.VMEM)
 HBM = pl.BlockSpec(memory_space=pltpu.HBM)
@@ -29,6 +30,25 @@
     n = row.shape[1]
     eye = lax.broadcasted_iota(jnp.int32, (n, n), 0) == lax.broadcasted_iota(jnp.int32, (n, n), 1)
     return jnp.sum(jnp.where(eye, row, 0.0), axis=1, keepdims=True)
+
+
+def pack(x):
+    rows, tokens = x.shape[-2:]
+    whole, rest = divmod(tokens, LANES)
+    blocks = [x[..., t * LANES : (t + 1) * LANES] for t in range(whole)]
+    if rest:
+        tail = x[..., whole * LANES :]
+        blocks.append(jnp.concatenate([tail[..., : rows // 2, :], tail[..., rows // 2 :, :]], axis=-1))
+    return jnp.concatenate(blocks, axis=-2)
+
+
+def unpack(x, rows):
+    whole, rest = divmod(x.shape[-2], rows)
+    blocks = [x[..., t * rows : (t + 1) * rows, :] for t in range(whole)]
+    if rest:
+        tail = x[..., whole * rows :, :]
+        blocks.append(jnp.concatenate([tail[..., : LANES // 2], tail[..., LANES // 2 :]], axis=-2))
+    return jnp.concatenate(blocks, axis=-1)
 
 
 def project_kernel(pair_hbm, gain_hbm, bias_hbm, w_hbm, mask_hbm, sides_ref, normed_ref, left_mask_ref, right_mask_ref, pair_ref, gain_ref, bias_ref, w_ref, mask_ref, column_ref, sems):
@@ -40,10 +60,10 @@
     ]
     for copy in copies:
         copy.start()
-    devices, both, tokens = sides_ref.shape
-    channels = pair_ref.shape[2]
+    devices = sides_ref.shape[0]
+    tokens, channels = normed_ref.shape
     hidden = w_ref.shape[1] // 4
-    share = both // 2
+    share = hidden // devices
     depth, length = left_mask_ref.shape
     copies[0].wait()
     mask_row = mask_ref[...].astype(jnp.float32)
@@ -61,37 +81,38 @@
     left = sigmoid(projected[:hidden]) * projected[hidden : 2 * hidden]
     right = sigmoid(projected[2 * hidden : 3 * hidden]) * projected[3 * hidden :]
     sides = jnp.concatenate([left.reshape(devices, share, tokens), right.reshape(devices, share, tokens)], axis=1)
-    sides_ref[...] = sides.astype(jnp.bfloat16)
-
-
-def triangle_kernel(halves, cols, row_count, col_count, got_ref, left_mask_ref, right_mask_ref, total_ref, wide_ref, sum_ref, flat_ref):
-    sources, both, _ = got_ref.shape
-    share = both // 2
+    sides_ref[...] = pack(sides).astype(jnp.bfloat16)
+
+
+def triangle_kernel(halves, cols, row_count, col_count, share, got_ref, left_mask_ref, right_mask_ref, total_ref, wide_ref, sum_ref, flat_ref):
+    sources = got_ref.shape[0]
+    both = 2 * share
     depth, length = left_mask_ref.shape
+    wide_step, sum_step = wide_ref.shape[0] // depth, sum_ref.shape[0] // length
     quads = sources // cols
     for source in range(sources):
         col, row = divmod(sources - 1 - source, quads)
-        piece = got_ref[source].astype(jnp.float32)
+        piece = unpack(got_ref[source].astype(jnp.float32), both)
         for k in range(row_count):
-            at = (row * row_count + k) * both
+            at = (row * row_count + k) * wide_step
             wide_ref[at : at + both, col * col_count : (col + 1) * col_count] = piece[:, k * col_count : (k + 1) * col_count]
     left_mask = left_mask_ref[...]
     right_mask = right_mask_ref[...]
     for c in range(share):
-        left = (wide_ref[pl.ds(c, depth, stride=both), 0:length] * left_mask).astype(jnp.bfloat16)
-        right = (wide_ref[pl.ds(share + c, depth, stride=both), 0:length] * right_mask).astype(jnp.bfloat16)
-        sum_ref[pl.ds(c, length, stride=share), 0:length] = lax.dot_general(
+        left = (wide_ref[pl.ds(c, depth, stride=wide_step), 0:length] * left_mask).astype(jnp.bfloat16)
+        right = (wide_ref[pl.ds(share + c, depth, stride=wide_step), 0:length] * right_mask).astype(jnp.bfloat16)
+        sum_ref[pl.ds(c, length, stride=sum_step), 0:length] = lax.dot_general(
             left, right, (((0,), (0,)), ((), ())), preferred_element_type=jnp.float32
         )
     for target in range(sources * halves):
         col, row = divmod(sources - 1 - target // halves, quads)
         row += (halves - 1 - target % halves) * quads
         for i in range(row_count):
-            at = (row * row_count + i) * share
+            at = (row * row_count + i) * sum_step
             flat_ref[target * share : (target + 1) * share, i * col_count : (i + 1) * col_count] = sum_ref[
                 at : at + share, col * col_count : (col + 1) * col_count
             ]
-        total_ref[target] = flat_ref[target * share : (target + 1) * share, :].astype(jnp.bfloat16)
+        total_ref[target] = pack(flat_ref[target * share : (target + 1) * share, :]).astype(jnp.bfloat16)
 
 
 def gate_kernel(normed_ref, w_ref, gain_ref, bias_ref, gate_ref, gain_out_ref, bias_out_ref):
@@ -101,11 +122,13 @@
 
 
 def output_kernel(total_ref, gate_ref, gain_ref, bias_ref, w_ref, out_ref):
-    sources, share, tokens = total_ref.shape
+    sources, packed, _ = total_ref.shape
+    tokens = gate_ref.shape[0]
     hidden = w_ref.shape[0]
-    halves = sources * share // hidden
-    parts = total_ref[...].astype(jnp.float32).reshape(sources // halves, halves, share, tokens)
-    total = jnp.sum(parts, axis=1).reshape(hidden, tokens)
+    share = packed * LANES // tokens
+    near = hidden // share
+    parts = total_ref[...].astype(jnp.float32).reshape(near, sources // near, packed, LANES)
+    total = unpack(jnp.sum(parts, axis=1), share).reshape(hidden, tokens)
     normed = layer_norm(total, gain_ref[...], bias_ref[...], 0).astype(jnp.bfloat16)
     output = lax.dot_general(normed, w_ref[...], (((0,), (0,)), ((), ())), preferred_element_type=jnp.float32)
     out_ref[...] = (gate_ref[...] * output).astype(jnp.bfloat16).reshape(out_ref.shape)
@@ -128,7 +151,7 @@
     sides, normed, left_mask, right_mask = pl.pallas_call(
         project_kernel,
         out_shape=(
-            jax.ShapeDtypeStruct((near, 2 * share, tokens), jnp.bfloat16),
+            jax.ShapeDtypeStruct((near, 2 * share * tokens // LANES, LANES), jnp.bfloat16),
             jax.ShapeDtypeStruct((tokens, channels), jnp.bfloat16),
             jax.ShapeDtypeStruct((depth, length), jnp.float32),
             jax.ShapeDtypeStruct((1, length), jnp.float32),
@@ -141,20 +164,20 @@
             pltpu.VMEM((1, channels), jnp.float32),
             pltpu.VMEM(w_in.shape, w_in.dtype),
             pltpu.VMEM((1, length), jnp.int32),
-            pltpu.VMEM((length, 128), jnp.float32),
+            pltpu.VMEM((length, LANES), jnp.float32),
             pltpu.SemaphoreType.DMA((5,)),
         ],
         compiler_params=LIMIT,
     )(*(pltpu.with_memory_space_constraint(x, pltpu.HBM) for x in arguments))
     got = lax.all_to_all(sides, ("quad", "col"), split_axis=0, concat_axis=0, tiled=True, axis_index_groups=[near_order])
     total = pl.pallas_call(
-        functools.partial(triangle_kernel, halves, cols, row_count, col_count),
-        out_shape=jax.ShapeDtypeStruct((devices, share, tokens), jnp.bfloat16),
+        functools.partial(triangle_kernel, halves, cols, row_count, col_count, share),
+        out_shape=jax.ShapeDtypeStruct((devices, share * tokens // LANES, LANES), jnp.bfloat16),
         in_specs=[VMEM] * 3,
         out_specs=VMEM,
         scratch_shapes=[
-            pltpu.VMEM((depth * 2 * share, 128), jnp.float32),
-            pltpu.VMEM((length * share, 128), jnp.float32),
+            pltpu.VMEM((depth * (2 * share + 8), LANES), jnp.float32),
+            pltpu.VMEM((length * (share + 8), LANES), jnp.float32),
             pltpu.VMEM((devices * share, tokens), jnp.float32),
         ],
         compiler_params=LIMIT,
@@ -221,7 +244,8 @@
 
     def per_shard(*args):
         near, hidden, length = rows * cols // halves, args[-1].shape[0], args[1].shape[0]
-        if hidden % (16 * near) == 0 and length <= 128:
+        tokens = args[0].shape[0] * args[0].shape[1]
+        if hidden % (16 * near) == 0 and length <= LANES and tokens % (LANES // 2) == 0:
             return per_device(rows, cols, halves, *args)
         return plain_per_device(rows, cols, *args)
 

time: 31.4 us -> 31.2 us (level)
  Pallas kernels: 5.06 us -> 5.79 us
  waiting for transfers between devices: 7.13 us -> 6.48 us
  blocking collectives: 10.4 us -> 10 us
    pallas_call x1, Pallas kernels: 2.27 us -> 2.96 us  [per_device(): pl.pallas_call(functools.partial(triangle_kernel, halves, cols, row_count...]
    all_to_all x1, waiting for transfers between devices: 7.13 us -> 6.48 us  [per_device(): lax.all_to_all(total, ('half', 'quad', 'col'), split_axis=0, concat_axis=...]
    all_to_all x1, blocking collectives: 10.4 us -> 10 us  [per_device(): lax.all_to_all(sides, ('quad', 'col'), split_axis=0, concat_axis=0, tiled...]
where the time goes in v8:
time: 31.2 us; the launch traced here: 30.9 us
  blocking collectives  10 us (32%)
  starting transfers between devices  7.89 us (25%)
  waiting for transfers between devices  6.48 us (21%)
  Pallas kernels  5.79 us (19%)
  local copies, waits for them, and re-layouts  0.65 us (2%)
    all_to_all x1, blocking collectives, per_device(): lax.all_to_all(sides, ('quad', 'col'), split_axis=0, concat_axis=0, tiled...  10 us
    all_to_all x1, starting transfers between devices, per_device(): lax.all_to_all(total, ('half', 'quad', 'col'), split_axis=0, concat_axis=...  7.89 us
    all_to_all x1, waiting for transfers between devices, per_device(): lax.all_to_all(total, ('half', 'quad', 'col'), split_axis=0, concat_axis=...  6.48 us
    pallas_call x1, Pallas kernels, per_device(): pl.pallas_call(functools.partial(triangle_kernel, halves, cols, row_count...  2.96 us
    pallas_call x1, Pallas kernels, per_device(): pl.pallas_call(project_kernel, out_shape=(jax.ShapeDtypeStruct((near, 2 *...  1.64 us
    pallas_call x1, Pallas kernels, per_device(): pl.pallas_call(output_kernel, out_shape=jax.ShapeDtypeStruct(pair.shape,...  1.01 us
    unnamed x8, local copies, waits for them, and re-layouts  0.65 us
  transfers between devices with their start and end apart: 1, of which 1 were waited for; matrix products, arithmetic and copies ran while one was open for 0% of the time, Pallas kernels for 1%

profile of v8, /device:TPU:1, one launch (start us, length us, event | category | flops | bytes accessed | tf_op | source)
XLA Modules:
  0.0 30.9 jit_solution(17841848660030369362)
XLA Ops:
  0.0 1.6 %shard_map.91 = (bf16[8,144,128]{2,1,0:T(8,128)(2,1)S(1)}, bf16[576,128]{1,0:T(8,128)(2,1)S(1)}, f32[48,96]{1,0:T(8,128)S(1)}, f32[1,96]{1,0:T(1,128)S(1)}) custom-call(bf16[12,48,128]{2,1,0:T(8,128)(2,1)} %pair_hbm.1, f32[1,128]{1,0:T(1,128)} %bitcast.7, f32[1,128]{1,0:T(1,128)} %bitcast.8, bf16[128,512]{1,0:T(8,128)(2,1)} %w_hbm.1, s32[1,96]{1,0:T(1,128)} %bitcast.9), custom_call_target="tpu_custom_call" | custom-call | tf_op jit(solution)/shard_map/pallas_call | solution.py:151
  1.6 10.0 %all_to_all.10.got_ref = bf16[8,144,128]{2,1,0:T(8,128)(2,1)S(1)} all-to-all(bf16[8,144,128]{2,1,0:T(8,128)(2,1)S(1)} %get-tuple-element.12), channel_id=1, replica_groups={{7,5,3,1,6,4,2,0},{15,13,11,9,14,12,10,8},{23,21,19,17,22,20,18,16},{31..., dimensions={0} | all-to-all | bytes 589824 | tf_op jit(solution)/shard_map/all_to_all | solution.py:172
  11.7 3.0 %shard_map.92 = bf16[16,72,128]{2,1,0:T(8,128)(2,1)} custom-call(bf16[8,144,128]{2,1,0:T(8,128)(2,1)S(1)} %all_to_all.10.got_ref, f32[48,96]{1,0:T(8,128)S(1)} %get-tuple-element.13.left_mask_ref, f32[1,96]{1,0:T(1,128)S(1)} %get-tuple-element.14.right_mask_ref), custom_call_target="tpu_custom_call" | custom-call | tf_op jit(solution)/shard_map/pallas_call | solution.py:173
  14.6 0.0 copy-start.1
  14.6 7.9 %all-to-all-start.1 = ((bf16[16,72,128]{2,1,0:T(8,128)(2,1)}), bf16[16,72,128]{2,1,0:T(8,128)(2,1)S(1)}, u32[]{:S(2)}, u32[]{:S(2)}) async-start(bf16[16,72,128]{2,1,0:T(8,128)(2,1)} %shard_map.92), calls=%async_computation.1 | async-start | bytes 589824 | tf_op jit(solution)/shard_map/all_to_all | solution.py:197
  22.5 0.0 copy-start.2
  22.5 0.0 copy-start.3
  22.5 0.0 copy-done.1
  22.5 0.6 %copy-done.2 = f32[128]{0:T(128)S(1)} copy-done((f32[128]{0:T(128)S(1)}, f32[128]{0:T(128)}, u32[]{:S(2)}) %copy-start.2) | copy-done | bytes 536
  23.2 0.0 copy-done.3
  23.2 0.0 copy-start
  23.2 0.2 shard_map.93
  23.4 6.5 %all-to-all-done.1.total_ref = bf16[16,72,128]{2,1,0:T(8,128)(2,1)S(1)} async-done(((bf16[16,72,128]{2,1,0:T(8,128)(2,1)}), bf16[16,72,128]{2,1,0:T(8,128)(2,1)S(1)}, u32[]{:S(2)}, u32[]{:S(2)}) %all-to-all-start.1) | async-done | bytes 294944 | tf_op jit(solution)/shard_map/all_to_all | solution.py:197
  29.9 0.0 copy-done
  29.9 1.0 %shard_map.94 = bf16[12,48,128]{2,1,0:T(8,128)(2,1)} custom-call(bf16[16,72,128]{2,1,0:T(8,128)(2,1)S(1)} %all-to-all-done.1.total_ref, f32[576,128]{1,0:T(8,128)S(1)} %get-tuple-element.16.gate_ref, f32[128,1]{1,0:T(8,128)S(1)} %get-tuple-element.17.gain_ref, f32[128,1]{1,0:T(8,128)S(1)} %get-tuple-element.18.bias_ref, bf16[128,128]{1,0:T(8,128)(2,1)S(1)} %copy-done), custom_call_target="tpu_custom_call" | custom-call | tf_op jit(solution)/shard_map/pallas_call | solution.py:198
Async XLA Ops:
  14.6 7.9 %copy-start.1 = (bf16[128,128]{1,0:T(8,128)(2,1)S(1)}, bf16[128,128]{1,0:T(8,128)(2,1)}, u32[]{:S(2)}) copy-start(bf16[128,128]{1,0:T(8,128)(2,1)} %w_ref.2) | copy-start | bytes 98308
  14.6 15.2 %all-to-all-start.1 = ((bf16[16,72,128]{2,1,0:T(8,128)(2,1)}), bf16[16,72,128]{2,1,0:T(8,128)(2,1)S(1)}, u32[]{:S(2)}, u32[]{:S(2)}) async-start(bf16[16,72,128]{2,1,0:T(8,128)(2,1)} %shard_map.92), calls=%async_computation.1 | async-start | bytes 589824 | tf_op jit(solution)/shard_map/all_to_all | solution.py:197
  22.5 0.7 %copy-start.2 = (f32[128]{0:T(128)S(1)}, f32[128]{0:T(128)}, u32[]{:S(2)}) copy-start(f32[128]{0:T(128)} %param.15) | copy-start | bytes 1540
  22.5 0.7 %copy-start.3 = (f32[128]{0:T(128)S(1)}, f32[128]{0:T(128)}, u32[]{:S(2)}) copy-start(f32[128]{0:T(128)} %param.16) | copy-start | bytes 1540
  23.2 6.7 %copy-start = (bf16[128,128]{1,0:T(8,128)(2,1)S(1)}, bf16[128,128]{1,0:T(8,128)(2,1)}, u32[]{:S(2)}) copy-start(bf16[128,128]{1,0:T(8,128)(2,1)} %w_ref.3) | copy-start | bytes 98308

commit v9 on v8

--- a/solution.py
+++ b/solution.py
@@ -9,6 +9,7 @@
 
 epsilon = 1e-05
 LANES = 128
+GROUP = 8
 AXES = ("half", "quad", "col")
 VMEM = pl.BlockSpec(memory_space=pltpu.VMEM)
 HBM = pl.BlockSpec(memory_space=pltpu.HBM)
@@ -51,7 +52,7 @@
     return jnp.concatenate(blocks, axis=-1)
 
 
-def project_kernel(pair_hbm, gain_hbm, bias_hbm, w_hbm, mask_hbm, sides_ref, normed_ref, left_mask_ref, right_mask_ref, pair_ref, gain_ref, bias_ref, w_ref, mask_ref, column_ref, sems):
+def project_kernel(pair_hbm, gain_hbm, bias_hbm, w_hbm, mask_hbm, sides_ref, normed_ref, spread_ref, row_mask_ref, column_mask_ref, pair_ref, gain_ref, bias_ref, w_ref, mask_ref, sems):
     copies = [
         pltpu.make_async_copy(source, target, sems.at[n])
         for n, (source, target) in enumerate(
@@ -64,13 +65,19 @@
     tokens, channels = normed_ref.shape
     hidden = w_ref.shape[1] // 4
     share = hidden // devices
-    depth, length = left_mask_ref.shape
+    group, lanes = spread_ref.shape
     copies[0].wait()
     mask_row = mask_ref[...].astype(jnp.float32)
-    right_mask_ref[...] = mask_row
-    column_ref[...] = jnp.broadcast_to(column(mask_row), column_ref.shape)
-    start = pl.multiple_of(lax.axis_index("half") * depth, depth)
-    left_mask_ref[...] = column_ref[pl.ds(start, depth), 0:length] * mask_row
+    row_mask_ref[...] = mask_row
+    column_mask_ref[...] = column(mask_row)
+    start = lax.axis_index("half") * (lanes // group)
+    token = lax.broadcasted_iota(jnp.int32, (mask_row.shape[1], lanes), 0)
+    lane = lax.broadcasted_iota(jnp.int32, (mask_row.shape[1], lanes), 1)
+    pick = jnp.where(lane // group + start == token, 1.0, 0.0)
+    kept = jnp.dot(mask_row.astype(jnp.bfloat16), pick.astype(jnp.bfloat16), preferred_element_type=jnp.float32)
+    channel = lax.broadcasted_iota(jnp.int32, (group, lanes), 0)
+    lane = lax.broadcasted_iota(jnp.int32, (group, lanes), 1)
+    spread_ref[...] = jnp.where(lane % group == channel, kept, 0.0)
     for copy in copies[1:4]:
         copy.wait()
     flat = pair_ref[...].reshape(tokens, channels).astype(jnp.float32)
@@ -84,35 +91,31 @@
     sides_ref[...] = pack(sides).astype(jnp.bfloat16)
 
 
-def triangle_kernel(halves, cols, row_count, col_count, share, got_ref, left_mask_ref, right_mask_ref, total_ref, wide_ref, sum_ref, flat_ref):
+def triangle_kernel(halves, cols, row_count, col_count, share, got_ref, spread_ref, row_mask_ref, column_mask_ref, total_ref, wide_ref, sum_ref):
     sources = got_ref.shape[0]
     both = 2 * share
-    depth, length = left_mask_ref.shape
-    wide_step, sum_step = wide_ref.shape[0] // depth, sum_ref.shape[0] // length
+    group, lanes = spread_ref.shape
+    depth = lanes // group
+    length = row_mask_ref.shape[1]
     quads = sources // cols
     for source in range(sources):
         col, row = divmod(sources - 1 - source, quads)
         piece = unpack(got_ref[source].astype(jnp.float32), both)
         for k in range(row_count):
-            at = (row * row_count + k) * wide_step
-            wide_ref[at : at + both, col * col_count : (col + 1) * col_count] = piece[:, k * col_count : (k + 1) * col_count]
-    left_mask = left_mask_ref[...]
-    right_mask = right_mask_ref[...]
-    for c in range(share):
-        left = (wide_ref[pl.ds(c, depth, stride=wide_step), 0:length] * left_mask).astype(jnp.bfloat16)
-        right = (wide_ref[pl.ds(share + c, depth, stride=wide_step), 0:length] * right_mask).astype(jnp.bfloat16)
-        sum_ref[pl.ds(c, length, stride=sum_step), 0:length] = lax.dot_general(
-            left, right, (((0,), (0,)), ((), ())), preferred_element_type=jnp.float32
-        )
+            wide_ref[row * row_count + k, :, col * col_count : (col + 1) * col_count] = piece[:, k * col_count : (k + 1) * col_count]
+    for part in range(share // group):
+        at = part * group
+        left = wide_ref[:, at : at + group, :].reshape(lanes, LANES).T[0:length] * column_mask_ref[...]
+        left = (left[:, None, :] * spread_ref[...][None]).reshape(length * group, lanes).astype(jnp.bfloat16)
+        right = wide_ref[:, share + at : share + at + group, :].reshape(lanes, LANES)[:, 0:length]
+        right = (right * row_mask_ref[...]).astype(jnp.bfloat16)
+        sums = jnp.dot(left, right, preferred_element_type=jnp.float32)
+        sum_ref[:, at : at + group, 0:length] = sums.reshape(length, group, length)
     for target in range(sources * halves):
         col, row = divmod(sources - 1 - target // halves, quads)
         row += (halves - 1 - target % halves) * quads
-        for i in range(row_count):
-            at = (row * row_count + i) * sum_step
-            flat_ref[target * share : (target + 1) * share, i * col_count : (i + 1) * col_count] = sum_ref[
-                at : at + share, col * col_count : (col + 1) * col_count
-            ]
-        total_ref[target] = pack(flat_ref[target * share : (target + 1) * share, :]).astype(jnp.bfloat16)
+        pieces = [sum_ref[row * row_count + i, :, col * col_count : (col + 1) * col_count] for i in range(row_count)]
+        total_ref[target] = pack(jnp.concatenate(pieces, axis=1)).astype(jnp.bfloat16)
 
 
 def gate_kernel(normed_ref, w_ref, gain_ref, bias_ref, gate_ref, gain_out_ref, bias_out_ref):
@@ -148,23 +151,23 @@
     depth = length // halves
     token_mask = token_mask.reshape(1, length)
     arguments = (pair, gain_in.reshape(1, channels), bias_in.reshape(1, channels), w_in, token_mask)
-    sides, normed, left_mask, right_mask = pl.pallas_call(
+    sides, normed, *masks = pl.pallas_call(
         project_kernel,
         out_shape=(
             jax.ShapeDtypeStruct((near, 2 * share * tokens // LANES, LANES), jnp.bfloat16),
             jax.ShapeDtypeStruct((tokens, channels), jnp.bfloat16),
-            jax.ShapeDtypeStruct((depth, length), jnp.float32),
+            jax.ShapeDtypeStruct((GROUP, GROUP * depth), jnp.float32),
             jax.ShapeDtypeStruct((1, length), jnp.float32),
+            jax.ShapeDtypeStruct((length, 1), jnp.float32),
         ),
         in_specs=[HBM] * 5,
-        out_specs=(VMEM, VMEM, VMEM, VMEM),
+        out_specs=(VMEM,) * 5,
         scratch_shapes=[
             pltpu.VMEM(pair.shape, pair.dtype),
             pltpu.VMEM((1, channels), jnp.float32),
             pltpu.VMEM((1, channels), jnp.float32),
             pltpu.VMEM(w_in.shape, w_in.dtype),
             pltpu.VMEM((1, length), jnp.int32),
-            pltpu.VMEM((length, LANES), jnp.float32),
             pltpu.SemaphoreType.DMA((5,)),
         ],
         compiler_params=LIMIT,
@@ -173,15 +176,14 @@
     total = pl.pallas_call(
         functools.partial(triangle_kernel, halves, cols, row_count, col_count, share),
         out_shape=jax.ShapeDtypeStruct((devices, share * tokens // LANES, LANES), jnp.bfloat16),
-        in_specs=[VMEM] * 3,
+        in_specs=[VMEM] * 4,
         out_specs=VMEM,
         scratch_shapes=[
-            pltpu.VMEM((depth * (2 * share + 8), LANES), jnp.float32),
-            pltpu.VMEM((length * (share + 8), LANES), jnp.float32),
-            pltpu.VMEM((devices * share, tokens), jnp.float32),
+            pltpu.VMEM((depth, 2 * share, LANES), jnp.float32),
+            pltpu.VMEM((length, share, LANES), jnp.float32),
         ],
         compiler_params=LIMIT,
-    )(got, left_mask, right_mask)
+    )(got, *masks)
     gate, gain_out, bias_out = pl.pallas_call(
         gate_kernel,
         out_shape=(

time: 31.2 us -> 30.3 us (0.971)
  Pallas kernels: 5.79 us -> 4.87 us
    pallas_call x1, Pallas kernels: 2.96 us -> 2.04 us  [per_device(): pl.pallas_call(functools.partial(triangle_kernel, halves, cols, row_count...]
where the time goes in v9:
time: 30.3 us; the launch traced here: 29.9 us
  blocking collectives  10 us (33%)
  starting transfers between devices  7.89 us (26%)
  waiting for transfers between devices  6.48 us (21%)
  Pallas kernels  4.87 us (16%)
  local copies, waits for them, and re-layouts  0.65 us (2%)
    all_to_all x1, blocking collectives, per_device(): lax.all_to_all(sides, ('quad', 'col'), split_axis=0, concat_axis=0, tiled...  10 us
    all_to_all x1, starting transfers between devices, per_device(): lax.all_to_all(total, ('half', 'quad', 'col'), split_axis=0, concat_axis=...  7.89 us
    all_to_all x1, waiting for transfers between devices, per_device(): lax.all_to_all(total, ('half', 'quad', 'col'), split_axis=0, concat_axis=...  6.48 us
    pallas_call x1, Pallas kernels, per_device(): pl.pallas_call(functools.partial(triangle_kernel, halves, cols, row_count...  2.04 us
    pallas_call x1, Pallas kernels, per_device(): pl.pallas_call(project_kernel, out_shape=(jax.ShapeDtypeStruct((near, 2 *...  1.64 us
    pallas_call x1, Pallas kernels, per_device(): pl.pallas_call(output_kernel, out_shape=jax.ShapeDtypeStruct(pair.shape,...  1.01 us
    unnamed x8, local copies, waits for them, and re-layouts  0.65 us
  transfers between devices with their start and end apart: 1, of which 1 were waited for; matrix products, arithmetic and copies ran while one was open for 0% of the time, Pallas kernels for 1%

profile of v9, /device:TPU:1, one launch (start us, length us, event | category | flops | bytes accessed | tf_op | source)
XLA Modules:
  0.0 29.9 jit_solution(8810571562145388475)
XLA Ops:
  0.0 1.6 %shard_map.91 = (bf16[8,144,128]{2,1,0:T(8,128)(2,1)S(1)}, bf16[576,128]{1,0:T(8,128)(2,1)S(1)}, f32[8,384]{1,0:T(8,128)S(1)}, f32[1,96]{1,0:T(1,128)S(1)}, f32[96,1]{1,0:T(8,128)S(1)}) custom-call(bf16[12,48,128]{2,1,0:T(8,128)(2,1)} %pair_hbm.1, f32[1,128]{1,0:T(1,128)} %bitcast.7, f32[1,128]{1,0:T(1,128)} %bitcast.8, bf16[128,512]{1,0:T(8,128)(2,1)} %w_hbm.1, ...), custom_call_target="tpu_custom_call" | custom-call | tf_op jit(solution)/shard_map/pallas_call | solution.py:154
  1.6 10.0 %all_to_all.10.got_ref = bf16[8,144,128]{2,1,0:T(8,128)(2,1)S(1)} all-to-all(bf16[8,144,128]{2,1,0:T(8,128)(2,1)S(1)} %get-tuple-element.13), channel_id=1, replica_groups={{7,5,3,1,6,4,2,0},{15,13,11,9,14,12,10,8},{23,21,19,17,22,20,18,16},{31..., dimensions={0} | all-to-all | bytes 589824 | tf_op jit(solution)/shard_map/all_to_all | solution.py:175
  11.7 2.0 %shard_map.92 = bf16[16,72,128]{2,1,0:T(8,128)(2,1)} custom-call(bf16[8,144,128]{2,1,0:T(8,128)(2,1)S(1)} %all_to_all.10.got_ref, f32[8,384]{1,0:T(8,128)S(1)} %get-tuple-element.14.spread_ref, f32[1,96]{1,0:T(1,128)S(1)} %get-tuple-element.15.row_mask_ref, f32[96,1]{1,0:T(8,128)S(1)} %get-tuple-element.16.column_mask_ref), custom_call_target="tpu_custom_call" | custom-call | tf_op jit(solution)/shard_map/pallas_call | solution.py:176
  13.7 0.0 copy-start.1
  13.7 7.9 %all-to-all-start.1 = ((bf16[16,72,128]{2,1,0:T(8,128)(2,1)}), bf16[16,72,128]{2,1,0:T(8,128)(2,1)S(1)}, u32[]{:S(2)}, u32[]{:S(2)}) async-start(bf16[16,72,128]{2,1,0:T(8,128)(2,1)} %shard_map.92), calls=%async_computation.1 | async-start | bytes 589824 | tf_op jit(solution)/shard_map/all_to_all | solution.py:199
  21.6 0.0 copy-start.2
  21.6 0.0 copy-start.3
  21.6 0.0 copy-done.1
  21.6 0.6 %copy-done.2 = f32[128]{0:T(128)S(1)} copy-done((f32[128]{0:T(128)S(1)}, f32[128]{0:T(128)}, u32[]{:S(2)}) %copy-start.2) | copy-done | bytes 536
  22.3 0.0 copy-done.3
  22.3 0.0 copy-start
  22.3 0.2 shard_map.93
  22.5 6.5 %all-to-all-done.1.total_ref = bf16[16,72,128]{2,1,0:T(8,128)(2,1)S(1)} async-done(((bf16[16,72,128]{2,1,0:T(8,128)(2,1)}), bf16[16,72,128]{2,1,0:T(8,128)(2,1)S(1)}, u32[]{:S(2)}, u32[]{:S(2)}) %all-to-all-start.1) | async-done | bytes 294944 | tf_op jit(solution)/shard_map/all_to_all | solution.py:199
  28.9 0.0 copy-done
  28.9 1.0 %shard_map.94 = bf16[12,48,128]{2,1,0:T(8,128)(2,1)} custom-call(bf16[16,72,128]{2,1,0:T(8,128)(2,1)S(1)} %all-to-all-done.1.total_ref, f32[576,128]{1,0:T(8,128)S(1)} %get-tuple-element.18.gate_ref, f32[128,1]{1,0:T(8,128)S(1)} %get-tuple-element.19.gain_ref, f32[128,1]{1,0:T(8,128)S(1)} %get-tuple-element.20.bias_ref, bf16[128,128]{1,0:T(8,128)(2,1)S(1)} %copy-done), custom_call_target="tpu_custom_call" | custom-call | tf_op jit(solution)/shard_map/pallas_call | solution.py:200
Async XLA Ops:
  13.7 7.9 %copy-start.1 = (bf16[128,128]{1,0:T(8,128)(2,1)S(1)}, bf16[128,128]{1,0:T(8,128)(2,1)}, u32[]{:S(2)}) copy-start(bf16[128,128]{1,0:T(8,128)(2,1)} %w_ref.2) | copy-start | bytes 98308
  13.7 15.2 %all-to-all-start.1 = ((bf16[16,72,128]{2,1,0:T(8,128)(2,1)}), bf16[16,72,128]{2,1,0:T(8,128)(2,1)S(1)}, u32[]{:S(2)}, u32[]{:S(2)}) async-start(bf16[16,72,128]{2,1,0:T(8,128)(2,1)} %shard_map.92), calls=%async_computation.1 | async-start | bytes 589824 | tf_op jit(solution)/shard_map/all_to_all | solution.py:199
  21.6 0.7 %copy-start.2 = (f32[128]{0:T(128)S(1)}, f32[128]{0:T(128)}, u32[]{:S(2)}) copy-start(f32[128]{0:T(128)} %param.15) | copy-start | bytes 1540
  21.6 0.7 %copy-start.3 = (f32[128]{0:T(128)S(1)}, f32[128]{0:T(128)}, u32[]{:S(2)}) copy-start(f32[128]{0:T(128)} %param.16) | copy-start | bytes 1540
  22.3 6.7 %copy-start = (bf16[128,128]{1,0:T(8,128)(2,1)S(1)}, bf16[128,128]{1,0:T(8,128)(2,1)}, u32[]{:S(2)}) copy-start(bf16[128,128]{1,0:T(8,128)(2,1)} %w_ref.3) | copy-start | bytes 98308

commit v10 on v9

--- a/solution.py
+++ b/solution.py
@@ -100,22 +100,25 @@
     quads = sources // cols
     for source in range(sources):
         col, row = divmod(sources - 1 - source, quads)
-        piece = unpack(got_ref[source].astype(jnp.float32), both)
+        piece = unpack(got_ref[source], both)
         for k in range(row_count):
             wide_ref[row * row_count + k, :, col * col_count : (col + 1) * col_count] = piece[:, k * col_count : (k + 1) * col_count]
+    wide = wide_ref[...].astype(jnp.float32)
+    parts = []
     for part in range(share // group):
         at = part * group
-        left = wide_ref[:, at : at + group, :].reshape(lanes, LANES).T[0:length] * column_mask_ref[...]
+        left = wide[:, at : at + group, :].reshape(lanes, LANES).T[0:length] * column_mask_ref[...]
         left = (left[:, None, :] * spread_ref[...][None]).reshape(length * group, lanes).astype(jnp.bfloat16)
-        right = wide_ref[:, share + at : share + at + group, :].reshape(lanes, LANES)[:, 0:length]
+        right = wide[:, share + at : share + at + group, :].reshape(lanes, LANES)[:, 0:length]
         right = (right * row_mask_ref[...]).astype(jnp.bfloat16)
         sums = jnp.dot(left, right, preferred_element_type=jnp.float32)
-        sum_ref[:, at : at + group, 0:length] = sums.reshape(length, group, length)
+        parts.append(sums.reshape(length, group, length))
+    sum_ref[:, :, 0:length] = jnp.concatenate(parts, axis=1).astype(jnp.bfloat16)
     for target in range(sources * halves):
         col, row = divmod(sources - 1 - target // halves, quads)
         row += (halves - 1 - target % halves) * quads
         pieces = [sum_ref[row * row_count + i, :, col * col_count : (col + 1) * col_count] for i in range(row_count)]
-        total_ref[target] = pack(jnp.concatenate(pieces, axis=1)).astype(jnp.bfloat16)
+        total_ref[target] = pack(jnp.concatenate(pieces, axis=1))
 
 
 def gate_kernel(normed_ref, w_ref, gain_ref, bias_ref, gate_ref, gain_out_ref, bias_out_ref):
@@ -179,8 +182,8 @@
         in_specs=[VMEM] * 4,
         out_specs=VMEM,
         scratch_shapes=[
-            pltpu.VMEM((depth, 2 * share, LANES), jnp.float32),
-            pltpu.VMEM((length, share, LANES), jnp.float32),
+            pltpu.VMEM((depth, 2 * share, LANES), jnp.bfloat16),
+            pltpu.VMEM((length, share, LANES), jnp.bfloat16),
         ],
         compiler_params=LIMIT,
     )(got, *masks)

time: 30.3 us -> 30.3 us (level)
  no operation moved by 1% of the time
where the time goes in v10:
time: 30.3 us; the launch traced here: 30 us
  blocking collectives  10 us (33%)
  starting transfers between devices  7.89 us (26%)
  waiting for transfers between devices  6.47 us (21%)
  Pallas kernels  4.95 us (16%)
  local copies, waits for them, and re-layouts  0.65 us (2%)
    all_to_all x1, blocking collectives, per_device(): lax.all_to_all(sides, ('quad', 'col'), split_axis=0, concat_axis=0, tiled...  10 us
    all_to_all x1, starting transfers between devices, per_device(): lax.all_to_all(total, ('half', 'quad', 'col'), split_axis=0, concat_axis=...  7.89 us
    all_to_all x1, waiting for transfers between devices, per_device(): lax.all_to_all(total, ('half', 'quad', 'col'), split_axis=0, concat_axis=...  6.47 us
    pallas_call x1, Pallas kernels, per_device(): pl.pallas_call(functools.partial(triangle_kernel, halves, cols, row_count...  2.12 us
    pallas_call x1, Pallas kernels, per_device(): pl.pallas_call(project_kernel, out_shape=(jax.ShapeDtypeStruct((near, 2 *...  1.64 us
    pallas_call x1, Pallas kernels, per_device(): pl.pallas_call(output_kernel, out_shape=jax.ShapeDtypeStruct(pair.shape,...  1.01 us
    unnamed x8, local copies, waits for them, and re-layouts  0.65 us
  transfers between devices with their start and end apart: 1, of which 1 were waited for; matrix products, arithmetic and copies ran while one was open for 0% of the time, Pallas kernels for 1%

profile of v10, /device:TPU:1, one launch (start us, length us, event | category | flops | bytes accessed | tf_op | source)
XLA Modules:
  0.0 30.0 jit_solution(7507022328476059531)
XLA Ops:
  0.0 1.6 %shard_map.91 = (bf16[8,144,128]{2,1,0:T(8,128)(2,1)S(1)}, bf16[576,128]{1,0:T(8,128)(2,1)S(1)}, f32[8,384]{1,0:T(8,128)S(1)}, f32[1,96]{1,0:T(1,128)S(1)}, f32[96,1]{1,0:T(8,128)S(1)}) custom-call(bf16[12,48,128]{2,1,0:T(8,128)(2,1)} %pair_hbm.1, f32[1,128]{1,0:T(1,128)} %bitcast.7, f32[1,128]{1,0:T(1,128)} %bitcast.8, bf16[128,512]{1,0:T(8,128)(2,1)} %w_hbm.1, ...), custom_call_target="tpu_custom_call" | custom-call | tf_op jit(solution)/shard_map/pallas_call | solution.py:157
  1.6 10.0 %all_to_all.10.got_ref = bf16[8,144,128]{2,1,0:T(8,128)(2,1)S(1)} all-to-all(bf16[8,144,128]{2,1,0:T(8,128)(2,1)S(1)} %get-tuple-element.13), channel_id=1, replica_groups={{7,5,3,1,6,4,2,0},{15,13,11,9,14,12,10,8},{23,21,19,17,22,20,18,16},{31..., dimensions={0} | all-to-all | bytes 589824 | tf_op jit(solution)/shard_map/all_to_all | solution.py:178
  11.7 2.1 %shard_map.92 = bf16[16,72,128]{2,1,0:T(8,128)(2,1)} custom-call(bf16[8,144,128]{2,1,0:T(8,128)(2,1)S(1)} %all_to_all.10.got_ref, f32[8,384]{1,0:T(8,128)S(1)} %get-tuple-element.14.spread_ref, f32[1,96]{1,0:T(1,128)S(1)} %get-tuple-element.15.row_mask_ref, f32[96,1]{1,0:T(8,128)S(1)} %get-tuple-element.16.column_mask_ref), custom_call_target="tpu_custom_call" | custom-call | tf_op jit(solution)/shard_map/pallas_call | solution.py:179
  13.8 0.0 copy-start.1
  13.8 7.9 %all-to-all-start.1 = ((bf16[16,72,128]{2,1,0:T(8,128)(2,1)}), bf16[16,72,128]{2,1,0:T(8,128)(2,1)S(1)}, u32[]{:S(2)}, u32[]{:S(2)}) async-start(bf16[16,72,128]{2,1,0:T(8,128)(2,1)} %shard_map.92), calls=%async_computation.1 | async-start | bytes 589824 | tf_op jit(solution)/shard_map/all_to_all | solution.py:202
  21.7 0.0 copy-start.2
  21.7 0.0 copy-start.3
  21.7 0.0 copy-done.1
  21.7 0.6 %copy-done.2 = f32[128]{0:T(128)S(1)} copy-done((f32[128]{0:T(128)S(1)}, f32[128]{0:T(128)}, u32[]{:S(2)}) %copy-start.2) | copy-done | bytes 536
  22.3 0.0 copy-done.3
  22.3 0.0 copy-start
  22.3 0.2 shard_map.93
  22.5 6.5 %all-to-all-done.1.total_ref = bf16[16,72,128]{2,1,0:T(8,128)(2,1)S(1)} async-done(((bf16[16,72,128]{2,1,0:T(8,128)(2,1)}), bf16[16,72,128]{2,1,0:T(8,128)(2,1)S(1)}, u32[]{:S(2)}, u32[]{:S(2)}) %all-to-all-start.1) | async-done | bytes 294944 | tf_op jit(solution)/shard_map/all_to_all | solution.py:202
  29.0 0.0 copy-done
  29.0 1.0 %shard_map.94 = bf16[12,48,128]{2,1,0:T(8,128)(2,1)} custom-call(bf16[16,72,128]{2,1,0:T(8,128)(2,1)S(1)} %all-to-all-done.1.total_ref, f32[576,128]{1,0:T(8,128)S(1)} %get-tuple-element.18.gate_ref, f32[128,1]{1,0:T(8,128)S(1)} %get-tuple-element.19.gain_ref, f32[128,1]{1,0:T(8,128)S(1)} %get-tuple-element.20.bias_ref, bf16[128,128]{1,0:T(8,128)(2,1)S(1)} %copy-done), custom_call_target="tpu_custom_call" | custom-call | tf_op jit(solution)/shard_map/pallas_call | solution.py:203
Async XLA Ops:
  13.8 7.9 %copy-start.1 = (bf16[128,128]{1,0:T(8,128)(2,1)S(1)}, bf16[128,128]{1,0:T(8,128)(2,1)}, u32[]{:S(2)}) copy-start(bf16[128,128]{1,0:T(8,128)(2,1)} %w_ref.2) | copy-start | bytes 98308
  13.8 15.2 %all-to-all-start.1 = ((bf16[16,72,128]{2,1,0:T(8,128)(2,1)}), bf16[16,72,128]{2,1,0:T(8,128)(2,1)S(1)}, u32[]{:S(2)}, u32[]{:S(2)}) async-start(bf16[16,72,128]{2,1,0:T(8,128)(2,1)} %shard_map.92), calls=%async_computation.1 | async-start | bytes 589824 | tf_op jit(solution)/shard_map/all_to_all | solution.py:202
  21.7 0.7 %copy-start.2 = (f32[128]{0:T(128)S(1)}, f32[128]{0:T(128)}, u32[]{:S(2)}) copy-start(f32[128]{0:T(128)} %param.15) | copy-start | bytes 1540
  21.7 0.7 %copy-start.3 = (f32[128]{0:T(128)S(1)}, f32[128]{0:T(128)}, u32[]{:S(2)}) copy-start(f32[128]{0:T(128)} %param.16) | copy-start | bytes 1540
  22.3 6.7 %copy-start = (bf16[128,128]{1,0:T(8,128)(2,1)S(1)}, bf16[128,128]{1,0:T(8,128)(2,1)}, u32[]{:S(2)}) copy-start(bf16[128,128]{1,0:T(8,128)(2,1)} %w_ref.3) | copy-start | bytes 98308

commit v11 on v9

--- a/solution.py
+++ b/solution.py
@@ -52,7 +52,28 @@
     return jnp.concatenate(blocks, axis=-1)
 
 
-def project_kernel(pair_hbm, gain_hbm, bias_hbm, w_hbm, mask_hbm, sides_ref, normed_ref, spread_ref, row_mask_ref, column_mask_ref, pair_ref, gain_ref, bias_ref, w_ref, mask_ref, sems):
+def arrange(x):
+    row_count, col_count, _ = x.shape
+    whole, spare = row_count // 3, LANES - 2 * col_count
+    blocks = []
+    for t in range(whole):
+        blocks += [x[2 * t], x[2 * t + 1], x[2 * whole + t, :spare]]
+    return jnp.concatenate(blocks + [x[2 * whole + t, spare:] for t in range(whole)], axis=0)
+
+
+def restore(x, row_count, col_count):
+    whole, spare = row_count // 3, LANES - 2 * col_count
+    rest = col_count - spare
+    rows = []
+    for t in range(whole):
+        rows += [x[t * LANES : t * LANES + col_count], x[t * LANES + col_count : t * LANES + 2 * col_count]]
+    for t in range(whole):
+        tail = whole * LANES + t * rest
+        rows += [x[t * LANES + 2 * col_count : (t + 1) * LANES], x[tail : tail + rest]]
+    return jnp.concatenate(rows, axis=0)
+
+
+def project_kernel(pair_hbm, gain_hbm, bias_hbm, w_hbm, mask_hbm, sides_ref, normed_ref, spread_ref, column_mask_ref, pair_ref, gain_ref, bias_ref, w_ref, mask_ref, sems):
     copies = [
         pltpu.make_async_copy(source, target, sems.at[n])
         for n, (source, target) in enumerate(
@@ -68,12 +89,16 @@
     group, lanes = spread_ref.shape
     copies[0].wait()
     mask_row = mask_ref[...].astype(jnp.float32)
-    row_mask_ref[...] = mask_row
     column_mask_ref[...] = column(mask_row)
     start = lax.axis_index("half") * (lanes // group)
     token = lax.broadcasted_iota(jnp.int32, (mask_row.shape[1], lanes), 0)
     lane = lax.broadcasted_iota(jnp.int32, (mask_row.shape[1], lanes), 1)
-    pick = jnp.where(lane // group + start == token, 1.0, 0.0)
+    row_count = pair_ref.shape[0]
+    whole = row_count // 3
+    quads = lanes // group // row_count
+    block, t, row = lane // LANES, lane // (quads * group) % whole, lane // group % quads
+    k = row * row_count + jnp.where(block < 2, 2 * t + block, 2 * whole + t)
+    pick = jnp.where(k + start == token, 1.0, 0.0)
     kept = jnp.dot(mask_row.astype(jnp.bfloat16), pick.astype(jnp.bfloat16), preferred_element_type=jnp.float32)
     channel = lax.broadcasted_iota(jnp.int32, (group, lanes), 0)
     lane = lax.broadcasted_iota(jnp.int32, (group, lanes), 1)
@@ -84,38 +109,72 @@
     normed = layer_norm(flat, gain_ref[...], bias_ref[...], -1).astype(jnp.bfloat16)
     normed_ref[...] = normed
     copies[4].wait()
-    projected = lax.dot_general(w_ref[...], normed, (((0,), (1,)), ((), ())), preferred_element_type=jnp.float32)
+    arranged = arrange(normed.reshape(pair_ref.shape))
+    projected = lax.dot_general(w_ref[...], arranged, (((0,), (1,)), ((), ())), preferred_element_type=jnp.float32)
     left = sigmoid(projected[:hidden]) * projected[hidden : 2 * hidden]
     right = sigmoid(projected[2 * hidden : 3 * hidden]) * projected[3 * hidden :]
     sides = jnp.concatenate([left.reshape(devices, share, tokens), right.reshape(devices, share, tokens)], axis=1)
     sides_ref[...] = pack(sides).astype(jnp.bfloat16)
 
 
-def triangle_kernel(halves, cols, row_count, col_count, share, got_ref, spread_ref, row_mask_ref, column_mask_ref, total_ref, wide_ref, sum_ref):
+def triangle_kernel(halves, cols, row_count, col_count, share, got_ref, spread_ref, mask_ref, total_ref):
     sources = got_ref.shape[0]
     both = 2 * share
     group, lanes = spread_ref.shape
-    depth = lanes // group
-    length = row_mask_ref.shape[1]
-    quads = sources // cols
-    for source in range(sources):
-        col, row = divmod(sources - 1 - source, quads)
-        piece = unpack(got_ref[source].astype(jnp.float32), both)
-        for k in range(row_count):
-            wide_ref[row * row_count + k, :, col * col_count : (col + 1) * col_count] = piece[:, k * col_count : (k + 1) * col_count]
-    for part in range(share // group):
-        at = part * group
-        left = wide_ref[:, at : at + group, :].reshape(lanes, LANES).T[0:length] * column_mask_ref[...]
-        left = (left[:, None, :] * spread_ref[...][None]).reshape(length * group, lanes).astype(jnp.bfloat16)
-        right = wide_ref[:, share + at : share + at + group, :].reshape(lanes, LANES)[:, 0:length]
-        right = (right * row_mask_ref[...]).astype(jnp.bfloat16)
-        sums = jnp.dot(left, right, preferred_element_type=jnp.float32)
-        sum_ref[:, at : at + group, 0:length] = sums.reshape(length, group, length)
+    length = mask_ref.shape[0]
+    rows, quads, parts = length // row_count, sources // cols, share // group
+    whole, spare = row_count // 3, LANES - 2 * col_count
+    rest = col_count - spare
+    blocks = [[got_ref[sources - 1 - (col * quads + row)].astype(jnp.float32) for row in range(quads)] for col in range(cols)]
+
+    def turned(picks):
+        return jnp.concatenate([blocks[col][row][at : at + group] for col, row, at in picks], axis=0).T
+
+    tail = turned([(col, row, whole * both + part * group) for col in range(cols) for part in range(parts) for row in range(quads)])
+
+    def side(which, part):
+        even, odd, third = [], [], []
+        for col in range(cols):
+            at = which * share + part * group
+            block = turned([(col, row, t * both + at) for t in range(whole) for row in range(quads)])
+            even.append(block[:col_count])
+            odd.append(block[col_count : 2 * col_count])
+            lane = (col * parts + part) * quads * group
+            at = which * LANES // 2
+            last = [tail[at + t * rest : at + (t + 1) * rest, lane : lane + quads * group] for t in range(whole)]
+            third += [block[2 * col_count :], jnp.concatenate(last, axis=1)]
+        tokens = [jnp.concatenate(pieces, axis=0) for pieces in (even, odd, third)]
+        return jnp.concatenate(tokens, axis=1) * mask_ref[...]
+
+    def placed(pieces):
+        return jnp.concatenate([jnp.zeros((piece, lanes), jnp.bfloat16) if isinstance(piece, int) else piece for piece in pieces], axis=0)
+
+    contract = (((1,), (1,)), ((), ()))
+    mains, lasts = [], []
+    for part in range(parts):
+        left, right = side(0, part), side(1, part).astype(jnp.bfloat16)
+        left = (left[:, None, :] * spread_ref[...][None]).reshape(rows, row_count, group, lanes)
+        pairs = left[:, : 2 * whole].reshape(rows, whole, 2, group, lanes)
+        left = jnp.concatenate([pairs[:, :, 0], pairs[:, :, 1], left[:, 2 * whole :]], axis=-1)
+        left = left.reshape(rows * whole * group, 3 * lanes).astype(jnp.bfloat16)
+        ours = [right[col * col_count : (col + 1) * col_count] for col in range(cols)]
+        weights = [
+            placed([p for mine in ours for p in (mine, LANES - col_count)]),
+            placed([p for mine in ours for p in (col_count, mine, spare)]),
+            placed([p for mine in ours for p in (2 * col_count, mine[:spare])]),
+        ]
+        weights = jnp.concatenate(weights, axis=1)
+        mains.append(lax.dot_general(left, weights, contract, preferred_element_type=jnp.float32))
+        weights = jnp.concatenate([mine[spare:] for mine in ours], axis=0)
+        lasts.append(lax.dot_general(left[:, 2 * lanes :], weights, contract, preferred_element_type=jnp.float32))
     for target in range(sources * halves):
         col, row = divmod(sources - 1 - target // halves, quads)
         row += (halves - 1 - target % halves) * quads
-        pieces = [sum_ref[row * row_count + i, :, col * col_count : (col + 1) * col_count] for i in range(row_count)]
-        total_ref[target] = pack(jnp.concatenate(pieces, axis=1)).astype(jnp.bfloat16)
+        spots = [(row * whole + t) * group for t in range(whole)]
+        tiles = [main[at : at + group, col * LANES : (col + 1) * LANES] for at in spots for main in mains]
+        last = [part[at : at + group, col * rest : (col + 1) * rest] for part in lasts for at in spots]
+        tiles.append(jnp.concatenate(last, axis=1))
+        total_ref[target] = jnp.concatenate(tiles, axis=0).astype(jnp.bfloat16)
 
 
 def gate_kernel(normed_ref, w_ref, gain_ref, bias_ref, gate_ref, gain_out_ref, bias_out_ref):
@@ -134,6 +193,7 @@
     total = unpack(jnp.sum(parts, axis=1), share).reshape(hidden, tokens)
     normed = layer_norm(total, gain_ref[...], bias_ref[...], 0).astype(jnp.bfloat16)
     output = lax.dot_general(normed, w_ref[...], (((0,), (0,)), ((), ())), preferred_element_type=jnp.float32)
+    output = restore(output, out_ref.shape[0], out_ref.shape[1])
     out_ref[...] = (gate_ref[...] * output).astype(jnp.bfloat16).reshape(out_ref.shape)
 
 
@@ -157,11 +217,10 @@
             jax.ShapeDtypeStruct((near, 2 * share * tokens // LANES, LANES), jnp.bfloat16),
             jax.ShapeDtypeStruct((tokens, channels), jnp.bfloat16),
             jax.ShapeDtypeStruct((GROUP, GROUP * depth), jnp.float32),
-            jax.ShapeDtypeStruct((1, length), jnp.float32),
             jax.ShapeDtypeStruct((length, 1), jnp.float32),
         ),
         in_specs=[HBM] * 5,
-        out_specs=(VMEM,) * 5,
+        out_specs=(VMEM,) * 4,
         scratch_shapes=[
             pltpu.VMEM(pair.shape, pair.dtype),
             pltpu.VMEM((1, channels), jnp.float32),
@@ -176,12 +235,8 @@
     total = pl.pallas_call(
         functools.partial(triangle_kernel, halves, cols, row_count, col_count, share),
         out_shape=jax.ShapeDtypeStruct((devices, share * tokens // LANES, LANES), jnp.bfloat16),
-        in_specs=[VMEM] * 4,
+        in_specs=[VMEM] * 3,
         out_specs=VMEM,
-        scratch_shapes=[
-            pltpu.VMEM((depth, 2 * share, LANES), jnp.float32),
-            pltpu.VMEM((length, share, LANES), jnp.float32),
-        ],
         compiler_params=LIMIT,
     )(got, *masks)
     gate, gain_out, bias_out = pl.pallas_call(
@@ -246,10 +301,12 @@
 
     def per_shard(*args):
         near, hidden, length = rows * cols // halves, args[-1].shape[0], args[1].shape[0]
-        tokens = args[0].shape[0] * args[0].shape[1]
-        if hidden % (16 * near) == 0 and length <= LANES and tokens % (LANES // 2) == 0:
-            return per_device(rows, cols, halves, *args)
-        return plain_per_device(rows, cols, *args)
+        row_count, col_count, _ = args[0].shape
+        spare = LANES - 2 * col_count
+        fits = hidden % (2 * GROUP * near) == 0 and cols == 2 and length <= LANES and row_count % 3 == 0
+        fits = fits and 0 < spare < col_count and row_count // 3 * (col_count - spare) * 2 == LANES
+        fits = fits and row_count // 3 * (rows // halves) * GROUP == LANES
+        return per_device(rows, cols, halves, *args) if fits else plain_per_device(rows, cols, *args)
 
     tokens = P(("groups", "half", "quad"), "col", None)
     in_specs = (tokens, P("groups"), P(), P(), P(), P(), P(), P(), P())

time: 30.3 us -> 29.8 us (0.983)
  Pallas kernels: 4.87 us -> 4.43 us
    pallas_call x1, Pallas kernels: 2.04 us -> 1.6 us  [per_device(): pl.pallas_call(functools.partial(triangle_kernel, halves, cols, row_count...]
where the time goes in v11:
time: 29.8 us; the launch traced here: 29.5 us
  blocking collectives  10 us (34%)
  starting transfers between devices  7.89 us (26%)
  waiting for transfers between devices  6.48 us (22%)
  Pallas kernels  4.43 us (15%)
  local copies, waits for them, and re-layouts  0.65 us (2%)
    all_to_all x1, blocking collectives, per_device(): lax.all_to_all(sides, ('quad', 'col'), split_axis=0, concat_axis=0, tiled...  10 us
    all_to_all x1, starting transfers between devices, per_device(): lax.all_to_all(total, ('half', 'quad', 'col'), split_axis=0, concat_axis=...  7.89 us
    all_to_all x1, waiting for transfers between devices, per_device(): lax.all_to_all(total, ('half', 'quad', 'col'), split_axis=0, concat_axis=...  6.48 us
    pallas_call x1, Pallas kernels, per_device(): pl.pallas_call(project_kernel, out_shape=(jax.ShapeDtypeStruct((near, 2 *...  1.64 us
    pallas_call x1, Pallas kernels, per_device(): pl.pallas_call(functools.partial(triangle_kernel, halves, cols, row_count...  1.6 us
    pallas_call x1, Pallas kernels, per_device(): pl.pallas_call(output_kernel, out_shape=jax.ShapeDtypeStruct(pair.shape,...  1.01 us
    unnamed x8, local copies, waits for them, and re-layouts  0.65 us
  transfers between devices with their start and end apart: 1, of which 1 were waited for; matrix products, arithmetic and copies ran while one was open for 0% of the time, Pallas kernels for 1%

profile of v11, /device:TPU:1, one launch (start us, length us, event | category | flops | bytes accessed | tf_op | source)
XLA Modules:
  0.0 29.5 jit_solution(12220863455525941017)
XLA Ops:
  0.0 1.6 %shard_map.91 = (bf16[8,144,128]{2,1,0:T(8,128)(2,1)S(1)}, bf16[576,128]{1,0:T(8,128)(2,1)S(1)}, f32[8,384]{1,0:T(8,128)S(1)}, f32[96,1]{1,0:T(8,128)S(1)}) custom-call(bf16[12,48,128]{2,1,0:T(8,128)(2,1)} %pair_hbm.1, f32[1,128]{1,0:T(1,128)} %bitcast.7, f32[1,128]{1,0:T(1,128)} %bitcast.8, bf16[128,512]{1,0:T(8,128)(2,1)} %w_hbm.1, s32[1,96]{1,0:T(1,128)} %bitcast.9), custom_call_target="tpu_custom_call" | custom-call | tf_op jit(solution)/shard_map/pallas_call | solution.py:214
  1.6 10.0 %all_to_all.10.got_ref = bf16[8,144,128]{2,1,0:T(8,128)(2,1)S(1)} all-to-all(bf16[8,144,128]{2,1,0:T(8,128)(2,1)S(1)} %get-tuple-element.12), channel_id=1, replica_groups={{7,5,3,1,6,4,2,0},{15,13,11,9,14,12,10,8},{23,21,19,17,22,20,18,16},{31..., dimensions={0} | all-to-all | bytes 589824 | tf_op jit(solution)/shard_map/all_to_all | solution.py:234
  11.7 1.6 %shard_map.92 = bf16[16,72,128]{2,1,0:T(8,128)(2,1)} custom-call(bf16[8,144,128]{2,1,0:T(8,128)(2,1)S(1)} %all_to_all.10.got_ref, f32[8,384]{1,0:T(8,128)S(1)} %get-tuple-element.13.spread_ref, f32[96,1]{1,0:T(8,128)S(1)} %get-tuple-element.14.mask_ref), custom_call_target="tpu_custom_call" | custom-call | tf_op jit(solution)/shard_map/pallas_call | solution.py:235
  13.3 0.0 copy-start.1
  13.3 7.9 %all-to-all-start.1 = ((bf16[16,72,128]{2,1,0:T(8,128)(2,1)}), bf16[16,72,128]{2,1,0:T(8,128)(2,1)S(1)}, u32[]{:S(2)}, u32[]{:S(2)}) async-start(bf16[16,72,128]{2,1,0:T(8,128)(2,1)} %shard_map.92), calls=%async_computation.1 | async-start | bytes 589824 | tf_op jit(solution)/shard_map/all_to_all | solution.py:254
  21.1 0.0 copy-start.2
  21.2 0.0 copy-start.3
  21.2 0.0 copy-done.1
  21.2 0.6 %copy-done.2 = f32[128]{0:T(128)S(1)} copy-done((f32[128]{0:T(128)S(1)}, f32[128]{0:T(128)}, u32[]{:S(2)}) %copy-start.2) | copy-done | bytes 536
  21.8 0.0 copy-done.3
  21.8 0.0 copy-start
  21.8 0.2 shard_map.93
  22.0 6.5 %all-to-all-done.1.total_ref = bf16[16,72,128]{2,1,0:T(8,128)(2,1)S(1)} async-done(((bf16[16,72,128]{2,1,0:T(8,128)(2,1)}), bf16[16,72,128]{2,1,0:T(8,128)(2,1)S(1)}, u32[]{:S(2)}, u32[]{:S(2)}) %all-to-all-start.1) | async-done | bytes 294944 | tf_op jit(solution)/shard_map/all_to_all | solution.py:254
  28.5 0.0 copy-done
  28.5 1.0 %shard_map.94 = bf16[12,48,128]{2,1,0:T(8,128)(2,1)} custom-call(bf16[16,72,128]{2,1,0:T(8,128)(2,1)S(1)} %all-to-all-done.1.total_ref, f32[576,128]{1,0:T(8,128)S(1)} %get-tuple-element.16.gate_ref, f32[128,1]{1,0:T(8,128)S(1)} %get-tuple-element.17.gain_ref, f32[128,1]{1,0:T(8,128)S(1)} %get-tuple-element.18.bias_ref, bf16[128,128]{1,0:T(8,128)(2,1)S(1)} %copy-done), custom_call_target="tpu_custom_call" | custom-call | tf_op jit(solution)/shard_map/pallas_call | solution.py:255
Async XLA Ops:
  13.3 7.9 %copy-start.1 = (bf16[128,128]{1,0:T(8,128)(2,1)S(1)}, bf16[128,128]{1,0:T(8,128)(2,1)}, u32[]{:S(2)}) copy-start(bf16[128,128]{1,0:T(8,128)(2,1)} %w_ref.2) | copy-start | bytes 98308
  13.3 15.2 %all-to-all-start.1 = ((bf16[16,72,128]{2,1,0:T(8,128)(2,1)}), bf16[16,72,128]{2,1,0:T(8,128)(2,1)S(1)}, u32[]{:S(2)}, u32[]{:S(2)}) async-start(bf16[16,72,128]{2,1,0:T(8,128)(2,1)} %shard_map.92), calls=%async_computation.1 | async-start | bytes 589824 | tf_op jit(solution)/shard_map/all_to_all | solution.py:254
  21.1 0.7 %copy-start.2 = (f32[128]{0:T(128)S(1)}, f32[128]{0:T(128)}, u32[]{:S(2)}) copy-start(f32[128]{0:T(128)} %param.15) | copy-start | bytes 1540
  21.2 0.7 %copy-start.3 = (f32[128]{0:T(128)S(1)}, f32[128]{0:T(128)}, u32[]{:S(2)}) copy-start(f32[128]{0:T(128)} %param.16) | copy-start | bytes 1540
  21.8 6.7 %copy-start = (bf16[128,128]{1,0:T(8,128)(2,1)S(1)}, bf16[128,128]{1,0:T(8,128)(2,1)}, u32[]{:S(2)}) copy-start(bf16[128,128]{1,0:T(8,128)(2,1)} %w_ref.3) | copy-start | bytes 98308

commit v12 on v11

--- a/solution.py
+++ b/solution.py
@@ -117,7 +117,7 @@
     sides_ref[...] = pack(sides).astype(jnp.bfloat16)
 
 
-def triangle_kernel(halves, cols, row_count, col_count, share, got_ref, spread_ref, mask_ref, total_ref):
+def triangle_kernel(far_order, cols, row_count, col_count, share, got_ref, spread_ref, mask_ref, total_ref):
     sources = got_ref.shape[0]
     both = 2 * share
     group, lanes = spread_ref.shape
@@ -167,9 +167,8 @@
         mains.append(lax.dot_general(left, weights, contract, preferred_element_type=jnp.float32))
         weights = jnp.concatenate([mine[spare:] for mine in ours], axis=0)
         lasts.append(lax.dot_general(left[:, 2 * lanes :], weights, contract, preferred_element_type=jnp.float32))
-    for target in range(sources * halves):
-        col, row = divmod(sources - 1 - target // halves, quads)
-        row += (halves - 1 - target % halves) * quads
+    for target, device in enumerate(far_order):
+        row, col = divmod(device, cols)
         spots = [(row * whole + t) * group for t in range(whole)]
         tiles = [main[at : at + group, col * LANES : (col + 1) * LANES] for at in spots for main in mains]
         last = [part[at : at + group, col * rest : (col + 1) * rest] for part in lasts for at in spots]
@@ -183,14 +182,16 @@
     bias_out_ref[...] = column(bias_ref[...])
 
 
-def output_kernel(total_ref, gate_ref, gain_ref, bias_ref, w_ref, out_ref):
-    sources, packed, _ = total_ref.shape
+def output_kernel(far_order, near_order, total_ref, gate_ref, gain_ref, bias_ref, w_ref, out_ref):
     tokens = gate_ref.shape[0]
     hidden = w_ref.shape[0]
-    share = packed * LANES // tokens
-    near = hidden // share
-    parts = total_ref[...].astype(jnp.float32).reshape(near, sources // near, packed, LANES)
-    total = unpack(jnp.sum(parts, axis=1), share).reshape(hidden, tokens)
+    near = len(near_order)
+    share = hidden // near
+    blocks = []
+    for index in near_order:
+        parts = [total_ref[source].astype(jnp.float32) for source, device in enumerate(far_order) if device % near == index]
+        blocks.append(unpack(sum(parts[1:], parts[0]), share))
+    total = jnp.concatenate(blocks, axis=0)
     normed = layer_norm(total, gain_ref[...], bias_ref[...], 0).astype(jnp.bfloat16)
     output = lax.dot_general(normed, w_ref[...], (((0,), (0,)), ((), ())), preferred_element_type=jnp.float32)
     output = restore(output, out_ref.shape[0], out_ref.shape[1])
@@ -204,7 +205,11 @@
     near = devices // halves
     quads = rows // halves
     near_order = [quad * cols + col for col in reversed(range(cols)) for quad in reversed(range(quads))]
-    far_order = [half * near + index for index in near_order for half in reversed(range(halves))]
+    far_order = []
+    for col in reversed(range(cols)):
+        for quad in range(quads):
+            for half in reversed(range(halves)):
+                far_order.append(half * near + (quads - 1 - quad if half else quad) * cols + col)
     share = hidden // near
     tokens = row_count * col_count
     length = rows * row_count
@@ -233,7 +238,7 @@
     )(*(pltpu.with_memory_space_constraint(x, pltpu.HBM) for x in arguments))
     got = lax.all_to_all(sides, ("quad", "col"), split_axis=0, concat_axis=0, tiled=True, axis_index_groups=[near_order])
     total = pl.pallas_call(
-        functools.partial(triangle_kernel, halves, cols, row_count, col_count, share),
+        functools.partial(triangle_kernel, far_order, cols, row_count, col_count, share),
         out_shape=jax.ShapeDtypeStruct((devices, share * tokens // LANES, LANES), jnp.bfloat16),
         in_specs=[VMEM] * 3,
         out_specs=VMEM,
@@ -253,7 +258,7 @@
     )(normed, w_gate, gain_out.reshape(1, hidden), bias_out.reshape(1, hidden))
     total = lax.all_to_all(total, ("half", "quad", "col"), split_axis=0, concat_axis=0, tiled=True, axis_index_groups=[far_order])
     return pl.pallas_call(
-        output_kernel,
+        functools.partial(output_kernel, far_order, near_order),
         out_shape=jax.ShapeDtypeStruct(pair.shape, jnp.bfloat16),
         in_specs=[VMEM] * 5,
         out_specs=VMEM,

time: 29.8 us -> 30.7 us (1.030)
  the two profiles are of different devices: /device:TPU:1 before, /device:TPU:0 now
where the time goes in v12:
time: 30.7 us; the launch traced here: 30.3 us
  blocking collectives  10.6 us (35%)
  starting transfers between devices  7.67 us (25%)
  waiting for transfers between devices  6.95 us (23%)
  Pallas kernels  4.45 us (14%)
  local copies, waits for them, and re-layouts  0.65 us (2%)
    all_to_all x1, blocking collectives, per_device(): lax.all_to_all(sides, ('quad', 'col'), split_axis=0, concat_axis=0, tiled...  10.6 us
    all_to_all x1, starting transfers between devices, per_device(): lax.all_to_all(total, ('half', 'quad', 'col'), split_axis=0, concat_axis=...  7.67 us
    all_to_all x1, waiting for transfers between devices, per_device(): lax.all_to_all(total, ('half', 'quad', 'col'), split_axis=0, concat_axis=...  6.95 us
    pallas_call x1, Pallas kernels, per_device(): pl.pallas_call(project_kernel, out_shape=(jax.ShapeDtypeStruct((near, 2 *...  1.64 us
    pallas_call x1, Pallas kernels, per_device(): pl.pallas_call(functools.partial(triangle_kernel, far_order, cols, row_co...  1.6 us
    pallas_call x1, Pallas kernels, per_device(): pl.pallas_call(functools.partial(output_kernel, far_order, near_order), o...  1.02 us
    unnamed x8, local copies, waits for them, and re-layouts  0.65 us
  transfers between devices with their start and end apart: 1, of which 1 were waited for; matrix products, arithmetic and copies ran while one was open for 0% of the time, Pallas kernels for 1%

profile of v12, /device:TPU:0, one launch (start us, length us, event | category | flops | bytes accessed | tf_op | source)
XLA Modules:
  0.0 30.3 jit_solution(6288399382147007404)
XLA Ops:
  0.0 1.6 %shard_map.91 = (bf16[8,144,128]{2,1,0:T(8,128)(2,1)S(1)}, bf16[576,128]{1,0:T(8,128)(2,1)S(1)}, f32[8,384]{1,0:T(8,128)S(1)}, f32[96,1]{1,0:T(8,128)S(1)}) custom-call(bf16[12,48,128]{2,1,0:T(8,128)(2,1)} %pair_hbm.1, f32[1,128]{1,0:T(1,128)} %bitcast.7, f32[1,128]{1,0:T(1,128)} %bitcast.8, bf16[128,512]{1,0:T(8,128)(2,1)} %w_hbm.1, s32[1,96]{1,0:T(1,128)} %bitcast.9), custom_call_target="tpu_custom_call" | custom-call | tf_op jit(solution)/shard_map/pallas_call | solution.py:219
  1.6 10.6 %all_to_all.10.got_ref = bf16[8,144,128]{2,1,0:T(8,128)(2,1)S(1)} all-to-all(bf16[8,144,128]{2,1,0:T(8,128)(2,1)S(1)} %get-tuple-element.12), channel_id=1, replica_groups={{7,5,3,1,6,4,2,0},{15,13,11,9,14,12,10,8},{23,21,19,17,22,20,18,16},{31..., dimensions={0} | all-to-all | bytes 589824 | tf_op jit(solution)/shard_map/all_to_all | solution.py:239
  12.2 1.6 %shard_map.92 = bf16[16,72,128]{2,1,0:T(8,128)(2,1)} custom-call(bf16[8,144,128]{2,1,0:T(8,128)(2,1)S(1)} %all_to_all.10.got_ref, f32[8,384]{1,0:T(8,128)S(1)} %get-tuple-element.13.spread_ref, f32[96,1]{1,0:T(8,128)S(1)} %get-tuple-element.14.mask_ref), custom_call_target="tpu_custom_call" | custom-call | tf_op jit(solution)/shard_map/pallas_call | solution.py:240
  13.8 0.0 copy-start.1
  13.8 7.7 %all-to-all-start.1 = ((bf16[16,72,128]{2,1,0:T(8,128)(2,1)}), bf16[16,72,128]{2,1,0:T(8,128)(2,1)S(1)}, u32[]{:S(2)}, u32[]{:S(2)}) async-start(bf16[16,72,128]{2,1,0:T(8,128)(2,1)} %shard_map.92), calls=%async_computation.1 | async-start | bytes 589824 | tf_op jit(solution)/shard_map/all_to_all | solution.py:259
  21.5 0.0 copy-start.2
  21.5 0.0 copy-start.3
  21.5 0.0 copy-done.1
  21.5 0.6 %copy-done.2 = f32[128]{0:T(128)S(1)} copy-done((f32[128]{0:T(128)S(1)}, f32[128]{0:T(128)}, u32[]{:S(2)}) %copy-start.2) | copy-done | bytes 536
  22.2 0.0 copy-done.3
  22.2 0.0 copy-start
  22.2 0.2 shard_map.93
  22.4 6.9 %all-to-all-done.1.total_ref = bf16[16,72,128]{2,1,0:T(8,128)(2,1)S(1)} async-done(((bf16[16,72,128]{2,1,0:T(8,128)(2,1)}), bf16[16,72,128]{2,1,0:T(8,128)(2,1)S(1)}, u32[]{:S(2)}, u32[]{:S(2)}) %all-to-all-start.1) | async-done | bytes 294944 | tf_op jit(solution)/shard_map/all_to_all | solution.py:259
  29.3 0.0 copy-done
  29.3 1.0 %shard_map.94 = bf16[12,48,128]{2,1,0:T(8,128)(2,1)} custom-call(bf16[16,72,128]{2,1,0:T(8,128)(2,1)S(1)} %all-to-all-done.1.total_ref, f32[576,128]{1,0:T(8,128)S(1)} %get-tuple-element.16.gate_ref, f32[128,1]{1,0:T(8,128)S(1)} %get-tuple-element.17.gain_ref, f32[128,1]{1,0:T(8,128)S(1)} %get-tuple-element.18.bias_ref, bf16[128,128]{1,0:T(8,128)(2,1)S(1)} %copy-done), custom_call_target="tpu_custom_call" | custom-call | tf_op jit(solution)/shard_map/pallas_call | solution.py:260
Async XLA Ops:
  13.8 7.7 %copy-start.1 = (bf16[128,128]{1,0:T(8,128)(2,1)S(1)}, bf16[128,128]{1,0:T(8,128)(2,1)}, u32[]{:S(2)}) copy-start(bf16[128,128]{1,0:T(8,128)(2,1)} %w_ref.2) | copy-start | bytes 98308
  13.8 15.5 %all-to-all-start.1 = ((bf16[16,72,128]{2,1,0:T(8,128)(2,1)}), bf16[16,72,128]{2,1,0:T(8,128)(2,1)S(1)}, u32[]{:S(2)}, u32[]{:S(2)}) async-start(bf16[16,72,128]{2,1,0:T(8,128)(2,1)} %shard_map.92), calls=%async_computation.1 | async-start | bytes 589824 | tf_op jit(solution)/shard_map/all_to_all | solution.py:259
  21.5 0.7 %copy-start.2 = (f32[128]{0:T(128)S(1)}, f32[128]{0:T(128)}, u32[]{:S(2)}) copy-start(f32[128]{0:T(128)} %param.15) | copy-start | bytes 1540
  21.5 0.7 %copy-start.3 = (f32[128]{0:T(128)S(1)}, f32[128]{0:T(128)}, u32[]{:S(2)}) copy-start(f32[128]{0:T(128)} %param.16) | copy-start | bytes 1540
  22.2 7.2 %copy-start = (bf16[128,128]{1,0:T(8,128)(2,1)S(1)}, bf16[128,128]{1,0:T(8,128)(2,1)}, u32[]{:S(2)}) copy-start(bf16[128,128]{1,0:T(8,128)(2,1)} %w_ref.3) | copy-start | bytes 98308

commit v13 on v12

--- a/solution.py
+++ b/solution.py
@@ -207,9 +207,9 @@
     near_order = [quad * cols + col for col in reversed(range(cols)) for quad in reversed(range(quads))]
     far_order = []
     for col in reversed(range(cols)):
-        for quad in range(quads):
-            for half in reversed(range(halves)):
-                far_order.append(half * near + (quads - 1 - quad if half else quad) * cols + col)
+        ahead = list(range(quads)) if col else list(range(1, quads)) + [0]
+        for quad, other in zip(ahead, reversed(range(quads))):
+            far_order += [near + other * cols + col, quad * cols + col]
     share = hidden // near
     tokens = row_count * col_count
     length = rows * row_count

time: 30.7 us -> 29.5 us (0.961)
  waiting for transfers between devices: 6.95 us -> 5.74 us
    all_to_all x1, waiting for transfers between devices: 6.95 us -> 5.74 us  [per_device(): lax.all_to_all(total, ('half', 'quad', 'col'), split_axis=0, concat_axis=...]
where the time goes in v13:
time: 29.5 us; the launch traced here: 29.2 us
  blocking collectives  10.6 us (36%)
  starting transfers between devices  7.71 us (26%)
  waiting for transfers between devices  5.74 us (19%)
  Pallas kernels  4.45 us (15%)
  local copies, waits for them, and re-layouts  0.65 us (2%)
    all_to_all x1, blocking collectives, per_device(): lax.all_to_all(sides, ('quad', 'col'), split_axis=0, concat_axis=0, tiled...  10.6 us
    all_to_all x1, starting transfers between devices, per_device(): lax.all_to_all(total, ('half', 'quad', 'col'), split_axis=0, concat_axis=...  7.71 us
    all_to_all x1, waiting for transfers between devices, per_device(): lax.all_to_all(total, ('half', 'quad', 'col'), split_axis=0, concat_axis=...  5.74 us
    pallas_call x1, Pallas kernels, per_device(): pl.pallas_call(project_kernel, out_shape=(jax.ShapeDtypeStruct((near, 2 *...  1.64 us
    pallas_call x1, Pallas kernels, per_device(): pl.pallas_call(functools.partial(triangle_kernel, far_order, cols, row_co...  1.6 us
    pallas_call x1, Pallas kernels, per_device(): pl.pallas_call(functools.partial(output_kernel, far_order, near_order), o...  1.02 us
    unnamed x8, local copies, waits for them, and re-layouts  0.65 us
  transfers between devices with their start and end apart: 1, of which 1 were waited for; matrix products, arithmetic and copies ran while one was open for 0% of the time, Pallas kernels for 1%

profile of v13, /device:TPU:0, one launch (start us, length us, event | category | flops | bytes accessed | tf_op | source)
XLA Modules:
  0.0 29.2 jit_solution(3985701741571683768)
XLA Ops:
  0.0 1.6 %shard_map.91 = (bf16[8,144,128]{2,1,0:T(8,128)(2,1)S(1)}, bf16[576,128]{1,0:T(8,128)(2,1)S(1)}, f32[8,384]{1,0:T(8,128)S(1)}, f32[96,1]{1,0:T(8,128)S(1)}) custom-call(bf16[12,48,128]{2,1,0:T(8,128)(2,1)} %pair_hbm.1, f32[1,128]{1,0:T(1,128)} %bitcast.7, f32[1,128]{1,0:T(1,128)} %bitcast.8, bf16[128,512]{1,0:T(8,128)(2,1)} %w_hbm.1, s32[1,96]{1,0:T(1,128)} %bitcast.9), custom_call_target="tpu_custom_call" | custom-call | tf_op jit(solution)/shard_map/pallas_call | solution.py:219
  1.6 10.6 %all_to_all.10.got_ref = bf16[8,144,128]{2,1,0:T(8,128)(2,1)S(1)} all-to-all(bf16[8,144,128]{2,1,0:T(8,128)(2,1)S(1)} %get-tuple-element.12), channel_id=1, replica_groups={{7,5,3,1,6,4,2,0},{15,13,11,9,14,12,10,8},{23,21,19,17,22,20,18,16},{31..., dimensions={0} | all-to-all | bytes 589824 | tf_op jit(solution)/shard_map/all_to_all | solution.py:239
  12.2 1.6 %shard_map.92 = bf16[16,72,128]{2,1,0:T(8,128)(2,1)} custom-call(bf16[8,144,128]{2,1,0:T(8,128)(2,1)S(1)} %all_to_all.10.got_ref, f32[8,384]{1,0:T(8,128)S(1)} %get-tuple-element.13.spread_ref, f32[96,1]{1,0:T(8,128)S(1)} %get-tuple-element.14.mask_ref), custom_call_target="tpu_custom_call" | custom-call | tf_op jit(solution)/shard_map/pallas_call | solution.py:240
  13.8 0.0 copy-start.1
  13.8 7.7 %all-to-all-start.1 = ((bf16[16,72,128]{2,1,0:T(8,128)(2,1)}), bf16[16,72,128]{2,1,0:T(8,128)(2,1)S(1)}, u32[]{:S(2)}, u32[]{:S(2)}) async-start(bf16[16,72,128]{2,1,0:T(8,128)(2,1)} %shard_map.92), calls=%async_computation.1 | async-start | bytes 589824 | tf_op jit(solution)/shard_map/all_to_all | solution.py:259
  21.5 0.0 copy-start.2
  21.6 0.0 copy-start.3
  21.6 0.0 copy-done.1
  21.6 0.6 %copy-done.2 = f32[128]{0:T(128)S(1)} copy-done((f32[128]{0:T(128)S(1)}, f32[128]{0:T(128)}, u32[]{:S(2)}) %copy-start.2) | copy-done | bytes 536
  22.2 0.0 copy-done.3
  22.2 0.0 copy-start
  22.2 0.2 shard_map.93
  22.4 5.7 %all-to-all-done.1.total_ref = bf16[16,72,128]{2,1,0:T(8,128)(2,1)S(1)} async-done(((bf16[16,72,128]{2,1,0:T(8,128)(2,1)}), bf16[16,72,128]{2,1,0:T(8,128)(2,1)S(1)}, u32[]{:S(2)}, u32[]{:S(2)}) %all-to-all-start.1) | async-done | bytes 294944 | tf_op jit(solution)/shard_map/all_to_all | solution.py:259
  28.2 0.0 copy-done
  28.2 1.0 %shard_map.94 = bf16[12,48,128]{2,1,0:T(8,128)(2,1)} custom-call(bf16[16,72,128]{2,1,0:T(8,128)(2,1)S(1)} %all-to-all-done.1.total_ref, f32[576,128]{1,0:T(8,128)S(1)} %get-tuple-element.16.gate_ref, f32[128,1]{1,0:T(8,128)S(1)} %get-tuple-element.17.gain_ref, f32[128,1]{1,0:T(8,128)S(1)} %get-tuple-element.18.bias_ref, bf16[128,128]{1,0:T(8,128)(2,1)S(1)} %copy-done), custom_call_target="tpu_custom_call" | custom-call | tf_op jit(solution)/shard_map/pallas_call | solution.py:260
Async XLA Ops:
  13.8 7.7 %copy-start.1 = (bf16[128,128]{1,0:T(8,128)(2,1)S(1)}, bf16[128,128]{1,0:T(8,128)(2,1)}, u32[]{:S(2)}) copy-start(bf16[128,128]{1,0:T(8,128)(2,1)} %w_ref.2) | copy-start | bytes 98308
  13.8 14.3 %all-to-all-start.1 = ((bf16[16,72,128]{2,1,0:T(8,128)(2,1)}), bf16[16,72,128]{2,1,0:T(8,128)(2,1)S(1)}, u32[]{:S(2)}, u32[]{:S(2)}) async-start(bf16[16,72,128]{2,1,0:T(8,128)(2,1)} %shard_map.92), calls=%async_computation.1 | async-start | bytes 589824 | tf_op jit(solution)/shard_map/all_to_all | solution.py:259
  21.5 0.7 %copy-start.2 = (f32[128]{0:T(128)S(1)}, f32[128]{0:T(128)}, u32[]{:S(2)}) copy-start(f32[128]{0:T(128)} %param.15) | copy-start | bytes 1540
  21.6 0.7 %copy-start.3 = (f32[128]{0:T(128)S(1)}, f32[128]{0:T(128)}, u32[]{:S(2)}) copy-start(f32[128]{0:T(128)} %param.16) | copy-start | bytes 1540
  22.2 5.9 %copy-start = (bf16[128,128]{1,0:T(8,128)(2,1)S(1)}, bf16[128,128]{1,0:T(8,128)(2,1)}, u32[]{:S(2)}) copy-start(bf16[128,128]{1,0:T(8,128)(2,1)} %w_ref.3) | copy-start | bytes 98308

commit v14 on v13

--- a/solution.py
+++ b/solution.py
@@ -208,7 +208,8 @@
     far_order = []
     for col in reversed(range(cols)):
         ahead = list(range(quads)) if col else list(range(1, quads)) + [0]
-        for quad, other in zip(ahead, reversed(range(quads))):
+        behind = [1] + [quad for quad in reversed(range(quads)) if quad != 1] if col else list(reversed(range(quads)))
+        for quad, other in zip(ahead, behind):
             far_order += [near + other * cols + col, quad * cols + col]
     share = hidden // near
     tokens = row_count * col_count

time: 29.5 us -> 28.4 us (0.963)
  starting transfers between devices: 7.71 us -> 6.76 us
    all_to_all x1, starting transfers between devices: 7.71 us -> 6.76 us  [per_device(): lax.all_to_all(total, ('half', 'quad', 'col'), split_axis=0, concat_axis=...]
where the time goes in v14:
time: 28.4 us; the launch traced here: 28 us
  blocking collectives  10.6 us (37%)
  starting transfers between devices  6.76 us (24%)
  waiting for transfers between devices  5.56 us (20%)
  Pallas kernels  4.44 us (16%)
  local copies, waits for them, and re-layouts  0.65 us (2%)
    all_to_all x1, blocking collectives, per_device(): lax.all_to_all(sides, ('quad', 'col'), split_axis=0, concat_axis=0, tiled...  10.6 us
    all_to_all x1, starting transfers between devices, per_device(): lax.all_to_all(total, ('half', 'quad', 'col'), split_axis=0, concat_axis=...  6.76 us
    all_to_all x1, waiting for transfers between devices, per_device(): lax.all_to_all(total, ('half', 'quad', 'col'), split_axis=0, concat_axis=...  5.56 us
    pallas_call x1, Pallas kernels, per_device(): pl.pallas_call(project_kernel, out_shape=(jax.ShapeDtypeStruct((near, 2 *...  1.64 us
    pallas_call x1, Pallas kernels, per_device(): pl.pallas_call(functools.partial(triangle_kernel, far_order, cols, row_co...  1.6 us
    pallas_call x1, Pallas kernels, per_device(): pl.pallas_call(functools.partial(output_kernel, far_order, near_order), o...  1.02 us
    unnamed x8, local copies, waits for them, and re-layouts  0.65 us
  transfers between devices with their start and end apart: 1, of which 1 were waited for; matrix products, arithmetic and copies ran while one was open for 0% of the time, Pallas kernels for 1%

profile of v14, /device:TPU:0, one launch (start us, length us, event | category | flops | bytes accessed | tf_op | source)
XLA Modules:
  0.0 28.0 jit_solution(13544283955398719605)
XLA Ops:
  0.0 1.6 %shard_map.91 = (bf16[8,144,128]{2,1,0:T(8,128)(2,1)S(1)}, bf16[576,128]{1,0:T(8,128)(2,1)S(1)}, f32[8,384]{1,0:T(8,128)S(1)}, f32[96,1]{1,0:T(8,128)S(1)}) custom-call(bf16[12,48,128]{2,1,0:T(8,128)(2,1)} %pair_hbm.1, f32[1,128]{1,0:T(1,128)} %bitcast.7, f32[1,128]{1,0:T(1,128)} %bitcast.8, bf16[128,512]{1,0:T(8,128)(2,1)} %w_hbm.1, s32[1,96]{1,0:T(1,128)} %bitcast.9), custom_call_target="tpu_custom_call" | custom-call | tf_op jit(solution)/shard_map/pallas_call | solution.py:220
  1.6 10.6 %all_to_all.10.got_ref = bf16[8,144,128]{2,1,0:T(8,128)(2,1)S(1)} all-to-all(bf16[8,144,128]{2,1,0:T(8,128)(2,1)S(1)} %get-tuple-element.12), channel_id=1, replica_groups={{7,5,3,1,6,4,2,0},{15,13,11,9,14,12,10,8},{23,21,19,17,22,20,18,16},{31..., dimensions={0} | all-to-all | bytes 589824 | tf_op jit(solution)/shard_map/all_to_all | solution.py:240
  12.2 1.6 %shard_map.92 = bf16[16,72,128]{2,1,0:T(8,128)(2,1)} custom-call(bf16[8,144,128]{2,1,0:T(8,128)(2,1)S(1)} %all_to_all.10.got_ref, f32[8,384]{1,0:T(8,128)S(1)} %get-tuple-element.13.spread_ref, f32[96,1]{1,0:T(8,128)S(1)} %get-tuple-element.14.mask_ref), custom_call_target="tpu_custom_call" | custom-call | tf_op jit(solution)/shard_map/pallas_call | solution.py:241
  13.8 0.0 copy-start.1
  13.8 6.8 %all-to-all-start.1 = ((bf16[16,72,128]{2,1,0:T(8,128)(2,1)}), bf16[16,72,128]{2,1,0:T(8,128)(2,1)S(1)}, u32[]{:S(2)}, u32[]{:S(2)}) async-start(bf16[16,72,128]{2,1,0:T(8,128)(2,1)} %shard_map.92), calls=%async_computation.1 | async-start | bytes 589824 | tf_op jit(solution)/shard_map/all_to_all | solution.py:260
  20.6 0.0 copy-start.2
  20.6 0.0 copy-start.3
  20.6 0.0 copy-done.1
  20.6 0.6 %copy-done.2 = f32[128]{0:T(128)S(1)} copy-done((f32[128]{0:T(128)S(1)}, f32[128]{0:T(128)}, u32[]{:S(2)}) %copy-start.2) | copy-done | bytes 536
  21.3 0.0 copy-done.3
  21.3 0.0 copy-start
  21.3 0.2 shard_map.93
  21.5 5.6 %all-to-all-done.1.total_ref = bf16[16,72,128]{2,1,0:T(8,128)(2,1)S(1)} async-done(((bf16[16,72,128]{2,1,0:T(8,128)(2,1)}), bf16[16,72,128]{2,1,0:T(8,128)(2,1)S(1)}, u32[]{:S(2)}, u32[]{:S(2)}) %all-to-all-start.1) | async-done | bytes 294944 | tf_op jit(solution)/shard_map/all_to_all | solution.py:260
  27.0 0.0 copy-done
  27.0 1.0 %shard_map.94 = bf16[12,48,128]{2,1,0:T(8,128)(2,1)} custom-call(bf16[16,72,128]{2,1,0:T(8,128)(2,1)S(1)} %all-to-all-done.1.total_ref, f32[576,128]{1,0:T(8,128)S(1)} %get-tuple-element.16.gate_ref, f32[128,1]{1,0:T(8,128)S(1)} %get-tuple-element.17.gain_ref, f32[128,1]{1,0:T(8,128)S(1)} %get-tuple-element.18.bias_ref, bf16[128,128]{1,0:T(8,128)(2,1)S(1)} %copy-done), custom_call_target="tpu_custom_call" | custom-call | tf_op jit(solution)/shard_map/pallas_call | solution.py:261
Async XLA Ops:
  13.8 6.8 %copy-start.1 = (bf16[128,128]{1,0:T(8,128)(2,1)S(1)}, bf16[128,128]{1,0:T(8,128)(2,1)}, u32[]{:S(2)}) copy-start(bf16[128,128]{1,0:T(8,128)(2,1)} %w_ref.2) | copy-start | bytes 98308
  13.8 13.2 %all-to-all-start.1 = ((bf16[16,72,128]{2,1,0:T(8,128)(2,1)}), bf16[16,72,128]{2,1,0:T(8,128)(2,1)S(1)}, u32[]{:S(2)}, u32[]{:S(2)}) async-start(bf16[16,72,128]{2,1,0:T(8,128)(2,1)} %shard_map.92), calls=%async_computation.1 | async-start | bytes 589824 | tf_op jit(solution)/shard_map/all_to_all | solution.py:260
  20.6 0.7 %copy-start.2 = (f32[128]{0:T(128)S(1)}, f32[128]{0:T(128)}, u32[]{:S(2)}) copy-start(f32[128]{0:T(128)} %param.15) | copy-start | bytes 1540
  20.6 0.7 %copy-start.3 = (f32[128]{0:T(128)S(1)}, f32[128]{0:T(128)}, u32[]{:S(2)}) copy-start(f32[128]{0:T(128)} %param.16) | copy-start | bytes 1540
  21.3 5.8 %copy-start = (bf16[128,128]{1,0:T(8,128)(2,1)S(1)}, bf16[128,128]{1,0:T(8,128)(2,1)}, u32[]{:S(2)}) copy-start(bf16[128,128]{1,0:T(8,128)(2,1)} %w_ref.3) | copy-start | bytes 98308

commit v15 on v14

--- a/solution.py
+++ b/solution.py
@@ -10,6 +10,7 @@
 epsilon = 1e-05
 LANES = 128
 GROUP = 8
+PIECES = 3
 AXES = ("half", "quad", "col")
 VMEM = pl.BlockSpec(memory_space=pltpu.VMEM)
 HBM = pl.BlockSpec(memory_space=pltpu.HBM)
@@ -43,15 +44,6 @@
     return jnp.concatenate(blocks, axis=-2)
 
 
-def unpack(x, rows):
-    whole, rest = divmod(x.shape[-2], rows)
-    blocks = [x[..., t * rows : (t + 1) * rows, :] for t in range(whole)]
-    if rest:
-        tail = x[..., whole * rows :, :]
-        blocks.append(jnp.concatenate([tail[..., : LANES // 2], tail[..., LANES // 2 :]], axis=-2))
-    return jnp.concatenate(blocks, axis=-1)
-
-
 def arrange(x):
     row_count, col_count, _ = x.shape
     whole, spare = row_count // 3, LANES - 2 * col_count
@@ -61,25 +53,12 @@
     return jnp.concatenate(blocks + [x[2 * whole + t, spare:] for t in range(whole)], axis=0)
 
 
-def restore(x, row_count, col_count):
-    whole, spare = row_count // 3, LANES - 2 * col_count
-    rest = col_count - spare
-    rows = []
-    for t in range(whole):
-        rows += [x[t * LANES : t * LANES + col_count], x[t * LANES + col_count : t * LANES + 2 * col_count]]
-    for t in range(whole):
-        tail = whole * LANES + t * rest
-        rows += [x[t * LANES + 2 * col_count : (t + 1) * LANES], x[tail : tail + rest]]
-    return jnp.concatenate(rows, axis=0)
-
-
 def project_kernel(pair_hbm, gain_hbm, bias_hbm, w_hbm, mask_hbm, sides_ref, normed_ref, spread_ref, column_mask_ref, pair_ref, gain_ref, bias_ref, w_ref, mask_ref, sems):
-    copies = [
-        pltpu.make_async_copy(source, target, sems.at[n])
-        for n, (source, target) in enumerate(
-            [(mask_hbm, mask_ref), (pair_hbm, pair_ref), (gain_hbm, gain_ref), (bias_hbm, bias_ref), (w_hbm, w_ref)]
-        )
-    ]
+    step = pair_ref.shape[0] // PIECES
+    pieces = [pl.ds(n * step, step) for n in range(PIECES)]
+    moves = [(mask_hbm, mask_ref), (gain_hbm, gain_ref), (bias_hbm, bias_ref)]
+    moves += [(pair_hbm.at[piece], pair_ref.at[piece]) for piece in pieces] + [(w_hbm, w_ref)]
+    copies = [pltpu.make_async_copy(source, target, sems.at[n]) for n, (source, target) in enumerate(moves)]
     for copy in copies:
         copy.start()
     devices = sides_ref.shape[0]
@@ -103,12 +82,24 @@
     channel = lax.broadcasted_iota(jnp.int32, (group, lanes), 0)
     lane = lax.broadcasted_iota(jnp.int32, (group, lanes), 1)
     spread_ref[...] = jnp.where(lane % group == channel, kept, 0.0)
-    for copy in copies[1:4]:
+    for copy in copies[1:3]:
         copy.wait()
-    flat = pair_ref[...].reshape(tokens, channels).astype(jnp.float32)
-    normed = layer_norm(flat, gain_ref[...], bias_ref[...], -1).astype(jnp.bfloat16)
+    ones = jnp.ones((channels, channels), jnp.bfloat16)
+    parts = []
+    for piece, copy in zip(pieces, copies[3:]):
+        copy.wait()
+        flat = pair_ref[piece].reshape(tokens // PIECES, channels)
+        mean = jnp.dot(flat, ones, preferred_element_type=jnp.float32) * (1.0 / channels)
+        centred = flat.astype(jnp.float32) - mean
+        square = centred * centred
+        high = square.astype(jnp.bfloat16)
+        low = (square - high.astype(jnp.float32)).astype(jnp.bfloat16)
+        variance = jnp.dot(jnp.concatenate([high, low], axis=1), jnp.concatenate([ones, ones], axis=0), preferred_element_type=jnp.float32)
+        scale = lax.rsqrt(variance * (1.0 / channels) + epsilon)
+        parts.append((centred * scale * gain_ref[...] + bias_ref[...]).astype(jnp.bfloat16))
+    normed = jnp.concatenate(parts, axis=0)
     normed_ref[...] = normed
-    copies[4].wait()
+    copies[-1].wait()
     arranged = arrange(normed.reshape(pair_ref.shape))
     projected = lax.dot_general(w_ref[...], arranged, (((0,), (1,)), ((), ())), preferred_element_type=jnp.float32)
     left = sigmoid(projected[:hidden]) * projected[hidden : 2 * hidden]
@@ -117,7 +108,7 @@
     sides_ref[...] = pack(sides).astype(jnp.bfloat16)
 
 
-def triangle_kernel(far_order, cols, row_count, col_count, share, got_ref, spread_ref, mask_ref, total_ref):
+def triangle_kernel(far_order, cols, row_count, col_count, share, got_ref, spread_ref, mask_ref, total_ref, left_ref):
     sources = got_ref.shape[0]
     both = 2 * share
     group, lanes = spread_ref.shape
@@ -152,11 +143,16 @@
     contract = (((1,), (1,)), ((), ()))
     mains, lasts = [], []
     for part in range(parts):
-        left, right = side(0, part), side(1, part).astype(jnp.bfloat16)
-        left = (left[:, None, :] * spread_ref[...][None]).reshape(rows, row_count, group, lanes)
-        pairs = left[:, : 2 * whole].reshape(rows, whole, 2, group, lanes)
-        left = jnp.concatenate([pairs[:, :, 0], pairs[:, :, 1], left[:, 2 * whole :]], axis=-1)
-        left = left.reshape(rows * whole * group, 3 * lanes).astype(jnp.bfloat16)
+        left_ref[part] = side(0, part)
+        right = side(1, part).astype(jnp.bfloat16)
+        left = []
+        for row in range(rows):
+            for t in range(whole):
+                at = row * row_count
+                picks = [at + 2 * t, at + 2 * t + 1, at + 2 * whole + t]
+                wide = [jnp.broadcast_to(left_ref[part, i : i + 1, :], (group, lanes)) * spread_ref[...] for i in picks]
+                left.append(jnp.concatenate(wide, axis=1))
+        left = jnp.concatenate(left, axis=0).astype(jnp.bfloat16)
         ours = [right[col * col_count : (col + 1) * col_count] for col in range(cols)]
         weights = [
             placed([p for mine in ours for p in (mine, LANES - col_count)]),
@@ -182,20 +178,42 @@
     bias_out_ref[...] = column(bias_ref[...])
 
 
-def output_kernel(far_order, near_order, total_ref, gate_ref, gain_ref, bias_ref, w_ref, out_ref):
-    tokens = gate_ref.shape[0]
-    hidden = w_ref.shape[0]
+def output_kernel(far_order, near_order, total_ref, gate_ref, gain_ref, bias_ref, w_ref, out_hbm, out_ref, sems):
+    row_count, col_count, channels = out_ref.shape
     near = len(near_order)
-    share = hidden // near
+    share = w_ref.shape[0] // near
+    whole, spare = row_count // 3, LANES - 2 * col_count
+    rest = col_count - spare
     blocks = []
     for index in near_order:
         parts = [total_ref[source].astype(jnp.float32) for source, device in enumerate(far_order) if device % near == index]
-        blocks.append(unpack(sum(parts[1:], parts[0]), share))
-    total = jnp.concatenate(blocks, axis=0)
-    normed = layer_norm(total, gain_ref[...], bias_ref[...], 0).astype(jnp.bfloat16)
-    output = lax.dot_general(normed, w_ref[...], (((0,), (0,)), ((), ())), preferred_element_type=jnp.float32)
-    output = restore(output, out_ref.shape[0], out_ref.shape[1])
-    out_ref[...] = (gate_ref[...] * output).astype(jnp.bfloat16).reshape(out_ref.shape)
+        blocks.append(sum(parts[1:], parts[0]))
+
+    def project(total):
+        normed = layer_norm(total, gain_ref[...], bias_ref[...], 0).astype(jnp.bfloat16)
+        return lax.dot_general(normed, w_ref[...], (((0,), (0,)), ((), ())), preferred_element_type=jnp.float32)
+
+    def store(row, at, values):
+        spot = pl.ds(row * col_count + at, values.shape[0])
+        out_ref[row, pl.ds(at, values.shape[0])] = (gate_ref[spot] * values).astype(jnp.bfloat16)
+
+    tails = [block[whole * share :] for block in blocks]
+    tails = [jnp.concatenate([tail[:, : LANES // 2], tail[:, LANES // 2 :]], axis=0) for tail in tails]
+    last = project(jnp.concatenate(tails, axis=0))
+    for t in range(whole):
+        store(2 * whole + t, spare, last[t * rest : (t + 1) * rest])
+    copies = []
+    for t in range(whole):
+        values = project(jnp.concatenate([block[t * share : (t + 1) * share] for block in blocks], axis=0))
+        store(2 * t, 0, values[:col_count])
+        store(2 * t + 1, 0, values[col_count : 2 * col_count])
+        store(2 * whole + t, 0, values[2 * col_count :])
+        for rows in (pl.ds(2 * t, 2), pl.ds(2 * whole + t, 1)):
+            copy = pltpu.make_async_copy(out_ref.at[rows], out_hbm.at[rows], sems.at[len(copies)])
+            copy.start()
+            copies.append(copy)
+    for copy in copies:
+        copy.wait()
 
 
 def per_device(rows, cols, halves, pair, token_mask, gain_in, bias_in, w_in, w_gate, gain_out, bias_out, w_out):
@@ -233,7 +251,7 @@
             pltpu.VMEM((1, channels), jnp.float32),
             pltpu.VMEM(w_in.shape, w_in.dtype),
             pltpu.VMEM((1, length), jnp.int32),
-            pltpu.SemaphoreType.DMA((5,)),
+            pltpu.SemaphoreType.DMA((PIECES + 4,)),
         ],
         compiler_params=LIMIT,
     )(*(pltpu.with_memory_space_constraint(x, pltpu.HBM) for x in arguments))
@@ -243,6 +261,7 @@
         out_shape=jax.ShapeDtypeStruct((devices, share * tokens // LANES, LANES), jnp.bfloat16),
         in_specs=[VMEM] * 3,
         out_specs=VMEM,
+        scratch_shapes=[pltpu.VMEM((share // GROUP, length, GROUP * depth), jnp.float32)],
         compiler_params=LIMIT,
     )(got, *masks)
     gate, gain_out, bias_out = pl.pallas_call(
@@ -262,7 +281,8 @@
         functools.partial(output_kernel, far_order, near_order),
         out_shape=jax.ShapeDtypeStruct(pair.shape, jnp.bfloat16),
         in_specs=[VMEM] * 5,
-        out_specs=VMEM,
+        out_specs=HBM,
+        scratch_shapes=[pltpu.VMEM(pair.shape, jnp.bfloat16), pltpu.SemaphoreType.DMA((2 * row_count // 3,))],
         compiler_params=LIMIT,
     )(total, gate, gain_out, bias_out, w_out)
 

time: 28.4 us -> 29.1 us (1.025)
  Pallas kernels: 4.44 us -> 5.2 us
    pallas_call x1, Pallas kernels: 1.64 us -> 2.31 us  [per_device(): pl.pallas_call(project_kernel, out_shape=(jax.ShapeDtypeStruct((near, 2 *...]
where the time goes in v15:
time: 29.1 us; the launch traced here: 28.8 us
  blocking collectives  10.6 us (36%)
  starting transfers between devices  6.76 us (23%)
  waiting for transfers between devices  5.55 us (19%)
  Pallas kernels  5.2 us (18%)
  local copies, waits for them, and re-layouts  0.65 us (2%)
    all_to_all x1, blocking collectives, per_device(): lax.all_to_all(sides, ('quad', 'col'), split_axis=0, concat_axis=0, tiled...  10.6 us
    all_to_all x1, starting transfers between devices, per_device(): lax.all_to_all(total, ('half', 'quad', 'col'), split_axis=0, concat_axis=...  6.76 us
    all_to_all x1, waiting for transfers between devices, per_device(): lax.all_to_all(total, ('half', 'quad', 'col'), split_axis=0, concat_axis=...  5.55 us
    pallas_call x1, Pallas kernels, per_device(): pl.pallas_call(project_kernel, out_shape=(jax.ShapeDtypeStruct((near, 2 *...  2.31 us
    pallas_call x1, Pallas kernels, per_device(): pl.pallas_call(functools.partial(triangle_kernel, far_order, cols, row_co...  1.57 us
    pallas_call x1, Pallas kernels, per_device(): pl.pallas_call(functools.partial(output_kernel, far_order, near_order), o...  1.14 us
    unnamed x8, local copies, waits for them, and re-layouts  0.65 us
  transfers between devices with their start and end apart: 1, of which 1 were waited for; matrix products, arithmetic and copies ran while one was open for 0% of the time, Pallas kernels for 1%

profile of v15, /device:TPU:0, one launch (start us, length us, event | category | flops | bytes accessed | tf_op | source)
XLA Modules:
  0.0 28.8 jit_solution(15554425755134154080)
XLA Ops:
  0.0 2.3 %shard_map.91 = (bf16[8,144,128]{2,1,0:T(8,128)(2,1)S(1)}, bf16[576,128]{1,0:T(8,128)(2,1)S(1)}, f32[8,384]{1,0:T(8,128)S(1)}, f32[96,1]{1,0:T(8,128)S(1)}) custom-call(bf16[12,48,128]{2,1,0:T(8,128)(2,1)} %pair_hbm.1, f32[1,128]{1,0:T(1,128)} %bitcast.7, f32[1,128]{1,0:T(1,128)} %bitcast.8, bf16[128,512]{1,0:T(8,128)(2,1)} %w_hbm.1, s32[1,96]{1,0:T(1,128)} %bitcast.9), custom_call_target="tpu_custom_call" | custom-call | tf_op jit(solution)/shard_map/pallas_call | solution.py:238
  2.3 10.6 %all_to_all.10.got_ref = bf16[8,144,128]{2,1,0:T(8,128)(2,1)S(1)} all-to-all(bf16[8,144,128]{2,1,0:T(8,128)(2,1)S(1)} %get-tuple-element.12), channel_id=1, replica_groups={{7,5,3,1,6,4,2,0},{15,13,11,9,14,12,10,8},{23,21,19,17,22,20,18,16},{31..., dimensions={0} | all-to-all | bytes 589824 | tf_op jit(solution)/shard_map/all_to_all | solution.py:258
  12.9 1.6 %shard_map.92 = bf16[16,72,128]{2,1,0:T(8,128)(2,1)} custom-call(bf16[8,144,128]{2,1,0:T(8,128)(2,1)S(1)} %all_to_all.10.got_ref, f32[8,384]{1,0:T(8,128)S(1)} %get-tuple-element.13.spread_ref, f32[96,1]{1,0:T(8,128)S(1)} %get-tuple-element.14.mask_ref), custom_call_target="tpu_custom_call" | custom-call | tf_op jit(solution)/shard_map/pallas_call | solution.py:259
  14.5 0.0 copy-start.1
  14.5 6.8 %all-to-all-start.1 = ((bf16[16,72,128]{2,1,0:T(8,128)(2,1)}), bf16[16,72,128]{2,1,0:T(8,128)(2,1)S(1)}, u32[]{:S(2)}, u32[]{:S(2)}) async-start(bf16[16,72,128]{2,1,0:T(8,128)(2,1)} %shard_map.92), calls=%async_computation.1 | async-start | bytes 589824 | tf_op jit(solution)/shard_map/all_to_all | solution.py:279
  21.2 0.0 copy-start.2
  21.2 0.0 copy-start.3
  21.3 0.0 copy-done.1
  21.3 0.6 %copy-done.2 = f32[128]{0:T(128)S(1)} copy-done((f32[128]{0:T(128)S(1)}, f32[128]{0:T(128)}, u32[]{:S(2)}) %copy-start.2) | copy-done | bytes 536
  21.9 0.0 copy-done.3
  21.9 0.0 copy-start
  21.9 0.2 shard_map.93
  22.1 5.6 %all-to-all-done.1.total_ref = bf16[16,72,128]{2,1,0:T(8,128)(2,1)S(1)} async-done(((bf16[16,72,128]{2,1,0:T(8,128)(2,1)}), bf16[16,72,128]{2,1,0:T(8,128)(2,1)S(1)}, u32[]{:S(2)}, u32[]{:S(2)}) %all-to-all-start.1) | async-done | bytes 294944 | tf_op jit(solution)/shard_map/all_to_all | solution.py:279
  27.7 0.0 copy-done
  27.7 1.1 %shard_map.94 = bf16[12,48,128]{2,1,0:T(8,128)(2,1)} custom-call(bf16[16,72,128]{2,1,0:T(8,128)(2,1)S(1)} %all-to-all-done.1.total_ref, f32[576,128]{1,0:T(8,128)S(1)} %get-tuple-element.16.gate_ref, f32[128,1]{1,0:T(8,128)S(1)} %get-tuple-element.17.gain_ref, f32[128,1]{1,0:T(8,128)S(1)} %get-tuple-element.18.bias_ref, bf16[128,128]{1,0:T(8,128)(2,1)S(1)} %copy-done), custom_call_target="tpu_custom_call" | custom-call | tf_op jit(solution)/shard_map/pallas_call | solution.py:280
Async XLA Ops:
  14.5 6.8 %copy-start.1 = (bf16[128,128]{1,0:T(8,128)(2,1)S(1)}, bf16[128,128]{1,0:T(8,128)(2,1)}, u32[]{:S(2)}) copy-start(bf16[128,128]{1,0:T(8,128)(2,1)} %w_ref.2) | copy-start | bytes 98308
  14.5 13.2 %all-to-all-start.1 = ((bf16[16,72,128]{2,1,0:T(8,128)(2,1)}), bf16[16,72,128]{2,1,0:T(8,128)(2,1)S(1)}, u32[]{:S(2)}, u32[]{:S(2)}) async-start(bf16[16,72,128]{2,1,0:T(8,128)(2,1)} %shard_map.92), calls=%async_computation.1 | async-start | bytes 589824 | tf_op jit(solution)/shard_map/all_to_all | solution.py:279
  21.2 0.7 %copy-start.2 = (f32[128]{0:T(128)S(1)}, f32[128]{0:T(128)}, u32[]{:S(2)}) copy-start(f32[128]{0:T(128)} %param.15) | copy-start | bytes 1540
  21.2 0.7 %copy-start.3 = (f32[128]{0:T(128)S(1)}, f32[128]{0:T(128)}, u32[]{:S(2)}) copy-start(f32[128]{0:T(128)} %param.16) | copy-start | bytes 1540
  21.9 5.8 %copy-start = (bf16[128,128]{1,0:T(8,128)(2,1)S(1)}, bf16[128,128]{1,0:T(8,128)(2,1)}, u32[]{:S(2)}) copy-start(bf16[128,128]{1,0:T(8,128)(2,1)} %w_ref.3) | copy-start | bytes 98308

commit v16 on v14

--- a/solution.py
+++ b/solution.py
@@ -73,7 +73,9 @@
     return jnp.concatenate(rows, axis=0)
 
 
-def project_kernel(pair_hbm, gain_hbm, bias_hbm, w_hbm, mask_hbm, sides_ref, normed_ref, spread_ref, column_mask_ref, pair_ref, gain_ref, bias_ref, w_ref, mask_ref, sems):
+def project_kernel(quads, cols, pair_hbm, gain_hbm, bias_hbm, w_hbm, mask_hbm, *refs):
+    piece_refs, refs = refs[: quads * cols], refs[quads * cols :]
+    normed_ref, spread_ref, column_mask_ref, pair_ref, gain_ref, bias_ref, w_ref, mask_ref, sems, sides_ref = refs
     copies = [
         pltpu.make_async_copy(source, target, sems.at[n])
         for n, (source, target) in enumerate(
@@ -83,21 +85,24 @@
     for copy in copies:
         copy.start()
     devices = sides_ref.shape[0]
+    my_quad, my_col = lax.axis_index("quad"), lax.axis_index("col")
     tokens, channels = normed_ref.shape
     hidden = w_ref.shape[1] // 4
     share = hidden // devices
     group, lanes = spread_ref.shape
     copies[0].wait()
     mask_row = mask_ref[...].astype(jnp.float32)
-    column_mask_ref[...] = column(mask_row)
+    mask_column = column(mask_row)
+    middle = mask_column.shape[0] // cols
+    swapped = jnp.concatenate([mask_column[middle:], mask_column[:middle]], axis=0)
+    column_mask_ref[...] = jnp.where(my_col == 0, mask_column, swapped)
     start = lax.axis_index("half") * (lanes // group)
     token = lax.broadcasted_iota(jnp.int32, (mask_row.shape[1], lanes), 0)
     lane = lax.broadcasted_iota(jnp.int32, (mask_row.shape[1], lanes), 1)
     row_count = pair_ref.shape[0]
     whole = row_count // 3
-    quads = lanes // group // row_count
     block, t, row = lane // LANES, lane // (quads * group) % whole, lane // group % quads
-    k = row * row_count + jnp.where(block < 2, 2 * t + block, 2 * whole + t)
+    k = (row ^ my_quad) * row_count + jnp.where(block < 2, 2 * t + block, 2 * whole + t)
     pick = jnp.where(k + start == token, 1.0, 0.0)
     kept = jnp.dot(mask_row.astype(jnp.bfloat16), pick.astype(jnp.bfloat16), preferred_element_type=jnp.float32)
     channel = lax.broadcasted_iota(jnp.int32, (group, lanes), 0)
@@ -115,17 +120,21 @@
     right = sigmoid(projected[2 * hidden : 3 * hidden]) * projected[3 * hidden :]
     sides = jnp.concatenate([left.reshape(devices, share, tokens), right.reshape(devices, share, tokens)], axis=1)
     sides_ref[...] = pack(sides).astype(jnp.bfloat16)
-
-
-def triangle_kernel(far_order, cols, row_count, col_count, share, got_ref, spread_ref, mask_ref, total_ref):
-    sources = got_ref.shape[0]
+    for step, piece_ref in enumerate(piece_refs):
+        piece_ref[...] = sides_ref[(my_quad * cols + my_col) ^ step]
+
+
+def triangle_kernel(far_order, cols, row_count, col_count, share, *refs):
+    *got_refs, spread_ref, mask_ref, total_ref = refs
+    sources = len(got_refs)
+    my_col = lax.axis_index("col")
     both = 2 * share
     group, lanes = spread_ref.shape
     length = mask_ref.shape[0]
     rows, quads, parts = length // row_count, sources // cols, share // group
     whole, spare = row_count // 3, LANES - 2 * col_count
     rest = col_count - spare
-    blocks = [[got_ref[sources - 1 - (col * quads + row)].astype(jnp.float32) for row in range(quads)] for col in range(cols)]
+    blocks = [[got_refs[row * cols + col][...].astype(jnp.float32) for row in range(quads)] for col in range(cols)]
 
     def turned(picks):
         return jnp.concatenate([blocks[col][row][at : at + group] for col, row, at in picks], axis=0).T
@@ -167,8 +176,10 @@
         mains.append(lax.dot_general(left, weights, contract, preferred_element_type=jnp.float32))
         weights = jnp.concatenate([mine[spare:] for mine in ours], axis=0)
         lasts.append(lax.dot_general(left[:, 2 * lanes :], weights, contract, preferred_element_type=jnp.float32))
-    for target, device in enumerate(far_order):
+    for device in range(rows * cols):
         row, col = divmod(device, cols)
+        other = (row + rows // 2) % rows * cols + 1 - col
+        target = jnp.where(my_col == 0, far_order.index(device), far_order.index(other))
         spots = [(row * whole + t) * group for t in range(whole)]
         tiles = [main[at : at + group, col * LANES : (col + 1) * LANES] for at in spots for main in mains]
         last = [part[at : at + group, col * rest : (col + 1) * rest] for part in lasts for at in spots]
@@ -182,13 +193,12 @@
     bias_out_ref[...] = column(bias_ref[...])
 
 
-def output_kernel(far_order, near_order, total_ref, gate_ref, gain_ref, bias_ref, w_ref, out_ref):
+def output_kernel(far_order, near, total_ref, gate_ref, gain_ref, bias_ref, w_ref, out_ref):
     tokens = gate_ref.shape[0]
     hidden = w_ref.shape[0]
-    near = len(near_order)
     share = hidden // near
     blocks = []
-    for index in near_order:
+    for index in range(near):
         parts = [total_ref[source].astype(jnp.float32) for source, device in enumerate(far_order) if device % near == index]
         blocks.append(unpack(sum(parts[1:], parts[0]), share))
     total = jnp.concatenate(blocks, axis=0)
@@ -204,7 +214,6 @@
     devices = rows * cols
     near = devices // halves
     quads = rows // halves
-    near_order = [quad * cols + col for col in reversed(range(cols)) for quad in reversed(range(quads))]
     far_order = []
     for col in reversed(range(cols)):
         ahead = list(range(quads)) if col else list(range(1, quads)) + [0]
@@ -217,16 +226,16 @@
     depth = length // halves
     token_mask = token_mask.reshape(1, length)
     arguments = (pair, gain_in.reshape(1, channels), bias_in.reshape(1, channels), w_in, token_mask)
-    sides, normed, *masks = pl.pallas_call(
-        project_kernel,
+    *pieces, normed, spread, mask = pl.pallas_call(
+        functools.partial(project_kernel, quads, cols),
         out_shape=(
-            jax.ShapeDtypeStruct((near, 2 * share * tokens // LANES, LANES), jnp.bfloat16),
+            *[jax.ShapeDtypeStruct((2 * share * tokens // LANES, LANES), jnp.bfloat16)] * near,
             jax.ShapeDtypeStruct((tokens, channels), jnp.bfloat16),
             jax.ShapeDtypeStruct((GROUP, GROUP * depth), jnp.float32),
             jax.ShapeDtypeStruct((length, 1), jnp.float32),
         ),
         in_specs=[HBM] * 5,
-        out_specs=(VMEM,) * 4,
+        out_specs=(VMEM,) * (near + 3),
         scratch_shapes=[
             pltpu.VMEM(pair.shape, pair.dtype),
             pltpu.VMEM((1, channels), jnp.float32),
@@ -234,17 +243,22 @@
             pltpu.VMEM(w_in.shape, w_in.dtype),
             pltpu.VMEM((1, length), jnp.int32),
             pltpu.SemaphoreType.DMA((5,)),
+            pltpu.VMEM((near, 2 * share * tokens // LANES, LANES), jnp.bfloat16),
         ],
         compiler_params=LIMIT,
     )(*(pltpu.with_memory_space_constraint(x, pltpu.HBM) for x in arguments))
-    got = lax.all_to_all(sides, ("quad", "col"), split_axis=0, concat_axis=0, tiled=True, axis_index_groups=[near_order])
+    got = pieces[:1] + [None] * (near - 1)
+    for quad in reversed(range(quads)):
+        for step in range(quad * cols, (quad + 1) * cols):
+            if step:
+                got[step] = lax.ppermute(pieces[step], ("quad", "col"), [(i, i ^ step) for i in range(near)])
     total = pl.pallas_call(
         functools.partial(triangle_kernel, far_order, cols, row_count, col_count, share),
         out_shape=jax.ShapeDtypeStruct((devices, share * tokens // LANES, LANES), jnp.bfloat16),
-        in_specs=[VMEM] * 3,
+        in_specs=[VMEM] * (near + 2),
         out_specs=VMEM,
         compiler_params=LIMIT,
-    )(got, *masks)
+    )(*got, spread, mask)
     gate, gain_out, bias_out = pl.pallas_call(
         gate_kernel,
         out_shape=(
@@ -259,7 +273,7 @@
     )(normed, w_gate, gain_out.reshape(1, hidden), bias_out.reshape(1, hidden))
     total = lax.all_to_all(total, ("half", "quad", "col"), split_axis=0, concat_axis=0, tiled=True, axis_index_groups=[far_order])
     return pl.pallas_call(
-        functools.partial(output_kernel, far_order, near_order),
+        functools.partial(output_kernel, far_order, near),
         out_shape=jax.ShapeDtypeStruct(pair.shape, jnp.bfloat16),
         in_specs=[VMEM] * 5,
         out_specs=VMEM,

time: 28.4 us -> 28.8 us (1.014)
  blocking collectives: 10.6 us -> 0 us
  starting transfers between devices: 6.76 us -> 13.6 us
  waiting for transfers between devices: 5.56 us -> 9.77 us
    all_to_all x1 -> x0, blocking collectives: 10.6 us -> none  [per_device(): lax.all_to_all(sides, ('quad', 'col'), split_axis=0, concat_axis=0, tiled...]
    ppermute x0 -> x7, starting transfers between devices: none -> 7.74 us  [per_device(): lax.ppermute(pieces[step], ('quad', 'col'), [(i, i ^ step) for i in range...]
    ppermute x0 -> x7, waiting for transfers between devices: none -> 4.21 us  [per_device(): lax.ppermute(pieces[step], ('quad', 'col'), [(i, i ^ step) for i in range...]
    all_to_all x1, starting transfers between devices: 6.76 us -> 5.85 us  [per_device(): lax.all_to_all(total, ('half', 'quad', 'col'), split_axis=0, concat_axis=...]
  transfers between devices with their start and end apart: 1 -> 8, of which waited for: 1 -> 4; matrix products, arithmetic and copies ran while one was open for 0% -> 0% of each run, Pallas kernels for 1% -> 1%
where the time goes in v16:
time: 28.8 us; the launch traced here: 28.5 us
  starting transfers between devices  13.6 us (47%)
  waiting for transfers between devices  9.77 us (34%)
  Pallas kernels  4.46 us (15%)
  local copies, waits for them, and re-layouts  0.65 us (2%)
    ppermute x7, starting transfers between devices, per_device(): lax.ppermute(pieces[step], ('quad', 'col'), [(i, i ^ step) for i in range...  7.74 us
    all_to_all x1, starting transfers between devices, per_device(): lax.all_to_all(total, ('half', 'quad', 'col'), split_axis=0, concat_axis=...  5.85 us
    all_to_all x1, waiting for transfers between devices, per_device(): lax.all_to_all(total, ('half', 'quad', 'col'), split_axis=0, concat_axis=...  5.55 us
    ppermute x7, waiting for transfers between devices, per_device(): lax.ppermute(pieces[step], ('quad', 'col'), [(i, i ^ step) for i in range...  4.21 us
    pallas_call x1, Pallas kernels, per_device(): pl.pallas_call(functools.partial(project_kernel, quads, cols), out_shape=...  1.66 us
    pallas_call x1, Pallas kernels, per_device(): pl.pallas_call(functools.partial(triangle_kernel, far_order, cols, row_co...  1.6 us
    pallas_call x1, Pallas kernels, per_device(): pl.pallas_call(functools.partial(output_kernel, far_order, near), out_sha...  1.02 us
    unnamed x8, local copies, waits for them, and re-layouts  0.65 us
  transfers between devices with their start and end apart: 8, of which 4 were waited for; matrix products, arithmetic and copies ran while one was open for 0% of the time, Pallas kernels for 1%

profile of v16, /device:TPU:0, one launch (start us, length us, event | category | flops | bytes accessed | tf_op | source)
XLA Modules:
  0.0 28.5 jit_solution(382355976325045920)
XLA Ops:
  0.0 1.7 %shard_map.91 = (bf16[144,128]{1,0:T(8,128)(2,1)S(1)}, bf16[144,128]{1,0:T(8,128)(2,1)S(1)}, bf16[144,128]{1,0:T(8,128)(2,1)S(1)}, bf16[144,128]{1,0:T(8,128)(2,...) custom-call(bf16[12,48,128]{2,1,0:T(8,128)(2,1)} %pair_hbm.1, ...), custom_call_target="tpu_custom_call" | custom-call | tf_op jit(solution)/shard_map/pallas_call | solution.py:229
  1.7 0.5 %collective-permute-start = (bf16[144,128]{1,0:T(8,128)(2,1)S(1)}, bf16[144,128]{1,0:T(8,128)(2,1)S(1)}, u32[]{:S(2)}, u32[]{:S(2)}) collective-permute-start(bf16[144,128]{1,0:T(8,128)(2,1)S(1)} %get-tuple-element.20), channel_id=1, source_target_pairs={{0,1},{1,0},{2,3},{3,2},{4,5},{5,4},{6,7},{7,6},{8,9},{9,8},{10,11... | collective-permute-start | bytes 110600 | tf_op jit(solution)/shard_map/ppermute | solution.py:254
  2.2 2.6 %collective-permute-start.1 = (bf16[144,128]{1,0:T(8,128)(2,1)S(1)}, bf16[144,128]{1,0:T(8,128)(2,1)S(1)}, u32[]{:S(2)}, u32[]{:S(2)}) collective-permute-start(bf16[144,128]{1,0:T(8,128)(2,1)S(1)} %get-tuple-element.21), channel_id=1, source_target_pairs={{0,2},{1,3},{2,0},{3,1},{4,6},{5,7},{6,4},{7,5},{8,10},{9,11},{10,... | collective-permute-start | bytes 110600 | tf_op jit(solution)/shard_map/ppermute | solution.py:254
  4.8 0.1 collective-permute-start.2
  4.8 1.8 %collective-permute-start.3 = (bf16[144,128]{1,0:T(8,128)(2,1)S(1)}, bf16[144,128]{1,0:T(8,128)(2,1)S(1)}, u32[]{:S(2)}, u32[]{:S(2)}) collective-permute-start(bf16[144,128]{1,0:T(8,128)(2,1)S(1)} %get-tuple-element.23), channel_id=1, source_target_pairs={{0,4},{1,5},{2,6},{3,7},{4,0},{5,1},{6,2},{7,3},{8,12},{9,13},{10,... | collective-permute-start | bytes 110600 | tf_op jit(solution)/shard_map/ppermute | solution.py:254
  6.6 0.0 collective-permute-start.4
  6.6 0.0 collective-permute-done.refs_1_
  6.7 2.6 %collective-permute-start.5 = (bf16[144,128]{1,0:T(8,128)(2,1)S(1)}, bf16[144,128]{1,0:T(8,128)(2,1)S(1)}, u32[]{:S(2)}, u32[]{:S(2)}) collective-permute-start(bf16[144,128]{1,0:T(8,128)(2,1)S(1)} %get-tuple-element.25), channel_id=1, source_target_pairs={{0,6},{1,7},{2,4},{3,5},{4,2},{5,3},{6,0},{7,1},{8,14},{9,15},{10,... | collective-permute-start | bytes 110600 | tf_op jit(solution)/shard_map/ppermute | solution.py:254
  9.3 0.0 collective-permute-done.1.refs_2_
  9.3 0.1 collective-permute-start.6
  9.4 0.0 collective-permute-done.2.refs_3_
  9.4 0.0 collective-permute-done.3.refs_4_
  9.4 0.8 %collective-permute-done.4.refs_5_ = bf16[144,128]{1,0:T(8,128)(2,1)S(1)} collective-permute-done((bf16[144,128]{1,0:T(8,128)(2,1)S(1)}, bf16[144,128]{1,0:T(8,128)(2,1)S(1)}, u32[]{:S(2)}, u32[]{:S(2)}) %collective-permute-start.4) | collective-permute-done | bytes 36896 | tf_op jit(solution)/shard_map/ppermute | solution.py:254
  10.2 2.0 %collective-permute-done.5.refs_6_ = bf16[144,128]{1,0:T(8,128)(2,1)S(1)} collective-permute-done((bf16[144,128]{1,0:T(8,128)(2,1)S(1)}, bf16[144,128]{1,0:T(8,128)(2,1)S(1)}, u32[]{:S(2)}, u32[]{:S(2)}) %collective-permute-start.5) | collective-permute-done | bytes 36896 | tf_op jit(solution)/shard_map/ppermute | solution.py:254
  12.2 1.5 %collective-permute-done.6.refs_7_ = bf16[144,128]{1,0:T(8,128)(2,1)S(1)} collective-permute-done((bf16[144,128]{1,0:T(8,128)(2,1)S(1)}, bf16[144,128]{1,0:T(8,128)(2,1)S(1)}, u32[]{:S(2)}, u32[]{:S(2)}) %collective-permute-start.6) | collective-permute-done | bytes 36896 | tf_op jit(solution)/shard_map/ppermute | solution.py:254
  13.6 1.6 %shard_map.92 = bf16[16,72,128]{2,1,0:T(8,128)(2,1)} custom-call(bf16[144,128]{1,0:T(8,128)(2,1)S(1)} %get-tuple-element.19.refs_0_, bf16[144,128]{1,0:T(8,128)(2,1)S(1)} %collective-permute-done.refs_1_, bf16[144,128]{1,0:T(8,128)(2,1)S(1)} %collective-permute-done.1.refs_2_, bf16[144,128]{1,0:T(8,128)(2,1)S(1)} %collective-permute-done.2.refs_3_, ...), custom_call_target="tpu_custom_call" | custom-call | tf_op jit(solution)/shard_map/pallas_call | solution.py:255
  15.2 5.9 %all-to-all-start = ((bf16[16,72,128]{2,1,0:T(8,128)(2,1)}), bf16[16,72,128]{2,1,0:T(8,128)(2,1)S(1)}, u32[]{:S(2)}, u32[]{:S(2)}) async-start(bf16[16,72,128]{2,1,0:T(8,128)(2,1)} %shard_map.92), calls=%async_computation | async-start | bytes 589824 | tf_op jit(solution)/shard_map/all_to_all | solution.py:274
  21.1 0.0 copy-start.3
  21.1 0.0 copy-done.1
  21.1 0.6 %copy-done.2 = f32[128]{0:T(128)S(1)} copy-done((f32[128]{0:T(128)S(1)}, f32[128]{0:T(128)}, u32[]{:S(2)}) %copy-start.2) | copy-done | bytes 536
  21.7 0.0 copy-done.3
  21.7 0.2 shard_map.93
  21.9 5.6 %all-to-all-done.total_ref = bf16[16,72,128]{2,1,0:T(8,128)(2,1)S(1)} async-done(((bf16[16,72,128]{2,1,0:T(8,128)(2,1)}), bf16[16,72,128]{2,1,0:T(8,128)(2,1)S(1)}, u32[]{:S(2)}, u32[]{:S(2)}) %all-to-all-start) | async-done | bytes 294944 | tf_op jit(solution)/shard_map/all_to_all | solution.py:274
  27.5 1.0 %shard_map.94 = bf16[12,48,128]{2,1,0:T(8,128)(2,1)} custom-call(bf16[16,72,128]{2,1,0:T(8,128)(2,1)S(1)} %all-to-all-done.total_ref, f32[576,128]{1,0:T(8,128)S(1)} %get-tuple-element.30.gate_ref, f32[128,1]{1,0:T(8,128)S(1)} %get-tuple-element.31.gain_ref, f32[128,1]{1,0:T(8,128)S(1)} %get-tuple-element.32.bias_ref, bf16[128,128]{1,0:T(8,128)(2,1)S(1)} %copy-done), custom_call_target="tpu_custom_call" | custom-call | tf_op jit(solution)/shard_map/pallas_call | solution.py:275
  (4 shorter events, 0.0 us)
Async XLA Ops:
  1.7 5.0 %collective-permute-start = (bf16[144,128]{1,0:T(8,128)(2,1)S(1)}, bf16[144,128]{1,0:T(8,128)(2,1)S(1)}, u32[]{:S(2)}, u32[]{:S(2)}) collective-permute-start(bf16[144,128]{1,0:T(8,128)(2,1)S(1)} %get-tuple-element.20), channel_id=1, source_target_pairs={{0,1},{1,0},{2,3},{3,2},{4,5},{5,4},{6,7},{7,6},{8,9},{9,8},{10,11... | collective-permute-start | bytes 110600 | tf_op jit(solution)/shard_map/ppermute | solution.py:254
  2.2 7.1 %collective-permute-start.1 = (bf16[144,128]{1,0:T(8,128)(2,1)S(1)}, bf16[144,128]{1,0:T(8,128)(2,1)S(1)}, u32[]{:S(2)}, u32[]{:S(2)}) collective-permute-start(bf16[144,128]{1,0:T(8,128)(2,1)S(1)} %get-tuple-element.21), channel_id=1, source_target_pairs={{0,2},{1,3},{2,0},{3,1},{4,6},{5,7},{6,4},{7,5},{8,10},{9,11},{10,... | collective-permute-start | bytes 110600 | tf_op jit(solution)/shard_map/ppermute | solution.py:254
  4.8 4.6 %collective-permute-start.2 = (bf16[144,128]{1,0:T(8,128)(2,1)S(1)}, bf16[144,128]{1,0:T(8,128)(2,1)S(1)}, u32[]{:S(2)}, u32[]{:S(2)}) collective-permute-start(bf16[144,128]{1,0:T(8,128)(2,1)S(1)} %get-tuple-element.22), channel_id=1, source_target_pairs={{0,3},{1,2},{2,1},{3,0},{4,7},{5,6},{6,5},{7,4},{8,11},{9,10},{10,... | collective-permute-start | bytes 110600 | tf_op jit(solution)/shard_map/ppermute | solution.py:254
  4.8 4.6 %collective-permute-start.3 = (bf16[144,128]{1,0:T(8,128)(2,1)S(1)}, bf16[144,128]{1,0:T(8,128)(2,1)S(1)}, u32[]{:S(2)}, u32[]{:S(2)}) collective-permute-start(bf16[144,128]{1,0:T(8,128)(2,1)S(1)} %get-tuple-element.23), channel_id=1, source_target_pairs={{0,4},{1,5},{2,6},{3,7},{4,0},{5,1},{6,2},{7,3},{8,12},{9,13},{10,... | collective-permute-start | bytes 110600 | tf_op jit(solution)/shard_map/ppermute | solution.py:254
  6.6 3.5 %collective-permute-start.4 = (bf16[144,128]{1,0:T(8,128)(2,1)S(1)}, bf16[144,128]{1,0:T(8,128)(2,1)S(1)}, u32[]{:S(2)}, u32[]{:S(2)}) collective-permute-start(bf16[144,128]{1,0:T(8,128)(2,1)S(1)} %get-tuple-element.24), channel_id=1, source_target_pairs={{0,5},{1,4},{2,7},{3,6},{4,1},{5,0},{6,3},{7,2},{8,13},{9,12},{10,... | collective-permute-start | bytes 110600 | tf_op jit(solution)/shard_map/ppermute | solution.py:254
  6.7 5.5 %collective-permute-start.5 = (bf16[144,128]{1,0:T(8,128)(2,1)S(1)}, bf16[144,128]{1,0:T(8,128)(2,1)S(1)}, u32[]{:S(2)}, u32[]{:S(2)}) collective-permute-start(bf16[144,128]{1,0:T(8,128)(2,1)S(1)} %get-tuple-element.25), channel_id=1, source_target_pairs={{0,6},{1,7},{2,4},{3,5},{4,2},{5,3},{6,0},{7,1},{8,14},{9,15},{10,... | collective-permute-start | bytes 110600 | tf_op jit(solution)/shard_map/ppermute | solution.py:254
  9.3 4.3 %collective-permute-start.6 = (bf16[144,128]{1,0:T(8,128)(2,1)S(1)}, bf16[144,128]{1,0:T(8,128)(2,1)S(1)}, u32[]{:S(2)}, u32[]{:S(2)}) collective-permute-start(bf16[144,128]{1,0:T(8,128)(2,1)S(1)} %get-tuple-element.26), channel_id=1, source_target_pairs={{0,7},{1,6},{2,5},{3,4},{4,3},{5,2},{6,1},{7,0},{8,15},{9,14},{10,... | collective-permute-start | bytes 110600 | tf_op jit(solution)/shard_map/ppermute | solution.py:254
  15.2 5.9 %copy-start.1 = (bf16[128,128]{1,0:T(8,128)(2,1)S(1)}, bf16[128,128]{1,0:T(8,128)(2,1)}, u32[]{:S(2)}) copy-start(bf16[128,128]{1,0:T(8,128)(2,1)} %w_ref.2) | copy-start | bytes 98308
  15.2 12.3 %all-to-all-start = ((bf16[16,72,128]{2,1,0:T(8,128)(2,1)}), bf16[16,72,128]{2,1,0:T(8,128)(2,1)S(1)}, u32[]{:S(2)}, u32[]{:S(2)}) async-start(bf16[16,72,128]{2,1,0:T(8,128)(2,1)} %shard_map.92), calls=%async_computation | async-start | bytes 589824 | tf_op jit(solution)/shard_map/all_to_all | solution.py:274
  21.1 0.7 %copy-start.2 = (f32[128]{0:T(128)S(1)}, f32[128]{0:T(128)}, u32[]{:S(2)}) copy-start(f32[128]{0:T(128)} %param.15) | copy-start | bytes 1540
  21.1 0.7 %copy-start.3 = (f32[128]{0:T(128)S(1)}, f32[128]{0:T(128)}, u32[]{:S(2)}) copy-start(f32[128]{0:T(128)} %param.16) | copy-start | bytes 1540
  21.7 5.8 %copy-start = (bf16[128,128]{1,0:T(8,128)(2,1)S(1)}, bf16[128,128]{1,0:T(8,128)(2,1)}, u32[]{:S(2)}) copy-start(bf16[128,128]{1,0:T(8,128)(2,1)} %w_ref.3) | copy-start | bytes 98308

commit v17 on v16

--- a/solution.py
+++ b/solution.py
@@ -124,9 +124,10 @@
         piece_ref[...] = sides_ref[(my_quad * cols + my_col) ^ step]
 
 
-def triangle_kernel(far_order, cols, row_count, col_count, share, *refs):
+def triangle_kernel(far_order, steps, cols, row_count, col_count, share, *refs):
     *got_refs, spread_ref, mask_ref, total_ref = refs
-    sources = len(got_refs)
+    got_refs = {step: ref for step, ref in zip(steps, got_refs)}
+    sources = len(steps)
     my_col = lax.axis_index("col")
     both = 2 * share
     group, lanes = spread_ref.shape
@@ -247,13 +248,12 @@
         ],
         compiler_params=LIMIT,
     )(*(pltpu.with_memory_space_constraint(x, pltpu.HBM) for x in arguments))
-    got = pieces[:1] + [None] * (near - 1)
-    for quad in reversed(range(quads)):
-        for step in range(quad * cols, (quad + 1) * cols):
-            if step:
-                got[step] = lax.ppermute(pieces[step], ("quad", "col"), [(i, i ^ step) for i in range(near)])
+    steps = [step for quad in (3, 1, 2, 0) for step in range(quad * cols, (quad + 1) * cols)]
+    got = []
+    for step in steps:
+        got.append(lax.ppermute(pieces[step], ("quad", "col"), [(i, i ^ step) for i in range(near)]) if step else pieces[0])
     total = pl.pallas_call(
-        functools.partial(triangle_kernel, far_order, cols, row_count, col_count, share),
+        functools.partial(triangle_kernel, far_order, steps, cols, row_count, col_count, share),
         out_shape=jax.ShapeDtypeStruct((devices, share * tokens // LANES, LANES), jnp.bfloat16),
         in_specs=[VMEM] * (near + 2),
         out_specs=VMEM,
@@ -323,7 +323,7 @@
         near, hidden, length = rows * cols // halves, args[-1].shape[0], args[1].shape[0]
         row_count, col_count, _ = args[0].shape
         spare = LANES - 2 * col_count
-        fits = hidden % (2 * GROUP * near) == 0 and cols == 2 and length <= LANES and row_count % 3 == 0
+        fits = hidden % (2 * GROUP * near) == 0 and cols == 2 and rows // halves == 4 and length <= LANES and row_count % 3 == 0
         fits = fits and 0 < spare < col_count and row_count // 3 * (col_count - spare) * 2 == LANES
         fits = fits and row_count // 3 * (rows // halves) * GROUP == LANES
         return per_device(rows, cols, halves, *args) if fits else plain_per_device(rows, cols, *args)

time: 28.8 us -> 28.6 us (level)
  waiting for transfers between devices: 9.77 us -> 9.06 us
  starting transfers between devices: 13.6 us -> 14 us
    ppermute x7, waiting for transfers between devices: 4.21 us -> 3.51 us  [per_device(): lax.ppermute(pieces[step], ('quad', 'col'), [(i, i ^ step) for i in range...]
    all_to_all x1, starting transfers between devices: 5.85 us -> 6.5 us  [per_device(): lax.all_to_all(total, ('half', 'quad', 'col'), split_axis=0, concat_axis=...]
  transfers between devices with their start and end apart: 8 -> 8, of which waited for: 4 -> 6; matrix products, arithmetic and copies ran while one was open for 0% -> 0% of each run, Pallas kernels for 1% -> 1%
where the time goes in v17:
time: 28.6 us; the launch traced here: 28.3 us
  starting transfers between devices  14 us (49%)
  waiting for transfers between devices  9.06 us (32%)
  Pallas kernels  4.46 us (16%)
  local copies, waits for them, and re-layouts  0.65 us (2%)
    ppermute x7, starting transfers between devices, per_device(): lax.ppermute(pieces[step], ('quad', 'col'), [(i, i ^ step) for i in range...  7.54 us
    all_to_all x1, starting transfers between devices, per_device(): lax.all_to_all(total, ('half', 'quad', 'col'), split_axis=0, concat_axis=...  6.5 us
    all_to_all x1, waiting for transfers between devices, per_device(): lax.all_to_all(total, ('half', 'quad', 'col'), split_axis=0, concat_axis=...  5.55 us
    ppermute x7, waiting for transfers between devices, per_device(): lax.ppermute(pieces[step], ('quad', 'col'), [(i, i ^ step) for i in range...  3.51 us
    pallas_call x1, Pallas kernels, per_device(): pl.pallas_call(functools.partial(project_kernel, quads, cols), out_shape=...  1.66 us
    pallas_call x1, Pallas kernels, per_device(): pl.pallas_call(functools.partial(triangle_kernel, far_order, steps, cols,...  1.6 us
    pallas_call x1, Pallas kernels, per_device(): pl.pallas_call(functools.partial(output_kernel, far_order, near), out_sha...  1.02 us
    unnamed x8, local copies, waits for them, and re-layouts  0.65 us
  transfers between devices with their start and end apart: 8, of which 6 were waited for; matrix products, arithmetic and copies ran while one was open for 0% of the time, Pallas kernels for 1%

profile of v17, /device:TPU:0, one launch (start us, length us, event | category | flops | bytes accessed | tf_op | source)
XLA Modules:
  0.0 28.3 jit_solution(13201196697586485574)
XLA Ops:
  0.0 1.7 %shard_map.91 = (bf16[144,128]{1,0:T(8,128)(2,1)S(1)}, bf16[144,128]{1,0:T(8,128)(2,1)S(1)}, bf16[144,128]{1,0:T(8,128)(2,1)S(1)}, bf16[144,128]{1,0:T(8,128)(2,...) custom-call(bf16[12,48,128]{2,1,0:T(8,128)(2,1)} %pair_hbm.1, ...), custom_call_target="tpu_custom_call" | custom-call | tf_op jit(solution)/shard_map/pallas_call | solution.py:230
  1.7 4.0 %collective-permute-start = (bf16[144,128]{1,0:T(8,128)(2,1)S(1)}, bf16[144,128]{1,0:T(8,128)(2,1)S(1)}, u32[]{:S(2)}, u32[]{:S(2)}) collective-permute-start(bf16[144,128]{1,0:T(8,128)(2,1)S(1)} %get-tuple-element.19), channel_id=1, source_target_pairs={{0,6},{1,7},{2,4},{3,5},{4,2},{5,3},{6,0},{7,1},{8,14},{9,15},{10,... | collective-permute-start | bytes 110600 | tf_op jit(solution)/shard_map/ppermute | solution.py:254
  5.7 0.0 collective-permute-start.1
  5.7 1.1 %collective-permute-start.2 = (bf16[144,128]{1,0:T(8,128)(2,1)S(1)}, bf16[144,128]{1,0:T(8,128)(2,1)S(1)}, u32[]{:S(2)}, u32[]{:S(2)}) collective-permute-start(bf16[144,128]{1,0:T(8,128)(2,1)S(1)} %get-tuple-element.21), channel_id=1, source_target_pairs={{0,2},{1,3},{2,0},{3,1},{4,6},{5,7},{6,4},{7,5},{8,10},{9,11},{10,... | collective-permute-start | bytes 110600 | tf_op jit(solution)/shard_map/ppermute | solution.py:254
  6.8 0.6 %collective-permute-start.3 = (bf16[144,128]{1,0:T(8,128)(2,1)S(1)}, bf16[144,128]{1,0:T(8,128)(2,1)S(1)}, u32[]{:S(2)}, u32[]{:S(2)}) collective-permute-start(bf16[144,128]{1,0:T(8,128)(2,1)S(1)} %get-tuple-element.22), channel_id=1, source_target_pairs={{0,3},{1,2},{2,1},{3,0},{4,7},{5,6},{6,5},{7,4},{8,11},{9,10},{10,... | collective-permute-start | bytes 110600 | tf_op jit(solution)/shard_map/ppermute | solution.py:254
  7.4 1.8 %collective-permute-start.4 = (bf16[144,128]{1,0:T(8,128)(2,1)S(1)}, bf16[144,128]{1,0:T(8,128)(2,1)S(1)}, u32[]{:S(2)}, u32[]{:S(2)}) collective-permute-start(bf16[144,128]{1,0:T(8,128)(2,1)S(1)} %get-tuple-element.23), channel_id=1, source_target_pairs={{0,4},{1,5},{2,6},{3,7},{4,0},{5,1},{6,2},{7,3},{8,12},{9,13},{10,... | collective-permute-start | bytes 110600 | tf_op jit(solution)/shard_map/ppermute | solution.py:254
  9.1 0.0 collective-permute-done.refs_0_
  9.1 0.1 collective-permute-start.5
  9.2 1.0 %collective-permute-done.1.refs_1_ = bf16[144,128]{1,0:T(8,128)(2,1)S(1)} collective-permute-done((bf16[144,128]{1,0:T(8,128)(2,1)S(1)}, bf16[144,128]{1,0:T(8,128)(2,1)S(1)}, u32[]{:S(2)}, u32[]{:S(2)}) %collective-permute-start.1) | collective-permute-done | bytes 36896 | tf_op jit(solution)/shard_map/ppermute | solution.py:254
  10.2 0.0 collective-permute-start.6
  10.2 0.5 %collective-permute-done.2.refs_2_ = bf16[144,128]{1,0:T(8,128)(2,1)S(1)} collective-permute-done((bf16[144,128]{1,0:T(8,128)(2,1)S(1)}, bf16[144,128]{1,0:T(8,128)(2,1)S(1)}, u32[]{:S(2)}, u32[]{:S(2)}) %collective-permute-start.2) | collective-permute-done | bytes 36896 | tf_op jit(solution)/shard_map/ppermute | solution.py:254
  10.7 0.3 %collective-permute-done.3.refs_3_ = bf16[144,128]{1,0:T(8,128)(2,1)S(1)} collective-permute-done((bf16[144,128]{1,0:T(8,128)(2,1)S(1)}, bf16[144,128]{1,0:T(8,128)(2,1)S(1)}, u32[]{:S(2)}, u32[]{:S(2)}) %collective-permute-start.3) | collective-permute-done | bytes 36896 | tf_op jit(solution)/shard_map/ppermute | solution.py:254
  11.0 0.3 %collective-permute-done.4.refs_4_ = bf16[144,128]{1,0:T(8,128)(2,1)S(1)} collective-permute-done((bf16[144,128]{1,0:T(8,128)(2,1)S(1)}, bf16[144,128]{1,0:T(8,128)(2,1)S(1)}, u32[]{:S(2)}, u32[]{:S(2)}) %collective-permute-start.4) | collective-permute-done | bytes 36896 | tf_op jit(solution)/shard_map/ppermute | solution.py:254
  11.3 1.4 %collective-permute-done.5.refs_5_ = bf16[144,128]{1,0:T(8,128)(2,1)S(1)} collective-permute-done((bf16[144,128]{1,0:T(8,128)(2,1)S(1)}, bf16[144,128]{1,0:T(8,128)(2,1)S(1)}, u32[]{:S(2)}, u32[]{:S(2)}) %collective-permute-start.5) | collective-permute-done | bytes 36896 | tf_op jit(solution)/shard_map/ppermute | solution.py:254
  12.7 0.0 collective-permute-done.6.refs_7_
  12.7 1.6 %shard_map.92 = bf16[16,72,128]{2,1,0:T(8,128)(2,1)} custom-call(bf16[144,128]{1,0:T(8,128)(2,1)S(1)} %collective-permute-done.refs_0_, bf16[144,128]{1,0:T(8,128)(2,1)S(1)} %collective-permute-done.1.refs_1_, bf16[144,128]{1,0:T(8,128)(2,1)S(1)} %collective-permute-done.2.refs_2_, bf16[144,128]{1,0:T(8,128)(2,1)S(1)} %collective-permute-done.3.refs_3_, ...), custom_call_target="tpu_custom_call" | custom-call | tf_op jit(solution)/shard_map/pallas_call | solution.py:255
  14.3 6.5 %all-to-all-start = ((bf16[16,72,128]{2,1,0:T(8,128)(2,1)}), bf16[16,72,128]{2,1,0:T(8,128)(2,1)S(1)}, u32[]{:S(2)}, u32[]{:S(2)}) async-start(bf16[16,72,128]{2,1,0:T(8,128)(2,1)} %shard_map.92), calls=%async_computation | async-start | bytes 589824 | tf_op jit(solution)/shard_map/all_to_all | solution.py:274
  20.8 0.0 copy-start.3
  20.8 0.0 copy-done.1
  20.9 0.6 %copy-done.2 = f32[128]{0:T(128)S(1)} copy-done((f32[128]{0:T(128)S(1)}, f32[128]{0:T(128)}, u32[]{:S(2)}) %copy-start.2) | copy-done | bytes 536
  21.5 0.0 copy-done.3
  21.5 0.2 shard_map.93
  21.7 5.5 %all-to-all-done.total_ref = bf16[16,72,128]{2,1,0:T(8,128)(2,1)S(1)} async-done(((bf16[16,72,128]{2,1,0:T(8,128)(2,1)}), bf16[16,72,128]{2,1,0:T(8,128)(2,1)S(1)}, u32[]{:S(2)}, u32[]{:S(2)}) %all-to-all-start) | async-done | bytes 294944 | tf_op jit(solution)/shard_map/all_to_all | solution.py:274
  27.3 1.0 %shard_map.94 = bf16[12,48,128]{2,1,0:T(8,128)(2,1)} custom-call(bf16[16,72,128]{2,1,0:T(8,128)(2,1)S(1)} %all-to-all-done.total_ref, f32[576,128]{1,0:T(8,128)S(1)} %get-tuple-element.30.gate_ref, f32[128,1]{1,0:T(8,128)S(1)} %get-tuple-element.31.gain_ref, f32[128,1]{1,0:T(8,128)S(1)} %get-tuple-element.32.bias_ref, bf16[128,128]{1,0:T(8,128)(2,1)S(1)} %copy-done), custom_call_target="tpu_custom_call" | custom-call | tf_op jit(solution)/shard_map/pallas_call | solution.py:275
  (4 shorter events, 0.0 us)
Async XLA Ops:
  1.7 7.5 %collective-permute-start = (bf16[144,128]{1,0:T(8,128)(2,1)S(1)}, bf16[144,128]{1,0:T(8,128)(2,1)S(1)}, u32[]{:S(2)}, u32[]{:S(2)}) collective-permute-start(bf16[144,128]{1,0:T(8,128)(2,1)S(1)} %get-tuple-element.19), channel_id=1, source_target_pairs={{0,6},{1,7},{2,4},{3,5},{4,2},{5,3},{6,0},{7,1},{8,14},{9,15},{10,... | collective-permute-start | bytes 110600 | tf_op jit(solution)/shard_map/ppermute | solution.py:254
  5.7 4.5 %collective-permute-start.1 = (bf16[144,128]{1,0:T(8,128)(2,1)S(1)}, bf16[144,128]{1,0:T(8,128)(2,1)S(1)}, u32[]{:S(2)}, u32[]{:S(2)}) collective-permute-start(bf16[144,128]{1,0:T(8,128)(2,1)S(1)} %get-tuple-element.20), channel_id=1, source_target_pairs={{0,7},{1,6},{2,5},{3,4},{4,3},{5,2},{6,1},{7,0},{8,15},{9,14},{10,... | collective-permute-start | bytes 110600 | tf_op jit(solution)/shard_map/ppermute | solution.py:254
  5.7 5.0 %collective-permute-start.2 = (bf16[144,128]{1,0:T(8,128)(2,1)S(1)}, bf16[144,128]{1,0:T(8,128)(2,1)S(1)}, u32[]{:S(2)}, u32[]{:S(2)}) collective-permute-start(bf16[144,128]{1,0:T(8,128)(2,1)S(1)} %get-tuple-element.21), channel_id=1, source_target_pairs={{0,2},{1,3},{2,0},{3,1},{4,6},{5,7},{6,4},{7,5},{8,10},{9,11},{10,... | collective-permute-start | bytes 110600 | tf_op jit(solution)/shard_map/ppermute | solution.py:254
  6.8 4.2 %collective-permute-start.3 = (bf16[144,128]{1,0:T(8,128)(2,1)S(1)}, bf16[144,128]{1,0:T(8,128)(2,1)S(1)}, u32[]{:S(2)}, u32[]{:S(2)}) collective-permute-start(bf16[144,128]{1,0:T(8,128)(2,1)S(1)} %get-tuple-element.22), channel_id=1, source_target_pairs={{0,3},{1,2},{2,1},{3,0},{4,7},{5,6},{6,5},{7,4},{8,11},{9,10},{10,... | collective-permute-start | bytes 110600 | tf_op jit(solution)/shard_map/ppermute | solution.py:254
  7.4 4.0 %collective-permute-start.4 = (bf16[144,128]{1,0:T(8,128)(2,1)S(1)}, bf16[144,128]{1,0:T(8,128)(2,1)S(1)}, u32[]{:S(2)}, u32[]{:S(2)}) collective-permute-start(bf16[144,128]{1,0:T(8,128)(2,1)S(1)} %get-tuple-element.23), channel_id=1, source_target_pairs={{0,4},{1,5},{2,6},{3,7},{4,0},{5,1},{6,2},{7,3},{8,12},{9,13},{10,... | collective-permute-start | bytes 110600 | tf_op jit(solution)/shard_map/ppermute | solution.py:254
  9.1 3.6 %collective-permute-start.5 = (bf16[144,128]{1,0:T(8,128)(2,1)S(1)}, bf16[144,128]{1,0:T(8,128)(2,1)S(1)}, u32[]{:S(2)}, u32[]{:S(2)}) collective-permute-start(bf16[144,128]{1,0:T(8,128)(2,1)S(1)} %get-tuple-element.24), channel_id=1, source_target_pairs={{0,5},{1,4},{2,7},{3,6},{4,1},{5,0},{6,3},{7,2},{8,13},{9,12},{10,... | collective-permute-start | bytes 110600 | tf_op jit(solution)/shard_map/ppermute | solution.py:254
  10.2 2.5 %collective-permute-start.6 = (bf16[144,128]{1,0:T(8,128)(2,1)S(1)}, bf16[144,128]{1,0:T(8,128)(2,1)S(1)}, u32[]{:S(2)}, u32[]{:S(2)}) collective-permute-start(bf16[144,128]{1,0:T(8,128)(2,1)S(1)} %get-tuple-element.26), channel_id=1, source_target_pairs={{0,1},{1,0},{2,3},{3,2},{4,5},{5,4},{6,7},{7,6},{8,9},{9,8},{10,11... | collective-permute-start | bytes 110600 | tf_op jit(solution)/shard_map/ppermute | solution.py:254
  14.3 6.5 %copy-start.1 = (bf16[128,128]{1,0:T(8,128)(2,1)S(1)}, bf16[128,128]{1,0:T(8,128)(2,1)}, u32[]{:S(2)}) copy-start(bf16[128,128]{1,0:T(8,128)(2,1)} %w_ref.2) | copy-start | bytes 98308
  14.3 12.9 %all-to-all-start = ((bf16[16,72,128]{2,1,0:T(8,128)(2,1)}), bf16[16,72,128]{2,1,0:T(8,128)(2,1)S(1)}, u32[]{:S(2)}, u32[]{:S(2)}) async-start(bf16[16,72,128]{2,1,0:T(8,128)(2,1)} %shard_map.92), calls=%async_computation | async-start | bytes 589824 | tf_op jit(solution)/shard_map/all_to_all | solution.py:274
  20.8 0.7 %copy-start.2 = (f32[128]{0:T(128)S(1)}, f32[128]{0:T(128)}, u32[]{:S(2)}) copy-start(f32[128]{0:T(128)} %param.15) | copy-start | bytes 1540
  20.8 0.7 %copy-start.3 = (f32[128]{0:T(128)S(1)}, f32[128]{0:T(128)}, u32[]{:S(2)}) copy-start(f32[128]{0:T(128)} %param.16) | copy-start | bytes 1540
  21.5 5.8 %copy-start = (bf16[128,128]{1,0:T(8,128)(2,1)S(1)}, bf16[128,128]{1,0:T(8,128)(2,1)}, u32[]{:S(2)}) copy-start(bf16[128,128]{1,0:T(8,128)(2,1)} %w_ref.3) | copy-start | bytes 98308

commit v18 on v14

--- a/solution.py
+++ b/solution.py
@@ -73,19 +73,26 @@
     return jnp.concatenate(rows, axis=0)
 
 
-def project_kernel(pair_hbm, gain_hbm, bias_hbm, w_hbm, mask_hbm, sides_ref, normed_ref, spread_ref, column_mask_ref, pair_ref, gain_ref, bias_ref, w_ref, mask_ref, sems):
-    copies = [
-        pltpu.make_async_copy(source, target, sems.at[n])
-        for n, (source, target) in enumerate(
-            [(mask_hbm, mask_ref), (pair_hbm, pair_ref), (gain_hbm, gain_ref), (bias_hbm, bias_ref), (w_hbm, w_ref)]
-        )
-    ]
+def project(flat, gain, bias, w, row_count):
+    ours = w.shape[1] // 4
+    normed = layer_norm(flat.astype(jnp.float32), gain, bias, -1).astype(jnp.bfloat16)
+    arranged = arrange(normed.reshape(row_count, -1, normed.shape[1]))
+    projected = lax.dot_general(w, arranged, (((0,), (1,)), ((), ())), preferred_element_type=jnp.float32)
+    left = sigmoid(projected[:ours]) * projected[ours : 2 * ours]
+    right = sigmoid(projected[2 * ours : 3 * ours]) * projected[3 * ours :]
+    return normed, left, right
+
+
+def own_kernel(quads, cols, pair_hbm, gain_hbm, bias_hbm, w_hbm, mask_hbm, sides_ref, normed_ref, spread_ref, column_mask_ref, w_ref, gain_ref, bias_ref, pair_ref, all_w_ref, mask_ref, sems):
+    moves = [(mask_hbm, mask_ref), (pair_hbm, pair_ref), (gain_hbm, gain_ref), (bias_hbm, bias_ref), (w_hbm, all_w_ref)]
+    copies = [pltpu.make_async_copy(source, target, sems.at[n]) for n, (source, target) in enumerate(moves)]
     for copy in copies:
         copy.start()
-    devices = sides_ref.shape[0]
-    tokens, channels = normed_ref.shape
-    hidden = w_ref.shape[1] // 4
-    share = hidden // devices
+    my_quad, my_col = lax.axis_index("quad"), lax.axis_index("col")
+    row_count, _, channels = pair_ref.shape
+    tokens = normed_ref.shape[0]
+    hidden = all_w_ref.shape[1] // 4
+    ours = hidden // cols
     group, lanes = spread_ref.shape
     copies[0].wait()
     mask_row = mask_ref[...].astype(jnp.float32)
@@ -93,39 +100,49 @@
     start = lax.axis_index("half") * (lanes // group)
     token = lax.broadcasted_iota(jnp.int32, (mask_row.shape[1], lanes), 0)
     lane = lax.broadcasted_iota(jnp.int32, (mask_row.shape[1], lanes), 1)
-    row_count = pair_ref.shape[0]
     whole = row_count // 3
-    quads = lanes // group // row_count
     block, t, row = lane // LANES, lane // (quads * group) % whole, lane // group % quads
-    k = row * row_count + jnp.where(block < 2, 2 * t + block, 2 * whole + t)
+    k = (row ^ my_quad) * row_count + jnp.where(block < 2, 2 * t + block, 2 * whole + t)
     pick = jnp.where(k + start == token, 1.0, 0.0)
     kept = jnp.dot(mask_row.astype(jnp.bfloat16), pick.astype(jnp.bfloat16), preferred_element_type=jnp.float32)
     channel = lax.broadcasted_iota(jnp.int32, (group, lanes), 0)
     lane = lax.broadcasted_iota(jnp.int32, (group, lanes), 1)
     spread_ref[...] = jnp.where(lane % group == channel, kept, 0.0)
-    for copy in copies[1:4]:
+    for copy in copies[1:]:
         copy.wait()
-    flat = pair_ref[...].reshape(tokens, channels).astype(jnp.float32)
-    normed = layer_norm(flat, gain_ref[...], bias_ref[...], -1).astype(jnp.bfloat16)
+    parts = [all_w_ref[:, at : at + hidden] for at in range(0, 4 * hidden, hidden)]
+    w_ref[...] = jnp.concatenate([jnp.where(my_col == 0, part[:, :ours], part[:, ours:]) for part in parts], axis=1)
+    flat = pair_ref[...].reshape(tokens, channels)
+    normed, left, right = project(flat, gain_ref[...], bias_ref[...], w_ref[...], row_count)
     normed_ref[...] = normed
-    copies[4].wait()
-    arranged = arrange(normed.reshape(pair_ref.shape))
-    projected = lax.dot_general(w_ref[...], arranged, (((0,), (1,)), ((), ())), preferred_element_type=jnp.float32)
-    left = sigmoid(projected[:hidden]) * projected[hidden : 2 * hidden]
-    right = sigmoid(projected[2 * hidden : 3 * hidden]) * projected[3 * hidden :]
-    sides = jnp.concatenate([left.reshape(devices, share, tokens), right.reshape(devices, share, tokens)], axis=1)
+    sides = jnp.concatenate([left.reshape(quads, -1, tokens), right.reshape(quads, -1, tokens)], axis=1)
     sides_ref[...] = pack(sides).astype(jnp.bfloat16)
 
 
-def triangle_kernel(far_order, cols, row_count, col_count, share, got_ref, spread_ref, mask_ref, total_ref):
-    sources = got_ref.shape[0]
+def other_kernel(pair_ref, sides_ref, gain_ref, bias_ref, w_ref, *refs):
+    *piece_refs, others_ref = refs
+    my_quad, my_col = lax.axis_index("quad"), lax.axis_index("col")
+    quads = sides_ref.shape[0]
+    row_count, col_count, channels = pair_ref.shape
+    tokens = row_count * col_count
+    _, left, right = project(pair_ref[...].reshape(tokens, channels), gain_ref[...], bias_ref[...], w_ref[...], row_count)
+    sides = jnp.concatenate([left.reshape(quads, -1, tokens), right.reshape(quads, -1, tokens)], axis=1)
+    others_ref[...] = pack(sides).astype(jnp.bfloat16)
+    for step, piece_ref in enumerate(piece_refs):
+        piece_ref[my_col] = sides_ref[my_quad ^ step]
+        piece_ref[1 - my_col] = others_ref[my_quad ^ step]
+
+
+def triangle_kernel(far_order, steps, cols, row_count, col_count, share, *refs):
+    *got_refs, spread_ref, mask_ref, total_ref = refs
+    got_refs = {step: ref for step, ref in zip(steps, got_refs)}
     both = 2 * share
     group, lanes = spread_ref.shape
     length = mask_ref.shape[0]
-    rows, quads, parts = length // row_count, sources // cols, share // group
+    rows, quads, parts = length // row_count, len(steps), share // group
     whole, spare = row_count // 3, LANES - 2 * col_count
     rest = col_count - spare
-    blocks = [[got_ref[sources - 1 - (col * quads + row)].astype(jnp.float32) for row in range(quads)] for col in range(cols)]
+    blocks = [[got_refs[row][col].astype(jnp.float32) for row in range(quads)] for col in range(cols)]
 
     def turned(picks):
         return jnp.concatenate([blocks[col][row][at : at + group] for col, row, at in picks], axis=0).T
@@ -204,7 +221,6 @@
     devices = rows * cols
     near = devices // halves
     quads = rows // halves
-    near_order = [quad * cols + col for col in reversed(range(cols)) for quad in reversed(range(quads))]
     far_order = []
     for col in reversed(range(cols)):
         ahead = list(range(quads)) if col else list(range(1, quads)) + [0]
@@ -216,35 +232,52 @@
     length = rows * row_count
     depth = length // halves
     token_mask = token_mask.reshape(1, length)
+    near_order = [quad * cols + col for col in range(cols) for quad in range(quads)]
+    packed = 2 * share * tokens // LANES
+    cost = pl.CostEstimate(flops=2 * tokens * channels * 4 * hidden, bytes_accessed=16 * tokens * channels, transcendentals=0)
+    other_pair = lax.ppermute(pair, "col", [(i, (i + 1) % cols) for i in range(cols)])
     arguments = (pair, gain_in.reshape(1, channels), bias_in.reshape(1, channels), w_in, token_mask)
-    sides, normed, *masks = pl.pallas_call(
-        project_kernel,
+    sides, normed, spread, mask, *weights = pl.pallas_call(
+        functools.partial(own_kernel, quads, cols),
         out_shape=(
-            jax.ShapeDtypeStruct((near, 2 * share * tokens // LANES, LANES), jnp.bfloat16),
+            jax.ShapeDtypeStruct((quads, packed, LANES), jnp.bfloat16),
             jax.ShapeDtypeStruct((tokens, channels), jnp.bfloat16),
             jax.ShapeDtypeStruct((GROUP, GROUP * depth), jnp.float32),
             jax.ShapeDtypeStruct((length, 1), jnp.float32),
+            jax.ShapeDtypeStruct((channels, 4 * hidden // cols), jnp.bfloat16),
+            jax.ShapeDtypeStruct((1, channels), jnp.float32),
+            jax.ShapeDtypeStruct((1, channels), jnp.float32),
         ),
         in_specs=[HBM] * 5,
-        out_specs=(VMEM,) * 4,
+        out_specs=(VMEM,) * 7,
         scratch_shapes=[
             pltpu.VMEM(pair.shape, pair.dtype),
-            pltpu.VMEM((1, channels), jnp.float32),
-            pltpu.VMEM((1, channels), jnp.float32),
             pltpu.VMEM(w_in.shape, w_in.dtype),
             pltpu.VMEM((1, length), jnp.int32),
             pltpu.SemaphoreType.DMA((5,)),
         ],
         compiler_params=LIMIT,
+        cost_estimate=cost,
     )(*(pltpu.with_memory_space_constraint(x, pltpu.HBM) for x in arguments))
-    got = lax.all_to_all(sides, ("quad", "col"), split_axis=0, concat_axis=0, tiled=True, axis_index_groups=[near_order])
+    w_ours, gain_in, bias_in = weights
+    pieces = pl.pallas_call(
+        other_kernel,
+        out_shape=[jax.ShapeDtypeStruct((cols, packed, LANES), jnp.bfloat16)] * quads,
+        in_specs=[VMEM] * 5,
+        out_specs=[VMEM] * quads,
+        scratch_shapes=[pltpu.VMEM((quads, packed, LANES), jnp.bfloat16)],
+        compiler_params=LIMIT,
+        cost_estimate=cost,
+    )(other_pair, sides, gain_in, bias_in, w_ours)
+    steps = [3, 1, 2, 0]
+    got = [lax.ppermute(pieces[step], "quad", [(i, i ^ step) for i in range(quads)]) if step else pieces[0] for step in steps]
     total = pl.pallas_call(
-        functools.partial(triangle_kernel, far_order, cols, row_count, col_count, share),
+        functools.partial(triangle_kernel, far_order, steps, cols, row_count, col_count, share),
         out_shape=jax.ShapeDtypeStruct((devices, share * tokens // LANES, LANES), jnp.bfloat16),
-        in_specs=[VMEM] * 3,
+        in_specs=[VMEM] * (quads + 2),
         out_specs=VMEM,
         compiler_params=LIMIT,
-    )(got, *masks)
+    )(*got, spread, mask)
     gate, gain_out, bias_out = pl.pallas_call(
         gate_kernel,
         out_shape=(
@@ -309,7 +342,7 @@
         near, hidden, length = rows * cols // halves, args[-1].shape[0], args[1].shape[0]
         row_count, col_count, _ = args[0].shape
         spare = LANES - 2 * col_count
-        fits = hidden % (2 * GROUP * near) == 0 and cols == 2 and length <= LANES and row_count % 3 == 0
+        fits = hidden % (2 * GROUP * near) == 0 and cols == 2 and rows // halves == 4 and length <= LANES and row_count % 3 == 0
         fits = fits and 0 < spare < col_count and row_count // 3 * (col_count - spare) * 2 == LANES
         fits = fits and row_count // 3 * (rows // halves) * GROUP == LANES
         return per_device(rows, cols, halves, *args) if fits else plain_per_device(rows, cols, *args)

time: 28.4 us -> 27.3 us (0.961)
  blocking collectives: 10.6 us -> 0 us
  starting transfers between devices: 6.76 us -> 11.2 us
  waiting for transfers between devices: 5.56 us -> 9.77 us
  Pallas kernels: 4.44 us -> 5.35 us
    all_to_all x1 -> x0, blocking collectives: 10.6 us -> none  [per_device(): lax.all_to_all(sides, ('quad', 'col'), split_axis=0, concat_axis=0, tiled...]
    ppermute x0 -> x4, starting transfers between devices: none -> 4.69 us  [the longest x3 4.24 us: per_device(): lax.ppermute(pieces[step], 'quad', [(i, i ^ step) for i in range(quads)])]
    ppermute x0 -> x4, waiting for transfers between devices: none -> 4.22 us  [the longest x3 4.21 us: per_device(): lax.ppermute(pieces[step], 'quad', [(i, i ^ step) for i in range(quads)])]
    pallas_call x2 -> x3, Pallas kernels: 3.24 us -> 4.14 us  [the longest x1 1.97 us: per_device(): pl.pallas_call(functools.partial(own_kernel, quads, cols), out_shape=(jax...]
  transfers between devices with their start and end apart: 1 -> 5, of which waited for: 1 -> 4; matrix products, arithmetic and copies ran while one was open for 0% -> 0% of each run, Pallas kernels for 1% -> 8%
where the time goes in v18:
time: 27.3 us; the launch traced here: 27 us
  starting transfers between devices  11.2 us (41%)
  waiting for transfers between devices  9.77 us (36%)
  Pallas kernels  5.35 us (20%)
  local copies, waits for them, and re-layouts  0.65 us (2%)
    all_to_all x1, starting transfers between devices, per_device(): lax.all_to_all(total, ('half', 'quad', 'col'), split_axis=0, concat_axis=...  6.52 us
    all_to_all x1, waiting for transfers between devices, per_device(): lax.all_to_all(total, ('half', 'quad', 'col'), split_axis=0, concat_axis=...  5.56 us
    ppermute x3, starting transfers between devices, per_device(): lax.ppermute(pieces[step], 'quad', [(i, i ^ step) for i in range(quads)])  4.24 us
    ppermute x3, waiting for transfers between devices, per_device(): lax.ppermute(pieces[step], 'quad', [(i, i ^ step) for i in range(quads)])  4.21 us
    pallas_call x1, Pallas kernels, per_device(): pl.pallas_call(functools.partial(own_kernel, quads, cols), out_shape=(jax...  1.97 us
    pallas_call x1, Pallas kernels, per_device(): pl.pallas_call(functools.partial(triangle_kernel, far_order, steps, cols,...  1.62 us
    pallas_call x1, Pallas kernels, per_device(): pl.pallas_call(functools.partial(output_kernel, far_order, near_order), o...  1.02 us
    unnamed x8, local copies, waits for them, and re-layouts  0.65 us
  transfers between devices with their start and end apart: 5, of which 4 were waited for; matrix products, arithmetic and copies ran while one was open for 0% of the time, Pallas kernels for 8%

profile of v18, /device:TPU:0, one launch (start us, length us, event | category | flops | bytes accessed | tf_op | source)
XLA Modules:
  0.0 27.0 jit_solution(11540167200296926209)
XLA Ops:
  0.0 0.5 %collective-permute-start = (bf16[12,48,128]{2,1,0:T(8,128)(2,1)}, bf16[12,48,128]{2,1,0:T(8,128)(2,1)S(1)}, u32[]{:S(2)}, u32[]{:S(2)}) collective-permute-start(bf16[12,48,128]{2,1,0:T(8,128)(2,1)} %pair_hbm.1), channel_id=1, source_target_pairs={{0,1},{1,0},{2,3},{3,2},{4,5},{5,4},{6,7},{7,6},{8,9},{9,8},{10,11... | collective-permute-start | bytes 442376 | tf_op jit(solution)/shard_map/ppermute | solution.py:238
  0.5 2.0 %shard_map.91 = (bf16[4,144,128]{2,1,0:T(8,128)(2,1)S(1)}, bf16[576,128]{1,0:T(8,128)(2,1)S(1)}, f32[8,384]{1,0:T(8,128)S(1)}, f32[96,1]{1,0:T(8,128)S(1)}, bf16...) custom-call(bf16[12,48,128]{2,1,0:T(8,128)(2,1)} %pair_hbm.1, f32[1,128]{1,0:T(1,128)} %bitcast.7, ...), custom_call_target="tpu_custom_call" | custom-call | flops 75497472 | bytes 1179648 | tf_op jit(solution)/shard_map/pallas_call | solution.py:240
  2.4 0.0 collective-permute-done.pair_ref
  2.4 0.6 %shard_map.92 = (bf16[2,144,128]{2,1,0:T(8,128)(2,1)S(1)}, bf16[2,144,128]{2,1,0:T(8,128)(2,1)S(1)}, bf16[2,144,128]{2,1,0:T(8,128)(2,1)S(1)}, bf16[2,144,128]{2,1,0:T(8,128)(2,1)S(1)}) custom-call(bf16[12,48,128]{2,1,0:T(8,128)(2,1)S(1)} %collective-permute-done.pair_ref, bf16[4,144,128]{2,1,0:T(8,128)(2,1)S(1)} %get-tuple-element.19.sides_ref, ...), custom_call_target="tpu_custom_call" | custom-call | flops 75497472 | bytes 1179648 | tf_op jit(solution)/shard_map/pallas_call | solution.py:263
  3.0 3.6 %collective-permute-start.1 = (bf16[2,144,128]{2,1,0:T(8,128)(2,1)S(1)}, bf16[2,144,128]{2,1,0:T(8,128)(2,1)S(1)}, u32[]{:S(2)}, u32[]{:S(2)}) collective-permute-start(bf16[2,144,128]{2,1,0:T(8,128)(2,1)S(1)} %get-tuple-element.23), channel_id=1, source_target_pairs={{0,6},{2,4},{4,2},{6,0},{1,7},{3,5},{5,3},{7,1},{8,14},{10,12},{12... | collective-permute-start | bytes 221192 | tf_op jit(solution)/shard_map/ppermute | solution.py:273
  6.6 0.5 %collective-permute-start.2 = (bf16[2,144,128]{2,1,0:T(8,128)(2,1)S(1)}, bf16[2,144,128]{2,1,0:T(8,128)(2,1)S(1)}, u32[]{:S(2)}, u32[]{:S(2)}) collective-permute-start(bf16[2,144,128]{2,1,0:T(8,128)(2,1)S(1)} %get-tuple-element.24), channel_id=1, source_target_pairs={{0,2},{2,0},{4,6},{6,4},{1,3},{3,1},{5,7},{7,5},{8,10},{10,8},{12,... | collective-permute-start | bytes 221192 | tf_op jit(solution)/shard_map/ppermute | solution.py:273
  7.1 0.1 collective-permute-start.3
  7.2 2.3 %collective-permute-done.1.refs_0_ = bf16[2,144,128]{2,1,0:T(8,128)(2,1)S(1)} collective-permute-done((bf16[2,144,128]{2,1,0:T(8,128)(2,1)S(1)}, bf16[2,144,128]{2,1,0:T(8,128)(2,1)S(1)}, u32[]{:S(2)}, u32[]{:S(2)}) %collective-permute-start.1) | collective-permute-done | bytes 73760 | tf_op jit(solution)/shard_map/ppermute | solution.py:273
  9.6 1.6 %collective-permute-done.2.refs_1_ = bf16[2,144,128]{2,1,0:T(8,128)(2,1)S(1)} collective-permute-done((bf16[2,144,128]{2,1,0:T(8,128)(2,1)S(1)}, bf16[2,144,128]{2,1,0:T(8,128)(2,1)S(1)}, u32[]{:S(2)}, u32[]{:S(2)}) %collective-permute-start.2) | collective-permute-done | bytes 73760 | tf_op jit(solution)/shard_map/ppermute | solution.py:273
  11.1 0.3 %collective-permute-done.3.refs_2_ = bf16[2,144,128]{2,1,0:T(8,128)(2,1)S(1)} collective-permute-done((bf16[2,144,128]{2,1,0:T(8,128)(2,1)S(1)}, bf16[2,144,128]{2,1,0:T(8,128)(2,1)S(1)}, u32[]{:S(2)}, u32[]{:S(2)}) %collective-permute-start.3) | collective-permute-done | bytes 73760 | tf_op jit(solution)/shard_map/ppermute | solution.py:273
  11.5 1.6 %shard_map.93 = bf16[16,72,128]{2,1,0:T(8,128)(2,1)} custom-call(bf16[2,144,128]{2,1,0:T(8,128)(2,1)S(1)} %collective-permute-done.1.refs_0_, bf16[2,144,128]{2,1,0:T(8,128)(2,1)S(1)} %collective-permute-done.2.refs_1_, bf16[2,144,128]{2,1,0:T(8,128)(2,1)S(1)} %collective-permute-done.3.refs_2_, bf16[2,144,128]{2,1,0:T(8,128)(2,1)S(1)} %get-tuple-element.26.refs_3_, ...), custom_call_target="tpu_custom_call" | custom-call | tf_op jit(solution)/shard_map/pallas_call | solution.py:274
  13.1 0.0 copy-start.1
  13.1 6.5 %all-to-all-start = ((bf16[16,72,128]{2,1,0:T(8,128)(2,1)}), bf16[16,72,128]{2,1,0:T(8,128)(2,1)S(1)}, u32[]{:S(2)}, u32[]{:S(2)}) async-start(bf16[16,72,128]{2,1,0:T(8,128)(2,1)} %shard_map.93), calls=%async_computation | async-start | bytes 589824 | tf_op jit(solution)/shard_map/all_to_all | solution.py:293
  19.6 0.0 copy-start.2
  19.6 0.0 copy-start.3
  19.6 0.0 copy-done.1
  19.6 0.6 %copy-done.2 = f32[128]{0:T(128)S(1)} copy-done((f32[128]{0:T(128)S(1)}, f32[128]{0:T(128)}, u32[]{:S(2)}) %copy-start.2) | copy-done | bytes 536
  20.3 0.0 copy-done.3
  20.3 0.0 copy-start
  20.3 0.2 shard_map.94
  20.5 5.6 %all-to-all-done.total_ref = bf16[16,72,128]{2,1,0:T(8,128)(2,1)S(1)} async-done(((bf16[16,72,128]{2,1,0:T(8,128)(2,1)}), bf16[16,72,128]{2,1,0:T(8,128)(2,1)S(1)}, u32[]{:S(2)}, u32[]{:S(2)}) %all-to-all-start) | async-done | bytes 294944 | tf_op jit(solution)/shard_map/all_to_all | solution.py:293
  26.0 0.0 copy-done
  26.0 1.0 %shard_map.95 = bf16[12,48,128]{2,1,0:T(8,128)(2,1)} custom-call(bf16[16,72,128]{2,1,0:T(8,128)(2,1)S(1)} %all-to-all-done.total_ref, f32[576,128]{1,0:T(8,128)S(1)} %get-tuple-element.30.gate_ref, f32[128,1]{1,0:T(8,128)S(1)} %get-tuple-element.31.gain_ref, f32[128,1]{1,0:T(8,128)S(1)} %get-tuple-element.32.bias_ref, bf16[128,128]{1,0:T(8,128)(2,1)S(1)} %copy-done), custom_call_target="tpu_custom_call" | custom-call | tf_op jit(solution)/shard_map/pallas_call | solution.py:294
Async XLA Ops:
  0.0 2.4 %collective-permute-start = (bf16[12,48,128]{2,1,0:T(8,128)(2,1)}, bf16[12,48,128]{2,1,0:T(8,128)(2,1)S(1)}, u32[]{:S(2)}, u32[]{:S(2)}) collective-permute-start(bf16[12,48,128]{2,1,0:T(8,128)(2,1)} %pair_hbm.1), channel_id=1, source_target_pairs={{0,1},{1,0},{2,3},{3,2},{4,5},{5,4},{6,7},{7,6},{8,9},{9,8},{10,11... | collective-permute-start | bytes 442376 | tf_op jit(solution)/shard_map/ppermute | solution.py:238
  3.0 6.5 %collective-permute-start.1 = (bf16[2,144,128]{2,1,0:T(8,128)(2,1)S(1)}, bf16[2,144,128]{2,1,0:T(8,128)(2,1)S(1)}, u32[]{:S(2)}, u32[]{:S(2)}) collective-permute-start(bf16[2,144,128]{2,1,0:T(8,128)(2,1)S(1)} %get-tuple-element.23), channel_id=1, source_target_pairs={{0,6},{2,4},{4,2},{6,0},{1,7},{3,5},{5,3},{7,1},{8,14},{10,12},{12... | collective-permute-start | bytes 221192 | tf_op jit(solution)/shard_map/ppermute | solution.py:273
  6.6 4.5 %collective-permute-start.2 = (bf16[2,144,128]{2,1,0:T(8,128)(2,1)S(1)}, bf16[2,144,128]{2,1,0:T(8,128)(2,1)S(1)}, u32[]{:S(2)}, u32[]{:S(2)}) collective-permute-start(bf16[2,144,128]{2,1,0:T(8,128)(2,1)S(1)} %get-tuple-element.24), channel_id=1, source_target_pairs={{0,2},{2,0},{4,6},{6,4},{1,3},{3,1},{5,7},{7,5},{8,10},{10,8},{12,... | collective-permute-start | bytes 221192 | tf_op jit(solution)/shard_map/ppermute | solution.py:273
  7.1 4.4 %collective-permute-start.3 = (bf16[2,144,128]{2,1,0:T(8,128)(2,1)S(1)}, bf16[2,144,128]{2,1,0:T(8,128)(2,1)S(1)}, u32[]{:S(2)}, u32[]{:S(2)}) collective-permute-start(bf16[2,144,128]{2,1,0:T(8,128)(2,1)S(1)} %get-tuple-element.25), channel_id=1, source_target_pairs={{0,4},{2,6},{4,0},{6,2},{1,5},{3,7},{5,1},{7,3},{8,12},{10,14},{12... | collective-permute-start | bytes 221192 | tf_op jit(solution)/shard_map/ppermute | solution.py:273
  13.1 6.5 %copy-start.1 = (bf16[128,128]{1,0:T(8,128)(2,1)S(1)}, bf16[128,128]{1,0:T(8,128)(2,1)}, u32[]{:S(2)}) copy-start(bf16[128,128]{1,0:T(8,128)(2,1)} %w_ref.2) | copy-start | bytes 98308
  13.1 12.9 %all-to-all-start = ((bf16[16,72,128]{2,1,0:T(8,128)(2,1)}), bf16[16,72,128]{2,1,0:T(8,128)(2,1)S(1)}, u32[]{:S(2)}, u32[]{:S(2)}) async-start(bf16[16,72,128]{2,1,0:T(8,128)(2,1)} %shard_map.93), calls=%async_computation | async-start | bytes 589824 | tf_op jit(solution)/shard_map/all_to_all | solution.py:293
  19.6 0.7 %copy-start.2 = (f32[128]{0:T(128)S(1)}, f32[128]{0:T(128)}, u32[]{:S(2)}) copy-start(f32[128]{0:T(128)} %param.15) | copy-start | bytes 1540
  19.6 0.7 %copy-start.3 = (f32[128]{0:T(128)S(1)}, f32[128]{0:T(128)}, u32[]{:S(2)}) copy-start(f32[128]{0:T(128)} %param.16) | copy-start | bytes 1540
  20.3 5.8 %copy-start = (bf16[128,128]{1,0:T(8,128)(2,1)S(1)}, bf16[128,128]{1,0:T(8,128)(2,1)}, u32[]{:S(2)}) copy-start(bf16[128,128]{1,0:T(8,128)(2,1)} %w_ref.3) | copy-start | bytes 98308

commit v19 on v18

--- a/solution.py
+++ b/solution.py
@@ -73,14 +73,18 @@
     return jnp.concatenate(rows, axis=0)
 
 
-def project(flat, gain, bias, w, row_count):
+def normalise(flat, gain, bias):
+    return layer_norm(flat.astype(jnp.float32), gain, bias, -1).astype(jnp.bfloat16)
+
+
+def project(normed, w, shape, quads):
     ours = w.shape[1] // 4
-    normed = layer_norm(flat.astype(jnp.float32), gain, bias, -1).astype(jnp.bfloat16)
-    arranged = arrange(normed.reshape(row_count, -1, normed.shape[1]))
-    projected = lax.dot_general(w, arranged, (((0,), (1,)), ((), ())), preferred_element_type=jnp.float32)
+    tokens = normed.shape[0]
+    projected = lax.dot_general(w, arrange(normed.reshape(shape)), (((0,), (1,)), ((), ())), preferred_element_type=jnp.float32)
     left = sigmoid(projected[:ours]) * projected[ours : 2 * ours]
     right = sigmoid(projected[2 * ours : 3 * ours]) * projected[3 * ours :]
-    return normed, left, right
+    sides = jnp.concatenate([left.reshape(quads, -1, tokens), right.reshape(quads, -1, tokens)], axis=1)
+    return pack(sides).astype(jnp.bfloat16)
 
 
 def own_kernel(quads, cols, pair_hbm, gain_hbm, bias_hbm, w_hbm, mask_hbm, sides_ref, normed_ref, spread_ref, column_mask_ref, w_ref, gain_ref, bias_ref, pair_ref, all_w_ref, mask_ref, sems):
@@ -108,26 +112,23 @@
     channel = lax.broadcasted_iota(jnp.int32, (group, lanes), 0)
     lane = lax.broadcasted_iota(jnp.int32, (group, lanes), 1)
     spread_ref[...] = jnp.where(lane % group == channel, kept, 0.0)
-    for copy in copies[1:]:
+    for copy in copies[1:4]:
         copy.wait()
+    normed = normalise(pair_ref[...].reshape(tokens, channels), gain_ref[...], bias_ref[...])
+    normed_ref[...] = normed
+    copies[4].wait()
     parts = [all_w_ref[:, at : at + hidden] for at in range(0, 4 * hidden, hidden)]
-    w_ref[...] = jnp.concatenate([jnp.where(my_col == 0, part[:, :ours], part[:, ours:]) for part in parts], axis=1)
-    flat = pair_ref[...].reshape(tokens, channels)
-    normed, left, right = project(flat, gain_ref[...], bias_ref[...], w_ref[...], row_count)
-    normed_ref[...] = normed
-    sides = jnp.concatenate([left.reshape(quads, -1, tokens), right.reshape(quads, -1, tokens)], axis=1)
-    sides_ref[...] = pack(sides).astype(jnp.bfloat16)
+    w = jnp.concatenate([jnp.where(my_col == 0, part[:, :ours], part[:, ours:]) for part in parts], axis=1)
+    w_ref[...] = w
+    sides_ref[...] = project(normed, w, pair_ref.shape, quads)
 
 
 def other_kernel(pair_ref, sides_ref, gain_ref, bias_ref, w_ref, *refs):
     *piece_refs, others_ref = refs
     my_quad, my_col = lax.axis_index("quad"), lax.axis_index("col")
     quads = sides_ref.shape[0]
-    row_count, col_count, channels = pair_ref.shape
-    tokens = row_count * col_count
-    _, left, right = project(pair_ref[...].reshape(tokens, channels), gain_ref[...], bias_ref[...], w_ref[...], row_count)
-    sides = jnp.concatenate([left.reshape(quads, -1, tokens), right.reshape(quads, -1, tokens)], axis=1)
-    others_ref[...] = pack(sides).astype(jnp.bfloat16)
+    normed = normalise(pair_ref[...].reshape(-1, pair_ref.shape[2]), gain_ref[...], bias_ref[...])
+    others_ref[...] = project(normed, w_ref[...], pair_ref.shape, quads)
     for step, piece_ref in enumerate(piece_refs):
         piece_ref[my_col] = sides_ref[my_quad ^ step]
         piece_ref[1 - my_col] = others_ref[my_quad ^ step]
@@ -269,7 +270,7 @@
         compiler_params=LIMIT,
         cost_estimate=cost,
     )(other_pair, sides, gain_in, bias_in, w_ours)
-    steps = [3, 1, 2, 0]
+    steps = [1, 2, 3, 0]
     got = [lax.ppermute(pieces[step], "quad", [(i, i ^ step) for i in range(quads)]) if step else pieces[0] for step in steps]
     total = pl.pallas_call(
         functools.partial(triangle_kernel, far_order, steps, cols, row_count, col_count, share),

time: 27.3 us -> 27.1 us (level)
  waiting for transfers between devices: 9.77 us -> 11 us
  starting transfers between devices: 11.2 us -> 10 us
    all_to_all x1, starting transfers between devices: 6.52 us -> 5.39 us  [per_device(): lax.all_to_all(total, ('half', 'quad', 'col'), split_axis=0, concat_axis=...]
    ppermute x3, waiting for transfers between devices: 4.21 us -> 5.25 us  [per_device(): lax.ppermute(pieces[step], 'quad', [(i, i ^ step) for i in range(quads)])]
  transfers between devices with their start and end apart: 5 -> 5, of which waited for: 4 -> 4; matrix products, arithmetic and copies ran while one was open for 0% -> 0% of each run, Pallas kernels for 8% -> 7%
where the time goes in v19:
time: 27.1 us; the launch traced here: 26.8 us
  waiting for transfers between devices  11 us (41%)
  starting transfers between devices  10 us (37%)
  Pallas kernels  5.09 us (19%)
  local copies, waits for them, and re-layouts  0.65 us (2%)
    all_to_all x1, waiting for transfers between devices, per_device(): lax.all_to_all(total, ('half', 'quad', 'col'), split_axis=0, concat_axis=...  5.71 us
    all_to_all x1, starting transfers between devices, per_device(): lax.all_to_all(total, ('half', 'quad', 'col'), split_axis=0, concat_axis=...  5.39 us
    ppermute x3, waiting for transfers between devices, per_device(): lax.ppermute(pieces[step], 'quad', [(i, i ^ step) for i in range(quads)])  5.25 us
    ppermute x3, starting transfers between devices, per_device(): lax.ppermute(pieces[step], 'quad', [(i, i ^ step) for i in range(quads)])  4.16 us
    pallas_call x1, Pallas kernels, per_device(): pl.pallas_call(functools.partial(own_kernel, quads, cols), out_shape=(jax...  1.7 us
    pallas_call x1, Pallas kernels, per_device(): pl.pallas_call(functools.partial(triangle_kernel, far_order, steps, cols,...  1.62 us
    pallas_call x1, Pallas kernels, per_device(): pl.pallas_call(functools.partial(output_kernel, far_order, near_order), o...  1.02 us
    unnamed x8, local copies, waits for them, and re-layouts  0.65 us
  transfers between devices with their start and end apart: 5, of which 4 were waited for; matrix products, arithmetic and copies ran while one was open for 0% of the time, Pallas kernels for 7%

profile of v19, /device:TPU:0, one launch (start us, length us, event | category | flops | bytes accessed | tf_op | source)
XLA Modules:
  0.0 26.8 jit_solution(8429853960974842438)
XLA Ops:
  0.0 0.5 %collective-permute-start = (bf16[12,48,128]{2,1,0:T(8,128)(2,1)}, bf16[12,48,128]{2,1,0:T(8,128)(2,1)S(1)}, u32[]{:S(2)}, u32[]{:S(2)}) collective-permute-start(bf16[12,48,128]{2,1,0:T(8,128)(2,1)} %pair_hbm.1), channel_id=1, source_target_pairs={{0,1},{1,0},{2,3},{3,2},{4,5},{5,4},{6,7},{7,6},{8,9},{9,8},{10,11... | collective-permute-start | bytes 442376 | tf_op jit(solution)/shard_map/ppermute | solution.py:239
  0.5 1.7 %shard_map.91 = (bf16[4,144,128]{2,1,0:T(8,128)(2,1)S(1)}, bf16[576,128]{1,0:T(8,128)(2,1)S(1)}, f32[8,384]{1,0:T(8,128)S(1)}, f32[96,1]{1,0:T(8,128)S(1)}, bf16...) custom-call(bf16[12,48,128]{2,1,0:T(8,128)(2,1)} %pair_hbm.1, f32[1,128]{1,0:T(1,128)} %bitcast.7, ...), custom_call_target="tpu_custom_call" | custom-call | flops 75497472 | bytes 1179648 | tf_op jit(solution)/shard_map/pallas_call | solution.py:241
  2.2 0.0 collective-permute-done.pair_ref
  2.2 0.6 %shard_map.92 = (bf16[2,144,128]{2,1,0:T(8,128)(2,1)S(1)}, bf16[2,144,128]{2,1,0:T(8,128)(2,1)S(1)}, bf16[2,144,128]{2,1,0:T(8,128)(2,1)S(1)}, bf16[2,144,128]{2,1,0:T(8,128)(2,1)S(1)}) custom-call(bf16[12,48,128]{2,1,0:T(8,128)(2,1)S(1)} %collective-permute-done.pair_ref, bf16[4,144,128]{2,1,0:T(8,128)(2,1)S(1)} %get-tuple-element.19.sides_ref, ...), custom_call_target="tpu_custom_call" | custom-call | flops 75497472 | bytes 1179648 | tf_op jit(solution)/shard_map/pallas_call | solution.py:264
  2.7 2.6 %collective-permute-start.1 = (bf16[2,144,128]{2,1,0:T(8,128)(2,1)S(1)}, bf16[2,144,128]{2,1,0:T(8,128)(2,1)S(1)}, u32[]{:S(2)}, u32[]{:S(2)}) collective-permute-start(bf16[2,144,128]{2,1,0:T(8,128)(2,1)S(1)} %get-tuple-element.23), channel_id=1, source_target_pairs={{0,2},{2,0},{4,6},{6,4},{1,3},{3,1},{5,7},{7,5},{8,10},{10,8},{12,... | collective-permute-start | bytes 221192 | tf_op jit(solution)/shard_map/ppermute | solution.py:274
  5.3 1.6 %collective-permute-start.2 = (bf16[2,144,128]{2,1,0:T(8,128)(2,1)S(1)}, bf16[2,144,128]{2,1,0:T(8,128)(2,1)S(1)}, u32[]{:S(2)}, u32[]{:S(2)}) collective-permute-start(bf16[2,144,128]{2,1,0:T(8,128)(2,1)S(1)} %get-tuple-element.24), channel_id=1, source_target_pairs={{0,4},{2,6},{4,0},{6,2},{1,5},{3,7},{5,1},{7,3},{8,12},{10,14},{12... | collective-permute-start | bytes 221192 | tf_op jit(solution)/shard_map/ppermute | solution.py:274
  6.9 0.0 collective-permute-start.3
  6.9 1.4 %collective-permute-done.1.refs_0_ = bf16[2,144,128]{2,1,0:T(8,128)(2,1)S(1)} collective-permute-done((bf16[2,144,128]{2,1,0:T(8,128)(2,1)S(1)}, bf16[2,144,128]{2,1,0:T(8,128)(2,1)S(1)}, u32[]{:S(2)}, u32[]{:S(2)}) %collective-permute-start.1) | collective-permute-done | bytes 73760 | tf_op jit(solution)/shard_map/ppermute | solution.py:274
  8.3 1.9 %collective-permute-done.2.refs_1_ = bf16[2,144,128]{2,1,0:T(8,128)(2,1)S(1)} collective-permute-done((bf16[2,144,128]{2,1,0:T(8,128)(2,1)S(1)}, bf16[2,144,128]{2,1,0:T(8,128)(2,1)S(1)}, u32[]{:S(2)}, u32[]{:S(2)}) %collective-permute-start.2) | collective-permute-done | bytes 73760 | tf_op jit(solution)/shard_map/ppermute | solution.py:274
  10.1 2.0 %collective-permute-done.3.refs_2_ = bf16[2,144,128]{2,1,0:T(8,128)(2,1)S(1)} collective-permute-done((bf16[2,144,128]{2,1,0:T(8,128)(2,1)S(1)}, bf16[2,144,128]{2,1,0:T(8,128)(2,1)S(1)}, u32[]{:S(2)}, u32[]{:S(2)}) %collective-permute-start.3) | collective-permute-done | bytes 73760 | tf_op jit(solution)/shard_map/ppermute | solution.py:274
  12.2 1.6 %shard_map.93 = bf16[16,72,128]{2,1,0:T(8,128)(2,1)} custom-call(bf16[2,144,128]{2,1,0:T(8,128)(2,1)S(1)} %collective-permute-done.1.refs_0_, bf16[2,144,128]{2,1,0:T(8,128)(2,1)S(1)} %collective-permute-done.2.refs_1_, bf16[2,144,128]{2,1,0:T(8,128)(2,1)S(1)} %collective-permute-done.3.refs_2_, bf16[2,144,128]{2,1,0:T(8,128)(2,1)S(1)} %get-tuple-element.26.refs_3_, ...), custom_call_target="tpu_custom_call" | custom-call | tf_op jit(solution)/shard_map/pallas_call | solution.py:275
  13.8 0.0 copy-start.1
  13.8 5.4 %all-to-all-start = ((bf16[16,72,128]{2,1,0:T(8,128)(2,1)}), bf16[16,72,128]{2,1,0:T(8,128)(2,1)S(1)}, u32[]{:S(2)}, u32[]{:S(2)}) async-start(bf16[16,72,128]{2,1,0:T(8,128)(2,1)} %shard_map.93), calls=%async_computation | async-start | bytes 589824 | tf_op jit(solution)/shard_map/all_to_all | solution.py:294
  19.2 0.0 copy-start.2
  19.2 0.0 copy-start.3
  19.2 0.0 copy-done.1
  19.2 0.6 %copy-done.2 = f32[128]{0:T(128)S(1)} copy-done((f32[128]{0:T(128)S(1)}, f32[128]{0:T(128)}, u32[]{:S(2)}) %copy-start.2) | copy-done | bytes 536
  19.8 0.0 copy-done.3
  19.8 0.0 copy-start
  19.8 0.2 shard_map.94
  20.0 5.7 %all-to-all-done.total_ref = bf16[16,72,128]{2,1,0:T(8,128)(2,1)S(1)} async-done(((bf16[16,72,128]{2,1,0:T(8,128)(2,1)}), bf16[16,72,128]{2,1,0:T(8,128)(2,1)S(1)}, u32[]{:S(2)}, u32[]{:S(2)}) %all-to-all-start) | async-done | bytes 294944 | tf_op jit(solution)/shard_map/all_to_all | solution.py:294
  25.8 0.0 copy-done
  25.8 1.0 %shard_map.95 = bf16[12,48,128]{2,1,0:T(8,128)(2,1)} custom-call(bf16[16,72,128]{2,1,0:T(8,128)(2,1)S(1)} %all-to-all-done.total_ref, f32[576,128]{1,0:T(8,128)S(1)} %get-tuple-element.30.gate_ref, f32[128,1]{1,0:T(8,128)S(1)} %get-tuple-element.31.gain_ref, f32[128,1]{1,0:T(8,128)S(1)} %get-tuple-element.32.bias_ref, bf16[128,128]{1,0:T(8,128)(2,1)S(1)} %copy-done), custom_call_target="tpu_custom_call" | custom-call | tf_op jit(solution)/shard_map/pallas_call | solution.py:295
Async XLA Ops:
  0.0 2.2 %collective-permute-start = (bf16[12,48,128]{2,1,0:T(8,128)(2,1)}, bf16[12,48,128]{2,1,0:T(8,128)(2,1)S(1)}, u32[]{:S(2)}, u32[]{:S(2)}) collective-permute-start(bf16[12,48,128]{2,1,0:T(8,128)(2,1)} %pair_hbm.1), channel_id=1, source_target_pairs={{0,1},{1,0},{2,3},{3,2},{4,5},{5,4},{6,7},{7,6},{8,9},{9,8},{10,11... | collective-permute-start | bytes 442376 | tf_op jit(solution)/shard_map/ppermute | solution.py:239
  2.7 5.5 %collective-permute-start.1 = (bf16[2,144,128]{2,1,0:T(8,128)(2,1)S(1)}, bf16[2,144,128]{2,1,0:T(8,128)(2,1)S(1)}, u32[]{:S(2)}, u32[]{:S(2)}) collective-permute-start(bf16[2,144,128]{2,1,0:T(8,128)(2,1)S(1)} %get-tuple-element.23), channel_id=1, source_target_pairs={{0,2},{2,0},{4,6},{6,4},{1,3},{3,1},{5,7},{7,5},{8,10},{10,8},{12,... | collective-permute-start | bytes 221192 | tf_op jit(solution)/shard_map/ppermute | solution.py:274
  5.3 4.8 %collective-permute-start.2 = (bf16[2,144,128]{2,1,0:T(8,128)(2,1)S(1)}, bf16[2,144,128]{2,1,0:T(8,128)(2,1)S(1)}, u32[]{:S(2)}, u32[]{:S(2)}) collective-permute-start(bf16[2,144,128]{2,1,0:T(8,128)(2,1)S(1)} %get-tuple-element.24), channel_id=1, source_target_pairs={{0,4},{2,6},{4,0},{6,2},{1,5},{3,7},{5,1},{7,3},{8,12},{10,14},{12... | collective-permute-start | bytes 221192 | tf_op jit(solution)/shard_map/ppermute | solution.py:274
  6.9 5.3 %collective-permute-start.3 = (bf16[2,144,128]{2,1,0:T(8,128)(2,1)S(1)}, bf16[2,144,128]{2,1,0:T(8,128)(2,1)S(1)}, u32[]{:S(2)}, u32[]{:S(2)}) collective-permute-start(bf16[2,144,128]{2,1,0:T(8,128)(2,1)S(1)} %get-tuple-element.25), channel_id=1, source_target_pairs={{0,6},{2,4},{4,2},{6,0},{1,7},{3,5},{5,3},{7,1},{8,14},{10,12},{12... | collective-permute-start | bytes 221192 | tf_op jit(solution)/shard_map/ppermute | solution.py:274
  13.8 5.4 %copy-start.1 = (bf16[128,128]{1,0:T(8,128)(2,1)S(1)}, bf16[128,128]{1,0:T(8,128)(2,1)}, u32[]{:S(2)}) copy-start(bf16[128,128]{1,0:T(8,128)(2,1)} %w_ref.2) | copy-start | bytes 98308
  13.8 12.0 %all-to-all-start = ((bf16[16,72,128]{2,1,0:T(8,128)(2,1)}), bf16[16,72,128]{2,1,0:T(8,128)(2,1)S(1)}, u32[]{:S(2)}, u32[]{:S(2)}) async-start(bf16[16,72,128]{2,1,0:T(8,128)(2,1)} %shard_map.93), calls=%async_computation | async-start | bytes 589824 | tf_op jit(solution)/shard_map/all_to_all | solution.py:294
  19.2 0.7 %copy-start.2 = (f32[128]{0:T(128)S(1)}, f32[128]{0:T(128)}, u32[]{:S(2)}) copy-start(f32[128]{0:T(128)} %param.15) | copy-start | bytes 1540
  19.2 0.7 %copy-start.3 = (f32[128]{0:T(128)S(1)}, f32[128]{0:T(128)}, u32[]{:S(2)}) copy-start(f32[128]{0:T(128)} %param.16) | copy-start | bytes 1540
  19.8 5.9 %copy-start = (bf16[128,128]{1,0:T(8,128)(2,1)S(1)}, bf16[128,128]{1,0:T(8,128)(2,1)}, u32[]{:S(2)}) copy-start(bf16[128,128]{1,0:T(8,128)(2,1)} %w_ref.3) | copy-start | bytes 98308

commit v20 on v19

--- a/solution.py
+++ b/solution.py
@@ -270,7 +270,7 @@
         compiler_params=LIMIT,
         cost_estimate=cost,
     )(other_pair, sides, gain_in, bias_in, w_ours)
-    steps = [1, 2, 3, 0]
+    steps = [3, 1, 2, 0]
     got = [lax.ppermute(pieces[step], "quad", [(i, i ^ step) for i in range(quads)]) if step else pieces[0] for step in steps]
     total = pl.pallas_call(
         functools.partial(triangle_kernel, far_order, steps, cols, row_count, col_count, share),

time: 27.1 us -> 27.1 us (level)
  waiting for transfers between devices: 11 us -> 9.77 us
  starting transfers between devices: 10 us -> 11.2 us
    all_to_all x1, starting transfers between devices: 5.39 us -> 6.51 us  [per_device(): lax.all_to_all(total, ('half', 'quad', 'col'), split_axis=0, concat_axis=...]
    ppermute x3, waiting for transfers between devices: 5.25 us -> 4.22 us  [per_device(): lax.ppermute(pieces[step], 'quad', [(i, i ^ step) for i in range(quads)])]
where the time goes in v20:
time: 27.1 us; the launch traced here: 26.8 us
  starting transfers between devices  11.2 us (41%)
  waiting for transfers between devices  9.77 us (36%)
  Pallas kernels  5.09 us (19%)
  local copies, waits for them, and re-layouts  0.65 us (2%)
    all_to_all x1, starting transfers between devices, per_device(): lax.all_to_all(total, ('half', 'quad', 'col'), split_axis=0, concat_axis=...  6.51 us
    all_to_all x1, waiting for transfers between devices, per_device(): lax.all_to_all(total, ('half', 'quad', 'col'), split_axis=0, concat_axis=...  5.55 us
    ppermute x3, starting transfers between devices, per_device(): lax.ppermute(pieces[step], 'quad', [(i, i ^ step) for i in range(quads)])  4.24 us
    ppermute x3, waiting for transfers between devices, per_device(): lax.ppermute(pieces[step], 'quad', [(i, i ^ step) for i in range(quads)])  4.22 us
    pallas_call x1, Pallas kernels, per_device(): pl.pallas_call(functools.partial(own_kernel, quads, cols), out_shape=(jax...  1.7 us
    pallas_call x1, Pallas kernels, per_device(): pl.pallas_call(functools.partial(triangle_kernel, far_order, steps, cols,...  1.62 us
    pallas_call x1, Pallas kernels, per_device(): pl.pallas_call(functools.partial(output_kernel, far_order, near_order), o...  1.02 us
    unnamed x8, local copies, waits for them, and re-layouts  0.65 us
  transfers between devices with their start and end apart: 5, of which 4 were waited for; matrix products, arithmetic and copies ran while one was open for 0% of the time, Pallas kernels for 7%

profile of v20, /device:TPU:0, one launch (start us, length us, event | category | flops | bytes accessed | tf_op | source)
XLA Modules:
  0.0 26.8 jit_solution(1271092417197663417)
XLA Ops:
  0.0 0.5 %collective-permute-start = (bf16[12,48,128]{2,1,0:T(8,128)(2,1)}, bf16[12,48,128]{2,1,0:T(8,128)(2,1)S(1)}, u32[]{:S(2)}, u32[]{:S(2)}) collective-permute-start(bf16[12,48,128]{2,1,0:T(8,128)(2,1)} %pair_hbm.1), channel_id=1, source_target_pairs={{0,1},{1,0},{2,3},{3,2},{4,5},{5,4},{6,7},{7,6},{8,9},{9,8},{10,11... | collective-permute-start | bytes 442376 | tf_op jit(solution)/shard_map/ppermute | solution.py:239
  0.5 1.7 %shard_map.91 = (bf16[4,144,128]{2,1,0:T(8,128)(2,1)S(1)}, bf16[576,128]{1,0:T(8,128)(2,1)S(1)}, f32[8,384]{1,0:T(8,128)S(1)}, f32[96,1]{1,0:T(8,128)S(1)}, bf16...) custom-call(bf16[12,48,128]{2,1,0:T(8,128)(2,1)} %pair_hbm.1, f32[1,128]{1,0:T(1,128)} %bitcast.7, ...), custom_call_target="tpu_custom_call" | custom-call | flops 75497472 | bytes 1179648 | tf_op jit(solution)/shard_map/pallas_call | solution.py:241
  2.2 0.0 collective-permute-done.pair_ref
  2.2 0.6 %shard_map.92 = (bf16[2,144,128]{2,1,0:T(8,128)(2,1)S(1)}, bf16[2,144,128]{2,1,0:T(8,128)(2,1)S(1)}, bf16[2,144,128]{2,1,0:T(8,128)(2,1)S(1)}, bf16[2,144,128]{2,1,0:T(8,128)(2,1)S(1)}) custom-call(bf16[12,48,128]{2,1,0:T(8,128)(2,1)S(1)} %collective-permute-done.pair_ref, bf16[4,144,128]{2,1,0:T(8,128)(2,1)S(1)} %get-tuple-element.19.sides_ref, ...), custom_call_target="tpu_custom_call" | custom-call | flops 75497472 | bytes 1179648 | tf_op jit(solution)/shard_map/pallas_call | solution.py:264
  2.7 3.6 %collective-permute-start.1 = (bf16[2,144,128]{2,1,0:T(8,128)(2,1)S(1)}, bf16[2,144,128]{2,1,0:T(8,128)(2,1)S(1)}, u32[]{:S(2)}, u32[]{:S(2)}) collective-permute-start(bf16[2,144,128]{2,1,0:T(8,128)(2,1)S(1)} %get-tuple-element.23), channel_id=1, source_target_pairs={{0,6},{2,4},{4,2},{6,0},{1,7},{3,5},{5,3},{7,1},{8,14},{10,12},{12... | collective-permute-start | bytes 221192 | tf_op jit(solution)/shard_map/ppermute | solution.py:274
  6.3 0.5 %collective-permute-start.2 = (bf16[2,144,128]{2,1,0:T(8,128)(2,1)S(1)}, bf16[2,144,128]{2,1,0:T(8,128)(2,1)S(1)}, u32[]{:S(2)}, u32[]{:S(2)}) collective-permute-start(bf16[2,144,128]{2,1,0:T(8,128)(2,1)S(1)} %get-tuple-element.24), channel_id=1, source_target_pairs={{0,2},{2,0},{4,6},{6,4},{1,3},{3,1},{5,7},{7,5},{8,10},{10,8},{12,... | collective-permute-start | bytes 221192 | tf_op jit(solution)/shard_map/ppermute | solution.py:274
  6.8 0.1 collective-permute-start.3
  7.0 2.3 %collective-permute-done.1.refs_0_ = bf16[2,144,128]{2,1,0:T(8,128)(2,1)S(1)} collective-permute-done((bf16[2,144,128]{2,1,0:T(8,128)(2,1)S(1)}, bf16[2,144,128]{2,1,0:T(8,128)(2,1)S(1)}, u32[]{:S(2)}, u32[]{:S(2)}) %collective-permute-start.1) | collective-permute-done | bytes 73760 | tf_op jit(solution)/shard_map/ppermute | solution.py:274
  9.3 1.6 %collective-permute-done.2.refs_1_ = bf16[2,144,128]{2,1,0:T(8,128)(2,1)S(1)} collective-permute-done((bf16[2,144,128]{2,1,0:T(8,128)(2,1)S(1)}, bf16[2,144,128]{2,1,0:T(8,128)(2,1)S(1)}, u32[]{:S(2)}, u32[]{:S(2)}) %collective-permute-start.2) | collective-permute-done | bytes 73760 | tf_op jit(solution)/shard_map/ppermute | solution.py:274
  10.9 0.3 %collective-permute-done.3.refs_2_ = bf16[2,144,128]{2,1,0:T(8,128)(2,1)S(1)} collective-permute-done((bf16[2,144,128]{2,1,0:T(8,128)(2,1)S(1)}, bf16[2,144,128]{2,1,0:T(8,128)(2,1)S(1)}, u32[]{:S(2)}, u32[]{:S(2)}) %collective-permute-start.3) | collective-permute-done | bytes 73760 | tf_op jit(solution)/shard_map/ppermute | solution.py:274
  11.2 1.6 %shard_map.93 = bf16[16,72,128]{2,1,0:T(8,128)(2,1)} custom-call(bf16[2,144,128]{2,1,0:T(8,128)(2,1)S(1)} %collective-permute-done.1.refs_0_, bf16[2,144,128]{2,1,0:T(8,128)(2,1)S(1)} %collective-permute-done.2.refs_1_, bf16[2,144,128]{2,1,0:T(8,128)(2,1)S(1)} %collective-permute-done.3.refs_2_, bf16[2,144,128]{2,1,0:T(8,128)(2,1)S(1)} %get-tuple-element.26.refs_3_, ...), custom_call_target="tpu_custom_call" | custom-call | tf_op jit(solution)/shard_map/pallas_call | solution.py:275
  12.8 0.0 copy-start.1
  12.8 6.5 %all-to-all-start = ((bf16[16,72,128]{2,1,0:T(8,128)(2,1)}), bf16[16,72,128]{2,1,0:T(8,128)(2,1)S(1)}, u32[]{:S(2)}, u32[]{:S(2)}) async-start(bf16[16,72,128]{2,1,0:T(8,128)(2,1)} %shard_map.93), calls=%async_computation | async-start | bytes 589824 | tf_op jit(solution)/shard_map/all_to_all | solution.py:294
  19.3 0.0 copy-start.2
  19.3 0.0 copy-start.3
  19.4 0.0 copy-done.1
  19.4 0.6 %copy-done.2 = f32[128]{0:T(128)S(1)} copy-done((f32[128]{0:T(128)S(1)}, f32[128]{0:T(128)}, u32[]{:S(2)}) %copy-start.2) | copy-done | bytes 536
  20.0 0.0 copy-done.3
  20.0 0.0 copy-start
  20.0 0.2 shard_map.94
  20.2 5.5 %all-to-all-done.total_ref = bf16[16,72,128]{2,1,0:T(8,128)(2,1)S(1)} async-done(((bf16[16,72,128]{2,1,0:T(8,128)(2,1)}), bf16[16,72,128]{2,1,0:T(8,128)(2,1)S(1)}, u32[]{:S(2)}, u32[]{:S(2)}) %all-to-all-start) | async-done | bytes 294944 | tf_op jit(solution)/shard_map/all_to_all | solution.py:294
  25.8 0.0 copy-done
  25.8 1.0 %shard_map.95 = bf16[12,48,128]{2,1,0:T(8,128)(2,1)} custom-call(bf16[16,72,128]{2,1,0:T(8,128)(2,1)S(1)} %all-to-all-done.total_ref, f32[576,128]{1,0:T(8,128)S(1)} %get-tuple-element.30.gate_ref, f32[128,1]{1,0:T(8,128)S(1)} %get-tuple-element.31.gain_ref, f32[128,1]{1,0:T(8,128)S(1)} %get-tuple-element.32.bias_ref, bf16[128,128]{1,0:T(8,128)(2,1)S(1)} %copy-done), custom_call_target="tpu_custom_call" | custom-call | tf_op jit(solution)/shard_map/pallas_call | solution.py:295
Async XLA Ops:
  0.0 2.2 %collective-permute-start = (bf16[12,48,128]{2,1,0:T(8,128)(2,1)}, bf16[12,48,128]{2,1,0:T(8,128)(2,1)S(1)}, u32[]{:S(2)}, u32[]{:S(2)}) collective-permute-start(bf16[12,48,128]{2,1,0:T(8,128)(2,1)} %pair_hbm.1), channel_id=1, source_target_pairs={{0,1},{1,0},{2,3},{3,2},{4,5},{5,4},{6,7},{7,6},{8,9},{9,8},{10,11... | collective-permute-start | bytes 442376 | tf_op jit(solution)/shard_map/ppermute | solution.py:239
  2.7 6.5 %collective-permute-start.1 = (bf16[2,144,128]{2,1,0:T(8,128)(2,1)S(1)}, bf16[2,144,128]{2,1,0:T(8,128)(2,1)S(1)}, u32[]{:S(2)}, u32[]{:S(2)}) collective-permute-start(bf16[2,144,128]{2,1,0:T(8,128)(2,1)S(1)} %get-tuple-element.23), channel_id=1, source_target_pairs={{0,6},{2,4},{4,2},{6,0},{1,7},{3,5},{5,3},{7,1},{8,14},{10,12},{12... | collective-permute-start | bytes 221192 | tf_op jit(solution)/shard_map/ppermute | solution.py:274
  6.3 4.5 %collective-permute-start.2 = (bf16[2,144,128]{2,1,0:T(8,128)(2,1)S(1)}, bf16[2,144,128]{2,1,0:T(8,128)(2,1)S(1)}, u32[]{:S(2)}, u32[]{:S(2)}) collective-permute-start(bf16[2,144,128]{2,1,0:T(8,128)(2,1)S(1)} %get-tuple-element.24), channel_id=1, source_target_pairs={{0,2},{2,0},{4,6},{6,4},{1,3},{3,1},{5,7},{7,5},{8,10},{10,8},{12,... | collective-permute-start | bytes 221192 | tf_op jit(solution)/shard_map/ppermute | solution.py:274
  6.8 4.4 %collective-permute-start.3 = (bf16[2,144,128]{2,1,0:T(8,128)(2,1)S(1)}, bf16[2,144,128]{2,1,0:T(8,128)(2,1)S(1)}, u32[]{:S(2)}, u32[]{:S(2)}) collective-permute-start(bf16[2,144,128]{2,1,0:T(8,128)(2,1)S(1)} %get-tuple-element.25), channel_id=1, source_target_pairs={{0,4},{2,6},{4,0},{6,2},{1,5},{3,7},{5,1},{7,3},{8,12},{10,14},{12... | collective-permute-start | bytes 221192 | tf_op jit(solution)/shard_map/ppermute | solution.py:274
  12.8 6.5 %copy-start.1 = (bf16[128,128]{1,0:T(8,128)(2,1)S(1)}, bf16[128,128]{1,0:T(8,128)(2,1)}, u32[]{:S(2)}) copy-start(bf16[128,128]{1,0:T(8,128)(2,1)} %w_ref.2) | copy-start | bytes 98308
  12.8 12.9 %all-to-all-start = ((bf16[16,72,128]{2,1,0:T(8,128)(2,1)}), bf16[16,72,128]{2,1,0:T(8,128)(2,1)S(1)}, u32[]{:S(2)}, u32[]{:S(2)}) async-start(bf16[16,72,128]{2,1,0:T(8,128)(2,1)} %shard_map.93), calls=%async_computation | async-start | bytes 589824 | tf_op jit(solution)/shard_map/all_to_all | solution.py:294
  19.3 0.7 %copy-start.2 = (f32[128]{0:T(128)S(1)}, f32[128]{0:T(128)}, u32[]{:S(2)}) copy-start(f32[128]{0:T(128)} %param.15) | copy-start | bytes 1540
  19.3 0.7 %copy-start.3 = (f32[128]{0:T(128)S(1)}, f32[128]{0:T(128)}, u32[]{:S(2)}) copy-start(f32[128]{0:T(128)} %param.16) | copy-start | bytes 1540
  20.0 5.8 %copy-start = (bf16[128,128]{1,0:T(8,128)(2,1)S(1)}, bf16[128,128]{1,0:T(8,128)(2,1)}, u32[]{:S(2)}) copy-start(bf16[128,128]{1,0:T(8,128)(2,1)} %w_ref.3) | copy-start | bytes 98308

commit v21 on v20

--- a/solution.py
+++ b/solution.py
@@ -225,7 +225,7 @@
     far_order = []
     for col in reversed(range(cols)):
         ahead = list(range(quads)) if col else list(range(1, quads)) + [0]
-        behind = [1] + [quad for quad in reversed(range(quads)) if quad != 1] if col else list(reversed(range(quads)))
+        behind = [0] + list(reversed(range(1, quads))) if col else list(reversed(range(quads)))
         for quad, other in zip(ahead, behind):
             far_order += [near + other * cols + col, quad * cols + col]
     share = hidden // near

time: 27.1 us -> 26.8 us (0.989)
  starting transfers between devices: 11.2 us -> 9.97 us
  waiting for transfers between devices: 9.77 us -> 10.7 us
    all_to_all x1, starting transfers between devices: 6.51 us -> 5.28 us  [per_device(): lax.all_to_all(total, ('half', 'quad', 'col'), split_axis=0, concat_axis=...]
    all_to_all x1, waiting for transfers between devices: 5.55 us -> 6.51 us  [per_device(): lax.all_to_all(total, ('half', 'quad', 'col'), split_axis=0, concat_axis=...]
where the time goes in v21:
time: 26.8 us; the launch traced here: 26.5 us
  waiting for transfers between devices  10.7 us (40%)
  starting transfers between devices  9.97 us (37%)
  Pallas kernels  5.09 us (19%)
  local copies, waits for them, and re-layouts  0.65 us (2%)
    all_to_all x1, waiting for transfers between devices, per_device(): lax.all_to_all(total, ('half', 'quad', 'col'), split_axis=0, concat_axis=...  6.51 us
    all_to_all x1, starting transfers between devices, per_device(): lax.all_to_all(total, ('half', 'quad', 'col'), split_axis=0, concat_axis=...  5.28 us
    ppermute x3, starting transfers between devices, per_device(): lax.ppermute(pieces[step], 'quad', [(i, i ^ step) for i in range(quads)])  4.24 us
    ppermute x3, waiting for transfers between devices, per_device(): lax.ppermute(pieces[step], 'quad', [(i, i ^ step) for i in range(quads)])  4.22 us
    pallas_call x1, Pallas kernels, per_device(): pl.pallas_call(functools.partial(own_kernel, quads, cols), out_shape=(jax...  1.7 us
    pallas_call x1, Pallas kernels, per_device(): pl.pallas_call(functools.partial(triangle_kernel, far_order, steps, cols,...  1.62 us
    pallas_call x1, Pallas kernels, per_device(): pl.pallas_call(functools.partial(output_kernel, far_order, near_order), o...  1.02 us
    unnamed x8, local copies, waits for them, and re-layouts  0.65 us
  transfers between devices with their start and end apart: 5, of which 4 were waited for; matrix products, arithmetic and copies ran while one was open for 0% of the time, Pallas kernels for 7%

profile of v21, /device:TPU:0, one launch (start us, length us, event | category | flops | bytes accessed | tf_op | source)
XLA Modules:
  0.0 26.5 jit_solution(10881837497571297203)
XLA Ops:
  0.0 0.5 %collective-permute-start = (bf16[12,48,128]{2,1,0:T(8,128)(2,1)}, bf16[12,48,128]{2,1,0:T(8,128)(2,1)S(1)}, u32[]{:S(2)}, u32[]{:S(2)}) collective-permute-start(bf16[12,48,128]{2,1,0:T(8,128)(2,1)} %pair_hbm.1), channel_id=1, source_target_pairs={{0,1},{1,0},{2,3},{3,2},{4,5},{5,4},{6,7},{7,6},{8,9},{9,8},{10,11... | collective-permute-start | bytes 442376 | tf_op jit(solution)/shard_map/ppermute | solution.py:239
  0.5 1.7 %shard_map.91 = (bf16[4,144,128]{2,1,0:T(8,128)(2,1)S(1)}, bf16[576,128]{1,0:T(8,128)(2,1)S(1)}, f32[8,384]{1,0:T(8,128)S(1)}, f32[96,1]{1,0:T(8,128)S(1)}, bf16...) custom-call(bf16[12,48,128]{2,1,0:T(8,128)(2,1)} %pair_hbm.1, f32[1,128]{1,0:T(1,128)} %bitcast.7, ...), custom_call_target="tpu_custom_call" | custom-call | flops 75497472 | bytes 1179648 | tf_op jit(solution)/shard_map/pallas_call | solution.py:241
  2.2 0.0 collective-permute-done.pair_ref
  2.2 0.6 %shard_map.92 = (bf16[2,144,128]{2,1,0:T(8,128)(2,1)S(1)}, bf16[2,144,128]{2,1,0:T(8,128)(2,1)S(1)}, bf16[2,144,128]{2,1,0:T(8,128)(2,1)S(1)}, bf16[2,144,128]{2,1,0:T(8,128)(2,1)S(1)}) custom-call(bf16[12,48,128]{2,1,0:T(8,128)(2,1)S(1)} %collective-permute-done.pair_ref, bf16[4,144,128]{2,1,0:T(8,128)(2,1)S(1)} %get-tuple-element.19.sides_ref, ...), custom_call_target="tpu_custom_call" | custom-call | flops 75497472 | bytes 1179648 | tf_op jit(solution)/shard_map/pallas_call | solution.py:264
  2.7 3.6 %collective-permute-start.1 = (bf16[2,144,128]{2,1,0:T(8,128)(2,1)S(1)}, bf16[2,144,128]{2,1,0:T(8,128)(2,1)S(1)}, u32[]{:S(2)}, u32[]{:S(2)}) collective-permute-start(bf16[2,144,128]{2,1,0:T(8,128)(2,1)S(1)} %get-tuple-element.23), channel_id=1, source_target_pairs={{0,6},{2,4},{4,2},{6,0},{1,7},{3,5},{5,3},{7,1},{8,14},{10,12},{12... | collective-permute-start | bytes 221192 | tf_op jit(solution)/shard_map/ppermute | solution.py:274
  6.3 0.5 %collective-permute-start.2 = (bf16[2,144,128]{2,1,0:T(8,128)(2,1)S(1)}, bf16[2,144,128]{2,1,0:T(8,128)(2,1)S(1)}, u32[]{:S(2)}, u32[]{:S(2)}) collective-permute-start(bf16[2,144,128]{2,1,0:T(8,128)(2,1)S(1)} %get-tuple-element.24), channel_id=1, source_target_pairs={{0,2},{2,0},{4,6},{6,4},{1,3},{3,1},{5,7},{7,5},{8,10},{10,8},{12,... | collective-permute-start | bytes 221192 | tf_op jit(solution)/shard_map/ppermute | solution.py:274
  6.8 0.1 collective-permute-start.3
  7.0 2.3 %collective-permute-done.1.refs_0_ = bf16[2,144,128]{2,1,0:T(8,128)(2,1)S(1)} collective-permute-done((bf16[2,144,128]{2,1,0:T(8,128)(2,1)S(1)}, bf16[2,144,128]{2,1,0:T(8,128)(2,1)S(1)}, u32[]{:S(2)}, u32[]{:S(2)}) %collective-permute-start.1) | collective-permute-done | bytes 73760 | tf_op jit(solution)/shard_map/ppermute | solution.py:274
  9.3 1.6 %collective-permute-done.2.refs_1_ = bf16[2,144,128]{2,1,0:T(8,128)(2,1)S(1)} collective-permute-done((bf16[2,144,128]{2,1,0:T(8,128)(2,1)S(1)}, bf16[2,144,128]{2,1,0:T(8,128)(2,1)S(1)}, u32[]{:S(2)}, u32[]{:S(2)}) %collective-permute-start.2) | collective-permute-done | bytes 73760 | tf_op jit(solution)/shard_map/ppermute | solution.py:274
  10.9 0.3 %collective-permute-done.3.refs_2_ = bf16[2,144,128]{2,1,0:T(8,128)(2,1)S(1)} collective-permute-done((bf16[2,144,128]{2,1,0:T(8,128)(2,1)S(1)}, bf16[2,144,128]{2,1,0:T(8,128)(2,1)S(1)}, u32[]{:S(2)}, u32[]{:S(2)}) %collective-permute-start.3) | collective-permute-done | bytes 73760 | tf_op jit(solution)/shard_map/ppermute | solution.py:274
  11.2 1.6 %shard_map.93 = bf16[16,72,128]{2,1,0:T(8,128)(2,1)} custom-call(bf16[2,144,128]{2,1,0:T(8,128)(2,1)S(1)} %collective-permute-done.1.refs_0_, bf16[2,144,128]{2,1,0:T(8,128)(2,1)S(1)} %collective-permute-done.2.refs_1_, bf16[2,144,128]{2,1,0:T(8,128)(2,1)S(1)} %collective-permute-done.3.refs_2_, bf16[2,144,128]{2,1,0:T(8,128)(2,1)S(1)} %get-tuple-element.26.refs_3_, ...), custom_call_target="tpu_custom_call" | custom-call | tf_op jit(solution)/shard_map/pallas_call | solution.py:275
  12.8 0.0 copy-start.1
  12.8 5.3 %all-to-all-start = ((bf16[16,72,128]{2,1,0:T(8,128)(2,1)}), bf16[16,72,128]{2,1,0:T(8,128)(2,1)S(1)}, u32[]{:S(2)}, u32[]{:S(2)}) async-start(bf16[16,72,128]{2,1,0:T(8,128)(2,1)} %shard_map.93), calls=%async_computation | async-start | bytes 589824 | tf_op jit(solution)/shard_map/all_to_all | solution.py:294
  18.1 0.0 copy-start.2
  18.1 0.0 copy-start.3
  18.1 0.0 copy-done.1
  18.1 0.6 %copy-done.2 = f32[128]{0:T(128)S(1)} copy-done((f32[128]{0:T(128)S(1)}, f32[128]{0:T(128)}, u32[]{:S(2)}) %copy-start.2) | copy-done | bytes 536
  18.8 0.0 copy-done.3
  18.8 0.0 copy-start
  18.8 0.2 shard_map.94
  19.0 6.5 %all-to-all-done.total_ref = bf16[16,72,128]{2,1,0:T(8,128)(2,1)S(1)} async-done(((bf16[16,72,128]{2,1,0:T(8,128)(2,1)}), bf16[16,72,128]{2,1,0:T(8,128)(2,1)S(1)}, u32[]{:S(2)}, u32[]{:S(2)}) %all-to-all-start) | async-done | bytes 294944 | tf_op jit(solution)/shard_map/all_to_all | solution.py:294
  25.5 0.0 copy-done
  25.5 1.0 %shard_map.95 = bf16[12,48,128]{2,1,0:T(8,128)(2,1)} custom-call(bf16[16,72,128]{2,1,0:T(8,128)(2,1)S(1)} %all-to-all-done.total_ref, f32[576,128]{1,0:T(8,128)S(1)} %get-tuple-element.30.gate_ref, f32[128,1]{1,0:T(8,128)S(1)} %get-tuple-element.31.gain_ref, f32[128,1]{1,0:T(8,128)S(1)} %get-tuple-element.32.bias_ref, bf16[128,128]{1,0:T(8,128)(2,1)S(1)} %copy-done), custom_call_target="tpu_custom_call" | custom-call | tf_op jit(solution)/shard_map/pallas_call | solution.py:295
Async XLA Ops:
  0.0 2.2 %collective-permute-start = (bf16[12,48,128]{2,1,0:T(8,128)(2,1)}, bf16[12,48,128]{2,1,0:T(8,128)(2,1)S(1)}, u32[]{:S(2)}, u32[]{:S(2)}) collective-permute-start(bf16[12,48,128]{2,1,0:T(8,128)(2,1)} %pair_hbm.1), channel_id=1, source_target_pairs={{0,1},{1,0},{2,3},{3,2},{4,5},{5,4},{6,7},{7,6},{8,9},{9,8},{10,11... | collective-permute-start | bytes 442376 | tf_op jit(solution)/shard_map/ppermute | solution.py:239
  2.7 6.5 %collective-permute-start.1 = (bf16[2,144,128]{2,1,0:T(8,128)(2,1)S(1)}, bf16[2,144,128]{2,1,0:T(8,128)(2,1)S(1)}, u32[]{:S(2)}, u32[]{:S(2)}) collective-permute-start(bf16[2,144,128]{2,1,0:T(8,128)(2,1)S(1)} %get-tuple-element.23), channel_id=1, source_target_pairs={{0,6},{2,4},{4,2},{6,0},{1,7},{3,5},{5,3},{7,1},{8,14},{10,12},{12... | collective-permute-start | bytes 221192 | tf_op jit(solution)/shard_map/ppermute | solution.py:274
  6.3 4.5 %collective-permute-start.2 = (bf16[2,144,128]{2,1,0:T(8,128)(2,1)S(1)}, bf16[2,144,128]{2,1,0:T(8,128)(2,1)S(1)}, u32[]{:S(2)}, u32[]{:S(2)}) collective-permute-start(bf16[2,144,128]{2,1,0:T(8,128)(2,1)S(1)} %get-tuple-element.24), channel_id=1, source_target_pairs={{0,2},{2,0},{4,6},{6,4},{1,3},{3,1},{5,7},{7,5},{8,10},{10,8},{12,... | collective-permute-start | bytes 221192 | tf_op jit(solution)/shard_map/ppermute | solution.py:274
  6.8 4.4 %collective-permute-start.3 = (bf16[2,144,128]{2,1,0:T(8,128)(2,1)S(1)}, bf16[2,144,128]{2,1,0:T(8,128)(2,1)S(1)}, u32[]{:S(2)}, u32[]{:S(2)}) collective-permute-start(bf16[2,144,128]{2,1,0:T(8,128)(2,1)S(1)} %get-tuple-element.25), channel_id=1, source_target_pairs={{0,4},{2,6},{4,0},{6,2},{1,5},{3,7},{5,1},{7,3},{8,12},{10,14},{12... | collective-permute-start | bytes 221192 | tf_op jit(solution)/shard_map/ppermute | solution.py:274
  12.8 5.3 %copy-start.1 = (bf16[128,128]{1,0:T(8,128)(2,1)S(1)}, bf16[128,128]{1,0:T(8,128)(2,1)}, u32[]{:S(2)}) copy-start(bf16[128,128]{1,0:T(8,128)(2,1)} %w_ref.2) | copy-start | bytes 98308
  12.8 12.7 %all-to-all-start = ((bf16[16,72,128]{2,1,0:T(8,128)(2,1)}), bf16[16,72,128]{2,1,0:T(8,128)(2,1)S(1)}, u32[]{:S(2)}, u32[]{:S(2)}) async-start(bf16[16,72,128]{2,1,0:T(8,128)(2,1)} %shard_map.93), calls=%async_computation | async-start | bytes 589824 | tf_op jit(solution)/shard_map/all_to_all | solution.py:294
  18.1 0.7 %copy-start.2 = (f32[128]{0:T(128)S(1)}, f32[128]{0:T(128)}, u32[]{:S(2)}) copy-start(f32[128]{0:T(128)} %param.15) | copy-start | bytes 1540
  18.1 0.7 %copy-start.3 = (f32[128]{0:T(128)S(1)}, f32[128]{0:T(128)}, u32[]{:S(2)}) copy-start(f32[128]{0:T(128)} %param.16) | copy-start | bytes 1540
  18.8 6.7 %copy-start = (bf16[128,128]{1,0:T(8,128)(2,1)S(1)}, bf16[128,128]{1,0:T(8,128)(2,1)}, u32[]{:S(2)}) copy-start(bf16[128,128]{1,0:T(8,128)(2,1)} %w_ref.3) | copy-start | bytes 98308

commit v22 on v21

--- a/solution.py
+++ b/solution.py
@@ -88,12 +88,16 @@
 
 
 def own_kernel(quads, cols, pair_hbm, gain_hbm, bias_hbm, w_hbm, mask_hbm, sides_ref, normed_ref, spread_ref, column_mask_ref, w_ref, gain_ref, bias_ref, pair_ref, all_w_ref, mask_ref, sems):
-    moves = [(mask_hbm, mask_ref), (pair_hbm, pair_ref), (gain_hbm, gain_ref), (bias_hbm, bias_ref), (w_hbm, all_w_ref)]
+    row_count, _, channels = pair_ref.shape
+    pair_rows = [pl.ds(at, row_count // 3) for at in range(0, row_count, row_count // 3)]
+    w_rows = [pl.ds(at, channels // 2) for at in range(0, channels, channels // 2)]
+    moves = [(mask_hbm, mask_ref), (gain_hbm, gain_ref), (bias_hbm, bias_ref)]
+    moves += [(pair_hbm.at[rows], pair_ref.at[rows]) for rows in pair_rows]
+    moves += [(w_hbm.at[rows], all_w_ref.at[rows]) for rows in w_rows]
     copies = [pltpu.make_async_copy(source, target, sems.at[n]) for n, (source, target) in enumerate(moves)]
     for copy in copies:
         copy.start()
     my_quad, my_col = lax.axis_index("quad"), lax.axis_index("col")
-    row_count, _, channels = pair_ref.shape
     tokens = normed_ref.shape[0]
     hidden = all_w_ref.shape[1] // 4
     ours = hidden // cols
@@ -112,11 +116,12 @@
     channel = lax.broadcasted_iota(jnp.int32, (group, lanes), 0)
     lane = lax.broadcasted_iota(jnp.int32, (group, lanes), 1)
     spread_ref[...] = jnp.where(lane % group == channel, kept, 0.0)
-    for copy in copies[1:4]:
+    for copy in copies[1:6]:
         copy.wait()
     normed = normalise(pair_ref[...].reshape(tokens, channels), gain_ref[...], bias_ref[...])
     normed_ref[...] = normed
-    copies[4].wait()
+    for copy in copies[6:]:
+        copy.wait()
     parts = [all_w_ref[:, at : at + hidden] for at in range(0, 4 * hidden, hidden)]
     w = jnp.concatenate([jnp.where(my_col == 0, part[:, :ours], part[:, ours:]) for part in parts], axis=1)
     w_ref[...] = w
@@ -255,7 +260,7 @@
             pltpu.VMEM(pair.shape, pair.dtype),
             pltpu.VMEM(w_in.shape, w_in.dtype),
             pltpu.VMEM((1, length), jnp.int32),
-            pltpu.SemaphoreType.DMA((5,)),
+            pltpu.SemaphoreType.DMA((8,)),
         ],
         compiler_params=LIMIT,
         cost_estimate=cost,

time: 26.8 us -> 26.8 us (level)
  no operation moved by 1% of the time
where the time goes in v22:
time: 26.8 us; the launch traced here: 26.5 us
  waiting for transfers between devices  10.7 us (40%)
  starting transfers between devices  9.98 us (37%)
  Pallas kernels  5.08 us (19%)
  local copies, waits for them, and re-layouts  0.65 us (2%)
    all_to_all x1, waiting for transfers between devices, per_device(): lax.all_to_all(total, ('half', 'quad', 'col'), split_axis=0, concat_axis=...  6.51 us
    all_to_all x1, starting transfers between devices, per_device(): lax.all_to_all(total, ('half', 'quad', 'col'), split_axis=0, concat_axis=...  5.28 us
    ppermute x3, starting transfers between devices, per_device(): lax.ppermute(pieces[step], 'quad', [(i, i ^ step) for i in range(quads)])  4.24 us
    ppermute x3, waiting for transfers between devices, per_device(): lax.ppermute(pieces[step], 'quad', [(i, i ^ step) for i in range(quads)])  4.21 us
    pallas_call x1, Pallas kernels, per_device(): pl.pallas_call(functools.partial(own_kernel, quads, cols), out_shape=(jax...  1.69 us
    pallas_call x1, Pallas kernels, per_device(): pl.pallas_call(functools.partial(triangle_kernel, far_order, steps, cols,...  1.62 us
    pallas_call x1, Pallas kernels, per_device(): pl.pallas_call(functools.partial(output_kernel, far_order, near_order), o...  1.02 us
    unnamed x8, local copies, waits for them, and re-layouts  0.65 us
  transfers between devices with their start and end apart: 5, of which 4 were waited for; matrix products, arithmetic and copies ran while one was open for 0% of the time, Pallas kernels for 7%

profile of v22, /device:TPU:0, one launch (start us, length us, event | category | flops | bytes accessed | tf_op | source)
XLA Modules:
  0.0 26.5 jit_solution(4729326363237614262)
XLA Ops:
  0.0 0.5 %collective-permute-start = (bf16[12,48,128]{2,1,0:T(8,128)(2,1)}, bf16[12,48,128]{2,1,0:T(8,128)(2,1)S(1)}, u32[]{:S(2)}, u32[]{:S(2)}) collective-permute-start(bf16[12,48,128]{2,1,0:T(8,128)(2,1)} %pair_hbm.1), channel_id=1, source_target_pairs={{0,1},{1,0},{2,3},{3,2},{4,5},{5,4},{6,7},{7,6},{8,9},{9,8},{10,11... | collective-permute-start | bytes 442376 | tf_op jit(solution)/shard_map/ppermute | solution.py:244
  0.5 1.7 %shard_map.91 = (bf16[4,144,128]{2,1,0:T(8,128)(2,1)S(1)}, bf16[576,128]{1,0:T(8,128)(2,1)S(1)}, f32[8,384]{1,0:T(8,128)S(1)}, f32[96,1]{1,0:T(8,128)S(1)}, bf16...) custom-call(bf16[12,48,128]{2,1,0:T(8,128)(2,1)} %pair_hbm.1, f32[1,128]{1,0:T(1,128)} %bitcast.7, ...), custom_call_target="tpu_custom_call" | custom-call | flops 75497472 | bytes 1179648 | tf_op jit(solution)/shard_map/pallas_call | solution.py:246
  2.2 0.0 collective-permute-done.pair_ref
  2.2 0.6 %shard_map.92 = (bf16[2,144,128]{2,1,0:T(8,128)(2,1)S(1)}, bf16[2,144,128]{2,1,0:T(8,128)(2,1)S(1)}, bf16[2,144,128]{2,1,0:T(8,128)(2,1)S(1)}, bf16[2,144,128]{2,1,0:T(8,128)(2,1)S(1)}) custom-call(bf16[12,48,128]{2,1,0:T(8,128)(2,1)S(1)} %collective-permute-done.pair_ref, bf16[4,144,128]{2,1,0:T(8,128)(2,1)S(1)} %get-tuple-element.19.sides_ref, ...), custom_call_target="tpu_custom_call" | custom-call | flops 75497472 | bytes 1179648 | tf_op jit(solution)/shard_map/pallas_call | solution.py:269
  2.7 3.6 %collective-permute-start.1 = (bf16[2,144,128]{2,1,0:T(8,128)(2,1)S(1)}, bf16[2,144,128]{2,1,0:T(8,128)(2,1)S(1)}, u32[]{:S(2)}, u32[]{:S(2)}) collective-permute-start(bf16[2,144,128]{2,1,0:T(8,128)(2,1)S(1)} %get-tuple-element.23), channel_id=1, source_target_pairs={{0,6},{2,4},{4,2},{6,0},{1,7},{3,5},{5,3},{7,1},{8,14},{10,12},{12... | collective-permute-start | bytes 221192 | tf_op jit(solution)/shard_map/ppermute | solution.py:279
  6.3 0.5 %collective-permute-start.2 = (bf16[2,144,128]{2,1,0:T(8,128)(2,1)S(1)}, bf16[2,144,128]{2,1,0:T(8,128)(2,1)S(1)}, u32[]{:S(2)}, u32[]{:S(2)}) collective-permute-start(bf16[2,144,128]{2,1,0:T(8,128)(2,1)S(1)} %get-tuple-element.24), channel_id=1, source_target_pairs={{0,2},{2,0},{4,6},{6,4},{1,3},{3,1},{5,7},{7,5},{8,10},{10,8},{12,... | collective-permute-start | bytes 221192 | tf_op jit(solution)/shard_map/ppermute | solution.py:279
  6.8 0.1 collective-permute-start.3
  7.0 2.3 %collective-permute-done.1.refs_0_ = bf16[2,144,128]{2,1,0:T(8,128)(2,1)S(1)} collective-permute-done((bf16[2,144,128]{2,1,0:T(8,128)(2,1)S(1)}, bf16[2,144,128]{2,1,0:T(8,128)(2,1)S(1)}, u32[]{:S(2)}, u32[]{:S(2)}) %collective-permute-start.1) | collective-permute-done | bytes 73760 | tf_op jit(solution)/shard_map/ppermute | solution.py:279
  9.3 1.6 %collective-permute-done.2.refs_1_ = bf16[2,144,128]{2,1,0:T(8,128)(2,1)S(1)} collective-permute-done((bf16[2,144,128]{2,1,0:T(8,128)(2,1)S(1)}, bf16[2,144,128]{2,1,0:T(8,128)(2,1)S(1)}, u32[]{:S(2)}, u32[]{:S(2)}) %collective-permute-start.2) | collective-permute-done | bytes 73760 | tf_op jit(solution)/shard_map/ppermute | solution.py:279
  10.9 0.3 %collective-permute-done.3.refs_2_ = bf16[2,144,128]{2,1,0:T(8,128)(2,1)S(1)} collective-permute-done((bf16[2,144,128]{2,1,0:T(8,128)(2,1)S(1)}, bf16[2,144,128]{2,1,0:T(8,128)(2,1)S(1)}, u32[]{:S(2)}, u32[]{:S(2)}) %collective-permute-start.3) | collective-permute-done | bytes 73760 | tf_op jit(solution)/shard_map/ppermute | solution.py:279
  11.2 1.6 %shard_map.93 = bf16[16,72,128]{2,1,0:T(8,128)(2,1)} custom-call(bf16[2,144,128]{2,1,0:T(8,128)(2,1)S(1)} %collective-permute-done.1.refs_0_, bf16[2,144,128]{2,1,0:T(8,128)(2,1)S(1)} %collective-permute-done.2.refs_1_, bf16[2,144,128]{2,1,0:T(8,128)(2,1)S(1)} %collective-permute-done.3.refs_2_, bf16[2,144,128]{2,1,0:T(8,128)(2,1)S(1)} %get-tuple-element.26.refs_3_, ...), custom_call_target="tpu_custom_call" | custom-call | tf_op jit(solution)/shard_map/pallas_call | solution.py:280
  12.8 0.0 copy-start.1
  12.8 5.3 %all-to-all-start = ((bf16[16,72,128]{2,1,0:T(8,128)(2,1)}), bf16[16,72,128]{2,1,0:T(8,128)(2,1)S(1)}, u32[]{:S(2)}, u32[]{:S(2)}) async-start(bf16[16,72,128]{2,1,0:T(8,128)(2,1)} %shard_map.93), calls=%async_computation | async-start | bytes 589824 | tf_op jit(solution)/shard_map/all_to_all | solution.py:299
  18.1 0.0 copy-start.2
  18.1 0.0 copy-start.3
  18.1 0.0 copy-done.1
  18.1 0.6 %copy-done.2 = f32[128]{0:T(128)S(1)} copy-done((f32[128]{0:T(128)S(1)}, f32[128]{0:T(128)}, u32[]{:S(2)}) %copy-start.2) | copy-done | bytes 536
  18.8 0.0 copy-done.3
  18.8 0.0 copy-start
  18.8 0.2 shard_map.94
  19.0 6.5 %all-to-all-done.total_ref = bf16[16,72,128]{2,1,0:T(8,128)(2,1)S(1)} async-done(((bf16[16,72,128]{2,1,0:T(8,128)(2,1)}), bf16[16,72,128]{2,1,0:T(8,128)(2,1)S(1)}, u32[]{:S(2)}, u32[]{:S(2)}) %all-to-all-start) | async-done | bytes 294944 | tf_op jit(solution)/shard_map/all_to_all | solution.py:299
  25.5 0.0 copy-done
  25.5 1.0 %shard_map.95 = bf16[12,48,128]{2,1,0:T(8,128)(2,1)} custom-call(bf16[16,72,128]{2,1,0:T(8,128)(2,1)S(1)} %all-to-all-done.total_ref, f32[576,128]{1,0:T(8,128)S(1)} %get-tuple-element.30.gate_ref, f32[128,1]{1,0:T(8,128)S(1)} %get-tuple-element.31.gain_ref, f32[128,1]{1,0:T(8,128)S(1)} %get-tuple-element.32.bias_ref, bf16[128,128]{1,0:T(8,128)(2,1)S(1)} %copy-done), custom_call_target="tpu_custom_call" | custom-call | tf_op jit(solution)/shard_map/pallas_call | solution.py:300
Async XLA Ops:
  0.0 2.2 %collective-permute-start = (bf16[12,48,128]{2,1,0:T(8,128)(2,1)}, bf16[12,48,128]{2,1,0:T(8,128)(2,1)S(1)}, u32[]{:S(2)}, u32[]{:S(2)}) collective-permute-start(bf16[12,48,128]{2,1,0:T(8,128)(2,1)} %pair_hbm.1), channel_id=1, source_target_pairs={{0,1},{1,0},{2,3},{3,2},{4,5},{5,4},{6,7},{7,6},{8,9},{9,8},{10,11... | collective-permute-start | bytes 442376 | tf_op jit(solution)/shard_map/ppermute | solution.py:244
  2.7 6.6 %collective-permute-start.1 = (bf16[2,144,128]{2,1,0:T(8,128)(2,1)S(1)}, bf16[2,144,128]{2,1,0:T(8,128)(2,1)S(1)}, u32[]{:S(2)}, u32[]{:S(2)}) collective-permute-start(bf16[2,144,128]{2,1,0:T(8,128)(2,1)S(1)} %get-tuple-element.23), channel_id=1, source_target_pairs={{0,6},{2,4},{4,2},{6,0},{1,7},{3,5},{5,3},{7,1},{8,14},{10,12},{12... | collective-permute-start | bytes 221192 | tf_op jit(solution)/shard_map/ppermute | solution.py:279
  6.3 4.5 %collective-permute-start.2 = (bf16[2,144,128]{2,1,0:T(8,128)(2,1)S(1)}, bf16[2,144,128]{2,1,0:T(8,128)(2,1)S(1)}, u32[]{:S(2)}, u32[]{:S(2)}) collective-permute-start(bf16[2,144,128]{2,1,0:T(8,128)(2,1)S(1)} %get-tuple-element.24), channel_id=1, source_target_pairs={{0,2},{2,0},{4,6},{6,4},{1,3},{3,1},{5,7},{7,5},{8,10},{10,8},{12,... | collective-permute-start | bytes 221192 | tf_op jit(solution)/shard_map/ppermute | solution.py:279
  6.8 4.4 %collective-permute-start.3 = (bf16[2,144,128]{2,1,0:T(8,128)(2,1)S(1)}, bf16[2,144,128]{2,1,0:T(8,128)(2,1)S(1)}, u32[]{:S(2)}, u32[]{:S(2)}) collective-permute-start(bf16[2,144,128]{2,1,0:T(8,128)(2,1)S(1)} %get-tuple-element.25), channel_id=1, source_target_pairs={{0,4},{2,6},{4,0},{6,2},{1,5},{3,7},{5,1},{7,3},{8,12},{10,14},{12... | collective-permute-start | bytes 221192 | tf_op jit(solution)/shard_map/ppermute | solution.py:279
  12.8 5.3 %copy-start.1 = (bf16[128,128]{1,0:T(8,128)(2,1)S(1)}, bf16[128,128]{1,0:T(8,128)(2,1)}, u32[]{:S(2)}) copy-start(bf16[128,128]{1,0:T(8,128)(2,1)} %w_ref.2) | copy-start | bytes 98308
  12.8 12.7 %all-to-all-start = ((bf16[16,72,128]{2,1,0:T(8,128)(2,1)}), bf16[16,72,128]{2,1,0:T(8,128)(2,1)S(1)}, u32[]{:S(2)}, u32[]{:S(2)}) async-start(bf16[16,72,128]{2,1,0:T(8,128)(2,1)} %shard_map.93), calls=%async_computation | async-start | bytes 589824 | tf_op jit(solution)/shard_map/all_to_all | solution.py:299
  18.1 0.7 %copy-start.2 = (f32[128]{0:T(128)S(1)}, f32[128]{0:T(128)}, u32[]{:S(2)}) copy-start(f32[128]{0:T(128)} %param.15) | copy-start | bytes 1540
  18.1 0.7 %copy-start.3 = (f32[128]{0:T(128)S(1)}, f32[128]{0:T(128)}, u32[]{:S(2)}) copy-start(f32[128]{0:T(128)} %param.16) | copy-start | bytes 1540
  18.8 6.7 %copy-start = (bf16[128,128]{1,0:T(8,128)(2,1)S(1)}, bf16[128,128]{1,0:T(8,128)(2,1)}, u32[]{:S(2)}) copy-start(bf16[128,128]{1,0:T(8,128)(2,1)} %w_ref.3) | copy-start | bytes 98308

commit v23 on v21

--- a/solution.py
+++ b/solution.py
@@ -87,18 +87,28 @@
     return pack(sides).astype(jnp.bfloat16)
 
 
-def own_kernel(quads, cols, pair_hbm, gain_hbm, bias_hbm, w_hbm, mask_hbm, sides_ref, normed_ref, spread_ref, column_mask_ref, w_ref, gain_ref, bias_ref, pair_ref, all_w_ref, mask_ref, sems):
-    moves = [(mask_hbm, mask_ref), (pair_hbm, pair_ref), (gain_hbm, gain_ref), (bias_hbm, bias_ref), (w_hbm, all_w_ref)]
+def own_kernel(quads, cols, pair_hbm, gain_hbm, bias_hbm, w_hbm, sides_ref, normed_ref, w_ref, gain_ref, bias_ref, pair_ref, all_w_ref, sems):
+    moves = [(pair_hbm, pair_ref), (gain_hbm, gain_ref), (bias_hbm, bias_ref), (w_hbm, all_w_ref)]
     copies = [pltpu.make_async_copy(source, target, sems.at[n]) for n, (source, target) in enumerate(moves)]
     for copy in copies:
         copy.start()
-    my_quad, my_col = lax.axis_index("quad"), lax.axis_index("col")
-    row_count, _, channels = pair_ref.shape
-    tokens = normed_ref.shape[0]
+    my_col = lax.axis_index("col")
     hidden = all_w_ref.shape[1] // 4
     ours = hidden // cols
+    for copy in copies[:3]:
+        copy.wait()
+    normed = normalise(pair_ref[...].reshape(normed_ref.shape), gain_ref[...], bias_ref[...])
+    normed_ref[...] = normed
+    copies[3].wait()
+    parts = [all_w_ref[:, at : at + hidden] for at in range(0, 4 * hidden, hidden)]
+    w = jnp.concatenate([jnp.where(my_col == 0, part[:, :ours], part[:, ours:]) for part in parts], axis=1)
+    w_ref[...] = w
+    sides_ref[...] = project(normed, w, pair_ref.shape, quads)
+
+
+def mask_kernel(quads, row_count, mask_ref, after_ref, spread_ref, column_mask_ref):
+    del after_ref
     group, lanes = spread_ref.shape
-    copies[0].wait()
     mask_row = mask_ref[...].astype(jnp.float32)
     column_mask_ref[...] = column(mask_row)
     start = lax.axis_index("half") * (lanes // group)
@@ -106,21 +116,12 @@
     lane = lax.broadcasted_iota(jnp.int32, (mask_row.shape[1], lanes), 1)
     whole = row_count // 3
     block, t, row = lane // LANES, lane // (quads * group) % whole, lane // group % quads
-    k = (row ^ my_quad) * row_count + jnp.where(block < 2, 2 * t + block, 2 * whole + t)
+    k = (row ^ lax.axis_index("quad")) * row_count + jnp.where(block < 2, 2 * t + block, 2 * whole + t)
     pick = jnp.where(k + start == token, 1.0, 0.0)
     kept = jnp.dot(mask_row.astype(jnp.bfloat16), pick.astype(jnp.bfloat16), preferred_element_type=jnp.float32)
     channel = lax.broadcasted_iota(jnp.int32, (group, lanes), 0)
     lane = lax.broadcasted_iota(jnp.int32, (group, lanes), 1)
     spread_ref[...] = jnp.where(lane % group == channel, kept, 0.0)
-    for copy in copies[1:4]:
-        copy.wait()
-    normed = normalise(pair_ref[...].reshape(tokens, channels), gain_ref[...], bias_ref[...])
-    normed_ref[...] = normed
-    copies[4].wait()
-    parts = [all_w_ref[:, at : at + hidden] for at in range(0, 4 * hidden, hidden)]
-    w = jnp.concatenate([jnp.where(my_col == 0, part[:, :ours], part[:, ours:]) for part in parts], axis=1)
-    w_ref[...] = w
-    sides_ref[...] = project(normed, w, pair_ref.shape, quads)
 
 
 def other_kernel(pair_ref, sides_ref, gain_ref, bias_ref, w_ref, *refs):
@@ -237,25 +238,22 @@
     packed = 2 * share * tokens // LANES
     cost = pl.CostEstimate(flops=2 * tokens * channels * 4 * hidden, bytes_accessed=16 * tokens * channels, transcendentals=0)
     other_pair = lax.ppermute(pair, "col", [(i, (i + 1) % cols) for i in range(cols)])
-    arguments = (pair, gain_in.reshape(1, channels), bias_in.reshape(1, channels), w_in, token_mask)
-    sides, normed, spread, mask, *weights = pl.pallas_call(
+    arguments = (pair, gain_in.reshape(1, channels), bias_in.reshape(1, channels), w_in)
+    sides, normed, *weights = pl.pallas_call(
         functools.partial(own_kernel, quads, cols),
         out_shape=(
             jax.ShapeDtypeStruct((quads, packed, LANES), jnp.bfloat16),
             jax.ShapeDtypeStruct((tokens, channels), jnp.bfloat16),
-            jax.ShapeDtypeStruct((GROUP, GROUP * depth), jnp.float32),
-            jax.ShapeDtypeStruct((length, 1), jnp.float32),
             jax.ShapeDtypeStruct((channels, 4 * hidden // cols), jnp.bfloat16),
             jax.ShapeDtypeStruct((1, channels), jnp.float32),
             jax.ShapeDtypeStruct((1, channels), jnp.float32),
         ),
-        in_specs=[HBM] * 5,
-        out_specs=(VMEM,) * 7,
+        in_specs=[HBM] * 4,
+        out_specs=(VMEM,) * 5,
         scratch_shapes=[
             pltpu.VMEM(pair.shape, pair.dtype),
             pltpu.VMEM(w_in.shape, w_in.dtype),
-            pltpu.VMEM((1, length), jnp.int32),
-            pltpu.SemaphoreType.DMA((5,)),
+            pltpu.SemaphoreType.DMA((4,)),
         ],
         compiler_params=LIMIT,
         cost_estimate=cost,
@@ -270,6 +268,16 @@
         compiler_params=LIMIT,
         cost_estimate=cost,
     )(other_pair, sides, gain_in, bias_in, w_ours)
+    spread, mask = pl.pallas_call(
+        functools.partial(mask_kernel, quads, row_count),
+        out_shape=(
+            jax.ShapeDtypeStruct((GROUP, GROUP * depth), jnp.float32),
+            jax.ShapeDtypeStruct((length, 1), jnp.float32),
+        ),
+        in_specs=[VMEM, VMEM],
+        out_specs=(VMEM, VMEM),
+        compiler_params=LIMIT,
+    )(token_mask, pieces[0])
     steps = [3, 1, 2, 0]
     got = [lax.ppermute(pieces[step], "quad", [(i, i ^ step) for i in range(quads)]) if step else pieces[0] for step in steps]
     total = pl.pallas_call(

time: 26.8 us -> 26.8 us (level)
  waiting for transfers between devices: 10.7 us -> 9.93 us
  local copies, waits for them, and re-layouts: 0.65 us -> 1.31 us
    ppermute x3, waiting for transfers between devices: 4.22 us -> 3.41 us  [per_device(): lax.ppermute(pieces[step], 'quad', [(i, i ^ step) for i in range(quads)])]
    unnamed x8 -> x10, local copies, waits for them, and re-layouts: 0.65 us -> 1.31 us
  transfers between devices with their start and end apart: 5 -> 5, of which waited for: 4 -> 4; matrix products, arithmetic and copies ran while one was open for 0% -> 0% of each run, Pallas kernels for 7% -> 8%
where the time goes in v23:
time: 26.8 us; the launch traced here: 26.5 us
  starting transfers between devices  9.97 us (37%)
  waiting for transfers between devices  9.93 us (37%)
  Pallas kernels  5.2 us (19%)
  local copies, waits for them, and re-layouts  1.31 us (5%)
    all_to_all x1, waiting for transfers between devices, per_device(): lax.all_to_all(total, ('half', 'quad', 'col'), split_axis=0, concat_axis=...  6.52 us
    all_to_all x1, starting transfers between devices, per_device(): lax.all_to_all(total, ('half', 'quad', 'col'), split_axis=0, concat_axis=...  5.28 us
    ppermute x3, starting transfers between devices, per_device(): lax.ppermute(pieces[step], 'quad', [(i, i ^ step) for i in range(quads)])  4.24 us
    ppermute x3, waiting for transfers between devices, per_device(): lax.ppermute(pieces[step], 'quad', [(i, i ^ step) for i in range(quads)])  3.41 us
    pallas_call x1, Pallas kernels, per_device(): pl.pallas_call(functools.partial(own_kernel, quads, cols), out_shape=(jax...  1.68 us
    pallas_call x1, Pallas kernels, per_device(): pl.pallas_call(functools.partial(triangle_kernel, far_order, steps, cols,...  1.61 us
    unnamed x10, local copies, waits for them, and re-layouts  1.31 us
    pallas_call x1, Pallas kernels, per_device(): pl.pallas_call(functools.partial(output_kernel, far_order, near_order), o...  1.02 us
  transfers between devices with their start and end apart: 5, of which 4 were waited for; matrix products, arithmetic and copies ran while one was open for 0% of the time, Pallas kernels for 8%

profile of v23, /device:TPU:0, one launch (start us, length us, event | category | flops | bytes accessed | tf_op | source)
XLA Modules:
  0.0 26.5 jit_solution(17263924457381183930)
XLA Ops:
  0.0 0.5 %collective-permute-start = (bf16[12,48,128]{2,1,0:T(8,128)(2,1)}, bf16[12,48,128]{2,1,0:T(8,128)(2,1)S(1)}, u32[]{:S(2)}, u32[]{:S(2)}) collective-permute-start(bf16[12,48,128]{2,1,0:T(8,128)(2,1)} %pair_hbm.1), channel_id=1, source_target_pairs={{0,1},{1,0},{2,3},{3,2},{4,5},{5,4},{6,7},{7,6},{8,9},{9,8},{10,11... | collective-permute-start | bytes 442376 | tf_op jit(solution)/shard_map/ppermute | solution.py:240
  0.5 1.7 %shard_map.91 = (bf16[4,144,128]{2,1,0:T(8,128)(2,1)S(1)}, bf16[576,128]{1,0:T(8,128)(2,1)S(1)}, bf16[128,256]{1,0:T(8,128)(2,1)S(1)}, f32[1,128]{1,0:T(1,128)S(1)}, f32[1,128]{1,0:T(1,128)S(1)}) custom-call(bf16[12,48,128]{2,1,0:T(8,128)(2,1)} %pair_hbm.1, f32[1,128]{1,0:T(1,128)} %bitcast.8, f32[1,128]{1,0:T(1,128)} %bitcast.9, bf16[128,512]{1,0:T(8,128)(2,1)} %w_hbm.1), custom_call_target="tpu_custom_call" | custom-call | flops 75497472 | bytes 1179648 | tf_op jit(solution)/shard_map/pallas_call | solution.py:242
  2.1 0.0 collective-permute-done.pair_ref
  2.1 0.6 %shard_map.92 = (bf16[2,144,128]{2,1,0:T(8,128)(2,1)S(1)}, bf16[2,144,128]{2,1,0:T(8,128)(2,1)S(1)}, bf16[2,144,128]{2,1,0:T(8,128)(2,1)S(1)}, bf16[2,144,128]{2,1,0:T(8,128)(2,1)S(1)}) custom-call(bf16[12,48,128]{2,1,0:T(8,128)(2,1)S(1)} %collective-permute-done.pair_ref, bf16[4,144,128]{2,1,0:T(8,128)(2,1)S(1)} %get-tuple-element.19.sides_ref, ...), custom_call_target="tpu_custom_call" | custom-call | flops 75497472 | bytes 1179648 | tf_op jit(solution)/shard_map/pallas_call | solution.py:262
  2.7 3.6 %collective-permute-start.1 = (bf16[2,144,128]{2,1,0:T(8,128)(2,1)S(1)}, bf16[2,144,128]{2,1,0:T(8,128)(2,1)S(1)}, u32[]{:S(2)}, u32[]{:S(2)}) collective-permute-start(bf16[2,144,128]{2,1,0:T(8,128)(2,1)S(1)} %get-tuple-element.23), channel_id=1, source_target_pairs={{0,6},{2,4},{4,2},{6,0},{1,7},{3,5},{5,3},{7,1},{8,14},{10,12},{12... | collective-permute-start | bytes 221192 | tf_op jit(solution)/shard_map/ppermute | solution.py:282
  6.3 0.5 %collective-permute-start.2 = (bf16[2,144,128]{2,1,0:T(8,128)(2,1)S(1)}, bf16[2,144,128]{2,1,0:T(8,128)(2,1)S(1)}, u32[]{:S(2)}, u32[]{:S(2)}) collective-permute-start(bf16[2,144,128]{2,1,0:T(8,128)(2,1)S(1)} %get-tuple-element.24), channel_id=1, source_target_pairs={{0,2},{2,0},{4,6},{6,4},{1,3},{3,1},{5,7},{7,5},{8,10},{10,8},{12,... | collective-permute-start | bytes 221192 | tf_op jit(solution)/shard_map/ppermute | solution.py:282
  6.8 0.1 collective-permute-start.3
  7.0 0.0 copy-start.2
  7.0 0.7 %copy-done.2 = s32[96]{0:T(128)S(1)} copy-done((s32[96]{0:T(128)S(1)}, s32[96]{0:T(128)}, u32[]{:S(2)}) %copy-start.2) | copy-done | bytes 408
  7.6 0.1 shard_map.93
  7.8 1.5 %collective-permute-done.1.refs_0_ = bf16[2,144,128]{2,1,0:T(8,128)(2,1)S(1)} collective-permute-done((bf16[2,144,128]{2,1,0:T(8,128)(2,1)S(1)}, bf16[2,144,128]{2,1,0:T(8,128)(2,1)S(1)}, u32[]{:S(2)}, u32[]{:S(2)}) %collective-permute-start.1) | collective-permute-done | bytes 73760 | tf_op jit(solution)/shard_map/ppermute | solution.py:282
  9.3 1.6 %collective-permute-done.2.refs_1_ = bf16[2,144,128]{2,1,0:T(8,128)(2,1)S(1)} collective-permute-done((bf16[2,144,128]{2,1,0:T(8,128)(2,1)S(1)}, bf16[2,144,128]{2,1,0:T(8,128)(2,1)S(1)}, u32[]{:S(2)}, u32[]{:S(2)}) %collective-permute-start.2) | collective-permute-done | bytes 73760 | tf_op jit(solution)/shard_map/ppermute | solution.py:282
  10.8 0.3 %collective-permute-done.3.refs_2_ = bf16[2,144,128]{2,1,0:T(8,128)(2,1)S(1)} collective-permute-done((bf16[2,144,128]{2,1,0:T(8,128)(2,1)S(1)}, bf16[2,144,128]{2,1,0:T(8,128)(2,1)S(1)}, u32[]{:S(2)}, u32[]{:S(2)}) %collective-permute-start.3) | collective-permute-done | bytes 73760 | tf_op jit(solution)/shard_map/ppermute | solution.py:282
  11.2 1.6 %shard_map.94 = bf16[16,72,128]{2,1,0:T(8,128)(2,1)} custom-call(bf16[2,144,128]{2,1,0:T(8,128)(2,1)S(1)} %collective-permute-done.1.refs_0_, bf16[2,144,128]{2,1,0:T(8,128)(2,1)S(1)} %collective-permute-done.2.refs_1_, bf16[2,144,128]{2,1,0:T(8,128)(2,1)S(1)} %collective-permute-done.3.refs_2_, ...), custom_call_target="tpu_custom_call" | custom-call | tf_op jit(solution)/shard_map/pallas_call | solution.py:283
  12.8 0.0 copy-start.1
  12.8 5.3 %all-to-all-start = ((bf16[16,72,128]{2,1,0:T(8,128)(2,1)}), bf16[16,72,128]{2,1,0:T(8,128)(2,1)S(1)}, u32[]{:S(2)}, u32[]{:S(2)}) async-start(bf16[16,72,128]{2,1,0:T(8,128)(2,1)} %shard_map.94), calls=%async_computation | async-start | bytes 589824 | tf_op jit(solution)/shard_map/all_to_all | solution.py:302
  18.1 0.0 copy-start.4
  18.1 0.0 copy-done.1
  18.1 0.6 %copy-done.3 = f32[128]{0:T(128)S(1)} copy-done((f32[128]{0:T(128)S(1)}, f32[128]{0:T(128)}, u32[]{:S(2)}) %copy-start.3) | copy-done | bytes 536
  18.7 0.0 copy-done.4
  18.7 0.2 shard_map.95
  18.9 6.5 %all-to-all-done.total_ref = bf16[16,72,128]{2,1,0:T(8,128)(2,1)S(1)} async-done(((bf16[16,72,128]{2,1,0:T(8,128)(2,1)}), bf16[16,72,128]{2,1,0:T(8,128)(2,1)S(1)}, u32[]{:S(2)}, u32[]{:S(2)}) %all-to-all-start) | async-done | bytes 294944 | tf_op jit(solution)/shard_map/all_to_all | solution.py:302
  25.5 0.0 copy-done
  25.5 1.0 %shard_map.96 = bf16[12,48,128]{2,1,0:T(8,128)(2,1)} custom-call(bf16[16,72,128]{2,1,0:T(8,128)(2,1)S(1)} %all-to-all-done.total_ref, f32[576,128]{1,0:T(8,128)S(1)} %get-tuple-element.30.gate_ref, f32[128,1]{1,0:T(8,128)S(1)} %get-tuple-element.31.gain_ref, f32[128,1]{1,0:T(8,128)S(1)} %get-tuple-element.32.bias_ref, bf16[128,128]{1,0:T(8,128)(2,1)S(1)} %copy-done), custom_call_target="tpu_custom_call" | custom-call | tf_op jit(solution)/shard_map/pallas_call | solution.py:303
  (2 shorter events, 0.0 us)
Async XLA Ops:
  0.0 2.1 %collective-permute-start = (bf16[12,48,128]{2,1,0:T(8,128)(2,1)}, bf16[12,48,128]{2,1,0:T(8,128)(2,1)S(1)}, u32[]{:S(2)}, u32[]{:S(2)}) collective-permute-start(bf16[12,48,128]{2,1,0:T(8,128)(2,1)} %pair_hbm.1), channel_id=1, source_target_pairs={{0,1},{1,0},{2,3},{3,2},{4,5},{5,4},{6,7},{7,6},{8,9},{9,8},{10,11... | collective-permute-start | bytes 442376 | tf_op jit(solution)/shard_map/ppermute | solution.py:240
  2.7 6.5 %collective-permute-start.1 = (bf16[2,144,128]{2,1,0:T(8,128)(2,1)S(1)}, bf16[2,144,128]{2,1,0:T(8,128)(2,1)S(1)}, u32[]{:S(2)}, u32[]{:S(2)}) collective-permute-start(bf16[2,144,128]{2,1,0:T(8,128)(2,1)S(1)} %get-tuple-element.23), channel_id=1, source_target_pairs={{0,6},{2,4},{4,2},{6,0},{1,7},{3,5},{5,3},{7,1},{8,14},{10,12},{12... | collective-permute-start | bytes 221192 | tf_op jit(solution)/shard_map/ppermute | solution.py:282
  6.3 4.5 %collective-permute-start.2 = (bf16[2,144,128]{2,1,0:T(8,128)(2,1)S(1)}, bf16[2,144,128]{2,1,0:T(8,128)(2,1)S(1)}, u32[]{:S(2)}, u32[]{:S(2)}) collective-permute-start(bf16[2,144,128]{2,1,0:T(8,128)(2,1)S(1)} %get-tuple-element.24), channel_id=1, source_target_pairs={{0,2},{2,0},{4,6},{6,4},{1,3},{3,1},{5,7},{7,5},{8,10},{10,8},{12,... | collective-permute-start | bytes 221192 | tf_op jit(solution)/shard_map/ppermute | solution.py:282
  6.8 4.4 %collective-permute-start.3 = (bf16[2,144,128]{2,1,0:T(8,128)(2,1)S(1)}, bf16[2,144,128]{2,1,0:T(8,128)(2,1)S(1)}, u32[]{:S(2)}, u32[]{:S(2)}) collective-permute-start(bf16[2,144,128]{2,1,0:T(8,128)(2,1)S(1)} %get-tuple-element.25), channel_id=1, source_target_pairs={{0,4},{2,6},{4,0},{6,2},{1,5},{3,7},{5,1},{7,3},{8,12},{10,14},{12... | collective-permute-start | bytes 221192 | tf_op jit(solution)/shard_map/ppermute | solution.py:282
  7.0 0.7 %copy-start.2 = (s32[96]{0:T(128)S(1)}, s32[96]{0:T(128)}, u32[]{:S(2)}) copy-start(s32[96]{0:T(128)} %param.10) | copy-start | bytes 1156
  12.8 5.3 %copy-start.1 = (bf16[128,128]{1,0:T(8,128)(2,1)S(1)}, bf16[128,128]{1,0:T(8,128)(2,1)}, u32[]{:S(2)}) copy-start(bf16[128,128]{1,0:T(8,128)(2,1)} %w_ref.2) | copy-start | bytes 98308
  12.8 12.7 %all-to-all-start = ((bf16[16,72,128]{2,1,0:T(8,128)(2,1)}), bf16[16,72,128]{2,1,0:T(8,128)(2,1)S(1)}, u32[]{:S(2)}, u32[]{:S(2)}) async-start(bf16[16,72,128]{2,1,0:T(8,128)(2,1)} %shard_map.94), calls=%async_computation | async-start | bytes 589824 | tf_op jit(solution)/shard_map/all_to_all | solution.py:302
  18.1 0.7 %copy-start.3 = (f32[128]{0:T(128)S(1)}, f32[128]{0:T(128)}, u32[]{:S(2)}) copy-start(f32[128]{0:T(128)} %param.15) | copy-start | bytes 1540
  18.1 0.7 %copy-start.4 = (f32[128]{0:T(128)S(1)}, f32[128]{0:T(128)}, u32[]{:S(2)}) copy-start(f32[128]{0:T(128)} %param.16) | copy-start | bytes 1540
  18.7 6.7 %copy-start = (bf16[128,128]{1,0:T(8,128)(2,1)S(1)}, bf16[128,128]{1,0:T(8,128)(2,1)}, u32[]{:S(2)}) copy-start(bf16[128,128]{1,0:T(8,128)(2,1)} %w_ref.3) | copy-start | bytes 98308

commit v24 on v23

--- a/solution.py
+++ b/solution.py
@@ -87,23 +87,14 @@
     return pack(sides).astype(jnp.bfloat16)
 
 
-def own_kernel(quads, cols, pair_hbm, gain_hbm, bias_hbm, w_hbm, sides_ref, normed_ref, w_ref, gain_ref, bias_ref, pair_ref, all_w_ref, sems):
-    moves = [(pair_hbm, pair_ref), (gain_hbm, gain_ref), (bias_hbm, bias_ref), (w_hbm, all_w_ref)]
+def own_kernel(pair_hbm, gain_hbm, bias_hbm, normed_ref, gain_ref, bias_ref, pair_ref, sems):
+    moves = [(pair_hbm, pair_ref), (gain_hbm, gain_ref), (bias_hbm, bias_ref)]
     copies = [pltpu.make_async_copy(source, target, sems.at[n]) for n, (source, target) in enumerate(moves)]
     for copy in copies:
         copy.start()
-    my_col = lax.axis_index("col")
-    hidden = all_w_ref.shape[1] // 4
-    ours = hidden // cols
-    for copy in copies[:3]:
+    for copy in copies:
         copy.wait()
-    normed = normalise(pair_ref[...].reshape(normed_ref.shape), gain_ref[...], bias_ref[...])
-    normed_ref[...] = normed
-    copies[3].wait()
-    parts = [all_w_ref[:, at : at + hidden] for at in range(0, 4 * hidden, hidden)]
-    w = jnp.concatenate([jnp.where(my_col == 0, part[:, :ours], part[:, ours:]) for part in parts], axis=1)
-    w_ref[...] = w
-    sides_ref[...] = project(normed, w, pair_ref.shape, quads)
+    normed_ref[...] = normalise(pair_ref[...].reshape(normed_ref.shape), gain_ref[...], bias_ref[...])
 
 
 def mask_kernel(quads, row_count, mask_ref, after_ref, spread_ref, column_mask_ref):
@@ -124,15 +115,20 @@
     spread_ref[...] = jnp.where(lane % group == channel, kept, 0.0)
 
 
-def other_kernel(pair_ref, sides_ref, gain_ref, bias_ref, w_ref, *refs):
-    *piece_refs, others_ref = refs
+def project_kernel(pair_ref, normed_ref, gain_ref, bias_ref, w_ref, *refs):
+    *piece_refs, own_ref, other_ref = refs
     my_quad, my_col = lax.axis_index("quad"), lax.axis_index("col")
-    quads = sides_ref.shape[0]
-    normed = normalise(pair_ref[...].reshape(-1, pair_ref.shape[2]), gain_ref[...], bias_ref[...])
-    others_ref[...] = project(normed, w_ref[...], pair_ref.shape, quads)
+    quads = own_ref.shape[0]
+    hidden = w_ref.shape[1] // 4
+    ours = hidden // piece_refs[0].shape[0]
+    parts = [w_ref[:, at : at + hidden] for at in range(0, 4 * hidden, hidden)]
+    w = jnp.concatenate([jnp.where(my_col == 0, part[:, :ours], part[:, ours:]) for part in parts], axis=1)
+    own_ref[...] = project(normed_ref[...], w, pair_ref.shape, quads)
+    normed = normalise(pair_ref[...].reshape(normed_ref.shape), gain_ref[...], bias_ref[...])
+    other_ref[...] = project(normed, w, pair_ref.shape, quads)
     for step, piece_ref in enumerate(piece_refs):
-        piece_ref[my_col] = sides_ref[my_quad ^ step]
-        piece_ref[1 - my_col] = others_ref[my_quad ^ step]
+        piece_ref[my_col] = own_ref[my_quad ^ step]
+        piece_ref[1 - my_col] = other_ref[my_quad ^ step]
 
 
 def triangle_kernel(far_order, steps, cols, row_count, col_count, share, *refs):
@@ -238,36 +234,29 @@
     packed = 2 * share * tokens // LANES
     cost = pl.CostEstimate(flops=2 * tokens * channels * 4 * hidden, bytes_accessed=16 * tokens * channels, transcendentals=0)
     other_pair = lax.ppermute(pair, "col", [(i, (i + 1) % cols) for i in range(cols)])
-    arguments = (pair, gain_in.reshape(1, channels), bias_in.reshape(1, channels), w_in)
-    sides, normed, *weights = pl.pallas_call(
-        functools.partial(own_kernel, quads, cols),
+    arguments = (pair, gain_in.reshape(1, channels), bias_in.reshape(1, channels))
+    normed, gain_in, bias_in = pl.pallas_call(
+        own_kernel,
         out_shape=(
-            jax.ShapeDtypeStruct((quads, packed, LANES), jnp.bfloat16),
             jax.ShapeDtypeStruct((tokens, channels), jnp.bfloat16),
-            jax.ShapeDtypeStruct((channels, 4 * hidden // cols), jnp.bfloat16),
             jax.ShapeDtypeStruct((1, channels), jnp.float32),
             jax.ShapeDtypeStruct((1, channels), jnp.float32),
         ),
-        in_specs=[HBM] * 4,
-        out_specs=(VMEM,) * 5,
-        scratch_shapes=[
-            pltpu.VMEM(pair.shape, pair.dtype),
-            pltpu.VMEM(w_in.shape, w_in.dtype),
-            pltpu.SemaphoreType.DMA((4,)),
-        ],
+        in_specs=[HBM] * 3,
+        out_specs=(VMEM,) * 3,
+        scratch_shapes=[pltpu.VMEM(pair.shape, pair.dtype), pltpu.SemaphoreType.DMA((3,))],
         compiler_params=LIMIT,
         cost_estimate=cost,
     )(*(pltpu.with_memory_space_constraint(x, pltpu.HBM) for x in arguments))
-    w_ours, gain_in, bias_in = weights
     pieces = pl.pallas_call(
-        other_kernel,
+        project_kernel,
         out_shape=[jax.ShapeDtypeStruct((cols, packed, LANES), jnp.bfloat16)] * quads,
         in_specs=[VMEM] * 5,
         out_specs=[VMEM] * quads,
-        scratch_shapes=[pltpu.VMEM((quads, packed, LANES), jnp.bfloat16)],
+        scratch_shapes=[pltpu.VMEM((quads, packed, LANES), jnp.bfloat16)] * 2,
         compiler_params=LIMIT,
         cost_estimate=cost,
-    )(other_pair, sides, gain_in, bias_in, w_ours)
+    )(other_pair, normed, gain_in, bias_in, w_in)
     spread, mask = pl.pallas_call(
         functools.partial(mask_kernel, quads, row_count),
         out_shape=(

time: 26.8 us -> 27 us (level)
  starting transfers between devices: 9.97 us -> 10.3 us
    ppermute x3, starting transfers between devices: 4.24 us -> 4.57 us  [per_device(): lax.ppermute(pieces[step], 'quad', [(i, i ^ step) for i in range(quads)])]
    unnamed x10 -> x12, local copies, waits for them, and re-layouts: 1.31 us -> 1.31 us
  transfers between devices with their start and end apart: 5 -> 5, of which waited for: 4 -> 4; matrix products, arithmetic and copies ran while one was open for 0% -> 0% of each run, Pallas kernels for 8% -> 6%
where the time goes in v24:
time: 27 us; the launch traced here: 26.7 us
  starting transfers between devices  10.3 us (38%)
  waiting for transfers between devices  9.92 us (37%)
  Pallas kernels  5.07 us (19%)
  local copies, waits for them, and re-layouts  1.31 us (5%)
    all_to_all x1, waiting for transfers between devices, per_device(): lax.all_to_all(total, ('half', 'quad', 'col'), split_axis=0, concat_axis=...  6.51 us
    all_to_all x1, starting transfers between devices, per_device(): lax.all_to_all(total, ('half', 'quad', 'col'), split_axis=0, concat_axis=...  5.29 us
    ppermute x3, starting transfers between devices, per_device(): lax.ppermute(pieces[step], 'quad', [(i, i ^ step) for i in range(quads)])  4.57 us
    ppermute x3, waiting for transfers between devices, per_device(): lax.ppermute(pieces[step], 'quad', [(i, i ^ step) for i in range(quads)])  3.41 us
    pallas_call x1, Pallas kernels, per_device(): pl.pallas_call(functools.partial(triangle_kernel, far_order, steps, cols,...  1.6 us
    unnamed x12, local copies, waits for them, and re-layouts  1.31 us
    pallas_call x1, Pallas kernels, per_device(): pl.pallas_call(own_kernel, out_shape=(jax.ShapeDtypeStruct((tokens, chann...  1.22 us
    pallas_call x1, Pallas kernels, per_device(): pl.pallas_call(functools.partial(output_kernel, far_order, near_order), o...  1.02 us
  transfers between devices with their start and end apart: 5, of which 4 were waited for; matrix products, arithmetic and copies ran while one was open for 0% of the time, Pallas kernels for 6%

profile of v24, /device:TPU:0, one launch (start us, length us, event | category | flops | bytes accessed | tf_op | source)
XLA Modules:
  0.0 26.7 jit_solution(8887514509475135065)
XLA Ops:
  0.0 0.5 %collective-permute-start = (bf16[12,48,128]{2,1,0:T(8,128)(2,1)}, bf16[12,48,128]{2,1,0:T(8,128)(2,1)S(1)}, u32[]{:S(2)}, u32[]{:S(2)}) collective-permute-start(bf16[12,48,128]{2,1,0:T(8,128)(2,1)} %pair_hbm.1), channel_id=1, source_target_pairs={{0,1},{1,0},{2,3},{3,2},{4,5},{5,4},{6,7},{7,6},{8,9},{9,8},{10,11... | collective-permute-start | bytes 442376 | tf_op jit(solution)/shard_map/ppermute | solution.py:236
  0.5 1.2 %shard_map.91 = (bf16[576,128]{1,0:T(8,128)(2,1)S(1)}, f32[1,128]{1,0:T(1,128)S(1)}, f32[1,128]{1,0:T(1,128)S(1)}) custom-call(bf16[12,48,128]{2,1,0:T(8,128)(2,1)} %pair_hbm.1, f32[1,128]{1,0:T(1,128)} %bitcast.8, f32[1,128]{1,0:T(1,128)} %bitcast.9), custom_call_target="tpu_custom_call" | custom-call | flops 75497472 | bytes 1179648 | tf_op jit(solution)/shard_map/pallas_call | solution.py:238
  1.7 0.0 collective-permute-done.pair_ref
  1.7 0.0 copy-done
  1.7 0.9 %shard_map.92 = (bf16[2,144,128]{2,1,0:T(8,128)(2,1)S(1)}, bf16[2,144,128]{2,1,0:T(8,128)(2,1)S(1)}, bf16[2,144,128]{2,1,0:T(8,128)(2,1)S(1)}, bf16[2,144,128]{2,1,0:T(8,128)(2,1)S(1)}) custom-call(bf16[12,48,128]{2,1,0:T(8,128)(2,1)S(1)} %collective-permute-done.pair_ref, bf16[576,128]{1,0:T(8,128)(2,1)S(1)} %get-tuple-element.17.normed_ref, ...), custom_call_target="tpu_custom_call" | custom-call | flops 75497472 | bytes 1179648 | tf_op jit(solution)/shard_map/pallas_call | solution.py:251
  2.6 3.9 %collective-permute-start.1 = (bf16[2,144,128]{2,1,0:T(8,128)(2,1)S(1)}, bf16[2,144,128]{2,1,0:T(8,128)(2,1)S(1)}, u32[]{:S(2)}, u32[]{:S(2)}) collective-permute-start(bf16[2,144,128]{2,1,0:T(8,128)(2,1)S(1)} %get-tuple-element.20), channel_id=1, source_target_pairs={{0,6},{2,4},{4,2},{6,0},{1,7},{3,5},{5,3},{7,1},{8,14},{10,12},{12... | collective-permute-start | bytes 221192 | tf_op jit(solution)/shard_map/ppermute | solution.py:271
  6.5 0.5 %collective-permute-start.2 = (bf16[2,144,128]{2,1,0:T(8,128)(2,1)S(1)}, bf16[2,144,128]{2,1,0:T(8,128)(2,1)S(1)}, u32[]{:S(2)}, u32[]{:S(2)}) collective-permute-start(bf16[2,144,128]{2,1,0:T(8,128)(2,1)S(1)} %get-tuple-element.21), channel_id=1, source_target_pairs={{0,2},{2,0},{4,6},{6,4},{1,3},{3,1},{5,7},{7,5},{8,10},{10,8},{12,... | collective-permute-start | bytes 221192 | tf_op jit(solution)/shard_map/ppermute | solution.py:271
  7.0 0.1 collective-permute-start.3
  7.2 0.0 copy-start.3
  7.2 0.7 %copy-done.3 = s32[96]{0:T(128)S(1)} copy-done((s32[96]{0:T(128)S(1)}, s32[96]{0:T(128)}, u32[]{:S(2)}) %copy-start.3) | copy-done | bytes 408
  7.8 0.1 shard_map.93
  8.0 1.2 %collective-permute-done.1.refs_0_ = bf16[2,144,128]{2,1,0:T(8,128)(2,1)S(1)} collective-permute-done((bf16[2,144,128]{2,1,0:T(8,128)(2,1)S(1)}, bf16[2,144,128]{2,1,0:T(8,128)(2,1)S(1)}, u32[]{:S(2)}, u32[]{:S(2)}) %collective-permute-start.1) | collective-permute-done | bytes 73760 | tf_op jit(solution)/shard_map/ppermute | solution.py:271
  9.2 1.7 %collective-permute-done.2.refs_1_ = bf16[2,144,128]{2,1,0:T(8,128)(2,1)S(1)} collective-permute-done((bf16[2,144,128]{2,1,0:T(8,128)(2,1)S(1)}, bf16[2,144,128]{2,1,0:T(8,128)(2,1)S(1)}, u32[]{:S(2)}, u32[]{:S(2)}) %collective-permute-start.2) | collective-permute-done | bytes 73760 | tf_op jit(solution)/shard_map/ppermute | solution.py:271
  10.9 0.5 %collective-permute-done.3.refs_2_ = bf16[2,144,128]{2,1,0:T(8,128)(2,1)S(1)} collective-permute-done((bf16[2,144,128]{2,1,0:T(8,128)(2,1)S(1)}, bf16[2,144,128]{2,1,0:T(8,128)(2,1)S(1)}, u32[]{:S(2)}, u32[]{:S(2)}) %collective-permute-start.3) | collective-permute-done | bytes 73760 | tf_op jit(solution)/shard_map/ppermute | solution.py:271
  11.4 1.6 %shard_map.94 = bf16[16,72,128]{2,1,0:T(8,128)(2,1)} custom-call(bf16[2,144,128]{2,1,0:T(8,128)(2,1)S(1)} %collective-permute-done.1.refs_0_, bf16[2,144,128]{2,1,0:T(8,128)(2,1)S(1)} %collective-permute-done.2.refs_1_, bf16[2,144,128]{2,1,0:T(8,128)(2,1)S(1)} %collective-permute-done.3.refs_2_, ...), custom_call_target="tpu_custom_call" | custom-call | tf_op jit(solution)/shard_map/pallas_call | solution.py:272
  13.0 5.3 %all-to-all-start = ((bf16[16,72,128]{2,1,0:T(8,128)(2,1)}), bf16[16,72,128]{2,1,0:T(8,128)(2,1)S(1)}, u32[]{:S(2)}, u32[]{:S(2)}) async-start(bf16[16,72,128]{2,1,0:T(8,128)(2,1)} %shard_map.94), calls=%async_computation | async-start | bytes 589824 | tf_op jit(solution)/shard_map/all_to_all | solution.py:291
  18.3 0.0 copy-start.5
  18.3 0.0 copy-done.2
  18.3 0.6 %copy-done.4 = f32[128]{0:T(128)S(1)} copy-done((f32[128]{0:T(128)S(1)}, f32[128]{0:T(128)}, u32[]{:S(2)}) %copy-start.4) | copy-done | bytes 536
  18.9 0.0 copy-done.5
  19.0 0.2 shard_map.95
  19.2 6.5 %all-to-all-done.total_ref = bf16[16,72,128]{2,1,0:T(8,128)(2,1)S(1)} async-done(((bf16[16,72,128]{2,1,0:T(8,128)(2,1)}), bf16[16,72,128]{2,1,0:T(8,128)(2,1)S(1)}, u32[]{:S(2)}, u32[]{:S(2)}) %all-to-all-start) | async-done | bytes 294944 | tf_op jit(solution)/shard_map/all_to_all | solution.py:291
  25.7 0.0 copy-done.1
  25.7 1.0 %shard_map.96 = bf16[12,48,128]{2,1,0:T(8,128)(2,1)} custom-call(bf16[16,72,128]{2,1,0:T(8,128)(2,1)S(1)} %all-to-all-done.total_ref, f32[576,128]{1,0:T(8,128)S(1)} %get-tuple-element.26.gate_ref, f32[128,1]{1,0:T(8,128)S(1)} %get-tuple-element.27.gain_ref, f32[128,1]{1,0:T(8,128)S(1)} %get-tuple-element.28.bias_ref, bf16[128,128]{1,0:T(8,128)(2,1)S(1)} %copy-done.1), custom_call_target="tpu_custom_call" | custom-call | tf_op jit(solution)/shard_map/pallas_call | solution.py:292
  (4 shorter events, 0.0 us)
Async XLA Ops:
  0.0 1.7 %collective-permute-start = (bf16[12,48,128]{2,1,0:T(8,128)(2,1)}, bf16[12,48,128]{2,1,0:T(8,128)(2,1)S(1)}, u32[]{:S(2)}, u32[]{:S(2)}) collective-permute-start(bf16[12,48,128]{2,1,0:T(8,128)(2,1)} %pair_hbm.1), channel_id=1, source_target_pairs={{0,1},{1,0},{2,3},{3,2},{4,5},{5,4},{6,7},{7,6},{8,9},{9,8},{10,11... | collective-permute-start | bytes 442376 | tf_op jit(solution)/shard_map/ppermute | solution.py:236
  0.5 1.2 %copy-start = (bf16[128,512]{1,0:T(8,128)(2,1)S(1)}, bf16[128,512]{1,0:T(8,128)(2,1)}, u32[]{:S(2)}) copy-start(bf16[128,512]{1,0:T(8,128)(2,1)} %w_ref.3) | copy-start | bytes 393220
  2.6 6.6 %collective-permute-start.1 = (bf16[2,144,128]{2,1,0:T(8,128)(2,1)S(1)}, bf16[2,144,128]{2,1,0:T(8,128)(2,1)S(1)}, u32[]{:S(2)}, u32[]{:S(2)}) collective-permute-start(bf16[2,144,128]{2,1,0:T(8,128)(2,1)S(1)} %get-tuple-element.20), channel_id=1, source_target_pairs={{0,6},{2,4},{4,2},{6,0},{1,7},{3,5},{5,3},{7,1},{8,14},{10,12},{12... | collective-permute-start | bytes 221192 | tf_op jit(solution)/shard_map/ppermute | solution.py:271
  6.5 4.4 %collective-permute-start.2 = (bf16[2,144,128]{2,1,0:T(8,128)(2,1)S(1)}, bf16[2,144,128]{2,1,0:T(8,128)(2,1)S(1)}, u32[]{:S(2)}, u32[]{:S(2)}) collective-permute-start(bf16[2,144,128]{2,1,0:T(8,128)(2,1)S(1)} %get-tuple-element.21), channel_id=1, source_target_pairs={{0,2},{2,0},{4,6},{6,4},{1,3},{3,1},{5,7},{7,5},{8,10},{10,8},{12,... | collective-permute-start | bytes 221192 | tf_op jit(solution)/shard_map/ppermute | solution.py:271
  7.0 4.4 %collective-permute-start.3 = (bf16[2,144,128]{2,1,0:T(8,128)(2,1)S(1)}, bf16[2,144,128]{2,1,0:T(8,128)(2,1)S(1)}, u32[]{:S(2)}, u32[]{:S(2)}) collective-permute-start(bf16[2,144,128]{2,1,0:T(8,128)(2,1)S(1)} %get-tuple-element.22), channel_id=1, source_target_pairs={{0,4},{2,6},{4,0},{6,2},{1,5},{3,7},{5,1},{7,3},{8,12},{10,14},{12... | collective-permute-start | bytes 221192 | tf_op jit(solution)/shard_map/ppermute | solution.py:271
  7.2 0.7 %copy-start.3 = (s32[96]{0:T(128)S(1)}, s32[96]{0:T(128)}, u32[]{:S(2)}) copy-start(s32[96]{0:T(128)} %param.10) | copy-start | bytes 1156
  13.0 5.3 %copy-start.2 = (bf16[128,128]{1,0:T(8,128)(2,1)S(1)}, bf16[128,128]{1,0:T(8,128)(2,1)}, u32[]{:S(2)}) copy-start(bf16[128,128]{1,0:T(8,128)(2,1)} %w_ref.4) | copy-start | bytes 98308
  13.0 12.7 %all-to-all-start = ((bf16[16,72,128]{2,1,0:T(8,128)(2,1)}), bf16[16,72,128]{2,1,0:T(8,128)(2,1)S(1)}, u32[]{:S(2)}, u32[]{:S(2)}) async-start(bf16[16,72,128]{2,1,0:T(8,128)(2,1)} %shard_map.94), calls=%async_computation | async-start | bytes 589824 | tf_op jit(solution)/shard_map/all_to_all | solution.py:291
  18.3 0.7 %copy-start.4 = (f32[128]{0:T(128)S(1)}, f32[128]{0:T(128)}, u32[]{:S(2)}) copy-start(f32[128]{0:T(128)} %param.15) | copy-start | bytes 1540
  18.3 0.7 %copy-start.5 = (f32[128]{0:T(128)S(1)}, f32[128]{0:T(128)}, u32[]{:S(2)}) copy-start(f32[128]{0:T(128)} %param.16) | copy-start | bytes 1540
  19.0 6.7 %copy-start.1 = (bf16[128,128]{1,0:T(8,128)(2,1)S(1)}, bf16[128,128]{1,0:T(8,128)(2,1)}, u32[]{:S(2)}) copy-start(bf16[128,128]{1,0:T(8,128)(2,1)} %w_ref.5) | copy-start | bytes 98308

commit v25 on v21

--- a/solution.py
+++ b/solution.py
@@ -168,6 +168,7 @@
         return jnp.concatenate([jnp.zeros((piece, lanes), jnp.bfloat16) if isinstance(piece, int) else piece for piece in pieces], axis=0)
 
     contract = (((1,), (1,)), ((), ()))
+    lane_block = lax.broadcasted_iota(jnp.int32, (group, LANES), 1) // rest
     mains, lasts = [], []
     for part in range(parts):
         left, right = side(0, part), side(1, part).astype(jnp.bfloat16)
@@ -183,14 +184,19 @@
         ]
         weights = jnp.concatenate(weights, axis=1)
         mains.append(lax.dot_general(left, weights, contract, preferred_element_type=jnp.float32))
-        weights = jnp.concatenate([mine[spare:] for mine in ours], axis=0)
+        gap = LANES // parts
+        pieces = [[gap * part] + [mine[spare:]] * whole + [LANES - gap * (part + 1)] for mine in ours]
+        weights = placed([p for piece in pieces for p in piece if not isinstance(p, int) or p])
         lasts.append(lax.dot_general(left[:, 2 * lanes :], weights, contract, preferred_element_type=jnp.float32))
     for target, device in enumerate(far_order):
         row, col = divmod(device, cols)
         spots = [(row * whole + t) * group for t in range(whole)]
         tiles = [main[at : at + group, col * LANES : (col + 1) * LANES] for at in spots for main in mains]
-        last = [part[at : at + group, col * rest : (col + 1) * rest] for part in lasts for at in spots]
-        tiles.append(jnp.concatenate(last, axis=1))
+        last = [part[at : at + group, col * LANES : (col + 1) * LANES] for part in lasts for at in spots]
+        tile = last[0]
+        for n in range(1, len(last)):
+            tile = jnp.where(lane_block >= n, last[n], tile)
+        tiles.append(tile)
         total_ref[target] = jnp.concatenate(tiles, axis=0).astype(jnp.bfloat16)
 
 
@@ -270,7 +276,7 @@
         compiler_params=LIMIT,
         cost_estimate=cost,
     )(other_pair, sides, gain_in, bias_in, w_ours)
-    steps = [3, 1, 2, 0]
+    steps = [3, 2, 1, 0]
     got = [lax.ppermute(pieces[step], "quad", [(i, i ^ step) for i in range(quads)]) if step else pieces[0] for step in steps]
     total = pl.pallas_call(
         functools.partial(triangle_kernel, far_order, steps, cols, row_count, col_count, share),

time: 26.8 us -> 27.4 us (1.022)
  starting transfers between devices: 9.97 us -> 10.8 us
    all_to_all x1, starting transfers between devices: 5.28 us -> 6.12 us  [per_device(): lax.all_to_all(total, ('half', 'quad', 'col'), split_axis=0, concat_axis=...]
where the time goes in v25:
time: 27.4 us; the launch traced here: 27.2 us
  starting transfers between devices  10.8 us (39%)
  waiting for transfers between devices  10.6 us (39%)
  Pallas kernels  5.05 us (18%)
  local copies, waits for them, and re-layouts  0.65 us (2%)
    all_to_all x1, waiting for transfers between devices, per_device(): lax.all_to_all(total, ('half', 'quad', 'col'), split_axis=0, concat_axis=...  6.42 us
    all_to_all x1, starting transfers between devices, per_device(): lax.all_to_all(total, ('half', 'quad', 'col'), split_axis=0, concat_axis=...  6.12 us
    ppermute x3, starting transfers between devices, per_device(): lax.ppermute(pieces[step], 'quad', [(i, i ^ step) for i in range(quads)])  4.24 us
    ppermute x3, waiting for transfers between devices, per_device(): lax.ppermute(pieces[step], 'quad', [(i, i ^ step) for i in range(quads)])  4.16 us
    pallas_call x1, Pallas kernels, per_device(): pl.pallas_call(functools.partial(own_kernel, quads, cols), out_shape=(jax...  1.7 us
    pallas_call x1, Pallas kernels, per_device(): pl.pallas_call(functools.partial(triangle_kernel, far_order, steps, cols,...  1.58 us
    pallas_call x1, Pallas kernels, per_device(): pl.pallas_call(functools.partial(output_kernel, far_order, near_order), o...  1.02 us
    unnamed x8, local copies, waits for them, and re-layouts  0.65 us
  transfers between devices with their start and end apart: 5, of which 4 were waited for; matrix products, arithmetic and copies ran while one was open for 0% of the time, Pallas kernels for 7%

profile of v25, /device:TPU:0, one launch (start us, length us, event | category | flops | bytes accessed | tf_op | source)
XLA Modules:
  0.0 27.2 jit_solution(11931700687358256088)
XLA Ops:
  0.0 0.5 %collective-permute-start = (bf16[12,48,128]{2,1,0:T(8,128)(2,1)}, bf16[12,48,128]{2,1,0:T(8,128)(2,1)S(1)}, u32[]{:S(2)}, u32[]{:S(2)}) collective-permute-start(bf16[12,48,128]{2,1,0:T(8,128)(2,1)} %pair_hbm.1), channel_id=1, source_target_pairs={{0,1},{1,0},{2,3},{3,2},{4,5},{5,4},{6,7},{7,6},{8,9},{9,8},{10,11... | collective-permute-start | bytes 442376 | tf_op jit(solution)/shard_map/ppermute | solution.py:245
  0.5 1.7 %shard_map.91 = (bf16[4,144,128]{2,1,0:T(8,128)(2,1)S(1)}, bf16[576,128]{1,0:T(8,128)(2,1)S(1)}, f32[8,384]{1,0:T(8,128)S(1)}, f32[96,1]{1,0:T(8,128)S(1)}, bf16...) custom-call(bf16[12,48,128]{2,1,0:T(8,128)(2,1)} %pair_hbm.1, f32[1,128]{1,0:T(1,128)} %bitcast.7, ...), custom_call_target="tpu_custom_call" | custom-call | flops 75497472 | bytes 1179648 | tf_op jit(solution)/shard_map/pallas_call | solution.py:247
  2.2 0.0 collective-permute-done.pair_ref
  2.2 0.6 %shard_map.92 = (bf16[2,144,128]{2,1,0:T(8,128)(2,1)S(1)}, bf16[2,144,128]{2,1,0:T(8,128)(2,1)S(1)}, bf16[2,144,128]{2,1,0:T(8,128)(2,1)S(1)}, bf16[2,144,128]{2,1,0:T(8,128)(2,1)S(1)}) custom-call(bf16[12,48,128]{2,1,0:T(8,128)(2,1)S(1)} %collective-permute-done.pair_ref, bf16[4,144,128]{2,1,0:T(8,128)(2,1)S(1)} %get-tuple-element.19.sides_ref, ...), custom_call_target="tpu_custom_call" | custom-call | flops 75497472 | bytes 1179648 | tf_op jit(solution)/shard_map/pallas_call | solution.py:270
  2.7 3.6 %collective-permute-start.1 = (bf16[2,144,128]{2,1,0:T(8,128)(2,1)S(1)}, bf16[2,144,128]{2,1,0:T(8,128)(2,1)S(1)}, u32[]{:S(2)}, u32[]{:S(2)}) collective-permute-start(bf16[2,144,128]{2,1,0:T(8,128)(2,1)S(1)} %get-tuple-element.23), channel_id=1, source_target_pairs={{0,6},{2,4},{4,2},{6,0},{1,7},{3,5},{5,3},{7,1},{8,14},{10,12},{12... | collective-permute-start | bytes 221192 | tf_op jit(solution)/shard_map/ppermute | solution.py:280
  6.3 0.4 %collective-permute-start.2 = (bf16[2,144,128]{2,1,0:T(8,128)(2,1)S(1)}, bf16[2,144,128]{2,1,0:T(8,128)(2,1)S(1)}, u32[]{:S(2)}, u32[]{:S(2)}) collective-permute-start(bf16[2,144,128]{2,1,0:T(8,128)(2,1)S(1)} %get-tuple-element.24), channel_id=1, source_target_pairs={{0,4},{2,6},{4,0},{6,2},{1,5},{3,7},{5,1},{7,3},{8,12},{10,14},{12... | collective-permute-start | bytes 221192 | tf_op jit(solution)/shard_map/ppermute | solution.py:280
  6.8 0.2 collective-permute-start.3
  7.0 2.4 %collective-permute-done.1.refs_0_ = bf16[2,144,128]{2,1,0:T(8,128)(2,1)S(1)} collective-permute-done((bf16[2,144,128]{2,1,0:T(8,128)(2,1)S(1)}, bf16[2,144,128]{2,1,0:T(8,128)(2,1)S(1)}, u32[]{:S(2)}, u32[]{:S(2)}) %collective-permute-start.1) | collective-permute-done | bytes 73760 | tf_op jit(solution)/shard_map/ppermute | solution.py:280
  9.4 1.6 %collective-permute-done.2.refs_1_ = bf16[2,144,128]{2,1,0:T(8,128)(2,1)S(1)} collective-permute-done((bf16[2,144,128]{2,1,0:T(8,128)(2,1)S(1)}, bf16[2,144,128]{2,1,0:T(8,128)(2,1)S(1)}, u32[]{:S(2)}, u32[]{:S(2)}) %collective-permute-start.2) | collective-permute-done | bytes 73760 | tf_op jit(solution)/shard_map/ppermute | solution.py:280
  11.0 0.1 collective-permute-done.3.refs_2_
  11.1 1.6 %shard_map.93 = bf16[16,72,128]{2,1,0:T(8,128)(2,1)} custom-call(bf16[2,144,128]{2,1,0:T(8,128)(2,1)S(1)} %collective-permute-done.1.refs_0_, bf16[2,144,128]{2,1,0:T(8,128)(2,1)S(1)} %collective-permute-done.2.refs_1_, bf16[2,144,128]{2,1,0:T(8,128)(2,1)S(1)} %collective-permute-done.3.refs_2_, bf16[2,144,128]{2,1,0:T(8,128)(2,1)S(1)} %get-tuple-element.26.refs_3_, ...), custom_call_target="tpu_custom_call" | custom-call | tf_op jit(solution)/shard_map/pallas_call | solution.py:281
  12.7 0.0 copy-start.1
  12.7 6.1 %all-to-all-start = ((bf16[16,72,128]{2,1,0:T(8,128)(2,1)}), bf16[16,72,128]{2,1,0:T(8,128)(2,1)S(1)}, u32[]{:S(2)}, u32[]{:S(2)}) async-start(bf16[16,72,128]{2,1,0:T(8,128)(2,1)} %shard_map.93), calls=%async_computation | async-start | bytes 589824 | tf_op jit(solution)/shard_map/all_to_all | solution.py:300
  18.8 0.0 copy-start.2
  18.9 0.0 copy-start.3
  18.9 0.0 copy-done.1
  18.9 0.6 %copy-done.2 = f32[128]{0:T(128)S(1)} copy-done((f32[128]{0:T(128)S(1)}, f32[128]{0:T(128)}, u32[]{:S(2)}) %copy-start.2) | copy-done | bytes 536
  19.5 0.0 copy-done.3
  19.5 0.0 copy-start
  19.5 0.2 shard_map.94
  19.7 6.4 %all-to-all-done.total_ref = bf16[16,72,128]{2,1,0:T(8,128)(2,1)S(1)} async-done(((bf16[16,72,128]{2,1,0:T(8,128)(2,1)}), bf16[16,72,128]{2,1,0:T(8,128)(2,1)S(1)}, u32[]{:S(2)}, u32[]{:S(2)}) %all-to-all-start) | async-done | bytes 294944 | tf_op jit(solution)/shard_map/all_to_all | solution.py:300
  26.1 0.0 copy-done
  26.1 1.0 %shard_map.95 = bf16[12,48,128]{2,1,0:T(8,128)(2,1)} custom-call(bf16[16,72,128]{2,1,0:T(8,128)(2,1)S(1)} %all-to-all-done.total_ref, f32[576,128]{1,0:T(8,128)S(1)} %get-tuple-element.30.gate_ref, f32[128,1]{1,0:T(8,128)S(1)} %get-tuple-element.31.gain_ref, f32[128,1]{1,0:T(8,128)S(1)} %get-tuple-element.32.bias_ref, bf16[128,128]{1,0:T(8,128)(2,1)S(1)} %copy-done), custom_call_target="tpu_custom_call" | custom-call | tf_op jit(solution)/shard_map/pallas_call | solution.py:301
Async XLA Ops:
  0.0 2.2 %collective-permute-start = (bf16[12,48,128]{2,1,0:T(8,128)(2,1)}, bf16[12,48,128]{2,1,0:T(8,128)(2,1)S(1)}, u32[]{:S(2)}, u32[]{:S(2)}) collective-permute-start(bf16[12,48,128]{2,1,0:T(8,128)(2,1)} %pair_hbm.1), channel_id=1, source_target_pairs={{0,1},{1,0},{2,3},{3,2},{4,5},{5,4},{6,7},{7,6},{8,9},{9,8},{10,11... | collective-permute-start | bytes 442376 | tf_op jit(solution)/shard_map/ppermute | solution.py:245
  2.7 6.7 %collective-permute-start.1 = (bf16[2,144,128]{2,1,0:T(8,128)(2,1)S(1)}, bf16[2,144,128]{2,1,0:T(8,128)(2,1)S(1)}, u32[]{:S(2)}, u32[]{:S(2)}) collective-permute-start(bf16[2,144,128]{2,1,0:T(8,128)(2,1)S(1)} %get-tuple-element.23), channel_id=1, source_target_pairs={{0,6},{2,4},{4,2},{6,0},{1,7},{3,5},{5,3},{7,1},{8,14},{10,12},{12... | collective-permute-start | bytes 221192 | tf_op jit(solution)/shard_map/ppermute | solution.py:280
  6.3 4.7 %collective-permute-start.2 = (bf16[2,144,128]{2,1,0:T(8,128)(2,1)S(1)}, bf16[2,144,128]{2,1,0:T(8,128)(2,1)S(1)}, u32[]{:S(2)}, u32[]{:S(2)}) collective-permute-start(bf16[2,144,128]{2,1,0:T(8,128)(2,1)S(1)} %get-tuple-element.24), channel_id=1, source_target_pairs={{0,4},{2,6},{4,0},{6,2},{1,5},{3,7},{5,1},{7,3},{8,12},{10,14},{12... | collective-permute-start | bytes 221192 | tf_op jit(solution)/shard_map/ppermute | solution.py:280
  6.8 4.4 %collective-permute-start.3 = (bf16[2,144,128]{2,1,0:T(8,128)(2,1)S(1)}, bf16[2,144,128]{2,1,0:T(8,128)(2,1)S(1)}, u32[]{:S(2)}, u32[]{:S(2)}) collective-permute-start(bf16[2,144,128]{2,1,0:T(8,128)(2,1)S(1)} %get-tuple-element.25), channel_id=1, source_target_pairs={{0,2},{2,0},{4,6},{6,4},{1,3},{3,1},{5,7},{7,5},{8,10},{10,8},{12,... | collective-permute-start | bytes 221192 | tf_op jit(solution)/shard_map/ppermute | solution.py:280
  12.7 6.1 %copy-start.1 = (bf16[128,128]{1,0:T(8,128)(2,1)S(1)}, bf16[128,128]{1,0:T(8,128)(2,1)}, u32[]{:S(2)}) copy-start(bf16[128,128]{1,0:T(8,128)(2,1)} %w_ref.2) | copy-start | bytes 98308
  12.7 13.4 %all-to-all-start = ((bf16[16,72,128]{2,1,0:T(8,128)(2,1)}), bf16[16,72,128]{2,1,0:T(8,128)(2,1)S(1)}, u32[]{:S(2)}, u32[]{:S(2)}) async-start(bf16[16,72,128]{2,1,0:T(8,128)(2,1)} %shard_map.93), calls=%async_computation | async-start | bytes 589824 | tf_op jit(solution)/shard_map/all_to_all | solution.py:300
  18.8 0.7 %copy-start.2 = (f32[128]{0:T(128)S(1)}, f32[128]{0:T(128)}, u32[]{:S(2)}) copy-start(f32[128]{0:T(128)} %param.15) | copy-start | bytes 1540
  18.9 0.7 %copy-start.3 = (f32[128]{0:T(128)S(1)}, f32[128]{0:T(128)}, u32[]{:S(2)}) copy-start(f32[128]{0:T(128)} %param.16) | copy-start | bytes 1540
  19.5 6.6 %copy-start = (bf16[128,128]{1,0:T(8,128)(2,1)S(1)}, bf16[128,128]{1,0:T(8,128)(2,1)}, u32[]{:S(2)}) copy-start(bf16[128,128]{1,0:T(8,128)(2,1)} %w_ref.3) | copy-start | bytes 98308

commit v26 on v25

--- a/solution.py
+++ b/solution.py
@@ -276,7 +276,7 @@
         compiler_params=LIMIT,
         cost_estimate=cost,
     )(other_pair, sides, gain_in, bias_in, w_ours)
-    steps = [3, 2, 1, 0]
+    steps = [3, 1, 2, 0]
     got = [lax.ppermute(pieces[step], "quad", [(i, i ^ step) for i in range(quads)]) if step else pieces[0] for step in steps]
     total = pl.pallas_call(
         functools.partial(triangle_kernel, far_order, steps, cols, row_count, col_count, share),

time: 27.4 us -> 26.8 us (0.978)
  starting transfers between devices: 10.8 us -> 9.97 us
    all_to_all x1, starting transfers between devices: 6.12 us -> 5.28 us  [per_device(): lax.all_to_all(total, ('half', 'quad', 'col'), split_axis=0, concat_axis=...]
where the time goes in v26:
time: 26.8 us; the launch traced here: 26.5 us
  waiting for transfers between devices  10.7 us (40%)
  starting transfers between devices  9.97 us (37%)
  Pallas kernels  5.05 us (19%)
  local copies, waits for them, and re-layouts  0.65 us (2%)
    all_to_all x1, waiting for transfers between devices, per_device(): lax.all_to_all(total, ('half', 'quad', 'col'), split_axis=0, concat_axis=...  6.52 us
    all_to_all x1, starting transfers between devices, per_device(): lax.all_to_all(total, ('half', 'quad', 'col'), split_axis=0, concat_axis=...  5.28 us
    ppermute x3, starting transfers between devices, per_device(): lax.ppermute(pieces[step], 'quad', [(i, i ^ step) for i in range(quads)])  4.24 us
    ppermute x3, waiting for transfers between devices, per_device(): lax.ppermute(pieces[step], 'quad', [(i, i ^ step) for i in range(quads)])  4.22 us
    pallas_call x1, Pallas kernels, per_device(): pl.pallas_call(functools.partial(own_kernel, quads, cols), out_shape=(jax...  1.7 us
    pallas_call x1, Pallas kernels, per_device(): pl.pallas_call(functools.partial(triangle_kernel, far_order, steps, cols,...  1.58 us
    pallas_call x1, Pallas kernels, per_device(): pl.pallas_call(functools.partial(output_kernel, far_order, near_order), o...  1.02 us
    unnamed x8, local copies, waits for them, and re-layouts  0.65 us
  transfers between devices with their start and end apart: 5, of which 4 were waited for; matrix products, arithmetic and copies ran while one was open for 0% of the time, Pallas kernels for 7%

profile of v26, /device:TPU:0, one launch (start us, length us, event | category | flops | bytes accessed | tf_op | source)
XLA Modules:
  0.0 26.5 jit_solution(9988370326133110092)
XLA Ops:
  0.0 0.5 %collective-permute-start = (bf16[12,48,128]{2,1,0:T(8,128)(2,1)}, bf16[12,48,128]{2,1,0:T(8,128)(2,1)S(1)}, u32[]{:S(2)}, u32[]{:S(2)}) collective-permute-start(bf16[12,48,128]{2,1,0:T(8,128)(2,1)} %pair_hbm.1), channel_id=1, source_target_pairs={{0,1},{1,0},{2,3},{3,2},{4,5},{5,4},{6,7},{7,6},{8,9},{9,8},{10,11... | collective-permute-start | bytes 442376 | tf_op jit(solution)/shard_map/ppermute | solution.py:245
  0.5 1.7 %shard_map.91 = (bf16[4,144,128]{2,1,0:T(8,128)(2,1)S(1)}, bf16[576,128]{1,0:T(8,128)(2,1)S(1)}, f32[8,384]{1,0:T(8,128)S(1)}, f32[96,1]{1,0:T(8,128)S(1)}, bf16...) custom-call(bf16[12,48,128]{2,1,0:T(8,128)(2,1)} %pair_hbm.1, f32[1,128]{1,0:T(1,128)} %bitcast.7, ...), custom_call_target="tpu_custom_call" | custom-call | flops 75497472 | bytes 1179648 | tf_op jit(solution)/shard_map/pallas_call | solution.py:247
  2.2 0.0 collective-permute-done.pair_ref
  2.2 0.6 %shard_map.92 = (bf16[2,144,128]{2,1,0:T(8,128)(2,1)S(1)}, bf16[2,144,128]{2,1,0:T(8,128)(2,1)S(1)}, bf16[2,144,128]{2,1,0:T(8,128)(2,1)S(1)}, bf16[2,144,128]{2,1,0:T(8,128)(2,1)S(1)}) custom-call(bf16[12,48,128]{2,1,0:T(8,128)(2,1)S(1)} %collective-permute-done.pair_ref, bf16[4,144,128]{2,1,0:T(8,128)(2,1)S(1)} %get-tuple-element.19.sides_ref, ...), custom_call_target="tpu_custom_call" | custom-call | flops 75497472 | bytes 1179648 | tf_op jit(solution)/shard_map/pallas_call | solution.py:270
  2.7 3.6 %collective-permute-start.1 = (bf16[2,144,128]{2,1,0:T(8,128)(2,1)S(1)}, bf16[2,144,128]{2,1,0:T(8,128)(2,1)S(1)}, u32[]{:S(2)}, u32[]{:S(2)}) collective-permute-start(bf16[2,144,128]{2,1,0:T(8,128)(2,1)S(1)} %get-tuple-element.23), channel_id=1, source_target_pairs={{0,6},{2,4},{4,2},{6,0},{1,7},{3,5},{5,3},{7,1},{8,14},{10,12},{12... | collective-permute-start | bytes 221192 | tf_op jit(solution)/shard_map/ppermute | solution.py:280
  6.3 0.5 %collective-permute-start.2 = (bf16[2,144,128]{2,1,0:T(8,128)(2,1)S(1)}, bf16[2,144,128]{2,1,0:T(8,128)(2,1)S(1)}, u32[]{:S(2)}, u32[]{:S(2)}) collective-permute-start(bf16[2,144,128]{2,1,0:T(8,128)(2,1)S(1)} %get-tuple-element.24), channel_id=1, source_target_pairs={{0,2},{2,0},{4,6},{6,4},{1,3},{3,1},{5,7},{7,5},{8,10},{10,8},{12,... | collective-permute-start | bytes 221192 | tf_op jit(solution)/shard_map/ppermute | solution.py:280
  6.8 0.1 collective-permute-start.3
  7.0 2.3 %collective-permute-done.1.refs_0_ = bf16[2,144,128]{2,1,0:T(8,128)(2,1)S(1)} collective-permute-done((bf16[2,144,128]{2,1,0:T(8,128)(2,1)S(1)}, bf16[2,144,128]{2,1,0:T(8,128)(2,1)S(1)}, u32[]{:S(2)}, u32[]{:S(2)}) %collective-permute-start.1) | collective-permute-done | bytes 73760 | tf_op jit(solution)/shard_map/ppermute | solution.py:280
  9.3 1.6 %collective-permute-done.2.refs_1_ = bf16[2,144,128]{2,1,0:T(8,128)(2,1)S(1)} collective-permute-done((bf16[2,144,128]{2,1,0:T(8,128)(2,1)S(1)}, bf16[2,144,128]{2,1,0:T(8,128)(2,1)S(1)}, u32[]{:S(2)}, u32[]{:S(2)}) %collective-permute-start.2) | collective-permute-done | bytes 73760 | tf_op jit(solution)/shard_map/ppermute | solution.py:280
  10.9 0.3 %collective-permute-done.3.refs_2_ = bf16[2,144,128]{2,1,0:T(8,128)(2,1)S(1)} collective-permute-done((bf16[2,144,128]{2,1,0:T(8,128)(2,1)S(1)}, bf16[2,144,128]{2,1,0:T(8,128)(2,1)S(1)}, u32[]{:S(2)}, u32[]{:S(2)}) %collective-permute-start.3) | collective-permute-done | bytes 73760 | tf_op jit(solution)/shard_map/ppermute | solution.py:280
  11.2 1.6 %shard_map.93 = bf16[16,72,128]{2,1,0:T(8,128)(2,1)} custom-call(bf16[2,144,128]{2,1,0:T(8,128)(2,1)S(1)} %collective-permute-done.1.refs_0_, bf16[2,144,128]{2,1,0:T(8,128)(2,1)S(1)} %collective-permute-done.2.refs_1_, bf16[2,144,128]{2,1,0:T(8,128)(2,1)S(1)} %collective-permute-done.3.refs_2_, bf16[2,144,128]{2,1,0:T(8,128)(2,1)S(1)} %get-tuple-element.26.refs_3_, ...), custom_call_target="tpu_custom_call" | custom-call | tf_op jit(solution)/shard_map/pallas_call | solution.py:281
  12.8 0.0 copy-start.1
  12.8 5.3 %all-to-all-start = ((bf16[16,72,128]{2,1,0:T(8,128)(2,1)}), bf16[16,72,128]{2,1,0:T(8,128)(2,1)S(1)}, u32[]{:S(2)}, u32[]{:S(2)}) async-start(bf16[16,72,128]{2,1,0:T(8,128)(2,1)} %shard_map.93), calls=%async_computation | async-start | bytes 589824 | tf_op jit(solution)/shard_map/all_to_all | solution.py:300
  18.1 0.0 copy-start.2
  18.1 0.0 copy-start.3
  18.1 0.0 copy-done.1
  18.1 0.6 %copy-done.2 = f32[128]{0:T(128)S(1)} copy-done((f32[128]{0:T(128)S(1)}, f32[128]{0:T(128)}, u32[]{:S(2)}) %copy-start.2) | copy-done | bytes 536
  18.7 0.0 copy-done.3
  18.7 0.0 copy-start
  18.7 0.2 shard_map.94
  18.9 6.5 %all-to-all-done.total_ref = bf16[16,72,128]{2,1,0:T(8,128)(2,1)S(1)} async-done(((bf16[16,72,128]{2,1,0:T(8,128)(2,1)}), bf16[16,72,128]{2,1,0:T(8,128)(2,1)S(1)}, u32[]{:S(2)}, u32[]{:S(2)}) %all-to-all-start) | async-done | bytes 294944 | tf_op jit(solution)/shard_map/all_to_all | solution.py:300
  25.5 0.0 copy-done
  25.5 1.0 %shard_map.95 = bf16[12,48,128]{2,1,0:T(8,128)(2,1)} custom-call(bf16[16,72,128]{2,1,0:T(8,128)(2,1)S(1)} %all-to-all-done.total_ref, f32[576,128]{1,0:T(8,128)S(1)} %get-tuple-element.30.gate_ref, f32[128,1]{1,0:T(8,128)S(1)} %get-tuple-element.31.gain_ref, f32[128,1]{1,0:T(8,128)S(1)} %get-tuple-element.32.bias_ref, bf16[128,128]{1,0:T(8,128)(2,1)S(1)} %copy-done), custom_call_target="tpu_custom_call" | custom-call | tf_op jit(solution)/shard_map/pallas_call | solution.py:301
Async XLA Ops:
  0.0 2.2 %collective-permute-start = (bf16[12,48,128]{2,1,0:T(8,128)(2,1)}, bf16[12,48,128]{2,1,0:T(8,128)(2,1)S(1)}, u32[]{:S(2)}, u32[]{:S(2)}) collective-permute-start(bf16[12,48,128]{2,1,0:T(8,128)(2,1)} %pair_hbm.1), channel_id=1, source_target_pairs={{0,1},{1,0},{2,3},{3,2},{4,5},{5,4},{6,7},{7,6},{8,9},{9,8},{10,11... | collective-permute-start | bytes 442376 | tf_op jit(solution)/shard_map/ppermute | solution.py:245
  2.7 6.5 %collective-permute-start.1 = (bf16[2,144,128]{2,1,0:T(8,128)(2,1)S(1)}, bf16[2,144,128]{2,1,0:T(8,128)(2,1)S(1)}, u32[]{:S(2)}, u32[]{:S(2)}) collective-permute-start(bf16[2,144,128]{2,1,0:T(8,128)(2,1)S(1)} %get-tuple-element.23), channel_id=1, source_target_pairs={{0,6},{2,4},{4,2},{6,0},{1,7},{3,5},{5,3},{7,1},{8,14},{10,12},{12... | collective-permute-start | bytes 221192 | tf_op jit(solution)/shard_map/ppermute | solution.py:280
  6.3 4.5 %collective-permute-start.2 = (bf16[2,144,128]{2,1,0:T(8,128)(2,1)S(1)}, bf16[2,144,128]{2,1,0:T(8,128)(2,1)S(1)}, u32[]{:S(2)}, u32[]{:S(2)}) collective-permute-start(bf16[2,144,128]{2,1,0:T(8,128)(2,1)S(1)} %get-tuple-element.24), channel_id=1, source_target_pairs={{0,2},{2,0},{4,6},{6,4},{1,3},{3,1},{5,7},{7,5},{8,10},{10,8},{12,... | collective-permute-start | bytes 221192 | tf_op jit(solution)/shard_map/ppermute | solution.py:280
  6.8 4.4 %collective-permute-start.3 = (bf16[2,144,128]{2,1,0:T(8,128)(2,1)S(1)}, bf16[2,144,128]{2,1,0:T(8,128)(2,1)S(1)}, u32[]{:S(2)}, u32[]{:S(2)}) collective-permute-start(bf16[2,144,128]{2,1,0:T(8,128)(2,1)S(1)} %get-tuple-element.25), channel_id=1, source_target_pairs={{0,4},{2,6},{4,0},{6,2},{1,5},{3,7},{5,1},{7,3},{8,12},{10,14},{12... | collective-permute-start | bytes 221192 | tf_op jit(solution)/shard_map/ppermute | solution.py:280
  12.8 5.3 %copy-start.1 = (bf16[128,128]{1,0:T(8,128)(2,1)S(1)}, bf16[128,128]{1,0:T(8,128)(2,1)}, u32[]{:S(2)}) copy-start(bf16[128,128]{1,0:T(8,128)(2,1)} %w_ref.2) | copy-start | bytes 98308
  12.8 12.7 %all-to-all-start = ((bf16[16,72,128]{2,1,0:T(8,128)(2,1)}), bf16[16,72,128]{2,1,0:T(8,128)(2,1)S(1)}, u32[]{:S(2)}, u32[]{:S(2)}) async-start(bf16[16,72,128]{2,1,0:T(8,128)(2,1)} %shard_map.93), calls=%async_computation | async-start | bytes 589824 | tf_op jit(solution)/shard_map/all_to_all | solution.py:300
  18.1 0.7 %copy-start.2 = (f32[128]{0:T(128)S(1)}, f32[128]{0:T(128)}, u32[]{:S(2)}) copy-start(f32[128]{0:T(128)} %param.15) | copy-start | bytes 1540
  18.1 0.7 %copy-start.3 = (f32[128]{0:T(128)S(1)}, f32[128]{0:T(128)}, u32[]{:S(2)}) copy-start(f32[128]{0:T(128)} %param.16) | copy-start | bytes 1540
  18.7 6.7 %copy-start = (bf16[128,128]{1,0:T(8,128)(2,1)S(1)}, bf16[128,128]{1,0:T(8,128)(2,1)}, u32[]{:S(2)}) copy-start(bf16[128,128]{1,0:T(8,128)(2,1)} %w_ref.3) | copy-start | bytes 98308

commit v27 on v26

--- a/solution.py
+++ b/solution.py
@@ -276,7 +276,7 @@
         compiler_params=LIMIT,
         cost_estimate=cost,
     )(other_pair, sides, gain_in, bias_in, w_ours)
-    steps = [3, 1, 2, 0]
+    steps = [1, 3, 2, 0]
     got = [lax.ppermute(pieces[step], "quad", [(i, i ^ step) for i in range(quads)]) if step else pieces[0] for step in steps]
     total = pl.pallas_call(
         functools.partial(triangle_kernel, far_order, steps, cols, row_count, col_count, share),

time: 26.8 us -> 27.7 us (1.034)
  starting transfers between devices: 9.97 us -> 11 us
    all_to_all x1, starting transfers between devices: 5.28 us -> 6.35 us  [per_device(): lax.all_to_all(total, ('half', 'quad', 'col'), split_axis=0, concat_axis=...]
where the time goes in v27:
time: 27.7 us; the launch traced here: 27.4 us
  starting transfers between devices  11 us (40%)
  waiting for transfers between devices  10.7 us (39%)
  Pallas kernels  5.04 us (18%)
  local copies, waits for them, and re-layouts  0.65 us (2%)
    all_to_all x1, waiting for transfers between devices, per_device(): lax.all_to_all(total, ('half', 'quad', 'col'), split_axis=0, concat_axis=...  6.42 us
    all_to_all x1, starting transfers between devices, per_device(): lax.all_to_all(total, ('half', 'quad', 'col'), split_axis=0, concat_axis=...  6.35 us
    ppermute x3, waiting for transfers between devices, per_device(): lax.ppermute(pieces[step], 'quad', [(i, i ^ step) for i in range(quads)])  4.29 us
    ppermute x3, starting transfers between devices, per_device(): lax.ppermute(pieces[step], 'quad', [(i, i ^ step) for i in range(quads)])  4.16 us
    pallas_call x1, Pallas kernels, per_device(): pl.pallas_call(functools.partial(own_kernel, quads, cols), out_shape=(jax...  1.7 us
    pallas_call x1, Pallas kernels, per_device(): pl.pallas_call(functools.partial(triangle_kernel, far_order, steps, cols,...  1.58 us
    pallas_call x1, Pallas kernels, per_device(): pl.pallas_call(functools.partial(output_kernel, far_order, near_order), o...  1.02 us
    unnamed x8, local copies, waits for them, and re-layouts  0.65 us
  transfers between devices with their start and end apart: 5, of which 4 were waited for; matrix products, arithmetic and copies ran while one was open for 0% of the time, Pallas kernels for 7%

profile of v27, /device:TPU:0, one launch (start us, length us, event | category | flops | bytes accessed | tf_op | source)
XLA Modules:
  0.0 27.4 jit_solution(7873869157226451275)
XLA Ops:
  0.0 0.5 %collective-permute-start = (bf16[12,48,128]{2,1,0:T(8,128)(2,1)}, bf16[12,48,128]{2,1,0:T(8,128)(2,1)S(1)}, u32[]{:S(2)}, u32[]{:S(2)}) collective-permute-start(bf16[12,48,128]{2,1,0:T(8,128)(2,1)} %pair_hbm.1), channel_id=1, source_target_pairs={{0,1},{1,0},{2,3},{3,2},{4,5},{5,4},{6,7},{7,6},{8,9},{9,8},{10,11... | collective-permute-start | bytes 442376 | tf_op jit(solution)/shard_map/ppermute | solution.py:245
  0.5 1.7 %shard_map.91 = (bf16[4,144,128]{2,1,0:T(8,128)(2,1)S(1)}, bf16[576,128]{1,0:T(8,128)(2,1)S(1)}, f32[8,384]{1,0:T(8,128)S(1)}, f32[96,1]{1,0:T(8,128)S(1)}, bf16...) custom-call(bf16[12,48,128]{2,1,0:T(8,128)(2,1)} %pair_hbm.1, f32[1,128]{1,0:T(1,128)} %bitcast.7, ...), custom_call_target="tpu_custom_call" | custom-call | flops 75497472 | bytes 1179648 | tf_op jit(solution)/shard_map/pallas_call | solution.py:247
  2.2 0.0 collective-permute-done.pair_ref
  2.2 0.6 %shard_map.92 = (bf16[2,144,128]{2,1,0:T(8,128)(2,1)S(1)}, bf16[2,144,128]{2,1,0:T(8,128)(2,1)S(1)}, bf16[2,144,128]{2,1,0:T(8,128)(2,1)S(1)}, bf16[2,144,128]{2,1,0:T(8,128)(2,1)S(1)}) custom-call(bf16[12,48,128]{2,1,0:T(8,128)(2,1)S(1)} %collective-permute-done.pair_ref, bf16[4,144,128]{2,1,0:T(8,128)(2,1)S(1)} %get-tuple-element.19.sides_ref, ...), custom_call_target="tpu_custom_call" | custom-call | flops 75497472 | bytes 1179648 | tf_op jit(solution)/shard_map/pallas_call | solution.py:270
  2.7 2.6 %collective-permute-start.1 = (bf16[2,144,128]{2,1,0:T(8,128)(2,1)S(1)}, bf16[2,144,128]{2,1,0:T(8,128)(2,1)S(1)}, u32[]{:S(2)}, u32[]{:S(2)}) collective-permute-start(bf16[2,144,128]{2,1,0:T(8,128)(2,1)S(1)} %get-tuple-element.23), channel_id=1, source_target_pairs={{0,2},{2,0},{4,6},{6,4},{1,3},{3,1},{5,7},{7,5},{8,10},{10,8},{12,... | collective-permute-start | bytes 221192 | tf_op jit(solution)/shard_map/ppermute | solution.py:280
  5.3 1.5 %collective-permute-start.2 = (bf16[2,144,128]{2,1,0:T(8,128)(2,1)S(1)}, bf16[2,144,128]{2,1,0:T(8,128)(2,1)S(1)}, u32[]{:S(2)}, u32[]{:S(2)}) collective-permute-start(bf16[2,144,128]{2,1,0:T(8,128)(2,1)S(1)} %get-tuple-element.24), channel_id=1, source_target_pairs={{0,6},{2,4},{4,2},{6,0},{1,7},{3,5},{5,3},{7,1},{8,14},{10,12},{12... | collective-permute-start | bytes 221192 | tf_op jit(solution)/shard_map/ppermute | solution.py:280
  6.8 0.1 collective-permute-start.3
  6.9 2.2 %collective-permute-done.1.refs_0_ = bf16[2,144,128]{2,1,0:T(8,128)(2,1)S(1)} collective-permute-done((bf16[2,144,128]{2,1,0:T(8,128)(2,1)S(1)}, bf16[2,144,128]{2,1,0:T(8,128)(2,1)S(1)}, u32[]{:S(2)}, u32[]{:S(2)}) %collective-permute-start.1) | collective-permute-done | bytes 73760 | tf_op jit(solution)/shard_map/ppermute | solution.py:280
  9.1 1.8 %collective-permute-done.2.refs_1_ = bf16[2,144,128]{2,1,0:T(8,128)(2,1)S(1)} collective-permute-done((bf16[2,144,128]{2,1,0:T(8,128)(2,1)S(1)}, bf16[2,144,128]{2,1,0:T(8,128)(2,1)S(1)}, u32[]{:S(2)}, u32[]{:S(2)}) %collective-permute-start.2) | collective-permute-done | bytes 73760 | tf_op jit(solution)/shard_map/ppermute | solution.py:280
  11.0 0.2 collective-permute-done.3.refs_2_
  11.2 1.6 %shard_map.93 = bf16[16,72,128]{2,1,0:T(8,128)(2,1)} custom-call(bf16[2,144,128]{2,1,0:T(8,128)(2,1)S(1)} %collective-permute-done.1.refs_0_, bf16[2,144,128]{2,1,0:T(8,128)(2,1)S(1)} %collective-permute-done.2.refs_1_, bf16[2,144,128]{2,1,0:T(8,128)(2,1)S(1)} %collective-permute-done.3.refs_2_, bf16[2,144,128]{2,1,0:T(8,128)(2,1)S(1)} %get-tuple-element.26.refs_3_, ...), custom_call_target="tpu_custom_call" | custom-call | tf_op jit(solution)/shard_map/pallas_call | solution.py:281
  12.8 0.0 copy-start.1
  12.8 6.3 %all-to-all-start = ((bf16[16,72,128]{2,1,0:T(8,128)(2,1)}), bf16[16,72,128]{2,1,0:T(8,128)(2,1)S(1)}, u32[]{:S(2)}, u32[]{:S(2)}) async-start(bf16[16,72,128]{2,1,0:T(8,128)(2,1)} %shard_map.93), calls=%async_computation | async-start | bytes 589824 | tf_op jit(solution)/shard_map/all_to_all | solution.py:300
  19.1 0.0 copy-start.2
  19.1 0.0 copy-start.3
  19.1 0.0 copy-done.1
  19.2 0.6 %copy-done.2 = f32[128]{0:T(128)S(1)} copy-done((f32[128]{0:T(128)S(1)}, f32[128]{0:T(128)}, u32[]{:S(2)}) %copy-start.2) | copy-done | bytes 536
  19.8 0.0 copy-done.3
  19.8 0.0 copy-start
  19.8 0.2 shard_map.94
  20.0 6.4 %all-to-all-done.total_ref = bf16[16,72,128]{2,1,0:T(8,128)(2,1)S(1)} async-done(((bf16[16,72,128]{2,1,0:T(8,128)(2,1)}), bf16[16,72,128]{2,1,0:T(8,128)(2,1)S(1)}, u32[]{:S(2)}, u32[]{:S(2)}) %all-to-all-start) | async-done | bytes 294944 | tf_op jit(solution)/shard_map/all_to_all | solution.py:300
  26.4 0.0 copy-done
  26.4 1.0 %shard_map.95 = bf16[12,48,128]{2,1,0:T(8,128)(2,1)} custom-call(bf16[16,72,128]{2,1,0:T(8,128)(2,1)S(1)} %all-to-all-done.total_ref, f32[576,128]{1,0:T(8,128)S(1)} %get-tuple-element.30.gate_ref, f32[128,1]{1,0:T(8,128)S(1)} %get-tuple-element.31.gain_ref, f32[128,1]{1,0:T(8,128)S(1)} %get-tuple-element.32.bias_ref, bf16[128,128]{1,0:T(8,128)(2,1)S(1)} %copy-done), custom_call_target="tpu_custom_call" | custom-call | tf_op jit(solution)/shard_map/pallas_call | solution.py:301
Async XLA Ops:
  0.0 2.2 %collective-permute-start = (bf16[12,48,128]{2,1,0:T(8,128)(2,1)}, bf16[12,48,128]{2,1,0:T(8,128)(2,1)S(1)}, u32[]{:S(2)}, u32[]{:S(2)}) collective-permute-start(bf16[12,48,128]{2,1,0:T(8,128)(2,1)} %pair_hbm.1), channel_id=1, source_target_pairs={{0,1},{1,0},{2,3},{3,2},{4,5},{5,4},{6,7},{7,6},{8,9},{9,8},{10,11... | collective-permute-start | bytes 442376 | tf_op jit(solution)/shard_map/ppermute | solution.py:245
  2.7 6.4 %collective-permute-start.1 = (bf16[2,144,128]{2,1,0:T(8,128)(2,1)S(1)}, bf16[2,144,128]{2,1,0:T(8,128)(2,1)S(1)}, u32[]{:S(2)}, u32[]{:S(2)}) collective-permute-start(bf16[2,144,128]{2,1,0:T(8,128)(2,1)S(1)} %get-tuple-element.23), channel_id=1, source_target_pairs={{0,2},{2,0},{4,6},{6,4},{1,3},{3,1},{5,7},{7,5},{8,10},{10,8},{12,... | collective-permute-start | bytes 221192 | tf_op jit(solution)/shard_map/ppermute | solution.py:280
  5.3 5.6 %collective-permute-start.2 = (bf16[2,144,128]{2,1,0:T(8,128)(2,1)S(1)}, bf16[2,144,128]{2,1,0:T(8,128)(2,1)S(1)}, u32[]{:S(2)}, u32[]{:S(2)}) collective-permute-start(bf16[2,144,128]{2,1,0:T(8,128)(2,1)S(1)} %get-tuple-element.24), channel_id=1, source_target_pairs={{0,6},{2,4},{4,2},{6,0},{1,7},{3,5},{5,3},{7,1},{8,14},{10,12},{12... | collective-permute-start | bytes 221192 | tf_op jit(solution)/shard_map/ppermute | solution.py:280
  6.8 4.4 %collective-permute-start.3 = (bf16[2,144,128]{2,1,0:T(8,128)(2,1)S(1)}, bf16[2,144,128]{2,1,0:T(8,128)(2,1)S(1)}, u32[]{:S(2)}, u32[]{:S(2)}) collective-permute-start(bf16[2,144,128]{2,1,0:T(8,128)(2,1)S(1)} %get-tuple-element.25), channel_id=1, source_target_pairs={{0,4},{2,6},{4,0},{6,2},{1,5},{3,7},{5,1},{7,3},{8,12},{10,14},{12... | collective-permute-start | bytes 221192 | tf_op jit(solution)/shard_map/ppermute | solution.py:280
  12.8 6.4 %copy-start.1 = (bf16[128,128]{1,0:T(8,128)(2,1)S(1)}, bf16[128,128]{1,0:T(8,128)(2,1)}, u32[]{:S(2)}) copy-start(bf16[128,128]{1,0:T(8,128)(2,1)} %w_ref.2) | copy-start | bytes 98308
  12.8 13.6 %all-to-all-start = ((bf16[16,72,128]{2,1,0:T(8,128)(2,1)}), bf16[16,72,128]{2,1,0:T(8,128)(2,1)S(1)}, u32[]{:S(2)}, u32[]{:S(2)}) async-start(bf16[16,72,128]{2,1,0:T(8,128)(2,1)} %shard_map.93), calls=%async_computation | async-start | bytes 589824 | tf_op jit(solution)/shard_map/all_to_all | solution.py:300
  19.1 0.7 %copy-start.2 = (f32[128]{0:T(128)S(1)}, f32[128]{0:T(128)}, u32[]{:S(2)}) copy-start(f32[128]{0:T(128)} %param.15) | copy-start | bytes 1540
  19.1 0.7 %copy-start.3 = (f32[128]{0:T(128)S(1)}, f32[128]{0:T(128)}, u32[]{:S(2)}) copy-start(f32[128]{0:T(128)} %param.16) | copy-start | bytes 1540
  19.8 6.6 %copy-start = (bf16[128,128]{1,0:T(8,128)(2,1)S(1)}, bf16[128,128]{1,0:T(8,128)(2,1)}, u32[]{:S(2)}) copy-start(bf16[128,128]{1,0:T(8,128)(2,1)} %w_ref.3) | copy-start | bytes 98308

commit v28 on v26

--- a/solution.py
+++ b/solution.py
@@ -135,7 +135,7 @@
 
 
 def triangle_kernel(far_order, steps, cols, row_count, col_count, share, *refs):
-    *got_refs, spread_ref, mask_ref, total_ref = refs
+    *got_refs, spread_ref, mask_ref, total_ref, left_ref, wide_ref = refs
     got_refs = {step: ref for step, ref in zip(steps, got_refs)}
     both = 2 * share
     group, lanes = spread_ref.shape
@@ -171,11 +171,17 @@
     lane_block = lax.broadcasted_iota(jnp.int32, (group, LANES), 1) // rest
     mains, lasts = [], []
     for part in range(parts):
-        left, right = side(0, part), side(1, part).astype(jnp.bfloat16)
-        left = (left[:, None, :] * spread_ref[...][None]).reshape(rows, row_count, group, lanes)
-        pairs = left[:, : 2 * whole].reshape(rows, whole, 2, group, lanes)
-        left = jnp.concatenate([pairs[:, :, 0], pairs[:, :, 1], left[:, 2 * whole :]], axis=-1)
-        left = left.reshape(rows * whole * group, 3 * lanes).astype(jnp.bfloat16)
+        left_ref[part] = side(0, part)
+        right = side(1, part).astype(jnp.bfloat16)
+        for row in range(rows):
+            for t in range(0, whole, 2):
+                pair = []
+                for at in (row * row_count, row * row_count + 2):
+                    picks = [at + 2 * t, at + 2 * t + 1, row * row_count + 2 * whole + t + len(pair)]
+                    copies = [jnp.broadcast_to(left_ref[part, i : i + 1, :], (group, lanes)) for i in picks]
+                    pair.append(jnp.concatenate([copy * spread_ref[...] for copy in copies], axis=1))
+                at = (row * whole + t) * group
+                wide_ref[part, at : at + 2 * group, :] = jnp.concatenate(pair, axis=0).astype(jnp.bfloat16)
         ours = [right[col * col_count : (col + 1) * col_count] for col in range(cols)]
         weights = [
             placed([p for mine in ours for p in (mine, LANES - col_count)]),
@@ -183,11 +189,11 @@
             placed([p for mine in ours for p in (2 * col_count, mine[:spare])]),
         ]
         weights = jnp.concatenate(weights, axis=1)
-        mains.append(lax.dot_general(left, weights, contract, preferred_element_type=jnp.float32))
+        mains.append(lax.dot_general(wide_ref[part], weights, contract, preferred_element_type=jnp.float32))
         gap = LANES // parts
         pieces = [[gap * part] + [mine[spare:]] * whole + [LANES - gap * (part + 1)] for mine in ours]
         weights = placed([p for piece in pieces for p in piece if not isinstance(p, int) or p])
-        lasts.append(lax.dot_general(left[:, 2 * lanes :], weights, contract, preferred_element_type=jnp.float32))
+        lasts.append(lax.dot_general(wide_ref[part, :, 2 * lanes :], weights, contract, preferred_element_type=jnp.float32))
     for target, device in enumerate(far_order):
         row, col = divmod(device, cols)
         spots = [(row * whole + t) * group for t in range(whole)]
@@ -283,6 +289,10 @@
         out_shape=jax.ShapeDtypeStruct((devices, share * tokens // LANES, LANES), jnp.bfloat16),
         in_specs=[VMEM] * (quads + 2),
         out_specs=VMEM,
+        scratch_shapes=[
+            pltpu.VMEM((share // GROUP, length, GROUP * depth), jnp.float32),
+            pltpu.VMEM((share // GROUP, length // 3 * GROUP, 3 * GROUP * depth), jnp.bfloat16),
+        ],
         compiler_params=LIMIT,
     )(*got, spread, mask)
     gate, gain_out, bias_out = pl.pallas_call(

time: 26.8 us -> 26.8 us (level)
  no operation moved by 1% of the time
where the time goes in v28:
time: 26.8 us; the launch traced here: 26.5 us
  waiting for transfers between devices  10.7 us (40%)
  starting transfers between devices  9.97 us (37%)
  Pallas kernels  5.07 us (19%)
  local copies, waits for them, and re-layouts  0.65 us (2%)
    all_to_all x1, waiting for transfers between devices, per_device(): lax.all_to_all(total, ('half', 'quad', 'col'), split_axis=0, concat_axis=...  6.52 us
    all_to_all x1, starting transfers between devices, per_device(): lax.all_to_all(total, ('half', 'quad', 'col'), split_axis=0, concat_axis=...  5.28 us
    ppermute x3, starting transfers between devices, per_device(): lax.ppermute(pieces[step], 'quad', [(i, i ^ step) for i in range(quads)])  4.24 us
    ppermute x3, waiting for transfers between devices, per_device(): lax.ppermute(pieces[step], 'quad', [(i, i ^ step) for i in range(quads)])  4.22 us
    pallas_call x1, Pallas kernels, per_device(): pl.pallas_call(functools.partial(own_kernel, quads, cols), out_shape=(jax...  1.7 us
    pallas_call x1, Pallas kernels, per_device(): pl.pallas_call(functools.partial(triangle_kernel, far_order, steps, cols,...  1.61 us
    pallas_call x1, Pallas kernels, per_device(): pl.pallas_call(functools.partial(output_kernel, far_order, near_order), o...  1.02 us
    unnamed x8, local copies, waits for them, and re-layouts  0.65 us
  transfers between devices with their start and end apart: 5, of which 4 were waited for; matrix products, arithmetic and copies ran while one was open for 0% of the time, Pallas kernels for 7%

profile of v28, /device:TPU:0, one launch (start us, length us, event | category | flops | bytes accessed | tf_op | source)
XLA Modules:
  0.0 26.5 jit_solution(18357392610902899291)
XLA Ops:
  0.0 0.5 %collective-permute-start = (bf16[12,48,128]{2,1,0:T(8,128)(2,1)}, bf16[12,48,128]{2,1,0:T(8,128)(2,1)S(1)}, u32[]{:S(2)}, u32[]{:S(2)}) collective-permute-start(bf16[12,48,128]{2,1,0:T(8,128)(2,1)} %pair_hbm.1), channel_id=1, source_target_pairs={{0,1},{1,0},{2,3},{3,2},{4,5},{5,4},{6,7},{7,6},{8,9},{9,8},{10,11... | collective-permute-start | bytes 442376 | tf_op jit(solution)/shard_map/ppermute | solution.py:251
  0.5 1.7 %shard_map.91 = (bf16[4,144,128]{2,1,0:T(8,128)(2,1)S(1)}, bf16[576,128]{1,0:T(8,128)(2,1)S(1)}, f32[8,384]{1,0:T(8,128)S(1)}, f32[96,1]{1,0:T(8,128)S(1)}, bf16...) custom-call(bf16[12,48,128]{2,1,0:T(8,128)(2,1)} %pair_hbm.1, f32[1,128]{1,0:T(1,128)} %bitcast.7, ...), custom_call_target="tpu_custom_call" | custom-call | flops 75497472 | bytes 1179648 | tf_op jit(solution)/shard_map/pallas_call | solution.py:253
  2.2 0.0 collective-permute-done.pair_ref
  2.2 0.6 %shard_map.92 = (bf16[2,144,128]{2,1,0:T(8,128)(2,1)S(1)}, bf16[2,144,128]{2,1,0:T(8,128)(2,1)S(1)}, bf16[2,144,128]{2,1,0:T(8,128)(2,1)S(1)}, bf16[2,144,128]{2,1,0:T(8,128)(2,1)S(1)}) custom-call(bf16[12,48,128]{2,1,0:T(8,128)(2,1)S(1)} %collective-permute-done.pair_ref, bf16[4,144,128]{2,1,0:T(8,128)(2,1)S(1)} %get-tuple-element.19.sides_ref, ...), custom_call_target="tpu_custom_call" | custom-call | flops 75497472 | bytes 1179648 | tf_op jit(solution)/shard_map/pallas_call | solution.py:276
  2.7 3.6 %collective-permute-start.1 = (bf16[2,144,128]{2,1,0:T(8,128)(2,1)S(1)}, bf16[2,144,128]{2,1,0:T(8,128)(2,1)S(1)}, u32[]{:S(2)}, u32[]{:S(2)}) collective-permute-start(bf16[2,144,128]{2,1,0:T(8,128)(2,1)S(1)} %get-tuple-element.23), channel_id=1, source_target_pairs={{0,6},{2,4},{4,2},{6,0},{1,7},{3,5},{5,3},{7,1},{8,14},{10,12},{12... | collective-permute-start | bytes 221192 | tf_op jit(solution)/shard_map/ppermute | solution.py:286
  6.3 0.5 %collective-permute-start.2 = (bf16[2,144,128]{2,1,0:T(8,128)(2,1)S(1)}, bf16[2,144,128]{2,1,0:T(8,128)(2,1)S(1)}, u32[]{:S(2)}, u32[]{:S(2)}) collective-permute-start(bf16[2,144,128]{2,1,0:T(8,128)(2,1)S(1)} %get-tuple-element.24), channel_id=1, source_target_pairs={{0,2},{2,0},{4,6},{6,4},{1,3},{3,1},{5,7},{7,5},{8,10},{10,8},{12,... | collective-permute-start | bytes 221192 | tf_op jit(solution)/shard_map/ppermute | solution.py:286
  6.8 0.1 collective-permute-start.3
  7.0 2.3 %collective-permute-done.1.refs_0_ = bf16[2,144,128]{2,1,0:T(8,128)(2,1)S(1)} collective-permute-done((bf16[2,144,128]{2,1,0:T(8,128)(2,1)S(1)}, bf16[2,144,128]{2,1,0:T(8,128)(2,1)S(1)}, u32[]{:S(2)}, u32[]{:S(2)}) %collective-permute-start.1) | collective-permute-done | bytes 73760 | tf_op jit(solution)/shard_map/ppermute | solution.py:286
  9.3 1.6 %collective-permute-done.2.refs_1_ = bf16[2,144,128]{2,1,0:T(8,128)(2,1)S(1)} collective-permute-done((bf16[2,144,128]{2,1,0:T(8,128)(2,1)S(1)}, bf16[2,144,128]{2,1,0:T(8,128)(2,1)S(1)}, u32[]{:S(2)}, u32[]{:S(2)}) %collective-permute-start.2) | collective-permute-done | bytes 73760 | tf_op jit(solution)/shard_map/ppermute | solution.py:286
  10.9 0.3 %collective-permute-done.3.refs_2_ = bf16[2,144,128]{2,1,0:T(8,128)(2,1)S(1)} collective-permute-done((bf16[2,144,128]{2,1,0:T(8,128)(2,1)S(1)}, bf16[2,144,128]{2,1,0:T(8,128)(2,1)S(1)}, u32[]{:S(2)}, u32[]{:S(2)}) %collective-permute-start.3) | collective-permute-done | bytes 73760 | tf_op jit(solution)/shard_map/ppermute | solution.py:286
  11.2 1.6 %shard_map.93 = bf16[16,72,128]{2,1,0:T(8,128)(2,1)} custom-call(bf16[2,144,128]{2,1,0:T(8,128)(2,1)S(1)} %collective-permute-done.1.refs_0_, bf16[2,144,128]{2,1,0:T(8,128)(2,1)S(1)} %collective-permute-done.2.refs_1_, bf16[2,144,128]{2,1,0:T(8,128)(2,1)S(1)} %collective-permute-done.3.refs_2_, bf16[2,144,128]{2,1,0:T(8,128)(2,1)S(1)} %get-tuple-element.26.refs_3_, ...), custom_call_target="tpu_custom_call" | custom-call | tf_op jit(solution)/shard_map/pallas_call | solution.py:287
  12.8 0.0 copy-start.1
  12.8 5.3 %all-to-all-start = ((bf16[16,72,128]{2,1,0:T(8,128)(2,1)}), bf16[16,72,128]{2,1,0:T(8,128)(2,1)S(1)}, u32[]{:S(2)}, u32[]{:S(2)}) async-start(bf16[16,72,128]{2,1,0:T(8,128)(2,1)} %shard_map.93), calls=%async_computation | async-start | bytes 589824 | tf_op jit(solution)/shard_map/all_to_all | solution.py:310
  18.1 0.0 copy-start.2
  18.1 0.0 copy-start.3
  18.1 0.0 copy-done.1
  18.1 0.6 %copy-done.2 = f32[128]{0:T(128)S(1)} copy-done((f32[128]{0:T(128)S(1)}, f32[128]{0:T(128)}, u32[]{:S(2)}) %copy-start.2) | copy-done | bytes 536
  18.7 0.0 copy-done.3
  18.8 0.0 copy-start
  18.8 0.2 shard_map.94
  19.0 6.5 %all-to-all-done.total_ref = bf16[16,72,128]{2,1,0:T(8,128)(2,1)S(1)} async-done(((bf16[16,72,128]{2,1,0:T(8,128)(2,1)}), bf16[16,72,128]{2,1,0:T(8,128)(2,1)S(1)}, u32[]{:S(2)}, u32[]{:S(2)}) %all-to-all-start) | async-done | bytes 294944 | tf_op jit(solution)/shard_map/all_to_all | solution.py:310
  25.5 0.0 copy-done
  25.5 1.0 %shard_map.95 = bf16[12,48,128]{2,1,0:T(8,128)(2,1)} custom-call(bf16[16,72,128]{2,1,0:T(8,128)(2,1)S(1)} %all-to-all-done.total_ref, f32[576,128]{1,0:T(8,128)S(1)} %get-tuple-element.30.gate_ref, f32[128,1]{1,0:T(8,128)S(1)} %get-tuple-element.31.gain_ref, f32[128,1]{1,0:T(8,128)S(1)} %get-tuple-element.32.bias_ref, bf16[128,128]{1,0:T(8,128)(2,1)S(1)} %copy-done), custom_call_target="tpu_custom_call" | custom-call | tf_op jit(solution)/shard_map/pallas_call | solution.py:311
Async XLA Ops:
  0.0 2.2 %collective-permute-start = (bf16[12,48,128]{2,1,0:T(8,128)(2,1)}, bf16[12,48,128]{2,1,0:T(8,128)(2,1)S(1)}, u32[]{:S(2)}, u32[]{:S(2)}) collective-permute-start(bf16[12,48,128]{2,1,0:T(8,128)(2,1)} %pair_hbm.1), channel_id=1, source_target_pairs={{0,1},{1,0},{2,3},{3,2},{4,5},{5,4},{6,7},{7,6},{8,9},{9,8},{10,11... | collective-permute-start | bytes 442376 | tf_op jit(solution)/shard_map/ppermute | solution.py:251
  2.7 6.5 %collective-permute-start.1 = (bf16[2,144,128]{2,1,0:T(8,128)(2,1)S(1)}, bf16[2,144,128]{2,1,0:T(8,128)(2,1)S(1)}, u32[]{:S(2)}, u32[]{:S(2)}) collective-permute-start(bf16[2,144,128]{2,1,0:T(8,128)(2,1)S(1)} %get-tuple-element.23), channel_id=1, source_target_pairs={{0,6},{2,4},{4,2},{6,0},{1,7},{3,5},{5,3},{7,1},{8,14},{10,12},{12... | collective-permute-start | bytes 221192 | tf_op jit(solution)/shard_map/ppermute | solution.py:286
  6.3 4.5 %collective-permute-start.2 = (bf16[2,144,128]{2,1,0:T(8,128)(2,1)S(1)}, bf16[2,144,128]{2,1,0:T(8,128)(2,1)S(1)}, u32[]{:S(2)}, u32[]{:S(2)}) collective-permute-start(bf16[2,144,128]{2,1,0:T(8,128)(2,1)S(1)} %get-tuple-element.24), channel_id=1, source_target_pairs={{0,2},{2,0},{4,6},{6,4},{1,3},{3,1},{5,7},{7,5},{8,10},{10,8},{12,... | collective-permute-start | bytes 221192 | tf_op jit(solution)/shard_map/ppermute | solution.py:286
  6.8 4.4 %collective-permute-start.3 = (bf16[2,144,128]{2,1,0:T(8,128)(2,1)S(1)}, bf16[2,144,128]{2,1,0:T(8,128)(2,1)S(1)}, u32[]{:S(2)}, u32[]{:S(2)}) collective-permute-start(bf16[2,144,128]{2,1,0:T(8,128)(2,1)S(1)} %get-tuple-element.25), channel_id=1, source_target_pairs={{0,4},{2,6},{4,0},{6,2},{1,5},{3,7},{5,1},{7,3},{8,12},{10,14},{12... | collective-permute-start | bytes 221192 | tf_op jit(solution)/shard_map/ppermute | solution.py:286
  12.8 5.3 %copy-start.1 = (bf16[128,128]{1,0:T(8,128)(2,1)S(1)}, bf16[128,128]{1,0:T(8,128)(2,1)}, u32[]{:S(2)}) copy-start(bf16[128,128]{1,0:T(8,128)(2,1)} %w_ref.2) | copy-start | bytes 98308
  12.8 12.7 %all-to-all-start = ((bf16[16,72,128]{2,1,0:T(8,128)(2,1)}), bf16[16,72,128]{2,1,0:T(8,128)(2,1)S(1)}, u32[]{:S(2)}, u32[]{:S(2)}) async-start(bf16[16,72,128]{2,1,0:T(8,128)(2,1)} %shard_map.93), calls=%async_computation | async-start | bytes 589824 | tf_op jit(solution)/shard_map/all_to_all | solution.py:310
  18.1 0.7 %copy-start.2 = (f32[128]{0:T(128)S(1)}, f32[128]{0:T(128)}, u32[]{:S(2)}) copy-start(f32[128]{0:T(128)} %param.15) | copy-start | bytes 1540
  18.1 0.7 %copy-start.3 = (f32[128]{0:T(128)S(1)}, f32[128]{0:T(128)}, u32[]{:S(2)}) copy-start(f32[128]{0:T(128)} %param.16) | copy-start | bytes 1540
  18.8 6.7 %copy-start = (bf16[128,128]{1,0:T(8,128)(2,1)S(1)}, bf16[128,128]{1,0:T(8,128)(2,1)}, u32[]{:S(2)}) copy-start(bf16[128,128]{1,0:T(8,128)(2,1)} %w_ref.3) | copy-start | bytes 98308

commit v29 on v28

--- a/solution.py
+++ b/solution.py
@@ -145,8 +145,13 @@
     rest = col_count - spare
     blocks = [[got_refs[row][col].astype(jnp.float32) for row in range(quads)] for col in range(cols)]
 
+    contract = (((1,), (1,)), ((), ()))
+    unit = lax.broadcasted_iota(jnp.int32, (LANES, LANES), 0) == lax.broadcasted_iota(jnp.int32, (LANES, LANES), 1)
+    unit = jnp.where(unit, 1.0, 0.0).astype(jnp.bfloat16)
+
     def turned(picks):
-        return jnp.concatenate([blocks[col][row][at : at + group] for col, row, at in picks], axis=0).T
+        block = jnp.concatenate([blocks[col][row][at : at + group] for col, row, at in picks], axis=0).astype(jnp.bfloat16)
+        return lax.dot_general(unit, block, contract, preferred_element_type=jnp.float32)
 
     tail = turned([(col, row, whole * both + part * group) for col in range(cols) for part in range(parts) for row in range(quads)])
 
@@ -167,7 +172,6 @@
     def placed(pieces):
         return jnp.concatenate([jnp.zeros((piece, lanes), jnp.bfloat16) if isinstance(piece, int) else piece for piece in pieces], axis=0)
 
-    contract = (((1,), (1,)), ((), ()))
     lane_block = lax.broadcasted_iota(jnp.int32, (group, LANES), 1) // rest
     mains, lasts = [], []
     for part in range(parts):

time: 26.8 us -> 27.1 us (1.011)
  Pallas kernels: 5.07 us -> 5.36 us
    pallas_call x1, Pallas kernels: 1.61 us -> 1.89 us  [per_device(): pl.pallas_call(functools.partial(triangle_kernel, far_order, steps, cols,...]
where the time goes in v29:
time: 27.1 us; the launch traced here: 26.8 us
  waiting for transfers between devices  10.7 us (39%)
  starting transfers between devices  9.97 us (37%)
  Pallas kernels  5.36 us (20%)
  local copies, waits for them, and re-layouts  0.65 us (2%)
    all_to_all x1, waiting for transfers between devices, per_device(): lax.all_to_all(total, ('half', 'quad', 'col'), split_axis=0, concat_axis=...  6.51 us
    all_to_all x1, starting transfers between devices, per_device(): lax.all_to_all(total, ('half', 'quad', 'col'), split_axis=0, concat_axis=...  5.28 us
    ppermute x3, starting transfers between devices, per_device(): lax.ppermute(pieces[step], 'quad', [(i, i ^ step) for i in range(quads)])  4.24 us
    ppermute x3, waiting for transfers between devices, per_device(): lax.ppermute(pieces[step], 'quad', [(i, i ^ step) for i in range(quads)])  4.22 us
    pallas_call x1, Pallas kernels, per_device(): pl.pallas_call(functools.partial(triangle_kernel, far_order, steps, cols,...  1.89 us
    pallas_call x1, Pallas kernels, per_device(): pl.pallas_call(functools.partial(own_kernel, quads, cols), out_shape=(jax...  1.7 us
    pallas_call x1, Pallas kernels, per_device(): pl.pallas_call(functools.partial(output_kernel, far_order, near_order), o...  1.02 us
    unnamed x8, local copies, waits for them, and re-layouts  0.65 us
  transfers between devices with their start and end apart: 5, of which 4 were waited for; matrix products, arithmetic and copies ran while one was open for 0% of the time, Pallas kernels for 7%

profile of v29, /device:TPU:0, one launch (start us, length us, event | category | flops | bytes accessed | tf_op | source)
XLA Modules:
  0.0 26.8 jit_solution(8620916808063096416)
XLA Ops:
  0.0 0.5 %collective-permute-start = (bf16[12,48,128]{2,1,0:T(8,128)(2,1)}, bf16[12,48,128]{2,1,0:T(8,128)(2,1)S(1)}, u32[]{:S(2)}, u32[]{:S(2)}) collective-permute-start(bf16[12,48,128]{2,1,0:T(8,128)(2,1)} %pair_hbm.1), channel_id=1, source_target_pairs={{0,1},{1,0},{2,3},{3,2},{4,5},{5,4},{6,7},{7,6},{8,9},{9,8},{10,11... | collective-permute-start | bytes 442376 | tf_op jit(solution)/shard_map/ppermute | solution.py:255
  0.5 1.7 %shard_map.91 = (bf16[4,144,128]{2,1,0:T(8,128)(2,1)S(1)}, bf16[576,128]{1,0:T(8,128)(2,1)S(1)}, f32[8,384]{1,0:T(8,128)S(1)}, f32[96,1]{1,0:T(8,128)S(1)}, bf16...) custom-call(bf16[12,48,128]{2,1,0:T(8,128)(2,1)} %pair_hbm.1, f32[1,128]{1,0:T(1,128)} %bitcast.7, ...), custom_call_target="tpu_custom_call" | custom-call | flops 75497472 | bytes 1179648 | tf_op jit(solution)/shard_map/pallas_call | solution.py:257
  2.2 0.0 collective-permute-done.pair_ref
  2.2 0.6 %shard_map.92 = (bf16[2,144,128]{2,1,0:T(8,128)(2,1)S(1)}, bf16[2,144,128]{2,1,0:T(8,128)(2,1)S(1)}, bf16[2,144,128]{2,1,0:T(8,128)(2,1)S(1)}, bf16[2,144,128]{2,1,0:T(8,128)(2,1)S(1)}) custom-call(bf16[12,48,128]{2,1,0:T(8,128)(2,1)S(1)} %collective-permute-done.pair_ref, bf16[4,144,128]{2,1,0:T(8,128)(2,1)S(1)} %get-tuple-element.19.sides_ref, ...), custom_call_target="tpu_custom_call" | custom-call | flops 75497472 | bytes 1179648 | tf_op jit(solution)/shard_map/pallas_call | solution.py:280
  2.7 3.6 %collective-permute-start.1 = (bf16[2,144,128]{2,1,0:T(8,128)(2,1)S(1)}, bf16[2,144,128]{2,1,0:T(8,128)(2,1)S(1)}, u32[]{:S(2)}, u32[]{:S(2)}) collective-permute-start(bf16[2,144,128]{2,1,0:T(8,128)(2,1)S(1)} %get-tuple-element.23), channel_id=1, source_target_pairs={{0,6},{2,4},{4,2},{6,0},{1,7},{3,5},{5,3},{7,1},{8,14},{10,12},{12... | collective-permute-start | bytes 221192 | tf_op jit(solution)/shard_map/ppermute | solution.py:290
  6.3 0.5 %collective-permute-start.2 = (bf16[2,144,128]{2,1,0:T(8,128)(2,1)S(1)}, bf16[2,144,128]{2,1,0:T(8,128)(2,1)S(1)}, u32[]{:S(2)}, u32[]{:S(2)}) collective-permute-start(bf16[2,144,128]{2,1,0:T(8,128)(2,1)S(1)} %get-tuple-element.24), channel_id=1, source_target_pairs={{0,2},{2,0},{4,6},{6,4},{1,3},{3,1},{5,7},{7,5},{8,10},{10,8},{12,... | collective-permute-start | bytes 221192 | tf_op jit(solution)/shard_map/ppermute | solution.py:290
  6.8 0.1 collective-permute-start.3
  7.0 2.3 %collective-permute-done.1.refs_0_ = bf16[2,144,128]{2,1,0:T(8,128)(2,1)S(1)} collective-permute-done((bf16[2,144,128]{2,1,0:T(8,128)(2,1)S(1)}, bf16[2,144,128]{2,1,0:T(8,128)(2,1)S(1)}, u32[]{:S(2)}, u32[]{:S(2)}) %collective-permute-start.1) | collective-permute-done | bytes 73760 | tf_op jit(solution)/shard_map/ppermute | solution.py:290
  9.3 1.6 %collective-permute-done.2.refs_1_ = bf16[2,144,128]{2,1,0:T(8,128)(2,1)S(1)} collective-permute-done((bf16[2,144,128]{2,1,0:T(8,128)(2,1)S(1)}, bf16[2,144,128]{2,1,0:T(8,128)(2,1)S(1)}, u32[]{:S(2)}, u32[]{:S(2)}) %collective-permute-start.2) | collective-permute-done | bytes 73760 | tf_op jit(solution)/shard_map/ppermute | solution.py:290
  10.9 0.3 %collective-permute-done.3.refs_2_ = bf16[2,144,128]{2,1,0:T(8,128)(2,1)S(1)} collective-permute-done((bf16[2,144,128]{2,1,0:T(8,128)(2,1)S(1)}, bf16[2,144,128]{2,1,0:T(8,128)(2,1)S(1)}, u32[]{:S(2)}, u32[]{:S(2)}) %collective-permute-start.3) | collective-permute-done | bytes 73760 | tf_op jit(solution)/shard_map/ppermute | solution.py:290
  11.2 1.9 %shard_map.93 = bf16[16,72,128]{2,1,0:T(8,128)(2,1)} custom-call(bf16[2,144,128]{2,1,0:T(8,128)(2,1)S(1)} %collective-permute-done.1.refs_0_, bf16[2,144,128]{2,1,0:T(8,128)(2,1)S(1)} %collective-permute-done.2.refs_1_, bf16[2,144,128]{2,1,0:T(8,128)(2,1)S(1)} %collective-permute-done.3.refs_2_, bf16[2,144,128]{2,1,0:T(8,128)(2,1)S(1)} %get-tuple-element.26.refs_3_, ...), custom_call_target="tpu_custom_call" | custom-call | tf_op jit(solution)/shard_map/pallas_call | solution.py:291
  13.1 0.0 copy-start.1
  13.1 5.3 %all-to-all-start = ((bf16[16,72,128]{2,1,0:T(8,128)(2,1)}), bf16[16,72,128]{2,1,0:T(8,128)(2,1)S(1)}, u32[]{:S(2)}, u32[]{:S(2)}) async-start(bf16[16,72,128]{2,1,0:T(8,128)(2,1)} %shard_map.93), calls=%async_computation | async-start | bytes 589824 | tf_op jit(solution)/shard_map/all_to_all | solution.py:314
  18.4 0.0 copy-start.2
  18.4 0.0 copy-start.3
  18.4 0.0 copy-done.1
  18.4 0.6 %copy-done.2 = f32[128]{0:T(128)S(1)} copy-done((f32[128]{0:T(128)S(1)}, f32[128]{0:T(128)}, u32[]{:S(2)}) %copy-start.2) | copy-done | bytes 536
  19.0 0.0 copy-done.3
  19.0 0.0 copy-start
  19.0 0.2 shard_map.94
  19.2 6.5 %all-to-all-done.total_ref = bf16[16,72,128]{2,1,0:T(8,128)(2,1)S(1)} async-done(((bf16[16,72,128]{2,1,0:T(8,128)(2,1)}), bf16[16,72,128]{2,1,0:T(8,128)(2,1)S(1)}, u32[]{:S(2)}, u32[]{:S(2)}) %all-to-all-start) | async-done | bytes 294944 | tf_op jit(solution)/shard_map/all_to_all | solution.py:314
  25.8 0.0 copy-done
  25.8 1.0 %shard_map.95 = bf16[12,48,128]{2,1,0:T(8,128)(2,1)} custom-call(bf16[16,72,128]{2,1,0:T(8,128)(2,1)S(1)} %all-to-all-done.total_ref, f32[576,128]{1,0:T(8,128)S(1)} %get-tuple-element.30.gate_ref, f32[128,1]{1,0:T(8,128)S(1)} %get-tuple-element.31.gain_ref, f32[128,1]{1,0:T(8,128)S(1)} %get-tuple-element.32.bias_ref, bf16[128,128]{1,0:T(8,128)(2,1)S(1)} %copy-done), custom_call_target="tpu_custom_call" | custom-call | tf_op jit(solution)/shard_map/pallas_call | solution.py:315
Async XLA Ops:
  0.0 2.2 %collective-permute-start = (bf16[12,48,128]{2,1,0:T(8,128)(2,1)}, bf16[12,48,128]{2,1,0:T(8,128)(2,1)S(1)}, u32[]{:S(2)}, u32[]{:S(2)}) collective-permute-start(bf16[12,48,128]{2,1,0:T(8,128)(2,1)} %pair_hbm.1), channel_id=1, source_target_pairs={{0,1},{1,0},{2,3},{3,2},{4,5},{5,4},{6,7},{7,6},{8,9},{9,8},{10,11... | collective-permute-start | bytes 442376 | tf_op jit(solution)/shard_map/ppermute | solution.py:255
  2.7 6.5 %collective-permute-start.1 = (bf16[2,144,128]{2,1,0:T(8,128)(2,1)S(1)}, bf16[2,144,128]{2,1,0:T(8,128)(2,1)S(1)}, u32[]{:S(2)}, u32[]{:S(2)}) collective-permute-start(bf16[2,144,128]{2,1,0:T(8,128)(2,1)S(1)} %get-tuple-element.23), channel_id=1, source_target_pairs={{0,6},{2,4},{4,2},{6,0},{1,7},{3,5},{5,3},{7,1},{8,14},{10,12},{12... | collective-permute-start | bytes 221192 | tf_op jit(solution)/shard_map/ppermute | solution.py:290
  6.3 4.5 %collective-permute-start.2 = (bf16[2,144,128]{2,1,0:T(8,128)(2,1)S(1)}, bf16[2,144,128]{2,1,0:T(8,128)(2,1)S(1)}, u32[]{:S(2)}, u32[]{:S(2)}) collective-permute-start(bf16[2,144,128]{2,1,0:T(8,128)(2,1)S(1)} %get-tuple-element.24), channel_id=1, source_target_pairs={{0,2},{2,0},{4,6},{6,4},{1,3},{3,1},{5,7},{7,5},{8,10},{10,8},{12,... | collective-permute-start | bytes 221192 | tf_op jit(solution)/shard_map/ppermute | solution.py:290
  6.8 4.4 %collective-permute-start.3 = (bf16[2,144,128]{2,1,0:T(8,128)(2,1)S(1)}, bf16[2,144,128]{2,1,0:T(8,128)(2,1)S(1)}, u32[]{:S(2)}, u32[]{:S(2)}) collective-permute-start(bf16[2,144,128]{2,1,0:T(8,128)(2,1)S(1)} %get-tuple-element.25), channel_id=1, source_target_pairs={{0,4},{2,6},{4,0},{6,2},{1,5},{3,7},{5,1},{7,3},{8,12},{10,14},{12... | collective-permute-start | bytes 221192 | tf_op jit(solution)/shard_map/ppermute | solution.py:290
  13.1 5.3 %copy-start.1 = (bf16[128,128]{1,0:T(8,128)(2,1)S(1)}, bf16[128,128]{1,0:T(8,128)(2,1)}, u32[]{:S(2)}) copy-start(bf16[128,128]{1,0:T(8,128)(2,1)} %w_ref.2) | copy-start | bytes 98308
  13.1 12.7 %all-to-all-start = ((bf16[16,72,128]{2,1,0:T(8,128)(2,1)}), bf16[16,72,128]{2,1,0:T(8,128)(2,1)S(1)}, u32[]{:S(2)}, u32[]{:S(2)}) async-start(bf16[16,72,128]{2,1,0:T(8,128)(2,1)} %shard_map.93), calls=%async_computation | async-start | bytes 589824 | tf_op jit(solution)/shard_map/all_to_all | solution.py:314
  18.4 0.7 %copy-start.2 = (f32[128]{0:T(128)S(1)}, f32[128]{0:T(128)}, u32[]{:S(2)}) copy-start(f32[128]{0:T(128)} %param.15) | copy-start | bytes 1540
  18.4 0.7 %copy-start.3 = (f32[128]{0:T(128)S(1)}, f32[128]{0:T(128)}, u32[]{:S(2)}) copy-start(f32[128]{0:T(128)} %param.16) | copy-start | bytes 1540
  19.0 6.7 %copy-start = (bf16[128,128]{1,0:T(8,128)(2,1)S(1)}, bf16[128,128]{1,0:T(8,128)(2,1)}, u32[]{:S(2)}) copy-start(bf16[128,128]{1,0:T(8,128)(2,1)} %w_ref.3) | copy-start | bytes 98308

commit v30 on v28

--- a/solution.py
+++ b/solution.py
@@ -43,15 +43,6 @@
     return jnp.concatenate(blocks, axis=-2)
 
 
-def unpack(x, rows):
-    whole, rest = divmod(x.shape[-2], rows)
-    blocks = [x[..., t * rows : (t + 1) * rows, :] for t in range(whole)]
-    if rest:
-        tail = x[..., whole * rows :, :]
-        blocks.append(jnp.concatenate([tail[..., : LANES // 2], tail[..., LANES // 2 :]], axis=-2))
-    return jnp.concatenate(blocks, axis=-1)
-
-
 def arrange(x):
     row_count, col_count, _ = x.shape
     whole, spare = row_count // 3, LANES - 2 * col_count
@@ -59,18 +50,6 @@
     for t in range(whole):
         blocks += [x[2 * t], x[2 * t + 1], x[2 * whole + t, :spare]]
     return jnp.concatenate(blocks + [x[2 * whole + t, spare:] for t in range(whole)], axis=0)
-
-
-def restore(x, row_count, col_count):
-    whole, spare = row_count // 3, LANES - 2 * col_count
-    rest = col_count - spare
-    rows = []
-    for t in range(whole):
-        rows += [x[t * LANES : t * LANES + col_count], x[t * LANES + col_count : t * LANES + 2 * col_count]]
-    for t in range(whole):
-        tail = whole * LANES + t * rest
-        rows += [x[t * LANES + 2 * col_count : (t + 1) * LANES], x[tail : tail + rest]]
-    return jnp.concatenate(rows, axis=0)
 
 
 def normalise(flat, gain, bias):
@@ -212,20 +191,50 @@
     bias_out_ref[...] = column(bias_ref[...])
 
 
-def output_kernel(far_order, near_order, total_ref, gate_ref, gain_ref, bias_ref, w_ref, out_ref):
-    tokens = gate_ref.shape[0]
-    hidden = w_ref.shape[0]
+def output_kernel(far_order, near_order, total_ref, gate_ref, gain_ref, bias_ref, w_ref, out_hbm, out_ref, sems):
+    row_count, col_count, _ = out_ref.shape
     near = len(near_order)
-    share = hidden // near
+    share = w_ref.shape[0] // near
+    whole, spare = row_count // 3, LANES - 2 * col_count
+    rest = col_count - spare
     blocks = []
     for index in near_order:
         parts = [total_ref[source].astype(jnp.float32) for source, device in enumerate(far_order) if device % near == index]
-        blocks.append(unpack(sum(parts[1:], parts[0]), share))
-    total = jnp.concatenate(blocks, axis=0)
-    normed = layer_norm(total, gain_ref[...], bias_ref[...], 0).astype(jnp.bfloat16)
-    output = lax.dot_general(normed, w_ref[...], (((0,), (0,)), ((), ())), preferred_element_type=jnp.float32)
-    output = restore(output, out_ref.shape[0], out_ref.shape[1])
-    out_ref[...] = (gate_ref[...] * output).astype(jnp.bfloat16).reshape(out_ref.shape)
+        blocks.append(sum(parts[1:], parts[0]))
+    tails = [block[whole * share :] for block in blocks]
+    tails = [jnp.concatenate([tail[:, : LANES // 2], tail[:, LANES // 2 :]], axis=0) for tail in tails]
+    columns = [jnp.concatenate([block[t * share : (t + 1) * share] for block in blocks], axis=0) for t in range(whole)]
+    columns.append(jnp.concatenate(tails, axis=0))
+
+    def project(picks):
+        total = jnp.concatenate([columns[pick] for pick in picks], axis=1)
+        normed = layer_norm(total, gain_ref[...], bias_ref[...], 0).astype(jnp.bfloat16)
+        return lax.dot_general(normed, w_ref[...], (((0,), (0,)), ((), ())), preferred_element_type=jnp.float32)
+
+    def store(row, at, values):
+        spot = pl.ds(row * col_count + at, values.shape[0])
+        out_ref[row, pl.ds(at, values.shape[0])] = (gate_ref[spot] * values).astype(jnp.bfloat16)
+
+    copies = []
+    half = whole // 2
+    for first in (0, half):
+        values = project(list(range(first, first + half)) + ([whole] if first == 0 else []))
+        if first == 0:
+            for t in range(whole):
+                at = half * LANES + t * rest
+                store(2 * whole + t, spare, values[at : at + rest])
+        for n in range(half):
+            t = first + n
+            tile = values[n * LANES : (n + 1) * LANES]
+            store(2 * t, 0, tile[:col_count])
+            store(2 * t + 1, 0, tile[col_count : 2 * col_count])
+            store(2 * whole + t, 0, tile[2 * col_count :])
+        for rows in (pl.ds(2 * first, 2 * half), pl.ds(2 * whole + first, half)):
+            copy = pltpu.make_async_copy(out_ref.at[rows], out_hbm.at[rows], sems.at[len(copies)])
+            copy.start()
+            copies.append(copy)
+    for copy in copies:
+        copy.wait()
 
 
 def per_device(rows, cols, halves, pair, token_mask, gain_in, bias_in, w_in, w_gate, gain_out, bias_out, w_out):
@@ -312,7 +321,8 @@
         functools.partial(output_kernel, far_order, near_order),
         out_shape=jax.ShapeDtypeStruct(pair.shape, jnp.bfloat16),
         in_specs=[VMEM] * 5,
-        out_specs=VMEM,
+        out_specs=HBM,
+        scratch_shapes=[pltpu.VMEM(pair.shape, jnp.bfloat16), pltpu.SemaphoreType.DMA((4,))],
         compiler_params=LIMIT,
     )(total, gate, gain_out, bias_out, w_out)
 
@@ -361,7 +371,7 @@
         spare = LANES - 2 * col_count
         fits = hidden % (2 * GROUP * near) == 0 and cols == 2 and rows // halves == 4 and length <= LANES and row_count % 3 == 0
         fits = fits and 0 < spare < col_count and row_count // 3 * (col_count - spare) * 2 == LANES
-        fits = fits and row_count // 3 * (rows // halves) * GROUP == LANES
+        fits = fits and row_count // 3 * (rows // halves) * GROUP == LANES and row_count % 6 == 0
         return per_device(rows, cols, halves, *args) if fits else plain_per_device(rows, cols, *args)
 
     tokens = P(("groups", "half", "quad"), "col", None)

time: 26.8 us -> 26.8 us (level)
  no operation moved by 1% of the time
where the time goes in v30:
time: 26.8 us; the launch traced here: 26.5 us
  waiting for transfers between devices  10.7 us (40%)
  starting transfers between devices  9.97 us (37%)
  Pallas kernels  5.1 us (19%)
  local copies, waits for them, and re-layouts  0.65 us (2%)
    all_to_all x1, waiting for transfers between devices, per_device(): lax.all_to_all(total, ('half', 'quad', 'col'), split_axis=0, concat_axis=...  6.52 us
    all_to_all x1, starting transfers between devices, per_device(): lax.all_to_all(total, ('half', 'quad', 'col'), split_axis=0, concat_axis=...  5.28 us
    ppermute x3, starting transfers between devices, per_device(): lax.ppermute(pieces[step], 'quad', [(i, i ^ step) for i in range(quads)])  4.24 us
    ppermute x3, waiting for transfers between devices, per_device(): lax.ppermute(pieces[step], 'quad', [(i, i ^ step) for i in range(quads)])  4.22 us
    pallas_call x1, Pallas kernels, per_device(): pl.pallas_call(functools.partial(own_kernel, quads, cols), out_shape=(jax...  1.7 us
    pallas_call x1, Pallas kernels, per_device(): pl.pallas_call(functools.partial(triangle_kernel, far_order, steps, cols,...  1.61 us
    pallas_call x1, Pallas kernels, per_device(): pl.pallas_call(functools.partial(output_kernel, far_order, near_order), o...  1.05 us
    unnamed x8, local copies, waits for them, and re-layouts  0.65 us
  transfers between devices with their start and end apart: 5, of which 4 were waited for; matrix products, arithmetic and copies ran while one was open for 0% of the time, Pallas kernels for 7%

profile of v30, /device:TPU:0, one launch (start us, length us, event | category | flops | bytes accessed | tf_op | source)
XLA Modules:
  0.0 26.5 jit_solution(3534846891542199479)
XLA Ops:
  0.0 0.5 %collective-permute-start = (bf16[12,48,128]{2,1,0:T(8,128)(2,1)}, bf16[12,48,128]{2,1,0:T(8,128)(2,1)S(1)}, u32[]{:S(2)}, u32[]{:S(2)}) collective-permute-start(bf16[12,48,128]{2,1,0:T(8,128)(2,1)} %pair_hbm.1), channel_id=1, source_target_pairs={{0,1},{1,0},{2,3},{3,2},{4,5},{5,4},{6,7},{7,6},{8,9},{9,8},{10,11... | collective-permute-start | bytes 442376 | tf_op jit(solution)/shard_map/ppermute | solution.py:260
  0.5 1.7 %shard_map.91 = (bf16[4,144,128]{2,1,0:T(8,128)(2,1)S(1)}, bf16[576,128]{1,0:T(8,128)(2,1)S(1)}, f32[8,384]{1,0:T(8,128)S(1)}, f32[96,1]{1,0:T(8,128)S(1)}, bf16...) custom-call(bf16[12,48,128]{2,1,0:T(8,128)(2,1)} %pair_hbm.1, f32[1,128]{1,0:T(1,128)} %bitcast.7, ...), custom_call_target="tpu_custom_call" | custom-call | flops 75497472 | bytes 1179648 | tf_op jit(solution)/shard_map/pallas_call | solution.py:262
  2.2 0.0 collective-permute-done.pair_ref
  2.2 0.6 %shard_map.92 = (bf16[2,144,128]{2,1,0:T(8,128)(2,1)S(1)}, bf16[2,144,128]{2,1,0:T(8,128)(2,1)S(1)}, bf16[2,144,128]{2,1,0:T(8,128)(2,1)S(1)}, bf16[2,144,128]{2,1,0:T(8,128)(2,1)S(1)}) custom-call(bf16[12,48,128]{2,1,0:T(8,128)(2,1)S(1)} %collective-permute-done.pair_ref, bf16[4,144,128]{2,1,0:T(8,128)(2,1)S(1)} %get-tuple-element.19.sides_ref, ...), custom_call_target="tpu_custom_call" | custom-call | flops 75497472 | bytes 1179648 | tf_op jit(solution)/shard_map/pallas_call | solution.py:285
  2.7 3.6 %collective-permute-start.1 = (bf16[2,144,128]{2,1,0:T(8,128)(2,1)S(1)}, bf16[2,144,128]{2,1,0:T(8,128)(2,1)S(1)}, u32[]{:S(2)}, u32[]{:S(2)}) collective-permute-start(bf16[2,144,128]{2,1,0:T(8,128)(2,1)S(1)} %get-tuple-element.23), channel_id=1, source_target_pairs={{0,6},{2,4},{4,2},{6,0},{1,7},{3,5},{5,3},{7,1},{8,14},{10,12},{12... | collective-permute-start | bytes 221192 | tf_op jit(solution)/shard_map/ppermute | solution.py:295
  6.3 0.5 %collective-permute-start.2 = (bf16[2,144,128]{2,1,0:T(8,128)(2,1)S(1)}, bf16[2,144,128]{2,1,0:T(8,128)(2,1)S(1)}, u32[]{:S(2)}, u32[]{:S(2)}) collective-permute-start(bf16[2,144,128]{2,1,0:T(8,128)(2,1)S(1)} %get-tuple-element.24), channel_id=1, source_target_pairs={{0,2},{2,0},{4,6},{6,4},{1,3},{3,1},{5,7},{7,5},{8,10},{10,8},{12,... | collective-permute-start | bytes 221192 | tf_op jit(solution)/shard_map/ppermute | solution.py:295
  6.8 0.1 collective-permute-start.3
  7.0 2.3 %collective-permute-done.1.refs_0_ = bf16[2,144,128]{2,1,0:T(8,128)(2,1)S(1)} collective-permute-done((bf16[2,144,128]{2,1,0:T(8,128)(2,1)S(1)}, bf16[2,144,128]{2,1,0:T(8,128)(2,1)S(1)}, u32[]{:S(2)}, u32[]{:S(2)}) %collective-permute-start.1) | collective-permute-done | bytes 73760 | tf_op jit(solution)/shard_map/ppermute | solution.py:295
  9.3 1.6 %collective-permute-done.2.refs_1_ = bf16[2,144,128]{2,1,0:T(8,128)(2,1)S(1)} collective-permute-done((bf16[2,144,128]{2,1,0:T(8,128)(2,1)S(1)}, bf16[2,144,128]{2,1,0:T(8,128)(2,1)S(1)}, u32[]{:S(2)}, u32[]{:S(2)}) %collective-permute-start.2) | collective-permute-done | bytes 73760 | tf_op jit(solution)/shard_map/ppermute | solution.py:295
  10.9 0.3 %collective-permute-done.3.refs_2_ = bf16[2,144,128]{2,1,0:T(8,128)(2,1)S(1)} collective-permute-done((bf16[2,144,128]{2,1,0:T(8,128)(2,1)S(1)}, bf16[2,144,128]{2,1,0:T(8,128)(2,1)S(1)}, u32[]{:S(2)}, u32[]{:S(2)}) %collective-permute-start.3) | collective-permute-done | bytes 73760 | tf_op jit(solution)/shard_map/ppermute | solution.py:295
  11.2 1.6 %shard_map.93 = bf16[16,72,128]{2,1,0:T(8,128)(2,1)} custom-call(bf16[2,144,128]{2,1,0:T(8,128)(2,1)S(1)} %collective-permute-done.1.refs_0_, bf16[2,144,128]{2,1,0:T(8,128)(2,1)S(1)} %collective-permute-done.2.refs_1_, bf16[2,144,128]{2,1,0:T(8,128)(2,1)S(1)} %collective-permute-done.3.refs_2_, bf16[2,144,128]{2,1,0:T(8,128)(2,1)S(1)} %get-tuple-element.26.refs_3_, ...), custom_call_target="tpu_custom_call" | custom-call | tf_op jit(solution)/shard_map/pallas_call | solution.py:296
  12.8 0.0 copy-start.1
  12.8 5.3 %all-to-all-start = ((bf16[16,72,128]{2,1,0:T(8,128)(2,1)}), bf16[16,72,128]{2,1,0:T(8,128)(2,1)S(1)}, u32[]{:S(2)}, u32[]{:S(2)}) async-start(bf16[16,72,128]{2,1,0:T(8,128)(2,1)} %shard_map.93), calls=%async_computation | async-start | bytes 589824 | tf_op jit(solution)/shard_map/all_to_all | solution.py:319
  18.1 0.0 copy-start.2
  18.1 0.0 copy-start.3
  18.1 0.0 copy-done.1
  18.1 0.6 %copy-done.2 = f32[128]{0:T(128)S(1)} copy-done((f32[128]{0:T(128)S(1)}, f32[128]{0:T(128)}, u32[]{:S(2)}) %copy-start.2) | copy-done | bytes 536
  18.7 0.0 copy-done.3
  18.8 0.0 copy-start
  18.8 0.2 shard_map.94
  19.0 6.5 %all-to-all-done.total_ref = bf16[16,72,128]{2,1,0:T(8,128)(2,1)S(1)} async-done(((bf16[16,72,128]{2,1,0:T(8,128)(2,1)}), bf16[16,72,128]{2,1,0:T(8,128)(2,1)S(1)}, u32[]{:S(2)}, u32[]{:S(2)}) %all-to-all-start) | async-done | bytes 294944 | tf_op jit(solution)/shard_map/all_to_all | solution.py:319
  25.5 0.0 copy-done
  25.5 1.0 %shard_map.95 = bf16[12,48,128]{2,1,0:T(8,128)(2,1)} custom-call(bf16[16,72,128]{2,1,0:T(8,128)(2,1)S(1)} %all-to-all-done.total_ref, f32[576,128]{1,0:T(8,128)S(1)} %get-tuple-element.30.gate_ref, f32[128,1]{1,0:T(8,128)S(1)} %get-tuple-element.31.gain_ref, f32[128,1]{1,0:T(8,128)S(1)} %get-tuple-element.32.bias_ref, bf16[128,128]{1,0:T(8,128)(2,1)S(1)} %copy-done), custom_call_target="tpu_custom_call" | custom-call | tf_op jit(solution)/shard_map/pallas_call | solution.py:320
Async XLA Ops:
  0.0 2.2 %collective-permute-start = (bf16[12,48,128]{2,1,0:T(8,128)(2,1)}, bf16[12,48,128]{2,1,0:T(8,128)(2,1)S(1)}, u32[]{:S(2)}, u32[]{:S(2)}) collective-permute-start(bf16[12,48,128]{2,1,0:T(8,128)(2,1)} %pair_hbm.1), channel_id=1, source_target_pairs={{0,1},{1,0},{2,3},{3,2},{4,5},{5,4},{6,7},{7,6},{8,9},{9,8},{10,11... | collective-permute-start | bytes 442376 | tf_op jit(solution)/shard_map/ppermute | solution.py:260
  2.7 6.5 %collective-permute-start.1 = (bf16[2,144,128]{2,1,0:T(8,128)(2,1)S(1)}, bf16[2,144,128]{2,1,0:T(8,128)(2,1)S(1)}, u32[]{:S(2)}, u32[]{:S(2)}) collective-permute-start(bf16[2,144,128]{2,1,0:T(8,128)(2,1)S(1)} %get-tuple-element.23), channel_id=1, source_target_pairs={{0,6},{2,4},{4,2},{6,0},{1,7},{3,5},{5,3},{7,1},{8,14},{10,12},{12... | collective-permute-start | bytes 221192 | tf_op jit(solution)/shard_map/ppermute | solution.py:295
  6.3 4.5 %collective-permute-start.2 = (bf16[2,144,128]{2,1,0:T(8,128)(2,1)S(1)}, bf16[2,144,128]{2,1,0:T(8,128)(2,1)S(1)}, u32[]{:S(2)}, u32[]{:S(2)}) collective-permute-start(bf16[2,144,128]{2,1,0:T(8,128)(2,1)S(1)} %get-tuple-element.24), channel_id=1, source_target_pairs={{0,2},{2,0},{4,6},{6,4},{1,3},{3,1},{5,7},{7,5},{8,10},{10,8},{12,... | collective-permute-start | bytes 221192 | tf_op jit(solution)/shard_map/ppermute | solution.py:295
  6.8 4.4 %collective-permute-start.3 = (bf16[2,144,128]{2,1,0:T(8,128)(2,1)S(1)}, bf16[2,144,128]{2,1,0:T(8,128)(2,1)S(1)}, u32[]{:S(2)}, u32[]{:S(2)}) collective-permute-start(bf16[2,144,128]{2,1,0:T(8,128)(2,1)S(1)} %get-tuple-element.25), channel_id=1, source_target_pairs={{0,4},{2,6},{4,0},{6,2},{1,5},{3,7},{5,1},{7,3},{8,12},{10,14},{12... | collective-permute-start | bytes 221192 | tf_op jit(solution)/shard_map/ppermute | solution.py:295
  12.8 5.3 %copy-start.1 = (bf16[128,128]{1,0:T(8,128)(2,1)S(1)}, bf16[128,128]{1,0:T(8,128)(2,1)}, u32[]{:S(2)}) copy-start(bf16[128,128]{1,0:T(8,128)(2,1)} %w_ref.2) | copy-start | bytes 98308
  12.8 12.7 %all-to-all-start = ((bf16[16,72,128]{2,1,0:T(8,128)(2,1)}), bf16[16,72,128]{2,1,0:T(8,128)(2,1)S(1)}, u32[]{:S(2)}, u32[]{:S(2)}) async-start(bf16[16,72,128]{2,1,0:T(8,128)(2,1)} %shard_map.93), calls=%async_computation | async-start | bytes 589824 | tf_op jit(solution)/shard_map/all_to_all | solution.py:319
  18.1 0.7 %copy-start.2 = (f32[128]{0:T(128)S(1)}, f32[128]{0:T(128)}, u32[]{:S(2)}) copy-start(f32[128]{0:T(128)} %param.15) | copy-start | bytes 1540
  18.1 0.7 %copy-start.3 = (f32[128]{0:T(128)S(1)}, f32[128]{0:T(128)}, u32[]{:S(2)}) copy-start(f32[128]{0:T(128)} %param.16) | copy-start | bytes 1540
  18.8 6.7 %copy-start = (bf16[128,128]{1,0:T(8,128)(2,1)S(1)}, bf16[128,128]{1,0:T(8,128)(2,1)}, u32[]{:S(2)}) copy-start(bf16[128,128]{1,0:T(8,128)(2,1)} %w_ref.3) | copy-start | bytes 98308

commit v31 on v28

--- a/solution.py
+++ b/solution.py
@@ -78,9 +78,9 @@
 
 
 def project(normed, w, shape, quads):
-    ours = w.shape[1] // 4
+    ours = w.shape[0] // 4
     tokens = normed.shape[0]
-    projected = lax.dot_general(w, arrange(normed.reshape(shape)), (((0,), (1,)), ((), ())), preferred_element_type=jnp.float32)
+    projected = lax.dot_general(w, arrange(normed.reshape(shape)), (((1,), (1,)), ((), ())), preferred_element_type=jnp.float32)
     left = sigmoid(projected[:ours]) * projected[ours : 2 * ours]
     right = sigmoid(projected[2 * ours : 3 * ours]) * projected[3 * ours :]
     sides = jnp.concatenate([left.reshape(quads, -1, tokens), right.reshape(quads, -1, tokens)], axis=1)
@@ -118,7 +118,7 @@
     normed_ref[...] = normed
     copies[4].wait()
     parts = [all_w_ref[:, at : at + hidden] for at in range(0, 4 * hidden, hidden)]
-    w = jnp.concatenate([jnp.where(my_col == 0, part[:, :ours], part[:, ours:]) for part in parts], axis=1)
+    w = jnp.concatenate([jnp.where(my_col == 0, part[:, :ours], part[:, ours:]) for part in parts], axis=1).T
     w_ref[...] = w
     sides_ref[...] = project(normed, w, pair_ref.shape, quads)
 
@@ -257,7 +257,7 @@
             jax.ShapeDtypeStruct((tokens, channels), jnp.bfloat16),
             jax.ShapeDtypeStruct((GROUP, GROUP * depth), jnp.float32),
             jax.ShapeDtypeStruct((length, 1), jnp.float32),
-            jax.ShapeDtypeStruct((channels, 4 * hidden // cols), jnp.bfloat16),
+            jax.ShapeDtypeStruct((4 * hidden // cols, channels), jnp.bfloat16),
             jax.ShapeDtypeStruct((1, channels), jnp.float32),
             jax.ShapeDtypeStruct((1, channels), jnp.float32),
         ),

time: 26.8 us -> 26.8 us (level)
  no operation moved by 1% of the time
where the time goes in v31:
time: 26.8 us; the launch traced here: 26.5 us
  waiting for transfers between devices  10.7 us (40%)
  starting transfers between devices  9.98 us (37%)
  Pallas kernels  5.05 us (19%)
  local copies, waits for them, and re-layouts  0.65 us (2%)
    all_to_all x1, waiting for transfers between devices, per_device(): lax.all_to_all(total, ('half', 'quad', 'col'), split_axis=0, concat_axis=...  6.52 us
    all_to_all x1, starting transfers between devices, per_device(): lax.all_to_all(total, ('half', 'quad', 'col'), split_axis=0, concat_axis=...  5.29 us
    ppermute x3, starting transfers between devices, per_device(): lax.ppermute(pieces[step], 'quad', [(i, i ^ step) for i in range(quads)])  4.24 us
    ppermute x3, waiting for transfers between devices, per_device(): lax.ppermute(pieces[step], 'quad', [(i, i ^ step) for i in range(quads)])  4.21 us
    pallas_call x1, Pallas kernels, per_device(): pl.pallas_call(functools.partial(own_kernel, quads, cols), out_shape=(jax...  1.71 us
    pallas_call x1, Pallas kernels, per_device(): pl.pallas_call(functools.partial(triangle_kernel, far_order, steps, cols,...  1.61 us
    pallas_call x1, Pallas kernels, per_device(): pl.pallas_call(functools.partial(output_kernel, far_order, near_order), o...  1.02 us
    unnamed x8, local copies, waits for them, and re-layouts  0.65 us
  transfers between devices with their start and end apart: 5, of which 4 were waited for; matrix products, arithmetic and copies ran while one was open for 0% of the time, Pallas kernels for 7%

profile of v31, /device:TPU:0, one launch (start us, length us, event | category | flops | bytes accessed | tf_op | source)
XLA Modules:
  0.0 26.5 jit_solution(4153698483600255655)
XLA Ops:
  0.0 0.5 %collective-permute-start = (bf16[12,48,128]{2,1,0:T(8,128)(2,1)}, bf16[12,48,128]{2,1,0:T(8,128)(2,1)S(1)}, u32[]{:S(2)}, u32[]{:S(2)}) collective-permute-start(bf16[12,48,128]{2,1,0:T(8,128)(2,1)} %pair_hbm.1), channel_id=1, source_target_pairs={{0,1},{1,0},{2,3},{3,2},{4,5},{5,4},{6,7},{7,6},{8,9},{9,8},{10,11... | collective-permute-start | bytes 442376 | tf_op jit(solution)/shard_map/ppermute | solution.py:251
  0.5 1.7 %shard_map.91 = (bf16[4,144,128]{2,1,0:T(8,128)(2,1)S(1)}, bf16[576,128]{1,0:T(8,128)(2,1)S(1)}, f32[8,384]{1,0:T(8,128)S(1)}, f32[96,1]{1,0:T(8,128)S(1)}, bf16...) custom-call(bf16[12,48,128]{2,1,0:T(8,128)(2,1)} %pair_hbm.1, f32[1,128]{1,0:T(1,128)} %bitcast.7, ...), custom_call_target="tpu_custom_call" | custom-call | flops 75497472 | bytes 1179648 | tf_op jit(solution)/shard_map/pallas_call | solution.py:253
  2.2 0.0 collective-permute-done.pair_ref
  2.2 0.5 %shard_map.92 = (bf16[2,144,128]{2,1,0:T(8,128)(2,1)S(1)}, bf16[2,144,128]{2,1,0:T(8,128)(2,1)S(1)}, bf16[2,144,128]{2,1,0:T(8,128)(2,1)S(1)}, bf16[2,144,128]{2,1,0:T(8,128)(2,1)S(1)}) custom-call(bf16[12,48,128]{2,1,0:T(8,128)(2,1)S(1)} %collective-permute-done.pair_ref, bf16[4,144,128]{2,1,0:T(8,128)(2,1)S(1)} %get-tuple-element.19.sides_ref, ...), custom_call_target="tpu_custom_call" | custom-call | flops 75497472 | bytes 1179648 | tf_op jit(solution)/shard_map/pallas_call | solution.py:276
  2.7 3.6 %collective-permute-start.1 = (bf16[2,144,128]{2,1,0:T(8,128)(2,1)S(1)}, bf16[2,144,128]{2,1,0:T(8,128)(2,1)S(1)}, u32[]{:S(2)}, u32[]{:S(2)}) collective-permute-start(bf16[2,144,128]{2,1,0:T(8,128)(2,1)S(1)} %get-tuple-element.23), channel_id=1, source_target_pairs={{0,6},{2,4},{4,2},{6,0},{1,7},{3,5},{5,3},{7,1},{8,14},{10,12},{12... | collective-permute-start | bytes 221192 | tf_op jit(solution)/shard_map/ppermute | solution.py:286
  6.3 0.5 %collective-permute-start.2 = (bf16[2,144,128]{2,1,0:T(8,128)(2,1)S(1)}, bf16[2,144,128]{2,1,0:T(8,128)(2,1)S(1)}, u32[]{:S(2)}, u32[]{:S(2)}) collective-permute-start(bf16[2,144,128]{2,1,0:T(8,128)(2,1)S(1)} %get-tuple-element.24), channel_id=1, source_target_pairs={{0,2},{2,0},{4,6},{6,4},{1,3},{3,1},{5,7},{7,5},{8,10},{10,8},{12,... | collective-permute-start | bytes 221192 | tf_op jit(solution)/shard_map/ppermute | solution.py:286
  6.8 0.1 collective-permute-start.3
  7.0 2.3 %collective-permute-done.1.refs_0_ = bf16[2,144,128]{2,1,0:T(8,128)(2,1)S(1)} collective-permute-done((bf16[2,144,128]{2,1,0:T(8,128)(2,1)S(1)}, bf16[2,144,128]{2,1,0:T(8,128)(2,1)S(1)}, u32[]{:S(2)}, u32[]{:S(2)}) %collective-permute-start.1) | collective-permute-done | bytes 73760 | tf_op jit(solution)/shard_map/ppermute | solution.py:286
  9.3 1.6 %collective-permute-done.2.refs_1_ = bf16[2,144,128]{2,1,0:T(8,128)(2,1)S(1)} collective-permute-done((bf16[2,144,128]{2,1,0:T(8,128)(2,1)S(1)}, bf16[2,144,128]{2,1,0:T(8,128)(2,1)S(1)}, u32[]{:S(2)}, u32[]{:S(2)}) %collective-permute-start.2) | collective-permute-done | bytes 73760 | tf_op jit(solution)/shard_map/ppermute | solution.py:286
  10.8 0.3 %collective-permute-done.3.refs_2_ = bf16[2,144,128]{2,1,0:T(8,128)(2,1)S(1)} collective-permute-done((bf16[2,144,128]{2,1,0:T(8,128)(2,1)S(1)}, bf16[2,144,128]{2,1,0:T(8,128)(2,1)S(1)}, u32[]{:S(2)}, u32[]{:S(2)}) %collective-permute-start.3) | collective-permute-done | bytes 73760 | tf_op jit(solution)/shard_map/ppermute | solution.py:286
  11.2 1.6 %shard_map.93 = bf16[16,72,128]{2,1,0:T(8,128)(2,1)} custom-call(bf16[2,144,128]{2,1,0:T(8,128)(2,1)S(1)} %collective-permute-done.1.refs_0_, bf16[2,144,128]{2,1,0:T(8,128)(2,1)S(1)} %collective-permute-done.2.refs_1_, bf16[2,144,128]{2,1,0:T(8,128)(2,1)S(1)} %collective-permute-done.3.refs_2_, bf16[2,144,128]{2,1,0:T(8,128)(2,1)S(1)} %get-tuple-element.26.refs_3_, ...), custom_call_target="tpu_custom_call" | custom-call | tf_op jit(solution)/shard_map/pallas_call | solution.py:287
  12.8 0.0 copy-start.1
  12.8 5.3 %all-to-all-start = ((bf16[16,72,128]{2,1,0:T(8,128)(2,1)}), bf16[16,72,128]{2,1,0:T(8,128)(2,1)S(1)}, u32[]{:S(2)}, u32[]{:S(2)}) async-start(bf16[16,72,128]{2,1,0:T(8,128)(2,1)} %shard_map.93), calls=%async_computation | async-start | bytes 589824 | tf_op jit(solution)/shard_map/all_to_all | solution.py:310
  18.1 0.0 copy-start.2
  18.1 0.0 copy-start.3
  18.1 0.0 copy-done.1
  18.1 0.6 %copy-done.2 = f32[128]{0:T(128)S(1)} copy-done((f32[128]{0:T(128)S(1)}, f32[128]{0:T(128)}, u32[]{:S(2)}) %copy-start.2) | copy-done | bytes 536
  18.7 0.0 copy-done.3
  18.7 0.0 copy-start
  18.8 0.2 shard_map.94
  18.9 6.5 %all-to-all-done.total_ref = bf16[16,72,128]{2,1,0:T(8,128)(2,1)S(1)} async-done(((bf16[16,72,128]{2,1,0:T(8,128)(2,1)}), bf16[16,72,128]{2,1,0:T(8,128)(2,1)S(1)}, u32[]{:S(2)}, u32[]{:S(2)}) %all-to-all-start) | async-done | bytes 294944 | tf_op jit(solution)/shard_map/all_to_all | solution.py:310
  25.5 0.0 copy-done
  25.5 1.0 %shard_map.95 = bf16[12,48,128]{2,1,0:T(8,128)(2,1)} custom-call(bf16[16,72,128]{2,1,0:T(8,128)(2,1)S(1)} %all-to-all-done.total_ref, f32[576,128]{1,0:T(8,128)S(1)} %get-tuple-element.30.gate_ref, f32[128,1]{1,0:T(8,128)S(1)} %get-tuple-element.31.gain_ref, f32[128,1]{1,0:T(8,128)S(1)} %get-tuple-element.32.bias_ref, bf16[128,128]{1,0:T(8,128)(2,1)S(1)} %copy-done), custom_call_target="tpu_custom_call" | custom-call | tf_op jit(solution)/shard_map/pallas_call | solution.py:311
Async XLA Ops:
  0.0 2.2 %collective-permute-start = (bf16[12,48,128]{2,1,0:T(8,128)(2,1)}, bf16[12,48,128]{2,1,0:T(8,128)(2,1)S(1)}, u32[]{:S(2)}, u32[]{:S(2)}) collective-permute-start(bf16[12,48,128]{2,1,0:T(8,128)(2,1)} %pair_hbm.1), channel_id=1, source_target_pairs={{0,1},{1,0},{2,3},{3,2},{4,5},{5,4},{6,7},{7,6},{8,9},{9,8},{10,11... | collective-permute-start | bytes 442376 | tf_op jit(solution)/shard_map/ppermute | solution.py:251
  2.7 6.6 %collective-permute-start.1 = (bf16[2,144,128]{2,1,0:T(8,128)(2,1)S(1)}, bf16[2,144,128]{2,1,0:T(8,128)(2,1)S(1)}, u32[]{:S(2)}, u32[]{:S(2)}) collective-permute-start(bf16[2,144,128]{2,1,0:T(8,128)(2,1)S(1)} %get-tuple-element.23), channel_id=1, source_target_pairs={{0,6},{2,4},{4,2},{6,0},{1,7},{3,5},{5,3},{7,1},{8,14},{10,12},{12... | collective-permute-start | bytes 221192 | tf_op jit(solution)/shard_map/ppermute | solution.py:286
  6.3 4.5 %collective-permute-start.2 = (bf16[2,144,128]{2,1,0:T(8,128)(2,1)S(1)}, bf16[2,144,128]{2,1,0:T(8,128)(2,1)S(1)}, u32[]{:S(2)}, u32[]{:S(2)}) collective-permute-start(bf16[2,144,128]{2,1,0:T(8,128)(2,1)S(1)} %get-tuple-element.24), channel_id=1, source_target_pairs={{0,2},{2,0},{4,6},{6,4},{1,3},{3,1},{5,7},{7,5},{8,10},{10,8},{12,... | collective-permute-start | bytes 221192 | tf_op jit(solution)/shard_map/ppermute | solution.py:286
  6.8 4.4 %collective-permute-start.3 = (bf16[2,144,128]{2,1,0:T(8,128)(2,1)S(1)}, bf16[2,144,128]{2,1,0:T(8,128)(2,1)S(1)}, u32[]{:S(2)}, u32[]{:S(2)}) collective-permute-start(bf16[2,144,128]{2,1,0:T(8,128)(2,1)S(1)} %get-tuple-element.25), channel_id=1, source_target_pairs={{0,4},{2,6},{4,0},{6,2},{1,5},{3,7},{5,1},{7,3},{8,12},{10,14},{12... | collective-permute-start | bytes 221192 | tf_op jit(solution)/shard_map/ppermute | solution.py:286
  12.8 5.3 %copy-start.1 = (bf16[128,128]{1,0:T(8,128)(2,1)S(1)}, bf16[128,128]{1,0:T(8,128)(2,1)}, u32[]{:S(2)}) copy-start(bf16[128,128]{1,0:T(8,128)(2,1)} %w_ref.2) | copy-start | bytes 98308
  12.8 12.7 %all-to-all-start = ((bf16[16,72,128]{2,1,0:T(8,128)(2,1)}), bf16[16,72,128]{2,1,0:T(8,128)(2,1)S(1)}, u32[]{:S(2)}, u32[]{:S(2)}) async-start(bf16[16,72,128]{2,1,0:T(8,128)(2,1)} %shard_map.93), calls=%async_computation | async-start | bytes 589824 | tf_op jit(solution)/shard_map/all_to_all | solution.py:310
  18.1 0.7 %copy-start.2 = (f32[128]{0:T(128)S(1)}, f32[128]{0:T(128)}, u32[]{:S(2)}) copy-start(f32[128]{0:T(128)} %param.15) | copy-start | bytes 1540
  18.1 0.7 %copy-start.3 = (f32[128]{0:T(128)S(1)}, f32[128]{0:T(128)}, u32[]{:S(2)}) copy-start(f32[128]{0:T(128)} %param.16) | copy-start | bytes 1540
  18.7 6.7 %copy-start = (bf16[128,128]{1,0:T(8,128)(2,1)S(1)}, bf16[128,128]{1,0:T(8,128)(2,1)}, u32[]{:S(2)}) copy-start(bf16[128,128]{1,0:T(8,128)(2,1)} %w_ref.3) | copy-start | bytes 98308

commit v32 on v31

--- a/solution.py
+++ b/solution.py
@@ -87,7 +87,12 @@
     return pack(sides).astype(jnp.bfloat16)
 
 
-def own_kernel(quads, cols, pair_hbm, gain_hbm, bias_hbm, w_hbm, mask_hbm, sides_ref, normed_ref, spread_ref, column_mask_ref, w_ref, gain_ref, bias_ref, pair_ref, all_w_ref, mask_ref, sems):
+def my_steps(steps):
+    my_col = lax.axis_index("col")
+    return [jnp.where(my_col == 0, first, second) for first, second in steps]
+
+
+def own_kernel(steps, quads, cols, pair_hbm, gain_hbm, bias_hbm, w_hbm, mask_hbm, sides_ref, normed_ref, spread_ref, column_mask_ref, w_ref, gain_ref, bias_ref, pair_ref, all_w_ref, mask_ref, sems):
     moves = [(mask_hbm, mask_ref), (pair_hbm, pair_ref), (gain_hbm, gain_ref), (bias_hbm, bias_ref), (w_hbm, all_w_ref)]
     copies = [pltpu.make_async_copy(source, target, sems.at[n]) for n, (source, target) in enumerate(moves)]
     for copy in copies:
@@ -105,8 +110,9 @@
     token = lax.broadcasted_iota(jnp.int32, (mask_row.shape[1], lanes), 0)
     lane = lax.broadcasted_iota(jnp.int32, (mask_row.shape[1], lanes), 1)
     whole = row_count // 3
-    block, t, row = lane // LANES, lane // (quads * group) % whole, lane // group % quads
-    k = (row ^ my_quad) * row_count + jnp.where(block < 2, 2 * t + block, 2 * whole + t)
+    block, t, slot = lane // LANES, lane // (quads * group) % whole, lane // group % quads
+    row = my_quad ^ sum(jnp.where(slot == n, step, 0) for n, step in enumerate(my_steps(steps)))
+    k = row * row_count + jnp.where(block < 2, 2 * t + block, 2 * whole + t)
     pick = jnp.where(k + start == token, 1.0, 0.0)
     kept = jnp.dot(mask_row.astype(jnp.bfloat16), pick.astype(jnp.bfloat16), preferred_element_type=jnp.float32)
     channel = lax.broadcasted_iota(jnp.int32, (group, lanes), 0)
@@ -123,24 +129,23 @@
     sides_ref[...] = project(normed, w, pair_ref.shape, quads)
 
 
-def other_kernel(pair_ref, sides_ref, gain_ref, bias_ref, w_ref, *refs):
+def other_kernel(steps, pair_ref, sides_ref, gain_ref, bias_ref, w_ref, *refs):
     *piece_refs, others_ref = refs
     my_quad, my_col = lax.axis_index("quad"), lax.axis_index("col")
     quads = sides_ref.shape[0]
     normed = normalise(pair_ref[...].reshape(-1, pair_ref.shape[2]), gain_ref[...], bias_ref[...])
     others_ref[...] = project(normed, w_ref[...], pair_ref.shape, quads)
-    for step, piece_ref in enumerate(piece_refs):
+    for step, piece_ref in zip(my_steps(steps), piece_refs):
         piece_ref[my_col] = sides_ref[my_quad ^ step]
         piece_ref[1 - my_col] = others_ref[my_quad ^ step]
 
 
-def triangle_kernel(far_order, steps, cols, row_count, col_count, share, *refs):
+def triangle_kernel(far_order, cols, row_count, col_count, share, *refs):
     *got_refs, spread_ref, mask_ref, total_ref, left_ref, wide_ref = refs
-    got_refs = {step: ref for step, ref in zip(steps, got_refs)}
     both = 2 * share
     group, lanes = spread_ref.shape
     length = mask_ref.shape[0]
-    rows, quads, parts = length // row_count, len(steps), share // group
+    rows, quads, parts = length // row_count, len(got_refs), share // group
     whole, spare = row_count // 3, LANES - 2 * col_count
     rest = col_count - spare
     blocks = [[got_refs[row][col].astype(jnp.float32) for row in range(quads)] for col in range(cols)]
@@ -248,10 +253,11 @@
     near_order = [quad * cols + col for col in range(cols) for quad in range(quads)]
     packed = 2 * share * tokens // LANES
     cost = pl.CostEstimate(flops=2 * tokens * channels * 4 * hidden, bytes_accessed=16 * tokens * channels, transcendentals=0)
+    steps = [(3, 1), (1, 2), (2, 3), (0, 0)]
     other_pair = lax.ppermute(pair, "col", [(i, (i + 1) % cols) for i in range(cols)])
     arguments = (pair, gain_in.reshape(1, channels), bias_in.reshape(1, channels), w_in, token_mask)
     sides, normed, spread, mask, *weights = pl.pallas_call(
-        functools.partial(own_kernel, quads, cols),
+        functools.partial(own_kernel, steps, quads, cols),
         out_shape=(
             jax.ShapeDtypeStruct((quads, packed, LANES), jnp.bfloat16),
             jax.ShapeDtypeStruct((tokens, channels), jnp.bfloat16),
@@ -274,7 +280,7 @@
     )(*(pltpu.with_memory_space_constraint(x, pltpu.HBM) for x in arguments))
     w_ours, gain_in, bias_in = weights
     pieces = pl.pallas_call(
-        other_kernel,
+        functools.partial(other_kernel, steps),
         out_shape=[jax.ShapeDtypeStruct((cols, packed, LANES), jnp.bfloat16)] * quads,
         in_specs=[VMEM] * 5,
         out_specs=[VMEM] * quads,
@@ -282,10 +288,12 @@
         compiler_params=LIMIT,
         cost_estimate=cost,
     )(other_pair, sides, gain_in, bias_in, w_ours)
-    steps = [3, 1, 2, 0]
-    got = [lax.ppermute(pieces[step], "quad", [(i, i ^ step) for i in range(quads)]) if step else pieces[0] for step in steps]
+    got = []
+    for piece, step in zip(pieces, steps):
+        moves = [(quad * cols + col, (quad ^ step[col]) * cols + col) for quad in range(quads) for col in range(cols)]
+        got.append(lax.ppermute(piece, ("quad", "col"), moves) if any(step) else piece)
     total = pl.pallas_call(
-        functools.partial(triangle_kernel, far_order, steps, cols, row_count, col_count, share),
+        functools.partial(triangle_kernel, far_order, cols, row_count, col_count, share),
         out_shape=jax.ShapeDtypeStruct((devices, share * tokens // LANES, LANES), jnp.bfloat16),
         in_specs=[VMEM] * (quads + 2),
         out_specs=VMEM,

time: 26.8 us -> 27 us (level)
    ppermute x3, waiting for transfers between devices: 4.21 us -> 4.5 us  [per_device(): lax.ppermute(piece, ('quad', 'col'), moves)]
  transfers between devices with their start and end apart: 5 -> 5, of which waited for: 4 -> 3; matrix products, arithmetic and copies ran while one was open for 0% -> 0% of each run, Pallas kernels for 7% -> 7%
where the time goes in v32:
time: 27 us; the launch traced here: 26.7 us
  waiting for transfers between devices  10.9 us (40%)
  starting transfers between devices  10 us (37%)
  Pallas kernels  5.06 us (19%)
  local copies, waits for them, and re-layouts  0.65 us (2%)
    all_to_all x1, waiting for transfers between devices, per_device(): lax.all_to_all(total, ('half', 'quad', 'col'), split_axis=0, concat_axis=...  6.4 us
    all_to_all x1, starting transfers between devices, per_device(): lax.all_to_all(total, ('half', 'quad', 'col'), split_axis=0, concat_axis=...  5.32 us
    ppermute x3, waiting for transfers between devices, per_device(): lax.ppermute(piece, ('quad', 'col'), moves)  4.5 us
    ppermute x3, starting transfers between devices, per_device(): lax.ppermute(piece, ('quad', 'col'), moves)  4.24 us
    pallas_call x1, Pallas kernels, per_device(): pl.pallas_call(functools.partial(own_kernel, steps, quads, cols), out_sha...  1.71 us
    pallas_call x1, Pallas kernels, per_device(): pl.pallas_call(functools.partial(triangle_kernel, far_order, cols, row_co...  1.61 us
    pallas_call x1, Pallas kernels, per_device(): pl.pallas_call(functools.partial(output_kernel, far_order, near_order), o...  1.02 us
    unnamed x8, local copies, waits for them, and re-layouts  0.65 us
  transfers between devices with their start and end apart: 5, of which 3 were waited for; matrix products, arithmetic and copies ran while one was open for 0% of the time, Pallas kernels for 7%

profile of v32, /device:TPU:0, one launch (start us, length us, event | category | flops | bytes accessed | tf_op | source)
XLA Modules:
  0.0 26.7 jit_solution(12616612628858498417)
XLA Ops:
  0.0 0.5 %collective-permute-start = (bf16[12,48,128]{2,1,0:T(8,128)(2,1)}, bf16[12,48,128]{2,1,0:T(8,128)(2,1)S(1)}, u32[]{:S(2)}, u32[]{:S(2)}) collective-permute-start(bf16[12,48,128]{2,1,0:T(8,128)(2,1)} %pair_hbm.1), channel_id=1, source_target_pairs={{0,1},{1,0},{2,3},{3,2},{4,5},{5,4},{6,7},{7,6},{8,9},{9,8},{10,11... | collective-permute-start | bytes 442376 | tf_op jit(solution)/shard_map/ppermute | solution.py:257
  0.5 1.7 %shard_map.91 = (bf16[4,144,128]{2,1,0:T(8,128)(2,1)S(1)}, bf16[576,128]{1,0:T(8,128)(2,1)S(1)}, f32[8,384]{1,0:T(8,128)S(1)}, f32[96,1]{1,0:T(8,128)S(1)}, bf16...) custom-call(bf16[12,48,128]{2,1,0:T(8,128)(2,1)} %pair_hbm.1, f32[1,128]{1,0:T(1,128)} %bitcast.7, ...), custom_call_target="tpu_custom_call" | custom-call | flops 75497472 | bytes 1179648 | tf_op jit(solution)/shard_map/pallas_call | solution.py:259
  2.2 0.0 collective-permute-done.pair_ref
  2.2 0.5 %shard_map.92 = (bf16[2,144,128]{2,1,0:T(8,128)(2,1)S(1)}, bf16[2,144,128]{2,1,0:T(8,128)(2,1)S(1)}, bf16[2,144,128]{2,1,0:T(8,128)(2,1)S(1)}, bf16[2,144,128]{2,1,0:T(8,128)(2,1)S(1)}) custom-call(bf16[12,48,128]{2,1,0:T(8,128)(2,1)S(1)} %collective-permute-done.pair_ref, bf16[4,144,128]{2,1,0:T(8,128)(2,1)S(1)} %get-tuple-element.19.sides_ref, ...), custom_call_target="tpu_custom_call" | custom-call | flops 75497472 | bytes 1179648 | tf_op jit(solution)/shard_map/pallas_call | solution.py:282
  2.7 3.6 %collective-permute-start.1 = (bf16[2,144,128]{2,1,0:T(8,128)(2,1)S(1)}, bf16[2,144,128]{2,1,0:T(8,128)(2,1)S(1)}, u32[]{:S(2)}, u32[]{:S(2)}) collective-permute-start(bf16[2,144,128]{2,1,0:T(8,128)(2,1)S(1)} %get-tuple-element.23), channel_id=1, source_target_pairs={{0,6},{1,3},{2,4},{3,1},{4,2},{5,7},{6,0},{7,5},{8,14},{9,11},{10,... | collective-permute-start | bytes 221192 | tf_op jit(solution)/shard_map/ppermute | solution.py:294
  6.3 0.5 %collective-permute-start.2 = (bf16[2,144,128]{2,1,0:T(8,128)(2,1)S(1)}, bf16[2,144,128]{2,1,0:T(8,128)(2,1)S(1)}, u32[]{:S(2)}, u32[]{:S(2)}) collective-permute-start(bf16[2,144,128]{2,1,0:T(8,128)(2,1)S(1)} %get-tuple-element.24), channel_id=1, source_target_pairs={{0,2},{1,5},{2,0},{3,7},{4,6},{5,1},{6,4},{7,3},{8,10},{9,13},{10,... | collective-permute-start | bytes 221192 | tf_op jit(solution)/shard_map/ppermute | solution.py:294
  6.8 0.1 collective-permute-start.3
  7.0 2.4 %collective-permute-done.1.refs_0_ = bf16[2,144,128]{2,1,0:T(8,128)(2,1)S(1)} collective-permute-done((bf16[2,144,128]{2,1,0:T(8,128)(2,1)S(1)}, bf16[2,144,128]{2,1,0:T(8,128)(2,1)S(1)}, u32[]{:S(2)}, u32[]{:S(2)}) %collective-permute-start.1) | collective-permute-done | bytes 73760 | tf_op jit(solution)/shard_map/ppermute | solution.py:294
  9.4 2.1 %collective-permute-done.2.refs_1_ = bf16[2,144,128]{2,1,0:T(8,128)(2,1)S(1)} collective-permute-done((bf16[2,144,128]{2,1,0:T(8,128)(2,1)S(1)}, bf16[2,144,128]{2,1,0:T(8,128)(2,1)S(1)}, u32[]{:S(2)}, u32[]{:S(2)}) %collective-permute-start.2) | collective-permute-done | bytes 73760 | tf_op jit(solution)/shard_map/ppermute | solution.py:294
  11.5 0.0 collective-permute-done.3.refs_2_
  11.5 1.6 %shard_map.93 = bf16[16,72,128]{2,1,0:T(8,128)(2,1)} custom-call(bf16[2,144,128]{2,1,0:T(8,128)(2,1)S(1)} %collective-permute-done.1.refs_0_, bf16[2,144,128]{2,1,0:T(8,128)(2,1)S(1)} %collective-permute-done.2.refs_1_, bf16[2,144,128]{2,1,0:T(8,128)(2,1)S(1)} %collective-permute-done.3.refs_2_, bf16[2,144,128]{2,1,0:T(8,128)(2,1)S(1)} %get-tuple-element.26.refs_3_, ...), custom_call_target="tpu_custom_call" | custom-call | tf_op jit(solution)/shard_map/pallas_call | solution.py:295
  13.1 0.0 copy-start.1
  13.1 5.3 %all-to-all-start = ((bf16[16,72,128]{2,1,0:T(8,128)(2,1)}), bf16[16,72,128]{2,1,0:T(8,128)(2,1)S(1)}, u32[]{:S(2)}, u32[]{:S(2)}) async-start(bf16[16,72,128]{2,1,0:T(8,128)(2,1)} %shard_map.93), calls=%async_computation | async-start | bytes 589824 | tf_op jit(solution)/shard_map/all_to_all | solution.py:318
  18.4 0.0 copy-start.2
  18.4 0.0 copy-start.3
  18.4 0.0 copy-done.1
  18.4 0.6 %copy-done.2 = f32[128]{0:T(128)S(1)} copy-done((f32[128]{0:T(128)S(1)}, f32[128]{0:T(128)}, u32[]{:S(2)}) %copy-start.2) | copy-done | bytes 536
  19.1 0.0 copy-done.3
  19.1 0.0 copy-start
  19.1 0.2 shard_map.94
  19.3 6.4 %all-to-all-done.total_ref = bf16[16,72,128]{2,1,0:T(8,128)(2,1)S(1)} async-done(((bf16[16,72,128]{2,1,0:T(8,128)(2,1)}), bf16[16,72,128]{2,1,0:T(8,128)(2,1)S(1)}, u32[]{:S(2)}, u32[]{:S(2)}) %all-to-all-start) | async-done | bytes 294944 | tf_op jit(solution)/shard_map/all_to_all | solution.py:318
  25.7 0.0 copy-done
  25.7 1.0 %shard_map.95 = bf16[12,48,128]{2,1,0:T(8,128)(2,1)} custom-call(bf16[16,72,128]{2,1,0:T(8,128)(2,1)S(1)} %all-to-all-done.total_ref, f32[576,128]{1,0:T(8,128)S(1)} %get-tuple-element.30.gate_ref, f32[128,1]{1,0:T(8,128)S(1)} %get-tuple-element.31.gain_ref, f32[128,1]{1,0:T(8,128)S(1)} %get-tuple-element.32.bias_ref, bf16[128,128]{1,0:T(8,128)(2,1)S(1)} %copy-done), custom_call_target="tpu_custom_call" | custom-call | tf_op jit(solution)/shard_map/pallas_call | solution.py:319
Async XLA Ops:
  0.0 2.2 %collective-permute-start = (bf16[12,48,128]{2,1,0:T(8,128)(2,1)}, bf16[12,48,128]{2,1,0:T(8,128)(2,1)S(1)}, u32[]{:S(2)}, u32[]{:S(2)}) collective-permute-start(bf16[12,48,128]{2,1,0:T(8,128)(2,1)} %pair_hbm.1), channel_id=1, source_target_pairs={{0,1},{1,0},{2,3},{3,2},{4,5},{5,4},{6,7},{7,6},{8,9},{9,8},{10,11... | collective-permute-start | bytes 442376 | tf_op jit(solution)/shard_map/ppermute | solution.py:257
  2.7 6.7 %collective-permute-start.1 = (bf16[2,144,128]{2,1,0:T(8,128)(2,1)S(1)}, bf16[2,144,128]{2,1,0:T(8,128)(2,1)S(1)}, u32[]{:S(2)}, u32[]{:S(2)}) collective-permute-start(bf16[2,144,128]{2,1,0:T(8,128)(2,1)S(1)} %get-tuple-element.23), channel_id=1, source_target_pairs={{0,6},{1,3},{2,4},{3,1},{4,2},{5,7},{6,0},{7,5},{8,14},{9,11},{10,... | collective-permute-start | bytes 221192 | tf_op jit(solution)/shard_map/ppermute | solution.py:294
  6.3 5.1 %collective-permute-start.2 = (bf16[2,144,128]{2,1,0:T(8,128)(2,1)S(1)}, bf16[2,144,128]{2,1,0:T(8,128)(2,1)S(1)}, u32[]{:S(2)}, u32[]{:S(2)}) collective-permute-start(bf16[2,144,128]{2,1,0:T(8,128)(2,1)S(1)} %get-tuple-element.24), channel_id=1, source_target_pairs={{0,2},{1,5},{2,0},{3,7},{4,6},{5,1},{6,4},{7,3},{8,10},{9,13},{10,... | collective-permute-start | bytes 221192 | tf_op jit(solution)/shard_map/ppermute | solution.py:294
  6.8 4.6 %collective-permute-start.3 = (bf16[2,144,128]{2,1,0:T(8,128)(2,1)S(1)}, bf16[2,144,128]{2,1,0:T(8,128)(2,1)S(1)}, u32[]{:S(2)}, u32[]{:S(2)}) collective-permute-start(bf16[2,144,128]{2,1,0:T(8,128)(2,1)S(1)} %get-tuple-element.25), channel_id=1, source_target_pairs={{0,4},{1,7},{2,6},{3,5},{4,0},{5,3},{6,2},{7,1},{8,12},{9,15},{10,... | collective-permute-start | bytes 221192 | tf_op jit(solution)/shard_map/ppermute | solution.py:294
  13.1 5.3 %copy-start.1 = (bf16[128,128]{1,0:T(8,128)(2,1)S(1)}, bf16[128,128]{1,0:T(8,128)(2,1)}, u32[]{:S(2)}) copy-start(bf16[128,128]{1,0:T(8,128)(2,1)} %w_ref.2) | copy-start | bytes 98308
  13.1 12.6 %all-to-all-start = ((bf16[16,72,128]{2,1,0:T(8,128)(2,1)}), bf16[16,72,128]{2,1,0:T(8,128)(2,1)S(1)}, u32[]{:S(2)}, u32[]{:S(2)}) async-start(bf16[16,72,128]{2,1,0:T(8,128)(2,1)} %shard_map.93), calls=%async_computation | async-start | bytes 589824 | tf_op jit(solution)/shard_map/all_to_all | solution.py:318
  18.4 0.7 %copy-start.2 = (f32[128]{0:T(128)S(1)}, f32[128]{0:T(128)}, u32[]{:S(2)}) copy-start(f32[128]{0:T(128)} %param.15) | copy-start | bytes 1540
  18.4 0.7 %copy-start.3 = (f32[128]{0:T(128)S(1)}, f32[128]{0:T(128)}, u32[]{:S(2)}) copy-start(f32[128]{0:T(128)} %param.16) | copy-start | bytes 1540
  19.1 6.6 %copy-start = (bf16[128,128]{1,0:T(8,128)(2,1)S(1)}, bf16[128,128]{1,0:T(8,128)(2,1)}, u32[]{:S(2)}) copy-start(bf16[128,128]{1,0:T(8,128)(2,1)} %w_ref.3) | copy-start | bytes 98308

commit v33 on v31

--- a/solution.py
+++ b/solution.py
@@ -236,10 +236,12 @@
     quads = rows // halves
     far_order = []
     for col in reversed(range(cols)):
-        ahead = list(range(quads)) if col else list(range(1, quads)) + [0]
+        ahead = list(range(1, quads)) + [0]
         behind = [0] + list(reversed(range(1, quads))) if col else list(reversed(range(quads)))
         for quad, other in zip(ahead, behind):
             far_order += [near + other * cols + col, quad * cols + col]
+    first, last = far_order.index(cols - 1), len(far_order) - cols
+    far_order[first], far_order[last] = far_order[last], far_order[first]
     share = hidden // near
     tokens = row_count * col_count
     length = rows * row_count

time: 26.8 us -> 27.7 us (1.034)
  the two profiles are of different devices: /device:TPU:0 before, /device:TPU:1 now
where the time goes in v33:
time: 27.7 us; the launch traced here: 27.4 us
  waiting for transfers between devices  11.2 us (40%)
  starting transfers between devices  10.4 us (38%)
  Pallas kernels  5.05 us (18%)
  local copies, waits for them, and re-layouts  0.65 us (2%)
    all_to_all x1, waiting for transfers between devices, per_device(): lax.all_to_all(total, ('half', 'quad', 'col'), split_axis=0, concat_axis=...  7.79 us
    all_to_all x1, starting transfers between devices, per_device(): lax.all_to_all(total, ('half', 'quad', 'col'), split_axis=0, concat_axis=...  6.18 us
    ppermute x3, starting transfers between devices, per_device(): lax.ppermute(pieces[step], 'quad', [(i, i ^ step) for i in range(quads)])  4.13 us
    ppermute x3, waiting for transfers between devices, per_device(): lax.ppermute(pieces[step], 'quad', [(i, i ^ step) for i in range(quads)])  3.46 us
    pallas_call x1, Pallas kernels, per_device(): pl.pallas_call(functools.partial(own_kernel, quads, cols), out_shape=(jax...  1.7 us
    pallas_call x1, Pallas kernels, per_device(): pl.pallas_call(functools.partial(triangle_kernel, far_order, steps, cols,...  1.61 us
    pallas_call x1, Pallas kernels, per_device(): pl.pallas_call(functools.partial(output_kernel, far_order, near_order), o...  1.02 us
    unnamed x8, local copies, waits for them, and re-layouts  0.65 us
  transfers between devices with their start and end apart: 5, of which 3 were waited for; matrix products, arithmetic and copies ran while one was open for 0% of the time, Pallas kernels for 7%

profile of v33, /device:TPU:1, one launch (start us, length us, event | category | flops | bytes accessed | tf_op | source)
XLA Modules:
  0.0 27.4 jit_solution(3697591410627738675)
XLA Ops:
  0.0 0.1 collective-permute-start
  0.1 1.7 %shard_map.91 = (bf16[4,144,128]{2,1,0:T(8,128)(2,1)S(1)}, bf16[576,128]{1,0:T(8,128)(2,1)S(1)}, f32[8,384]{1,0:T(8,128)S(1)}, f32[96,1]{1,0:T(8,128)S(1)}, bf16...) custom-call(bf16[12,48,128]{2,1,0:T(8,128)(2,1)} %pair_hbm.1, f32[1,128]{1,0:T(1,128)} %bitcast.7, ...), custom_call_target="tpu_custom_call" | custom-call | flops 75497472 | bytes 1179648 | tf_op jit(solution)/shard_map/pallas_call | solution.py:255
  1.8 0.0 collective-permute-done.pair_ref
  1.8 0.5 %shard_map.92 = (bf16[2,144,128]{2,1,0:T(8,128)(2,1)S(1)}, bf16[2,144,128]{2,1,0:T(8,128)(2,1)S(1)}, bf16[2,144,128]{2,1,0:T(8,128)(2,1)S(1)}, bf16[2,144,128]{2,1,0:T(8,128)(2,1)S(1)}) custom-call(bf16[12,48,128]{2,1,0:T(8,128)(2,1)S(1)} %collective-permute-done.pair_ref, bf16[4,144,128]{2,1,0:T(8,128)(2,1)S(1)} %get-tuple-element.19.sides_ref, ...), custom_call_target="tpu_custom_call" | custom-call | flops 75497472 | bytes 1179648 | tf_op jit(solution)/shard_map/pallas_call | solution.py:278
  2.3 3.8 %collective-permute-start.1 = (bf16[2,144,128]{2,1,0:T(8,128)(2,1)S(1)}, bf16[2,144,128]{2,1,0:T(8,128)(2,1)S(1)}, u32[]{:S(2)}, u32[]{:S(2)}) collective-permute-start(bf16[2,144,128]{2,1,0:T(8,128)(2,1)S(1)} %get-tuple-element.23), channel_id=1, source_target_pairs={{0,6},{2,4},{4,2},{6,0},{1,7},{3,5},{5,3},{7,1},{8,14},{10,12},{12... | collective-permute-start | bytes 221192 | tf_op jit(solution)/shard_map/ppermute | solution.py:288
  6.1 0.2 collective-permute-start.2
  6.3 0.1 collective-permute-start.3
  6.5 2.3 %collective-permute-done.1.refs_0_ = bf16[2,144,128]{2,1,0:T(8,128)(2,1)S(1)} collective-permute-done((bf16[2,144,128]{2,1,0:T(8,128)(2,1)S(1)}, bf16[2,144,128]{2,1,0:T(8,128)(2,1)S(1)}, u32[]{:S(2)}, u32[]{:S(2)}) %collective-permute-start.1) | collective-permute-done | bytes 73760 | tf_op jit(solution)/shard_map/ppermute | solution.py:288
  8.7 1.2 %collective-permute-done.2.refs_1_ = bf16[2,144,128]{2,1,0:T(8,128)(2,1)S(1)} collective-permute-done((bf16[2,144,128]{2,1,0:T(8,128)(2,1)S(1)}, bf16[2,144,128]{2,1,0:T(8,128)(2,1)S(1)}, u32[]{:S(2)}, u32[]{:S(2)}) %collective-permute-start.2) | collective-permute-done | bytes 73760 | tf_op jit(solution)/shard_map/ppermute | solution.py:288
  9.9 0.0 collective-permute-done.3.refs_2_
  9.9 1.6 %shard_map.93 = bf16[16,72,128]{2,1,0:T(8,128)(2,1)} custom-call(bf16[2,144,128]{2,1,0:T(8,128)(2,1)S(1)} %collective-permute-done.1.refs_0_, bf16[2,144,128]{2,1,0:T(8,128)(2,1)S(1)} %collective-permute-done.2.refs_1_, bf16[2,144,128]{2,1,0:T(8,128)(2,1)S(1)} %collective-permute-done.3.refs_2_, bf16[2,144,128]{2,1,0:T(8,128)(2,1)S(1)} %get-tuple-element.26.refs_3_, ...), custom_call_target="tpu_custom_call" | custom-call | tf_op jit(solution)/shard_map/pallas_call | solution.py:289
  11.5 0.0 copy-start.1
  11.5 6.2 %all-to-all-start = ((bf16[16,72,128]{2,1,0:T(8,128)(2,1)}), bf16[16,72,128]{2,1,0:T(8,128)(2,1)S(1)}, u32[]{:S(2)}, u32[]{:S(2)}) async-start(bf16[16,72,128]{2,1,0:T(8,128)(2,1)} %shard_map.93), calls=%async_computation | async-start | bytes 589824 | tf_op jit(solution)/shard_map/all_to_all | solution.py:312
  17.7 0.0 copy-start.2
  17.7 0.0 copy-start.3
  17.7 0.0 copy-done.1
  17.7 0.6 %copy-done.2 = f32[128]{0:T(128)S(1)} copy-done((f32[128]{0:T(128)S(1)}, f32[128]{0:T(128)}, u32[]{:S(2)}) %copy-start.2) | copy-done | bytes 536
  18.4 0.0 copy-done.3
  18.4 0.0 copy-start
  18.4 0.2 shard_map.94
  18.6 7.8 %all-to-all-done.total_ref = bf16[16,72,128]{2,1,0:T(8,128)(2,1)S(1)} async-done(((bf16[16,72,128]{2,1,0:T(8,128)(2,1)}), bf16[16,72,128]{2,1,0:T(8,128)(2,1)S(1)}, u32[]{:S(2)}, u32[]{:S(2)}) %all-to-all-start) | async-done | bytes 294944 | tf_op jit(solution)/shard_map/all_to_all | solution.py:312
  26.4 0.0 copy-done
  26.4 1.0 %shard_map.95 = bf16[12,48,128]{2,1,0:T(8,128)(2,1)} custom-call(bf16[16,72,128]{2,1,0:T(8,128)(2,1)S(1)} %all-to-all-done.total_ref, f32[576,128]{1,0:T(8,128)S(1)} %get-tuple-element.30.gate_ref, f32[128,1]{1,0:T(8,128)S(1)} %get-tuple-element.31.gain_ref, f32[128,1]{1,0:T(8,128)S(1)} %get-tuple-element.32.bias_ref, bf16[128,128]{1,0:T(8,128)(2,1)S(1)} %copy-done), custom_call_target="tpu_custom_call" | custom-call | tf_op jit(solution)/shard_map/pallas_call | solution.py:313
Async XLA Ops:
  0.0 1.8 %collective-permute-start = (bf16[12,48,128]{2,1,0:T(8,128)(2,1)}, bf16[12,48,128]{2,1,0:T(8,128)(2,1)S(1)}, u32[]{:S(2)}, u32[]{:S(2)}) collective-permute-start(bf16[12,48,128]{2,1,0:T(8,128)(2,1)} %pair_hbm.1), channel_id=1, source_target_pairs={{0,1},{1,0},{2,3},{3,2},{4,5},{5,4},{6,7},{7,6},{8,9},{9,8},{10,11... | collective-permute-start | bytes 442376 | tf_op jit(solution)/shard_map/ppermute | solution.py:253
  2.3 6.4 %collective-permute-start.1 = (bf16[2,144,128]{2,1,0:T(8,128)(2,1)S(1)}, bf16[2,144,128]{2,1,0:T(8,128)(2,1)S(1)}, u32[]{:S(2)}, u32[]{:S(2)}) collective-permute-start(bf16[2,144,128]{2,1,0:T(8,128)(2,1)S(1)} %get-tuple-element.23), channel_id=1, source_target_pairs={{0,6},{2,4},{4,2},{6,0},{1,7},{3,5},{5,3},{7,1},{8,14},{10,12},{12... | collective-permute-start | bytes 221192 | tf_op jit(solution)/shard_map/ppermute | solution.py:288
  6.1 3.8 %collective-permute-start.2 = (bf16[2,144,128]{2,1,0:T(8,128)(2,1)S(1)}, bf16[2,144,128]{2,1,0:T(8,128)(2,1)S(1)}, u32[]{:S(2)}, u32[]{:S(2)}) collective-permute-start(bf16[2,144,128]{2,1,0:T(8,128)(2,1)S(1)} %get-tuple-element.24), channel_id=1, source_target_pairs={{0,2},{2,0},{4,6},{6,4},{1,3},{3,1},{5,7},{7,5},{8,10},{10,8},{12,... | collective-permute-start | bytes 221192 | tf_op jit(solution)/shard_map/ppermute | solution.py:288
  6.3 3.6 %collective-permute-start.3 = (bf16[2,144,128]{2,1,0:T(8,128)(2,1)S(1)}, bf16[2,144,128]{2,1,0:T(8,128)(2,1)S(1)}, u32[]{:S(2)}, u32[]{:S(2)}) collective-permute-start(bf16[2,144,128]{2,1,0:T(8,128)(2,1)S(1)} %get-tuple-element.25), channel_id=1, source_target_pairs={{0,4},{2,6},{4,0},{6,2},{1,5},{3,7},{5,1},{7,3},{8,12},{10,14},{12... | collective-permute-start | bytes 221192 | tf_op jit(solution)/shard_map/ppermute | solution.py:288
  11.5 6.2 %copy-start.1 = (bf16[128,128]{1,0:T(8,128)(2,1)S(1)}, bf16[128,128]{1,0:T(8,128)(2,1)}, u32[]{:S(2)}) copy-start(bf16[128,128]{1,0:T(8,128)(2,1)} %w_ref.2) | copy-start | bytes 98308
  11.5 14.8 %all-to-all-start = ((bf16[16,72,128]{2,1,0:T(8,128)(2,1)}), bf16[16,72,128]{2,1,0:T(8,128)(2,1)S(1)}, u32[]{:S(2)}, u32[]{:S(2)}) async-start(bf16[16,72,128]{2,1,0:T(8,128)(2,1)} %shard_map.93), calls=%async_computation | async-start | bytes 589824 | tf_op jit(solution)/shard_map/all_to_all | solution.py:312
  17.7 0.7 %copy-start.2 = (f32[128]{0:T(128)S(1)}, f32[128]{0:T(128)}, u32[]{:S(2)}) copy-start(f32[128]{0:T(128)} %param.15) | copy-start | bytes 1540
  17.7 0.7 %copy-start.3 = (f32[128]{0:T(128)S(1)}, f32[128]{0:T(128)}, u32[]{:S(2)}) copy-start(f32[128]{0:T(128)} %param.16) | copy-start | bytes 1540
  18.4 8.0 %copy-start = (bf16[128,128]{1,0:T(8,128)(2,1)S(1)}, bf16[128,128]{1,0:T(8,128)(2,1)}, u32[]{:S(2)}) copy-start(bf16[128,128]{1,0:T(8,128)(2,1)} %w_ref.3) | copy-start | bytes 98308

commit v34 on v31

--- a/solution.py
+++ b/solution.py
@@ -237,7 +237,7 @@
     far_order = []
     for col in reversed(range(cols)):
         ahead = list(range(quads)) if col else list(range(1, quads)) + [0]
-        behind = [0] + list(reversed(range(1, quads))) if col else list(reversed(range(quads)))
+        behind = [0] + list(reversed(range(1, quads))) if col else list(range(quads))
         for quad, other in zip(ahead, behind):
             far_order += [near + other * cols + col, quad * cols + col]
     share = hidden // near

time: 26.8 us -> 26.9 us (level)
  no operation moved by 1% of the time
where the time goes in v34:
time: 26.9 us; the launch traced here: 26.5 us
  waiting for transfers between devices  10.7 us (40%)
  starting transfers between devices  9.98 us (37%)
  Pallas kernels  5.05 us (19%)
  local copies, waits for them, and re-layouts  0.65 us (2%)
    all_to_all x1, waiting for transfers between devices, per_device(): lax.all_to_all(total, ('half', 'quad', 'col'), split_axis=0, concat_axis=...  6.51 us
    all_to_all x1, starting transfers between devices, per_device(): lax.all_to_all(total, ('half', 'quad', 'col'), split_axis=0, concat_axis=...  5.29 us
    ppermute x3, starting transfers between devices, per_device(): lax.ppermute(pieces[step], 'quad', [(i, i ^ step) for i in range(quads)])  4.24 us
    ppermute x3, waiting for transfers between devices, per_device(): lax.ppermute(pieces[step], 'quad', [(i, i ^ step) for i in range(quads)])  4.21 us
    pallas_call x1, Pallas kernels, per_device(): pl.pallas_call(functools.partial(own_kernel, quads, cols), out_shape=(jax...  1.71 us
    pallas_call x1, Pallas kernels, per_device(): pl.pallas_call(functools.partial(triangle_kernel, far_order, steps, cols,...  1.61 us
    pallas_call x1, Pallas kernels, per_device(): pl.pallas_call(functools.partial(output_kernel, far_order, near_order), o...  1.02 us
    unnamed x8, local copies, waits for them, and re-layouts  0.65 us
  transfers between devices with their start and end apart: 5, of which 4 were waited for; matrix products, arithmetic and copies ran while one was open for 0% of the time, Pallas kernels for 7%

profile of v34, /device:TPU:0, one launch (start us, length us, event | category | flops | bytes accessed | tf_op | source)
XLA Modules:
  0.0 26.5 jit_solution(8794731127531119008)
XLA Ops:
  0.0 0.5 %collective-permute-start = (bf16[12,48,128]{2,1,0:T(8,128)(2,1)}, bf16[12,48,128]{2,1,0:T(8,128)(2,1)S(1)}, u32[]{:S(2)}, u32[]{:S(2)}) collective-permute-start(bf16[12,48,128]{2,1,0:T(8,128)(2,1)} %pair_hbm.1), channel_id=1, source_target_pairs={{0,1},{1,0},{2,3},{3,2},{4,5},{5,4},{6,7},{7,6},{8,9},{9,8},{10,11... | collective-permute-start | bytes 442376 | tf_op jit(solution)/shard_map/ppermute | solution.py:251
  0.5 1.7 %shard_map.91 = (bf16[4,144,128]{2,1,0:T(8,128)(2,1)S(1)}, bf16[576,128]{1,0:T(8,128)(2,1)S(1)}, f32[8,384]{1,0:T(8,128)S(1)}, f32[96,1]{1,0:T(8,128)S(1)}, bf16...) custom-call(bf16[12,48,128]{2,1,0:T(8,128)(2,1)} %pair_hbm.1, f32[1,128]{1,0:T(1,128)} %bitcast.7, ...), custom_call_target="tpu_custom_call" | custom-call | flops 75497472 | bytes 1179648 | tf_op jit(solution)/shard_map/pallas_call | solution.py:253
  2.2 0.0 collective-permute-done.pair_ref
  2.2 0.5 %shard_map.92 = (bf16[2,144,128]{2,1,0:T(8,128)(2,1)S(1)}, bf16[2,144,128]{2,1,0:T(8,128)(2,1)S(1)}, bf16[2,144,128]{2,1,0:T(8,128)(2,1)S(1)}, bf16[2,144,128]{2,1,0:T(8,128)(2,1)S(1)}) custom-call(bf16[12,48,128]{2,1,0:T(8,128)(2,1)S(1)} %collective-permute-done.pair_ref, bf16[4,144,128]{2,1,0:T(8,128)(2,1)S(1)} %get-tuple-element.19.sides_ref, ...), custom_call_target="tpu_custom_call" | custom-call | flops 75497472 | bytes 1179648 | tf_op jit(solution)/shard_map/pallas_call | solution.py:276
  2.7 3.6 %collective-permute-start.1 = (bf16[2,144,128]{2,1,0:T(8,128)(2,1)S(1)}, bf16[2,144,128]{2,1,0:T(8,128)(2,1)S(1)}, u32[]{:S(2)}, u32[]{:S(2)}) collective-permute-start(bf16[2,144,128]{2,1,0:T(8,128)(2,1)S(1)} %get-tuple-element.23), channel_id=1, source_target_pairs={{0,6},{2,4},{4,2},{6,0},{1,7},{3,5},{5,3},{7,1},{8,14},{10,12},{12... | collective-permute-start | bytes 221192 | tf_op jit(solution)/shard_map/ppermute | solution.py:286
  6.3 0.5 %collective-permute-start.2 = (bf16[2,144,128]{2,1,0:T(8,128)(2,1)S(1)}, bf16[2,144,128]{2,1,0:T(8,128)(2,1)S(1)}, u32[]{:S(2)}, u32[]{:S(2)}) collective-permute-start(bf16[2,144,128]{2,1,0:T(8,128)(2,1)S(1)} %get-tuple-element.24), channel_id=1, source_target_pairs={{0,2},{2,0},{4,6},{6,4},{1,3},{3,1},{5,7},{7,5},{8,10},{10,8},{12,... | collective-permute-start | bytes 221192 | tf_op jit(solution)/shard_map/ppermute | solution.py:286
  6.8 0.1 collective-permute-start.3
  7.0 2.3 %collective-permute-done.1.refs_0_ = bf16[2,144,128]{2,1,0:T(8,128)(2,1)S(1)} collective-permute-done((bf16[2,144,128]{2,1,0:T(8,128)(2,1)S(1)}, bf16[2,144,128]{2,1,0:T(8,128)(2,1)S(1)}, u32[]{:S(2)}, u32[]{:S(2)}) %collective-permute-start.1) | collective-permute-done | bytes 73760 | tf_op jit(solution)/shard_map/ppermute | solution.py:286
  9.3 1.6 %collective-permute-done.2.refs_1_ = bf16[2,144,128]{2,1,0:T(8,128)(2,1)S(1)} collective-permute-done((bf16[2,144,128]{2,1,0:T(8,128)(2,1)S(1)}, bf16[2,144,128]{2,1,0:T(8,128)(2,1)S(1)}, u32[]{:S(2)}, u32[]{:S(2)}) %collective-permute-start.2) | collective-permute-done | bytes 73760 | tf_op jit(solution)/shard_map/ppermute | solution.py:286
  10.8 0.3 %collective-permute-done.3.refs_2_ = bf16[2,144,128]{2,1,0:T(8,128)(2,1)S(1)} collective-permute-done((bf16[2,144,128]{2,1,0:T(8,128)(2,1)S(1)}, bf16[2,144,128]{2,1,0:T(8,128)(2,1)S(1)}, u32[]{:S(2)}, u32[]{:S(2)}) %collective-permute-start.3) | collective-permute-done | bytes 73760 | tf_op jit(solution)/shard_map/ppermute | solution.py:286
  11.2 1.6 %shard_map.93 = bf16[16,72,128]{2,1,0:T(8,128)(2,1)} custom-call(bf16[2,144,128]{2,1,0:T(8,128)(2,1)S(1)} %collective-permute-done.1.refs_0_, bf16[2,144,128]{2,1,0:T(8,128)(2,1)S(1)} %collective-permute-done.2.refs_1_, bf16[2,144,128]{2,1,0:T(8,128)(2,1)S(1)} %collective-permute-done.3.refs_2_, bf16[2,144,128]{2,1,0:T(8,128)(2,1)S(1)} %get-tuple-element.26.refs_3_, ...), custom_call_target="tpu_custom_call" | custom-call | tf_op jit(solution)/shard_map/pallas_call | solution.py:287
  12.8 0.0 copy-start.1
  12.8 5.3 %all-to-all-start = ((bf16[16,72,128]{2,1,0:T(8,128)(2,1)}), bf16[16,72,128]{2,1,0:T(8,128)(2,1)S(1)}, u32[]{:S(2)}, u32[]{:S(2)}) async-start(bf16[16,72,128]{2,1,0:T(8,128)(2,1)} %shard_map.93), calls=%async_computation | async-start | bytes 589824 | tf_op jit(solution)/shard_map/all_to_all | solution.py:310
  18.1 0.0 copy-start.2
  18.1 0.0 copy-start.3
  18.1 0.0 copy-done.1
  18.1 0.6 %copy-done.2 = f32[128]{0:T(128)S(1)} copy-done((f32[128]{0:T(128)S(1)}, f32[128]{0:T(128)}, u32[]{:S(2)}) %copy-start.2) | copy-done | bytes 536
  18.7 0.0 copy-done.3
  18.7 0.0 copy-start
  18.8 0.2 shard_map.94
  18.9 6.5 %all-to-all-done.total_ref = bf16[16,72,128]{2,1,0:T(8,128)(2,1)S(1)} async-done(((bf16[16,72,128]{2,1,0:T(8,128)(2,1)}), bf16[16,72,128]{2,1,0:T(8,128)(2,1)S(1)}, u32[]{:S(2)}, u32[]{:S(2)}) %all-to-all-start) | async-done | bytes 294944 | tf_op jit(solution)/shard_map/all_to_all | solution.py:310
  25.5 0.0 copy-done
  25.5 1.0 %shard_map.95 = bf16[12,48,128]{2,1,0:T(8,128)(2,1)} custom-call(bf16[16,72,128]{2,1,0:T(8,128)(2,1)S(1)} %all-to-all-done.total_ref, f32[576,128]{1,0:T(8,128)S(1)} %get-tuple-element.30.gate_ref, f32[128,1]{1,0:T(8,128)S(1)} %get-tuple-element.31.gain_ref, f32[128,1]{1,0:T(8,128)S(1)} %get-tuple-element.32.bias_ref, bf16[128,128]{1,0:T(8,128)(2,1)S(1)} %copy-done), custom_call_target="tpu_custom_call" | custom-call | tf_op jit(solution)/shard_map/pallas_call | solution.py:311
Async XLA Ops:
  0.0 2.2 %collective-permute-start = (bf16[12,48,128]{2,1,0:T(8,128)(2,1)}, bf16[12,48,128]{2,1,0:T(8,128)(2,1)S(1)}, u32[]{:S(2)}, u32[]{:S(2)}) collective-permute-start(bf16[12,48,128]{2,1,0:T(8,128)(2,1)} %pair_hbm.1), channel_id=1, source_target_pairs={{0,1},{1,0},{2,3},{3,2},{4,5},{5,4},{6,7},{7,6},{8,9},{9,8},{10,11... | collective-permute-start | bytes 442376 | tf_op jit(solution)/shard_map/ppermute | solution.py:251
  2.7 6.6 %collective-permute-start.1 = (bf16[2,144,128]{2,1,0:T(8,128)(2,1)S(1)}, bf16[2,144,128]{2,1,0:T(8,128)(2,1)S(1)}, u32[]{:S(2)}, u32[]{:S(2)}) collective-permute-start(bf16[2,144,128]{2,1,0:T(8,128)(2,1)S(1)} %get-tuple-element.23), channel_id=1, source_target_pairs={{0,6},{2,4},{4,2},{6,0},{1,7},{3,5},{5,3},{7,1},{8,14},{10,12},{12... | collective-permute-start | bytes 221192 | tf_op jit(solution)/shard_map/ppermute | solution.py:286
  6.3 4.5 %collective-permute-start.2 = (bf16[2,144,128]{2,1,0:T(8,128)(2,1)S(1)}, bf16[2,144,128]{2,1,0:T(8,128)(2,1)S(1)}, u32[]{:S(2)}, u32[]{:S(2)}) collective-permute-start(bf16[2,144,128]{2,1,0:T(8,128)(2,1)S(1)} %get-tuple-element.24), channel_id=1, source_target_pairs={{0,2},{2,0},{4,6},{6,4},{1,3},{3,1},{5,7},{7,5},{8,10},{10,8},{12,... | collective-permute-start | bytes 221192 | tf_op jit(solution)/shard_map/ppermute | solution.py:286
  6.8 4.4 %collective-permute-start.3 = (bf16[2,144,128]{2,1,0:T(8,128)(2,1)S(1)}, bf16[2,144,128]{2,1,0:T(8,128)(2,1)S(1)}, u32[]{:S(2)}, u32[]{:S(2)}) collective-permute-start(bf16[2,144,128]{2,1,0:T(8,128)(2,1)S(1)} %get-tuple-element.25), channel_id=1, source_target_pairs={{0,4},{2,6},{4,0},{6,2},{1,5},{3,7},{5,1},{7,3},{8,12},{10,14},{12... | collective-permute-start | bytes 221192 | tf_op jit(solution)/shard_map/ppermute | solution.py:286
  12.8 5.3 %copy-start.1 = (bf16[128,128]{1,0:T(8,128)(2,1)S(1)}, bf16[128,128]{1,0:T(8,128)(2,1)}, u32[]{:S(2)}) copy-start(bf16[128,128]{1,0:T(8,128)(2,1)} %w_ref.2) | copy-start | bytes 98308
  12.8 12.7 %all-to-all-start = ((bf16[16,72,128]{2,1,0:T(8,128)(2,1)}), bf16[16,72,128]{2,1,0:T(8,128)(2,1)S(1)}, u32[]{:S(2)}, u32[]{:S(2)}) async-start(bf16[16,72,128]{2,1,0:T(8,128)(2,1)} %shard_map.93), calls=%async_computation | async-start | bytes 589824 | tf_op jit(solution)/shard_map/all_to_all | solution.py:310
  18.1 0.7 %copy-start.2 = (f32[128]{0:T(128)S(1)}, f32[128]{0:T(128)}, u32[]{:S(2)}) copy-start(f32[128]{0:T(128)} %param.15) | copy-start | bytes 1540
  18.1 0.7 %copy-start.3 = (f32[128]{0:T(128)S(1)}, f32[128]{0:T(128)}, u32[]{:S(2)}) copy-start(f32[128]{0:T(128)} %param.16) | copy-start | bytes 1540
  18.7 6.7 %copy-start = (bf16[128,128]{1,0:T(8,128)(2,1)S(1)}, bf16[128,128]{1,0:T(8,128)(2,1)}, u32[]{:S(2)}) copy-start(bf16[128,128]{1,0:T(8,128)(2,1)} %w_ref.3) | copy-start | bytes 98308

commit v35 on v31

--- a/solution.py
+++ b/solution.py
@@ -223,7 +223,7 @@
         blocks.append(unpack(sum(parts[1:], parts[0]), share))
     total = jnp.concatenate(blocks, axis=0)
     normed = layer_norm(total, gain_ref[...], bias_ref[...], 0).astype(jnp.bfloat16)
-    output = lax.dot_general(normed, w_ref[...], (((0,), (0,)), ((), ())), preferred_element_type=jnp.float32)
+    output = jnp.dot(normed.T, w_ref[...], preferred_element_type=jnp.float32)
     output = restore(output, out_ref.shape[0], out_ref.shape[1])
     out_ref[...] = (gate_ref[...] * output).astype(jnp.bfloat16).reshape(out_ref.shape)
 

time: 26.8 us -> 26.8 us (level)
  no operation moved by 1% of the time
where the time goes in v35:
time: 26.8 us; the launch traced here: 26.5 us
  waiting for transfers between devices  10.7 us (40%)
  starting transfers between devices  9.98 us (37%)
  Pallas kernels  5.05 us (19%)
  local copies, waits for them, and re-layouts  0.65 us (2%)
    all_to_all x1, waiting for transfers between devices, per_device(): lax.all_to_all(total, ('half', 'quad', 'col'), split_axis=0, concat_axis=...  6.52 us
    all_to_all x1, starting transfers between devices, per_device(): lax.all_to_all(total, ('half', 'quad', 'col'), split_axis=0, concat_axis=...  5.29 us
    ppermute x3, starting transfers between devices, per_device(): lax.ppermute(pieces[step], 'quad', [(i, i ^ step) for i in range(quads)])  4.24 us
    ppermute x3, waiting for transfers between devices, per_device(): lax.ppermute(pieces[step], 'quad', [(i, i ^ step) for i in range(quads)])  4.21 us
    pallas_call x1, Pallas kernels, per_device(): pl.pallas_call(functools.partial(own_kernel, quads, cols), out_shape=(jax...  1.71 us
    pallas_call x1, Pallas kernels, per_device(): pl.pallas_call(functools.partial(triangle_kernel, far_order, steps, cols,...  1.61 us
    pallas_call x1, Pallas kernels, per_device(): pl.pallas_call(functools.partial(output_kernel, far_order, near_order), o...  1.02 us
    unnamed x8, local copies, waits for them, and re-layouts  0.65 us
  transfers between devices with their start and end apart: 5, of which 4 were waited for; matrix products, arithmetic and copies ran while one was open for 0% of the time, Pallas kernels for 7%

profile of v35, /device:TPU:0, one launch (start us, length us, event | category | flops | bytes accessed | tf_op | source)
XLA Modules:
  0.0 26.5 jit_solution(4153698483600255655)
XLA Ops:
  0.0 0.5 %collective-permute-start = (bf16[12,48,128]{2,1,0:T(8,128)(2,1)}, bf16[12,48,128]{2,1,0:T(8,128)(2,1)S(1)}, u32[]{:S(2)}, u32[]{:S(2)}) collective-permute-start(bf16[12,48,128]{2,1,0:T(8,128)(2,1)} %pair_hbm.1), channel_id=1, source_target_pairs={{0,1},{1,0},{2,3},{3,2},{4,5},{5,4},{6,7},{7,6},{8,9},{9,8},{10,11... | collective-permute-start | bytes 442376 | tf_op jit(solution)/shard_map/ppermute | solution.py:251
  0.5 1.7 %shard_map.91 = (bf16[4,144,128]{2,1,0:T(8,128)(2,1)S(1)}, bf16[576,128]{1,0:T(8,128)(2,1)S(1)}, f32[8,384]{1,0:T(8,128)S(1)}, f32[96,1]{1,0:T(8,128)S(1)}, bf16...) custom-call(bf16[12,48,128]{2,1,0:T(8,128)(2,1)} %pair_hbm.1, f32[1,128]{1,0:T(1,128)} %bitcast.7, ...), custom_call_target="tpu_custom_call" | custom-call | flops 75497472 | bytes 1179648 | tf_op jit(solution)/shard_map/pallas_call | solution.py:253
  2.2 0.0 collective-permute-done.pair_ref
  2.2 0.5 %shard_map.92 = (bf16[2,144,128]{2,1,0:T(8,128)(2,1)S(1)}, bf16[2,144,128]{2,1,0:T(8,128)(2,1)S(1)}, bf16[2,144,128]{2,1,0:T(8,128)(2,1)S(1)}, bf16[2,144,128]{2,1,0:T(8,128)(2,1)S(1)}) custom-call(bf16[12,48,128]{2,1,0:T(8,128)(2,1)S(1)} %collective-permute-done.pair_ref, bf16[4,144,128]{2,1,0:T(8,128)(2,1)S(1)} %get-tuple-element.19.sides_ref, ...), custom_call_target="tpu_custom_call" | custom-call | flops 75497472 | bytes 1179648 | tf_op jit(solution)/shard_map/pallas_call | solution.py:276
  2.7 3.6 %collective-permute-start.1 = (bf16[2,144,128]{2,1,0:T(8,128)(2,1)S(1)}, bf16[2,144,128]{2,1,0:T(8,128)(2,1)S(1)}, u32[]{:S(2)}, u32[]{:S(2)}) collective-permute-start(bf16[2,144,128]{2,1,0:T(8,128)(2,1)S(1)} %get-tuple-element.23), channel_id=1, source_target_pairs={{0,6},{2,4},{4,2},{6,0},{1,7},{3,5},{5,3},{7,1},{8,14},{10,12},{12... | collective-permute-start | bytes 221192 | tf_op jit(solution)/shard_map/ppermute | solution.py:286
  6.3 0.5 %collective-permute-start.2 = (bf16[2,144,128]{2,1,0:T(8,128)(2,1)S(1)}, bf16[2,144,128]{2,1,0:T(8,128)(2,1)S(1)}, u32[]{:S(2)}, u32[]{:S(2)}) collective-permute-start(bf16[2,144,128]{2,1,0:T(8,128)(2,1)S(1)} %get-tuple-element.24), channel_id=1, source_target_pairs={{0,2},{2,0},{4,6},{6,4},{1,3},{3,1},{5,7},{7,5},{8,10},{10,8},{12,... | collective-permute-start | bytes 221192 | tf_op jit(solution)/shard_map/ppermute | solution.py:286
  6.8 0.1 collective-permute-start.3
  7.0 2.3 %collective-permute-done.1.refs_0_ = bf16[2,144,128]{2,1,0:T(8,128)(2,1)S(1)} collective-permute-done((bf16[2,144,128]{2,1,0:T(8,128)(2,1)S(1)}, bf16[2,144,128]{2,1,0:T(8,128)(2,1)S(1)}, u32[]{:S(2)}, u32[]{:S(2)}) %collective-permute-start.1) | collective-permute-done | bytes 73760 | tf_op jit(solution)/shard_map/ppermute | solution.py:286
  9.3 1.6 %collective-permute-done.2.refs_1_ = bf16[2,144,128]{2,1,0:T(8,128)(2,1)S(1)} collective-permute-done((bf16[2,144,128]{2,1,0:T(8,128)(2,1)S(1)}, bf16[2,144,128]{2,1,0:T(8,128)(2,1)S(1)}, u32[]{:S(2)}, u32[]{:S(2)}) %collective-permute-start.2) | collective-permute-done | bytes 73760 | tf_op jit(solution)/shard_map/ppermute | solution.py:286
  10.8 0.3 %collective-permute-done.3.refs_2_ = bf16[2,144,128]{2,1,0:T(8,128)(2,1)S(1)} collective-permute-done((bf16[2,144,128]{2,1,0:T(8,128)(2,1)S(1)}, bf16[2,144,128]{2,1,0:T(8,128)(2,1)S(1)}, u32[]{:S(2)}, u32[]{:S(2)}) %collective-permute-start.3) | collective-permute-done | bytes 73760 | tf_op jit(solution)/shard_map/ppermute | solution.py:286
  11.2 1.6 %shard_map.93 = bf16[16,72,128]{2,1,0:T(8,128)(2,1)} custom-call(bf16[2,144,128]{2,1,0:T(8,128)(2,1)S(1)} %collective-permute-done.1.refs_0_, bf16[2,144,128]{2,1,0:T(8,128)(2,1)S(1)} %collective-permute-done.2.refs_1_, bf16[2,144,128]{2,1,0:T(8,128)(2,1)S(1)} %collective-permute-done.3.refs_2_, bf16[2,144,128]{2,1,0:T(8,128)(2,1)S(1)} %get-tuple-element.26.refs_3_, ...), custom_call_target="tpu_custom_call" | custom-call | tf_op jit(solution)/shard_map/pallas_call | solution.py:287
  12.8 0.0 copy-start.1
  12.8 5.3 %all-to-all-start = ((bf16[16,72,128]{2,1,0:T(8,128)(2,1)}), bf16[16,72,128]{2,1,0:T(8,128)(2,1)S(1)}, u32[]{:S(2)}, u32[]{:S(2)}) async-start(bf16[16,72,128]{2,1,0:T(8,128)(2,1)} %shard_map.93), calls=%async_computation | async-start | bytes 589824 | tf_op jit(solution)/shard_map/all_to_all | solution.py:310
  18.1 0.0 copy-start.2
  18.1 0.0 copy-start.3
  18.1 0.0 copy-done.1
  18.1 0.6 %copy-done.2 = f32[128]{0:T(128)S(1)} copy-done((f32[128]{0:T(128)S(1)}, f32[128]{0:T(128)}, u32[]{:S(2)}) %copy-start.2) | copy-done | bytes 536
  18.7 0.0 copy-done.3
  18.7 0.0 copy-start
  18.8 0.2 shard_map.94
  18.9 6.5 %all-to-all-done.total_ref = bf16[16,72,128]{2,1,0:T(8,128)(2,1)S(1)} async-done(((bf16[16,72,128]{2,1,0:T(8,128)(2,1)}), bf16[16,72,128]{2,1,0:T(8,128)(2,1)S(1)}, u32[]{:S(2)}, u32[]{:S(2)}) %all-to-all-start) | async-done | bytes 294944 | tf_op jit(solution)/shard_map/all_to_all | solution.py:310
  25.5 0.0 copy-done
  25.5 1.0 %shard_map.95 = bf16[12,48,128]{2,1,0:T(8,128)(2,1)} custom-call(bf16[16,72,128]{2,1,0:T(8,128)(2,1)S(1)} %all-to-all-done.total_ref, f32[576,128]{1,0:T(8,128)S(1)} %get-tuple-element.30.gate_ref, f32[128,1]{1,0:T(8,128)S(1)} %get-tuple-element.31.gain_ref, f32[128,1]{1,0:T(8,128)S(1)} %get-tuple-element.32.bias_ref, bf16[128,128]{1,0:T(8,128)(2,1)S(1)} %copy-done), custom_call_target="tpu_custom_call" | custom-call | tf_op jit(solution)/shard_map/pallas_call | solution.py:311
Async XLA Ops:
  0.0 2.2 %collective-permute-start = (bf16[12,48,128]{2,1,0:T(8,128)(2,1)}, bf16[12,48,128]{2,1,0:T(8,128)(2,1)S(1)}, u32[]{:S(2)}, u32[]{:S(2)}) collective-permute-start(bf16[12,48,128]{2,1,0:T(8,128)(2,1)} %pair_hbm.1), channel_id=1, source_target_pairs={{0,1},{1,0},{2,3},{3,2},{4,5},{5,4},{6,7},{7,6},{8,9},{9,8},{10,11... | collective-permute-start | bytes 442376 | tf_op jit(solution)/shard_map/ppermute | solution.py:251
  2.7 6.6 %collective-permute-start.1 = (bf16[2,144,128]{2,1,0:T(8,128)(2,1)S(1)}, bf16[2,144,128]{2,1,0:T(8,128)(2,1)S(1)}, u32[]{:S(2)}, u32[]{:S(2)}) collective-permute-start(bf16[2,144,128]{2,1,0:T(8,128)(2,1)S(1)} %get-tuple-element.23), channel_id=1, source_target_pairs={{0,6},{2,4},{4,2},{6,0},{1,7},{3,5},{5,3},{7,1},{8,14},{10,12},{12... | collective-permute-start | bytes 221192 | tf_op jit(solution)/shard_map/ppermute | solution.py:286
  6.3 4.5 %collective-permute-start.2 = (bf16[2,144,128]{2,1,0:T(8,128)(2,1)S(1)}, bf16[2,144,128]{2,1,0:T(8,128)(2,1)S(1)}, u32[]{:S(2)}, u32[]{:S(2)}) collective-permute-start(bf16[2,144,128]{2,1,0:T(8,128)(2,1)S(1)} %get-tuple-element.24), channel_id=1, source_target_pairs={{0,2},{2,0},{4,6},{6,4},{1,3},{3,1},{5,7},{7,5},{8,10},{10,8},{12,... | collective-permute-start | bytes 221192 | tf_op jit(solution)/shard_map/ppermute | solution.py:286
  6.8 4.4 %collective-permute-start.3 = (bf16[2,144,128]{2,1,0:T(8,128)(2,1)S(1)}, bf16[2,144,128]{2,1,0:T(8,128)(2,1)S(1)}, u32[]{:S(2)}, u32[]{:S(2)}) collective-permute-start(bf16[2,144,128]{2,1,0:T(8,128)(2,1)S(1)} %get-tuple-element.25), channel_id=1, source_target_pairs={{0,4},{2,6},{4,0},{6,2},{1,5},{3,7},{5,1},{7,3},{8,12},{10,14},{12... | collective-permute-start | bytes 221192 | tf_op jit(solution)/shard_map/ppermute | solution.py:286
  12.8 5.3 %copy-start.1 = (bf16[128,128]{1,0:T(8,128)(2,1)S(1)}, bf16[128,128]{1,0:T(8,128)(2,1)}, u32[]{:S(2)}) copy-start(bf16[128,128]{1,0:T(8,128)(2,1)} %w_ref.2) | copy-start | bytes 98308
  12.8 12.7 %all-to-all-start = ((bf16[16,72,128]{2,1,0:T(8,128)(2,1)}), bf16[16,72,128]{2,1,0:T(8,128)(2,1)S(1)}, u32[]{:S(2)}, u32[]{:S(2)}) async-start(bf16[16,72,128]{2,1,0:T(8,128)(2,1)} %shard_map.93), calls=%async_computation | async-start | bytes 589824 | tf_op jit(solution)/shard_map/all_to_all | solution.py:310
  18.1 0.7 %copy-start.2 = (f32[128]{0:T(128)S(1)}, f32[128]{0:T(128)}, u32[]{:S(2)}) copy-start(f32[128]{0:T(128)} %param.15) | copy-start | bytes 1540
  18.1 0.7 %copy-start.3 = (f32[128]{0:T(128)S(1)}, f32[128]{0:T(128)}, u32[]{:S(2)}) copy-start(f32[128]{0:T(128)} %param.16) | copy-start | bytes 1540
  18.7 6.7 %copy-start = (bf16[128,128]{1,0:T(8,128)(2,1)S(1)}, bf16[128,128]{1,0:T(8,128)(2,1)}, u32[]{:S(2)}) copy-start(bf16[128,128]{1,0:T(8,128)(2,1)} %w_ref.3) | copy-start | bytes 98308

commit v36 on v31

--- a/solution.py
+++ b/solution.py
@@ -88,7 +88,10 @@
 
 
 def own_kernel(quads, cols, pair_hbm, gain_hbm, bias_hbm, w_hbm, mask_hbm, sides_ref, normed_ref, spread_ref, column_mask_ref, w_ref, gain_ref, bias_ref, pair_ref, all_w_ref, mask_ref, sems):
-    moves = [(mask_hbm, mask_ref), (pair_hbm, pair_ref), (gain_hbm, gain_ref), (bias_hbm, bias_ref), (w_hbm, all_w_ref)]
+    step = pair_ref.shape[0] // 2
+    halves = [pl.ds(0, step), pl.ds(step, step)]
+    moves = [(mask_hbm, mask_ref), (gain_hbm, gain_ref), (bias_hbm, bias_ref)]
+    moves += [(pair_hbm.at[half], pair_ref.at[half]) for half in halves] + [(w_hbm, all_w_ref)]
     copies = [pltpu.make_async_copy(source, target, sems.at[n]) for n, (source, target) in enumerate(moves)]
     for copy in copies:
         copy.start()
@@ -112,11 +115,15 @@
     channel = lax.broadcasted_iota(jnp.int32, (group, lanes), 0)
     lane = lax.broadcasted_iota(jnp.int32, (group, lanes), 1)
     spread_ref[...] = jnp.where(lane % group == channel, kept, 0.0)
-    for copy in copies[1:4]:
+    for copy in copies[1:3]:
         copy.wait()
-    normed = normalise(pair_ref[...].reshape(tokens, channels), gain_ref[...], bias_ref[...])
+    parts = []
+    for half, copy in zip(halves, copies[3:5]):
+        copy.wait()
+        parts.append(normalise(pair_ref[half].reshape(tokens // 2, channels), gain_ref[...], bias_ref[...]))
+    normed = jnp.concatenate(parts, axis=0)
     normed_ref[...] = normed
-    copies[4].wait()
+    copies[5].wait()
     parts = [all_w_ref[:, at : at + hidden] for at in range(0, 4 * hidden, hidden)]
     w = jnp.concatenate([jnp.where(my_col == 0, part[:, :ours], part[:, ours:]) for part in parts], axis=1).T
     w_ref[...] = w
@@ -267,7 +274,7 @@
             pltpu.VMEM(pair.shape, pair.dtype),
             pltpu.VMEM(w_in.shape, w_in.dtype),
             pltpu.VMEM((1, length), jnp.int32),
-            pltpu.SemaphoreType.DMA((5,)),
+            pltpu.SemaphoreType.DMA((6,)),
         ],
         compiler_params=LIMIT,
         cost_estimate=cost,

time: 26.8 us -> 26.9 us (level)
  transfers between devices with their start and end apart: 5 -> 5, of which waited for: 4 -> 4; matrix products, arithmetic and copies ran while one was open for 0% -> 0% of each run, Pallas kernels for 7% -> 8%
where the time goes in v36:
time: 26.9 us; the launch traced here: 26.7 us
  waiting for transfers between devices  10.7 us (40%)
  starting transfers between devices  9.98 us (37%)
  Pallas kernels  5.24 us (19%)
  local copies, waits for them, and re-layouts  0.65 us (2%)
    all_to_all x1, waiting for transfers between devices, per_device(): lax.all_to_all(total, ('half', 'quad', 'col'), split_axis=0, concat_axis=...  6.51 us
    all_to_all x1, starting transfers between devices, per_device(): lax.all_to_all(total, ('half', 'quad', 'col'), split_axis=0, concat_axis=...  5.29 us
    ppermute x3, starting transfers between devices, per_device(): lax.ppermute(pieces[step], 'quad', [(i, i ^ step) for i in range(quads)])  4.24 us
    ppermute x3, waiting for transfers between devices, per_device(): lax.ppermute(pieces[step], 'quad', [(i, i ^ step) for i in range(quads)])  4.21 us
    pallas_call x1, Pallas kernels, per_device(): pl.pallas_call(functools.partial(own_kernel, quads, cols), out_shape=(jax...  1.88 us
    pallas_call x1, Pallas kernels, per_device(): pl.pallas_call(functools.partial(triangle_kernel, far_order, steps, cols,...  1.61 us
    pallas_call x1, Pallas kernels, per_device(): pl.pallas_call(functools.partial(output_kernel, far_order, near_order), o...  1.02 us
    unnamed x8, local copies, waits for them, and re-layouts  0.65 us
  transfers between devices with their start and end apart: 5, of which 4 were waited for; matrix products, arithmetic and copies ran while one was open for 0% of the time, Pallas kernels for 8%

profile of v36, /device:TPU:0, one launch (start us, length us, event | category | flops | bytes accessed | tf_op | source)
XLA Modules:
  0.0 26.7 jit_solution(4358429017697217569)
XLA Ops:
  0.0 0.5 %collective-permute-start = (bf16[12,48,128]{2,1,0:T(8,128)(2,1)}, bf16[12,48,128]{2,1,0:T(8,128)(2,1)S(1)}, u32[]{:S(2)}, u32[]{:S(2)}) collective-permute-start(bf16[12,48,128]{2,1,0:T(8,128)(2,1)} %pair_hbm.1), channel_id=1, source_target_pairs={{0,1},{1,0},{2,3},{3,2},{4,5},{5,4},{6,7},{7,6},{8,9},{9,8},{10,11... | collective-permute-start | bytes 442376 | tf_op jit(solution)/shard_map/ppermute | solution.py:258
  0.5 1.9 %shard_map.91 = (bf16[4,144,128]{2,1,0:T(8,128)(2,1)S(1)}, bf16[576,128]{1,0:T(8,128)(2,1)S(1)}, f32[8,384]{1,0:T(8,128)S(1)}, f32[96,1]{1,0:T(8,128)S(1)}, bf16...) custom-call(bf16[12,48,128]{2,1,0:T(8,128)(2,1)} %pair_hbm.1, f32[1,128]{1,0:T(1,128)} %bitcast.7, ...), custom_call_target="tpu_custom_call" | custom-call | flops 75497472 | bytes 1179648 | tf_op jit(solution)/shard_map/pallas_call | solution.py:260
  2.3 0.0 collective-permute-done.pair_ref
  2.4 0.5 %shard_map.92 = (bf16[2,144,128]{2,1,0:T(8,128)(2,1)S(1)}, bf16[2,144,128]{2,1,0:T(8,128)(2,1)S(1)}, bf16[2,144,128]{2,1,0:T(8,128)(2,1)S(1)}, bf16[2,144,128]{2,1,0:T(8,128)(2,1)S(1)}) custom-call(bf16[12,48,128]{2,1,0:T(8,128)(2,1)S(1)} %collective-permute-done.pair_ref, bf16[4,144,128]{2,1,0:T(8,128)(2,1)S(1)} %get-tuple-element.19.sides_ref, ...), custom_call_target="tpu_custom_call" | custom-call | flops 75497472 | bytes 1179648 | tf_op jit(solution)/shard_map/pallas_call | solution.py:283
  2.9 3.6 %collective-permute-start.1 = (bf16[2,144,128]{2,1,0:T(8,128)(2,1)S(1)}, bf16[2,144,128]{2,1,0:T(8,128)(2,1)S(1)}, u32[]{:S(2)}, u32[]{:S(2)}) collective-permute-start(bf16[2,144,128]{2,1,0:T(8,128)(2,1)S(1)} %get-tuple-element.23), channel_id=1, source_target_pairs={{0,6},{2,4},{4,2},{6,0},{1,7},{3,5},{5,3},{7,1},{8,14},{10,12},{12... | collective-permute-start | bytes 221192 | tf_op jit(solution)/shard_map/ppermute | solution.py:293
  6.5 0.5 %collective-permute-start.2 = (bf16[2,144,128]{2,1,0:T(8,128)(2,1)S(1)}, bf16[2,144,128]{2,1,0:T(8,128)(2,1)S(1)}, u32[]{:S(2)}, u32[]{:S(2)}) collective-permute-start(bf16[2,144,128]{2,1,0:T(8,128)(2,1)S(1)} %get-tuple-element.24), channel_id=1, source_target_pairs={{0,2},{2,0},{4,6},{6,4},{1,3},{3,1},{5,7},{7,5},{8,10},{10,8},{12,... | collective-permute-start | bytes 221192 | tf_op jit(solution)/shard_map/ppermute | solution.py:293
  7.0 0.1 collective-permute-start.3
  7.1 2.3 %collective-permute-done.1.refs_0_ = bf16[2,144,128]{2,1,0:T(8,128)(2,1)S(1)} collective-permute-done((bf16[2,144,128]{2,1,0:T(8,128)(2,1)S(1)}, bf16[2,144,128]{2,1,0:T(8,128)(2,1)S(1)}, u32[]{:S(2)}, u32[]{:S(2)}) %collective-permute-start.1) | collective-permute-done | bytes 73760 | tf_op jit(solution)/shard_map/ppermute | solution.py:293
  9.5 1.6 %collective-permute-done.2.refs_1_ = bf16[2,144,128]{2,1,0:T(8,128)(2,1)S(1)} collective-permute-done((bf16[2,144,128]{2,1,0:T(8,128)(2,1)S(1)}, bf16[2,144,128]{2,1,0:T(8,128)(2,1)S(1)}, u32[]{:S(2)}, u32[]{:S(2)}) %collective-permute-start.2) | collective-permute-done | bytes 73760 | tf_op jit(solution)/shard_map/ppermute | solution.py:293
  11.0 0.3 %collective-permute-done.3.refs_2_ = bf16[2,144,128]{2,1,0:T(8,128)(2,1)S(1)} collective-permute-done((bf16[2,144,128]{2,1,0:T(8,128)(2,1)S(1)}, bf16[2,144,128]{2,1,0:T(8,128)(2,1)S(1)}, u32[]{:S(2)}, u32[]{:S(2)}) %collective-permute-start.3) | collective-permute-done | bytes 73760 | tf_op jit(solution)/shard_map/ppermute | solution.py:293
  11.4 1.6 %shard_map.93 = bf16[16,72,128]{2,1,0:T(8,128)(2,1)} custom-call(bf16[2,144,128]{2,1,0:T(8,128)(2,1)S(1)} %collective-permute-done.1.refs_0_, bf16[2,144,128]{2,1,0:T(8,128)(2,1)S(1)} %collective-permute-done.2.refs_1_, bf16[2,144,128]{2,1,0:T(8,128)(2,1)S(1)} %collective-permute-done.3.refs_2_, bf16[2,144,128]{2,1,0:T(8,128)(2,1)S(1)} %get-tuple-element.26.refs_3_, ...), custom_call_target="tpu_custom_call" | custom-call | tf_op jit(solution)/shard_map/pallas_call | solution.py:294
  13.0 0.0 copy-start.1
  13.0 5.3 %all-to-all-start = ((bf16[16,72,128]{2,1,0:T(8,128)(2,1)}), bf16[16,72,128]{2,1,0:T(8,128)(2,1)S(1)}, u32[]{:S(2)}, u32[]{:S(2)}) async-start(bf16[16,72,128]{2,1,0:T(8,128)(2,1)} %shard_map.93), calls=%async_computation | async-start | bytes 589824 | tf_op jit(solution)/shard_map/all_to_all | solution.py:317
  18.3 0.0 copy-start.2
  18.3 0.0 copy-start.3
  18.3 0.0 copy-done.1
  18.3 0.6 %copy-done.2 = f32[128]{0:T(128)S(1)} copy-done((f32[128]{0:T(128)S(1)}, f32[128]{0:T(128)}, u32[]{:S(2)}) %copy-start.2) | copy-done | bytes 536
  18.9 0.0 copy-done.3
  18.9 0.0 copy-start
  18.9 0.2 shard_map.94
  19.1 6.5 %all-to-all-done.total_ref = bf16[16,72,128]{2,1,0:T(8,128)(2,1)S(1)} async-done(((bf16[16,72,128]{2,1,0:T(8,128)(2,1)}), bf16[16,72,128]{2,1,0:T(8,128)(2,1)S(1)}, u32[]{:S(2)}, u32[]{:S(2)}) %all-to-all-start) | async-done | bytes 294944 | tf_op jit(solution)/shard_map/all_to_all | solution.py:317
  25.6 0.0 copy-done
  25.6 1.0 %shard_map.95 = bf16[12,48,128]{2,1,0:T(8,128)(2,1)} custom-call(bf16[16,72,128]{2,1,0:T(8,128)(2,1)S(1)} %all-to-all-done.total_ref, f32[576,128]{1,0:T(8,128)S(1)} %get-tuple-element.30.gate_ref, f32[128,1]{1,0:T(8,128)S(1)} %get-tuple-element.31.gain_ref, f32[128,1]{1,0:T(8,128)S(1)} %get-tuple-element.32.bias_ref, bf16[128,128]{1,0:T(8,128)(2,1)S(1)} %copy-done), custom_call_target="tpu_custom_call" | custom-call | tf_op jit(solution)/shard_map/pallas_call | solution.py:318
Async XLA Ops:
  0.0 2.3 %collective-permute-start = (bf16[12,48,128]{2,1,0:T(8,128)(2,1)}, bf16[12,48,128]{2,1,0:T(8,128)(2,1)S(1)}, u32[]{:S(2)}, u32[]{:S(2)}) collective-permute-start(bf16[12,48,128]{2,1,0:T(8,128)(2,1)} %pair_hbm.1), channel_id=1, source_target_pairs={{0,1},{1,0},{2,3},{3,2},{4,5},{5,4},{6,7},{7,6},{8,9},{9,8},{10,11... | collective-permute-start | bytes 442376 | tf_op jit(solution)/shard_map/ppermute | solution.py:258
  2.9 6.6 %collective-permute-start.1 = (bf16[2,144,128]{2,1,0:T(8,128)(2,1)S(1)}, bf16[2,144,128]{2,1,0:T(8,128)(2,1)S(1)}, u32[]{:S(2)}, u32[]{:S(2)}) collective-permute-start(bf16[2,144,128]{2,1,0:T(8,128)(2,1)S(1)} %get-tuple-element.23), channel_id=1, source_target_pairs={{0,6},{2,4},{4,2},{6,0},{1,7},{3,5},{5,3},{7,1},{8,14},{10,12},{12... | collective-permute-start | bytes 221192 | tf_op jit(solution)/shard_map/ppermute | solution.py:293
  6.5 4.5 %collective-permute-start.2 = (bf16[2,144,128]{2,1,0:T(8,128)(2,1)S(1)}, bf16[2,144,128]{2,1,0:T(8,128)(2,1)S(1)}, u32[]{:S(2)}, u32[]{:S(2)}) collective-permute-start(bf16[2,144,128]{2,1,0:T(8,128)(2,1)S(1)} %get-tuple-element.24), channel_id=1, source_target_pairs={{0,2},{2,0},{4,6},{6,4},{1,3},{3,1},{5,7},{7,5},{8,10},{10,8},{12,... | collective-permute-start | bytes 221192 | tf_op jit(solution)/shard_map/ppermute | solution.py:293
  7.0 4.4 %collective-permute-start.3 = (bf16[2,144,128]{2,1,0:T(8,128)(2,1)S(1)}, bf16[2,144,128]{2,1,0:T(8,128)(2,1)S(1)}, u32[]{:S(2)}, u32[]{:S(2)}) collective-permute-start(bf16[2,144,128]{2,1,0:T(8,128)(2,1)S(1)} %get-tuple-element.25), channel_id=1, source_target_pairs={{0,4},{2,6},{4,0},{6,2},{1,5},{3,7},{5,1},{7,3},{8,12},{10,14},{12... | collective-permute-start | bytes 221192 | tf_op jit(solution)/shard_map/ppermute | solution.py:293
  13.0 5.3 %copy-start.1 = (bf16[128,128]{1,0:T(8,128)(2,1)S(1)}, bf16[128,128]{1,0:T(8,128)(2,1)}, u32[]{:S(2)}) copy-start(bf16[128,128]{1,0:T(8,128)(2,1)} %w_ref.2) | copy-start | bytes 98308
  13.0 12.7 %all-to-all-start = ((bf16[16,72,128]{2,1,0:T(8,128)(2,1)}), bf16[16,72,128]{2,1,0:T(8,128)(2,1)S(1)}, u32[]{:S(2)}, u32[]{:S(2)}) async-start(bf16[16,72,128]{2,1,0:T(8,128)(2,1)} %shard_map.93), calls=%async_computation | async-start | bytes 589824 | tf_op jit(solution)/shard_map/all_to_all | solution.py:317
  18.3 0.7 %copy-start.2 = (f32[128]{0:T(128)S(1)}, f32[128]{0:T(128)}, u32[]{:S(2)}) copy-start(f32[128]{0:T(128)} %param.15) | copy-start | bytes 1540
  18.3 0.7 %copy-start.3 = (f32[128]{0:T(128)S(1)}, f32[128]{0:T(128)}, u32[]{:S(2)}) copy-start(f32[128]{0:T(128)} %param.16) | copy-start | bytes 1540
  18.9 6.7 %copy-start = (bf16[128,128]{1,0:T(8,128)(2,1)S(1)}, bf16[128,128]{1,0:T(8,128)(2,1)}, u32[]{:S(2)}) copy-start(bf16[128,128]{1,0:T(8,128)(2,1)} %w_ref.3) | copy-start | bytes 98308

commit v37 on v31

--- a/solution.py
+++ b/solution.py
@@ -169,11 +169,23 @@
 
     contract = (((1,), (1,)), ((), ()))
     lane_block = lax.broadcasted_iota(jnp.int32, (group, LANES), 1) // rest
-    mains, lasts = [], []
+    gap = LANES // parts
+    weights = []
+    for part in range(parts):
+        right = side(1, part).astype(jnp.bfloat16)
+        ours = [right[col * col_count : (col + 1) * col_count] for col in range(cols)]
+        main = [
+            placed([p for mine in ours for p in (mine, LANES - col_count)]),
+            placed([p for mine in ours for p in (col_count, mine, spare)]),
+            placed([p for mine in ours for p in (2 * col_count, mine[:spare])]),
+        ]
+        pieces = [[gap * part] + [mine[spare:]] * whole + [LANES - gap * (part + 1)] for mine in ours]
+        last = placed([p for piece in pieces for p in piece if not isinstance(p, int) or p])
+        weights.append((jnp.concatenate(main, axis=1), last))
     for part in range(parts):
         left_ref[part] = side(0, part)
-        right = side(1, part).astype(jnp.bfloat16)
-        for row in range(rows):
+    for row in range(rows):
+        for part in range(parts):
             for t in range(0, whole, 2):
                 pair = []
                 for at in (row * row_count, row * row_count + 2):
@@ -182,18 +194,10 @@
                     pair.append(jnp.concatenate([copy * spread_ref[...] for copy in copies], axis=1))
                 at = (row * whole + t) * group
                 wide_ref[part, at : at + 2 * group, :] = jnp.concatenate(pair, axis=0).astype(jnp.bfloat16)
-        ours = [right[col * col_count : (col + 1) * col_count] for col in range(cols)]
-        weights = [
-            placed([p for mine in ours for p in (mine, LANES - col_count)]),
-            placed([p for mine in ours for p in (col_count, mine, spare)]),
-            placed([p for mine in ours for p in (2 * col_count, mine[:spare])]),
-        ]
-        weights = jnp.concatenate(weights, axis=1)
-        mains.append(lax.dot_general(wide_ref[part], weights, contract, preferred_element_type=jnp.float32))
-        gap = LANES // parts
-        pieces = [[gap * part] + [mine[spare:]] * whole + [LANES - gap * (part + 1)] for mine in ours]
-        weights = placed([p for piece in pieces for p in piece if not isinstance(p, int) or p])
-        lasts.append(lax.dot_general(wide_ref[part, :, 2 * lanes :], weights, contract, preferred_element_type=jnp.float32))
+    mains, lasts = [], []
+    for part, (main, last) in enumerate(weights):
+        mains.append(lax.dot_general(wide_ref[part], main, contract, preferred_element_type=jnp.float32))
+        lasts.append(lax.dot_general(wide_ref[part, :, 2 * lanes :], last, contract, preferred_element_type=jnp.float32))
     for target, device in enumerate(far_order):
         row, col = divmod(device, cols)
         spots = [(row * whole + t) * group for t in range(whole)]

time: 26.8 us -> 26.8 us (level)
  no operation moved by 1% of the time
where the time goes in v37:
time: 26.8 us; the launch traced here: 26.5 us
  waiting for transfers between devices  10.7 us (40%)
  starting transfers between devices  9.99 us (37%)
  Pallas kernels  5.07 us (19%)
  local copies, waits for them, and re-layouts  0.65 us (2%)
    all_to_all x1, waiting for transfers between devices, per_device(): lax.all_to_all(total, ('half', 'quad', 'col'), split_axis=0, concat_axis=...  6.51 us
    all_to_all x1, starting transfers between devices, per_device(): lax.all_to_all(total, ('half', 'quad', 'col'), split_axis=0, concat_axis=...  5.29 us
    ppermute x3, starting transfers between devices, per_device(): lax.ppermute(pieces[step], 'quad', [(i, i ^ step) for i in range(quads)])  4.24 us
    ppermute x3, waiting for transfers between devices, per_device(): lax.ppermute(pieces[step], 'quad', [(i, i ^ step) for i in range(quads)])  4.21 us
    pallas_call x1, Pallas kernels, per_device(): pl.pallas_call(functools.partial(own_kernel, quads, cols), out_shape=(jax...  1.71 us
    pallas_call x1, Pallas kernels, per_device(): pl.pallas_call(functools.partial(triangle_kernel, far_order, steps, cols,...  1.63 us
    pallas_call x1, Pallas kernels, per_device(): pl.pallas_call(functools.partial(output_kernel, far_order, near_order), o...  1.02 us
    unnamed x8, local copies, waits for them, and re-layouts  0.65 us
  transfers between devices with their start and end apart: 5, of which 4 were waited for; matrix products, arithmetic and copies ran while one was open for 0% of the time, Pallas kernels for 7%

profile of v37, /device:TPU:0, one launch (start us, length us, event | category | flops | bytes accessed | tf_op | source)
XLA Modules:
  0.0 26.5 jit_solution(4656660460168614351)
XLA Ops:
  0.0 0.5 %collective-permute-start = (bf16[12,48,128]{2,1,0:T(8,128)(2,1)}, bf16[12,48,128]{2,1,0:T(8,128)(2,1)S(1)}, u32[]{:S(2)}, u32[]{:S(2)}) collective-permute-start(bf16[12,48,128]{2,1,0:T(8,128)(2,1)} %pair_hbm.1), channel_id=1, source_target_pairs={{0,1},{1,0},{2,3},{3,2},{4,5},{5,4},{6,7},{7,6},{8,9},{9,8},{10,11... | collective-permute-start | bytes 442376 | tf_op jit(solution)/shard_map/ppermute | solution.py:255
  0.5 1.7 %shard_map.91 = (bf16[4,144,128]{2,1,0:T(8,128)(2,1)S(1)}, bf16[576,128]{1,0:T(8,128)(2,1)S(1)}, f32[8,384]{1,0:T(8,128)S(1)}, f32[96,1]{1,0:T(8,128)S(1)}, bf16...) custom-call(bf16[12,48,128]{2,1,0:T(8,128)(2,1)} %pair_hbm.1, f32[1,128]{1,0:T(1,128)} %bitcast.7, ...), custom_call_target="tpu_custom_call" | custom-call | flops 75497472 | bytes 1179648 | tf_op jit(solution)/shard_map/pallas_call | solution.py:257
  2.2 0.0 collective-permute-done.pair_ref
  2.2 0.5 %shard_map.92 = (bf16[2,144,128]{2,1,0:T(8,128)(2,1)S(1)}, bf16[2,144,128]{2,1,0:T(8,128)(2,1)S(1)}, bf16[2,144,128]{2,1,0:T(8,128)(2,1)S(1)}, bf16[2,144,128]{2,1,0:T(8,128)(2,1)S(1)}) custom-call(bf16[12,48,128]{2,1,0:T(8,128)(2,1)S(1)} %collective-permute-done.pair_ref, bf16[4,144,128]{2,1,0:T(8,128)(2,1)S(1)} %get-tuple-element.19.sides_ref, ...), custom_call_target="tpu_custom_call" | custom-call | flops 75497472 | bytes 1179648 | tf_op jit(solution)/shard_map/pallas_call | solution.py:280
  2.7 3.6 %collective-permute-start.1 = (bf16[2,144,128]{2,1,0:T(8,128)(2,1)S(1)}, bf16[2,144,128]{2,1,0:T(8,128)(2,1)S(1)}, u32[]{:S(2)}, u32[]{:S(2)}) collective-permute-start(bf16[2,144,128]{2,1,0:T(8,128)(2,1)S(1)} %get-tuple-element.23), channel_id=1, source_target_pairs={{0,6},{2,4},{4,2},{6,0},{1,7},{3,5},{5,3},{7,1},{8,14},{10,12},{12... | collective-permute-start | bytes 221192 | tf_op jit(solution)/shard_map/ppermute | solution.py:290
  6.3 0.5 %collective-permute-start.2 = (bf16[2,144,128]{2,1,0:T(8,128)(2,1)S(1)}, bf16[2,144,128]{2,1,0:T(8,128)(2,1)S(1)}, u32[]{:S(2)}, u32[]{:S(2)}) collective-permute-start(bf16[2,144,128]{2,1,0:T(8,128)(2,1)S(1)} %get-tuple-element.24), channel_id=1, source_target_pairs={{0,2},{2,0},{4,6},{6,4},{1,3},{3,1},{5,7},{7,5},{8,10},{10,8},{12,... | collective-permute-start | bytes 221192 | tf_op jit(solution)/shard_map/ppermute | solution.py:290
  6.8 0.1 collective-permute-start.3
  7.0 2.3 %collective-permute-done.1.refs_0_ = bf16[2,144,128]{2,1,0:T(8,128)(2,1)S(1)} collective-permute-done((bf16[2,144,128]{2,1,0:T(8,128)(2,1)S(1)}, bf16[2,144,128]{2,1,0:T(8,128)(2,1)S(1)}, u32[]{:S(2)}, u32[]{:S(2)}) %collective-permute-start.1) | collective-permute-done | bytes 73760 | tf_op jit(solution)/shard_map/ppermute | solution.py:290
  9.3 1.6 %collective-permute-done.2.refs_1_ = bf16[2,144,128]{2,1,0:T(8,128)(2,1)S(1)} collective-permute-done((bf16[2,144,128]{2,1,0:T(8,128)(2,1)S(1)}, bf16[2,144,128]{2,1,0:T(8,128)(2,1)S(1)}, u32[]{:S(2)}, u32[]{:S(2)}) %collective-permute-start.2) | collective-permute-done | bytes 73760 | tf_op jit(solution)/shard_map/ppermute | solution.py:290
  10.8 0.3 %collective-permute-done.3.refs_2_ = bf16[2,144,128]{2,1,0:T(8,128)(2,1)S(1)} collective-permute-done((bf16[2,144,128]{2,1,0:T(8,128)(2,1)S(1)}, bf16[2,144,128]{2,1,0:T(8,128)(2,1)S(1)}, u32[]{:S(2)}, u32[]{:S(2)}) %collective-permute-start.3) | collective-permute-done | bytes 73760 | tf_op jit(solution)/shard_map/ppermute | solution.py:290
  11.2 1.6 %shard_map.93 = bf16[16,72,128]{2,1,0:T(8,128)(2,1)} custom-call(bf16[2,144,128]{2,1,0:T(8,128)(2,1)S(1)} %collective-permute-done.1.refs_0_, bf16[2,144,128]{2,1,0:T(8,128)(2,1)S(1)} %collective-permute-done.2.refs_1_, bf16[2,144,128]{2,1,0:T(8,128)(2,1)S(1)} %collective-permute-done.3.refs_2_, bf16[2,144,128]{2,1,0:T(8,128)(2,1)S(1)} %get-tuple-element.26.refs_3_, ...), custom_call_target="tpu_custom_call" | custom-call | tf_op jit(solution)/shard_map/pallas_call | solution.py:291
  12.8 0.0 copy-start.1
  12.8 5.3 %all-to-all-start = ((bf16[16,72,128]{2,1,0:T(8,128)(2,1)}), bf16[16,72,128]{2,1,0:T(8,128)(2,1)S(1)}, u32[]{:S(2)}, u32[]{:S(2)}) async-start(bf16[16,72,128]{2,1,0:T(8,128)(2,1)} %shard_map.93), calls=%async_computation | async-start | bytes 589824 | tf_op jit(solution)/shard_map/all_to_all | solution.py:314
  18.1 0.0 copy-start.2
  18.1 0.0 copy-start.3
  18.1 0.0 copy-done.1
  18.1 0.6 %copy-done.2 = f32[128]{0:T(128)S(1)} copy-done((f32[128]{0:T(128)S(1)}, f32[128]{0:T(128)}, u32[]{:S(2)}) %copy-start.2) | copy-done | bytes 536
  18.8 0.0 copy-done.3
  18.8 0.0 copy-start
  18.8 0.2 shard_map.94
  19.0 6.5 %all-to-all-done.total_ref = bf16[16,72,128]{2,1,0:T(8,128)(2,1)S(1)} async-done(((bf16[16,72,128]{2,1,0:T(8,128)(2,1)}), bf16[16,72,128]{2,1,0:T(8,128)(2,1)S(1)}, u32[]{:S(2)}, u32[]{:S(2)}) %all-to-all-start) | async-done | bytes 294944 | tf_op jit(solution)/shard_map/all_to_all | solution.py:314
  25.5 0.0 copy-done
  25.5 1.0 %shard_map.95 = bf16[12,48,128]{2,1,0:T(8,128)(2,1)} custom-call(bf16[16,72,128]{2,1,0:T(8,128)(2,1)S(1)} %all-to-all-done.total_ref, f32[576,128]{1,0:T(8,128)S(1)} %get-tuple-element.30.gate_ref, f32[128,1]{1,0:T(8,128)S(1)} %get-tuple-element.31.gain_ref, f32[128,1]{1,0:T(8,128)S(1)} %get-tuple-element.32.bias_ref, bf16[128,128]{1,0:T(8,128)(2,1)S(1)} %copy-done), custom_call_target="tpu_custom_call" | custom-call | tf_op jit(solution)/shard_map/pallas_call | solution.py:315
Async XLA Ops:
  0.0 2.2 %collective-permute-start = (bf16[12,48,128]{2,1,0:T(8,128)(2,1)}, bf16[12,48,128]{2,1,0:T(8,128)(2,1)S(1)}, u32[]{:S(2)}, u32[]{:S(2)}) collective-permute-start(bf16[12,48,128]{2,1,0:T(8,128)(2,1)} %pair_hbm.1), channel_id=1, source_target_pairs={{0,1},{1,0},{2,3},{3,2},{4,5},{5,4},{6,7},{7,6},{8,9},{9,8},{10,11... | collective-permute-start | bytes 442376 | tf_op jit(solution)/shard_map/ppermute | solution.py:255
  2.7 6.6 %collective-permute-start.1 = (bf16[2,144,128]{2,1,0:T(8,128)(2,1)S(1)}, bf16[2,144,128]{2,1,0:T(8,128)(2,1)S(1)}, u32[]{:S(2)}, u32[]{:S(2)}) collective-permute-start(bf16[2,144,128]{2,1,0:T(8,128)(2,1)S(1)} %get-tuple-element.23), channel_id=1, source_target_pairs={{0,6},{2,4},{4,2},{6,0},{1,7},{3,5},{5,3},{7,1},{8,14},{10,12},{12... | collective-permute-start | bytes 221192 | tf_op jit(solution)/shard_map/ppermute | solution.py:290
  6.3 4.5 %collective-permute-start.2 = (bf16[2,144,128]{2,1,0:T(8,128)(2,1)S(1)}, bf16[2,144,128]{2,1,0:T(8,128)(2,1)S(1)}, u32[]{:S(2)}, u32[]{:S(2)}) collective-permute-start(bf16[2,144,128]{2,1,0:T(8,128)(2,1)S(1)} %get-tuple-element.24), channel_id=1, source_target_pairs={{0,2},{2,0},{4,6},{6,4},{1,3},{3,1},{5,7},{7,5},{8,10},{10,8},{12,... | collective-permute-start | bytes 221192 | tf_op jit(solution)/shard_map/ppermute | solution.py:290
  6.8 4.4 %collective-permute-start.3 = (bf16[2,144,128]{2,1,0:T(8,128)(2,1)S(1)}, bf16[2,144,128]{2,1,0:T(8,128)(2,1)S(1)}, u32[]{:S(2)}, u32[]{:S(2)}) collective-permute-start(bf16[2,144,128]{2,1,0:T(8,128)(2,1)S(1)} %get-tuple-element.25), channel_id=1, source_target_pairs={{0,4},{2,6},{4,0},{6,2},{1,5},{3,7},{5,1},{7,3},{8,12},{10,14},{12... | collective-permute-start | bytes 221192 | tf_op jit(solution)/shard_map/ppermute | solution.py:290
  12.8 5.3 %copy-start.1 = (bf16[128,128]{1,0:T(8,128)(2,1)S(1)}, bf16[128,128]{1,0:T(8,128)(2,1)}, u32[]{:S(2)}) copy-start(bf16[128,128]{1,0:T(8,128)(2,1)} %w_ref.2) | copy-start | bytes 98308
  12.8 12.7 %all-to-all-start = ((bf16[16,72,128]{2,1,0:T(8,128)(2,1)}), bf16[16,72,128]{2,1,0:T(8,128)(2,1)S(1)}, u32[]{:S(2)}, u32[]{:S(2)}) async-start(bf16[16,72,128]{2,1,0:T(8,128)(2,1)} %shard_map.93), calls=%async_computation | async-start | bytes 589824 | tf_op jit(solution)/shard_map/all_to_all | solution.py:314
  18.1 0.7 %copy-start.2 = (f32[128]{0:T(128)S(1)}, f32[128]{0:T(128)}, u32[]{:S(2)}) copy-start(f32[128]{0:T(128)} %param.15) | copy-start | bytes 1540
  18.1 0.7 %copy-start.3 = (f32[128]{0:T(128)S(1)}, f32[128]{0:T(128)}, u32[]{:S(2)}) copy-start(f32[128]{0:T(128)} %param.16) | copy-start | bytes 1540
  18.8 6.7 %copy-start = (bf16[128,128]{1,0:T(8,128)(2,1)S(1)}, bf16[128,128]{1,0:T(8,128)(2,1)}, u32[]{:S(2)}) copy-start(bf16[128,128]{1,0:T(8,128)(2,1)} %w_ref.3) | copy-start | bytes 98308

commit v38 on v32

--- a/solution.py
+++ b/solution.py
@@ -253,7 +253,7 @@
     near_order = [quad * cols + col for col in range(cols) for quad in range(quads)]
     packed = 2 * share * tokens // LANES
     cost = pl.CostEstimate(flops=2 * tokens * channels * 4 * hidden, bytes_accessed=16 * tokens * channels, transcendentals=0)
-    steps = [(3, 1), (1, 2), (2, 3), (0, 0)]
+    steps = [(3, 3), (1, 2), (2, 1), (0, 0)]
     other_pair = lax.ppermute(pair, "col", [(i, (i + 1) % cols) for i in range(cols)])
     arguments = (pair, gain_in.reshape(1, channels), bias_in.reshape(1, channels), w_in, token_mask)
     sides, normed, spread, mask, *weights = pl.pallas_call(

time: 27 us -> 27.3 us (1.011)
  starting transfers between devices: 10 us -> 10.6 us
  waiting for transfers between devices: 10.9 us -> 10.6 us
    all_to_all x1, starting transfers between devices: 5.32 us -> 5.86 us  [per_device(): lax.all_to_all(total, ('half', 'quad', 'col'), split_axis=0, concat_axis=...]
    ppermute x3, waiting for transfers between devices: 4.5 us -> 4.22 us  [per_device(): lax.ppermute(piece, ('quad', 'col'), moves)]
  transfers between devices with their start and end apart: 5 -> 5, of which waited for: 3 -> 4; matrix products, arithmetic and copies ran while one was open for 0% -> 0% of each run, Pallas kernels for 7% -> 7%
where the time goes in v38:
time: 27.3 us; the launch traced here: 27 us
  starting transfers between devices  10.6 us (39%)
  waiting for transfers between devices  10.6 us (39%)
  Pallas kernels  5.05 us (18%)
  local copies, waits for them, and re-layouts  0.65 us (2%)
    all_to_all x1, waiting for transfers between devices, per_device(): lax.all_to_all(total, ('half', 'quad', 'col'), split_axis=0, concat_axis=...  6.42 us
    all_to_all x1, starting transfers between devices, per_device(): lax.all_to_all(total, ('half', 'quad', 'col'), split_axis=0, concat_axis=...  5.86 us
    ppermute x3, starting transfers between devices, per_device(): lax.ppermute(piece, ('quad', 'col'), moves)  4.24 us
    ppermute x3, waiting for transfers between devices, per_device(): lax.ppermute(piece, ('quad', 'col'), moves)  4.22 us
    pallas_call x1, Pallas kernels, per_device(): pl.pallas_call(functools.partial(own_kernel, steps, quads, cols), out_sha...  1.71 us
    pallas_call x1, Pallas kernels, per_device(): pl.pallas_call(functools.partial(triangle_kernel, far_order, cols, row_co...  1.61 us
    pallas_call x1, Pallas kernels, per_device(): pl.pallas_call(functools.partial(output_kernel, far_order, near_order), o...  1.02 us
    unnamed x8, local copies, waits for them, and re-layouts  0.65 us
  transfers between devices with their start and end apart: 5, of which 4 were waited for; matrix products, arithmetic and copies ran while one was open for 0% of the time, Pallas kernels for 7%

profile of v38, /device:TPU:0, one launch (start us, length us, event | category | flops | bytes accessed | tf_op | source)
XLA Modules:
  0.0 27.0 jit_solution(16998113825359979115)
XLA Ops:
  0.0 0.5 %collective-permute-start = (bf16[12,48,128]{2,1,0:T(8,128)(2,1)}, bf16[12,48,128]{2,1,0:T(8,128)(2,1)S(1)}, u32[]{:S(2)}, u32[]{:S(2)}) collective-permute-start(bf16[12,48,128]{2,1,0:T(8,128)(2,1)} %pair_hbm.1), channel_id=1, source_target_pairs={{0,1},{1,0},{2,3},{3,2},{4,5},{5,4},{6,7},{7,6},{8,9},{9,8},{10,11... | collective-permute-start | bytes 442376 | tf_op jit(solution)/shard_map/ppermute | solution.py:257
  0.5 1.7 %shard_map.91 = (bf16[4,144,128]{2,1,0:T(8,128)(2,1)S(1)}, bf16[576,128]{1,0:T(8,128)(2,1)S(1)}, f32[8,384]{1,0:T(8,128)S(1)}, f32[96,1]{1,0:T(8,128)S(1)}, bf16...) custom-call(bf16[12,48,128]{2,1,0:T(8,128)(2,1)} %pair_hbm.1, f32[1,128]{1,0:T(1,128)} %bitcast.7, ...), custom_call_target="tpu_custom_call" | custom-call | flops 75497472 | bytes 1179648 | tf_op jit(solution)/shard_map/pallas_call | solution.py:259
  2.2 0.0 collective-permute-done.pair_ref
  2.2 0.5 %shard_map.92 = (bf16[2,144,128]{2,1,0:T(8,128)(2,1)S(1)}, bf16[2,144,128]{2,1,0:T(8,128)(2,1)S(1)}, bf16[2,144,128]{2,1,0:T(8,128)(2,1)S(1)}, bf16[2,144,128]{2,1,0:T(8,128)(2,1)S(1)}) custom-call(bf16[12,48,128]{2,1,0:T(8,128)(2,1)S(1)} %collective-permute-done.pair_ref, bf16[4,144,128]{2,1,0:T(8,128)(2,1)S(1)} %get-tuple-element.19.sides_ref, ...), custom_call_target="tpu_custom_call" | custom-call | flops 75497472 | bytes 1179648 | tf_op jit(solution)/shard_map/pallas_call | solution.py:282
  2.7 3.6 %collective-permute-start.1 = (bf16[2,144,128]{2,1,0:T(8,128)(2,1)S(1)}, bf16[2,144,128]{2,1,0:T(8,128)(2,1)S(1)}, u32[]{:S(2)}, u32[]{:S(2)}) collective-permute-start(bf16[2,144,128]{2,1,0:T(8,128)(2,1)S(1)} %get-tuple-element.23), channel_id=1, source_target_pairs={{0,6},{1,7},{2,4},{3,5},{4,2},{5,3},{6,0},{7,1},{8,14},{9,15},{10,... | collective-permute-start | bytes 221192 | tf_op jit(solution)/shard_map/ppermute | solution.py:294
  6.3 0.5 %collective-permute-start.2 = (bf16[2,144,128]{2,1,0:T(8,128)(2,1)S(1)}, bf16[2,144,128]{2,1,0:T(8,128)(2,1)S(1)}, u32[]{:S(2)}, u32[]{:S(2)}) collective-permute-start(bf16[2,144,128]{2,1,0:T(8,128)(2,1)S(1)} %get-tuple-element.24), channel_id=1, source_target_pairs={{0,2},{1,5},{2,0},{3,7},{4,6},{5,1},{6,4},{7,3},{8,10},{9,13},{10,... | collective-permute-start | bytes 221192 | tf_op jit(solution)/shard_map/ppermute | solution.py:294
  6.8 0.1 collective-permute-start.3
  7.0 2.5 %collective-permute-done.1.refs_0_ = bf16[2,144,128]{2,1,0:T(8,128)(2,1)S(1)} collective-permute-done((bf16[2,144,128]{2,1,0:T(8,128)(2,1)S(1)}, bf16[2,144,128]{2,1,0:T(8,128)(2,1)S(1)}, u32[]{:S(2)}, u32[]{:S(2)}) %collective-permute-start.1) | collective-permute-done | bytes 73760 | tf_op jit(solution)/shard_map/ppermute | solution.py:294
  9.4 1.5 %collective-permute-done.2.refs_1_ = bf16[2,144,128]{2,1,0:T(8,128)(2,1)S(1)} collective-permute-done((bf16[2,144,128]{2,1,0:T(8,128)(2,1)S(1)}, bf16[2,144,128]{2,1,0:T(8,128)(2,1)S(1)}, u32[]{:S(2)}, u32[]{:S(2)}) %collective-permute-start.2) | collective-permute-done | bytes 73760 | tf_op jit(solution)/shard_map/ppermute | solution.py:294
  10.9 0.2 collective-permute-done.3.refs_2_
  11.2 1.6 %shard_map.93 = bf16[16,72,128]{2,1,0:T(8,128)(2,1)} custom-call(bf16[2,144,128]{2,1,0:T(8,128)(2,1)S(1)} %collective-permute-done.1.refs_0_, bf16[2,144,128]{2,1,0:T(8,128)(2,1)S(1)} %collective-permute-done.2.refs_1_, bf16[2,144,128]{2,1,0:T(8,128)(2,1)S(1)} %collective-permute-done.3.refs_2_, bf16[2,144,128]{2,1,0:T(8,128)(2,1)S(1)} %get-tuple-element.26.refs_3_, ...), custom_call_target="tpu_custom_call" | custom-call | tf_op jit(solution)/shard_map/pallas_call | solution.py:295
  12.8 0.0 copy-start.1
  12.8 5.9 %all-to-all-start = ((bf16[16,72,128]{2,1,0:T(8,128)(2,1)}), bf16[16,72,128]{2,1,0:T(8,128)(2,1)S(1)}, u32[]{:S(2)}, u32[]{:S(2)}) async-start(bf16[16,72,128]{2,1,0:T(8,128)(2,1)} %shard_map.93), calls=%async_computation | async-start | bytes 589824 | tf_op jit(solution)/shard_map/all_to_all | solution.py:318
  18.7 0.0 copy-start.2
  18.7 0.0 copy-start.3
  18.7 0.0 copy-done.1
  18.7 0.6 %copy-done.2 = f32[128]{0:T(128)S(1)} copy-done((f32[128]{0:T(128)S(1)}, f32[128]{0:T(128)}, u32[]{:S(2)}) %copy-start.2) | copy-done | bytes 536
  19.3 0.0 copy-done.3
  19.3 0.0 copy-start
  19.3 0.2 shard_map.94
  19.5 6.4 %all-to-all-done.total_ref = bf16[16,72,128]{2,1,0:T(8,128)(2,1)S(1)} async-done(((bf16[16,72,128]{2,1,0:T(8,128)(2,1)}), bf16[16,72,128]{2,1,0:T(8,128)(2,1)S(1)}, u32[]{:S(2)}, u32[]{:S(2)}) %all-to-all-start) | async-done | bytes 294944 | tf_op jit(solution)/shard_map/all_to_all | solution.py:318
  25.9 0.0 copy-done
  26.0 1.0 %shard_map.95 = bf16[12,48,128]{2,1,0:T(8,128)(2,1)} custom-call(bf16[16,72,128]{2,1,0:T(8,128)(2,1)S(1)} %all-to-all-done.total_ref, f32[576,128]{1,0:T(8,128)S(1)} %get-tuple-element.30.gate_ref, f32[128,1]{1,0:T(8,128)S(1)} %get-tuple-element.31.gain_ref, f32[128,1]{1,0:T(8,128)S(1)} %get-tuple-element.32.bias_ref, bf16[128,128]{1,0:T(8,128)(2,1)S(1)} %copy-done), custom_call_target="tpu_custom_call" | custom-call | tf_op jit(solution)/shard_map/pallas_call | solution.py:319
Async XLA Ops:
  0.0 2.2 %collective-permute-start = (bf16[12,48,128]{2,1,0:T(8,128)(2,1)}, bf16[12,48,128]{2,1,0:T(8,128)(2,1)S(1)}, u32[]{:S(2)}, u32[]{:S(2)}) collective-permute-start(bf16[12,48,128]{2,1,0:T(8,128)(2,1)} %pair_hbm.1), channel_id=1, source_target_pairs={{0,1},{1,0},{2,3},{3,2},{4,5},{5,4},{6,7},{7,6},{8,9},{9,8},{10,11... | collective-permute-start | bytes 442376 | tf_op jit(solution)/shard_map/ppermute | solution.py:257
  2.7 6.7 %collective-permute-start.1 = (bf16[2,144,128]{2,1,0:T(8,128)(2,1)S(1)}, bf16[2,144,128]{2,1,0:T(8,128)(2,1)S(1)}, u32[]{:S(2)}, u32[]{:S(2)}) collective-permute-start(bf16[2,144,128]{2,1,0:T(8,128)(2,1)S(1)} %get-tuple-element.23), channel_id=1, source_target_pairs={{0,6},{1,7},{2,4},{3,5},{4,2},{5,3},{6,0},{7,1},{8,14},{9,15},{10,... | collective-permute-start | bytes 221192 | tf_op jit(solution)/shard_map/ppermute | solution.py:294
  6.3 4.6 %collective-permute-start.2 = (bf16[2,144,128]{2,1,0:T(8,128)(2,1)S(1)}, bf16[2,144,128]{2,1,0:T(8,128)(2,1)S(1)}, u32[]{:S(2)}, u32[]{:S(2)}) collective-permute-start(bf16[2,144,128]{2,1,0:T(8,128)(2,1)S(1)} %get-tuple-element.24), channel_id=1, source_target_pairs={{0,2},{1,5},{2,0},{3,7},{4,6},{5,1},{6,4},{7,3},{8,10},{9,13},{10,... | collective-permute-start | bytes 221192 | tf_op jit(solution)/shard_map/ppermute | solution.py:294
  6.8 4.4 %collective-permute-start.3 = (bf16[2,144,128]{2,1,0:T(8,128)(2,1)S(1)}, bf16[2,144,128]{2,1,0:T(8,128)(2,1)S(1)}, u32[]{:S(2)}, u32[]{:S(2)}) collective-permute-start(bf16[2,144,128]{2,1,0:T(8,128)(2,1)S(1)} %get-tuple-element.25), channel_id=1, source_target_pairs={{0,4},{1,3},{2,6},{3,1},{4,0},{5,7},{6,2},{7,5},{8,12},{9,11},{10,... | collective-permute-start | bytes 221192 | tf_op jit(solution)/shard_map/ppermute | solution.py:294
  12.8 5.9 %copy-start.1 = (bf16[128,128]{1,0:T(8,128)(2,1)S(1)}, bf16[128,128]{1,0:T(8,128)(2,1)}, u32[]{:S(2)}) copy-start(bf16[128,128]{1,0:T(8,128)(2,1)} %w_ref.2) | copy-start | bytes 98308
  12.8 13.1 %all-to-all-start = ((bf16[16,72,128]{2,1,0:T(8,128)(2,1)}), bf16[16,72,128]{2,1,0:T(8,128)(2,1)S(1)}, u32[]{:S(2)}, u32[]{:S(2)}) async-start(bf16[16,72,128]{2,1,0:T(8,128)(2,1)} %shard_map.93), calls=%async_computation | async-start | bytes 589824 | tf_op jit(solution)/shard_map/all_to_all | solution.py:318
  18.7 0.7 %copy-start.2 = (f32[128]{0:T(128)S(1)}, f32[128]{0:T(128)}, u32[]{:S(2)}) copy-start(f32[128]{0:T(128)} %param.15) | copy-start | bytes 1540
  18.7 0.7 %copy-start.3 = (f32[128]{0:T(128)S(1)}, f32[128]{0:T(128)}, u32[]{:S(2)}) copy-start(f32[128]{0:T(128)} %param.16) | copy-start | bytes 1540
  19.3 6.6 %copy-start = (bf16[128,128]{1,0:T(8,128)(2,1)S(1)}, bf16[128,128]{1,0:T(8,128)(2,1)}, u32[]{:S(2)}) copy-start(bf16[128,128]{1,0:T(8,128)(2,1)} %w_ref.3) | copy-start | bytes 98308

commit v39 on v34

--- a/solution.py
+++ b/solution.py
@@ -236,10 +236,9 @@
     quads = rows // halves
     far_order = []
     for col in reversed(range(cols)):
-        ahead = list(range(quads)) if col else list(range(1, quads)) + [0]
-        behind = [0] + list(reversed(range(1, quads))) if col else list(range(quads))
-        for quad, other in zip(ahead, behind):
-            far_order += [near + other * cols + col, quad * cols + col]
+        ours = [quad * cols + col for quad in (range(quads) if col else [*range(1, quads), 0])]
+        behind = [near + quad * cols + col for quad in reversed(range(quads))]
+        far_order += behind[-1:] + ours + behind[:-1] if col else behind + ours
     share = hidden // near
     tokens = row_count * col_count
     length = rows * row_count

time: 26.9 us -> 27.7 us (1.030)
  waiting for transfers between devices: 10.7 us -> 11.7 us
    all_to_all x1, waiting for transfers between devices: 6.51 us -> 7.46 us  [per_device(): lax.all_to_all(total, ('half', 'quad', 'col'), split_axis=0, concat_axis=...]
where the time goes in v39:
time: 27.7 us; the launch traced here: 27.4 us
  waiting for transfers between devices  11.7 us (42%)
  starting transfers between devices  9.98 us (36%)
  Pallas kernels  5.05 us (18%)
  local copies, waits for them, and re-layouts  0.65 us (2%)
    all_to_all x1, waiting for transfers between devices, per_device(): lax.all_to_all(total, ('half', 'quad', 'col'), split_axis=0, concat_axis=...  7.46 us
    all_to_all x1, starting transfers between devices, per_device(): lax.all_to_all(total, ('half', 'quad', 'col'), split_axis=0, concat_axis=...  5.29 us
    ppermute x3, starting transfers between devices, per_device(): lax.ppermute(pieces[step], 'quad', [(i, i ^ step) for i in range(quads)])  4.24 us
    ppermute x3, waiting for transfers between devices, per_device(): lax.ppermute(pieces[step], 'quad', [(i, i ^ step) for i in range(quads)])  4.21 us
    pallas_call x1, Pallas kernels, per_device(): pl.pallas_call(functools.partial(own_kernel, quads, cols), out_shape=(jax...  1.71 us
    pallas_call x1, Pallas kernels, per_device(): pl.pallas_call(functools.partial(triangle_kernel, far_order, steps, cols,...  1.61 us
    pallas_call x1, Pallas kernels, per_device(): pl.pallas_call(functools.partial(output_kernel, far_order, near_order), o...  1.01 us
    unnamed x8, local copies, waits for them, and re-layouts  0.65 us
  transfers between devices with their start and end apart: 5, of which 4 were waited for; matrix products, arithmetic and copies ran while one was open for 0% of the time, Pallas kernels for 7%

profile of v39, /device:TPU:0, one launch (start us, length us, event | category | flops | bytes accessed | tf_op | source)
XLA Modules:
  0.0 27.4 jit_solution(16334461932602102675)
XLA Ops:
  0.0 0.5 %collective-permute-start = (bf16[12,48,128]{2,1,0:T(8,128)(2,1)}, bf16[12,48,128]{2,1,0:T(8,128)(2,1)S(1)}, u32[]{:S(2)}, u32[]{:S(2)}) collective-permute-start(bf16[12,48,128]{2,1,0:T(8,128)(2,1)} %pair_hbm.1), channel_id=1, source_target_pairs={{0,1},{1,0},{2,3},{3,2},{4,5},{5,4},{6,7},{7,6},{8,9},{9,8},{10,11... | collective-permute-start | bytes 442376 | tf_op jit(solution)/shard_map/ppermute | solution.py:250
  0.5 1.7 %shard_map.91 = (bf16[4,144,128]{2,1,0:T(8,128)(2,1)S(1)}, bf16[576,128]{1,0:T(8,128)(2,1)S(1)}, f32[8,384]{1,0:T(8,128)S(1)}, f32[96,1]{1,0:T(8,128)S(1)}, bf16...) custom-call(bf16[12,48,128]{2,1,0:T(8,128)(2,1)} %pair_hbm.1, f32[1,128]{1,0:T(1,128)} %bitcast.7, ...), custom_call_target="tpu_custom_call" | custom-call | flops 75497472 | bytes 1179648 | tf_op jit(solution)/shard_map/pallas_call | solution.py:252
  2.2 0.0 collective-permute-done.pair_ref
  2.2 0.5 %shard_map.92 = (bf16[2,144,128]{2,1,0:T(8,128)(2,1)S(1)}, bf16[2,144,128]{2,1,0:T(8,128)(2,1)S(1)}, bf16[2,144,128]{2,1,0:T(8,128)(2,1)S(1)}, bf16[2,144,128]{2,1,0:T(8,128)(2,1)S(1)}) custom-call(bf16[12,48,128]{2,1,0:T(8,128)(2,1)S(1)} %collective-permute-done.pair_ref, bf16[4,144,128]{2,1,0:T(8,128)(2,1)S(1)} %get-tuple-element.19.sides_ref, ...), custom_call_target="tpu_custom_call" | custom-call | flops 75497472 | bytes 1179648 | tf_op jit(solution)/shard_map/pallas_call | solution.py:275
  2.7 3.6 %collective-permute-start.1 = (bf16[2,144,128]{2,1,0:T(8,128)(2,1)S(1)}, bf16[2,144,128]{2,1,0:T(8,128)(2,1)S(1)}, u32[]{:S(2)}, u32[]{:S(2)}) collective-permute-start(bf16[2,144,128]{2,1,0:T(8,128)(2,1)S(1)} %get-tuple-element.23), channel_id=1, source_target_pairs={{0,6},{2,4},{4,2},{6,0},{1,7},{3,5},{5,3},{7,1},{8,14},{10,12},{12... | collective-permute-start | bytes 221192 | tf_op jit(solution)/shard_map/ppermute | solution.py:285
  6.3 0.5 %collective-permute-start.2 = (bf16[2,144,128]{2,1,0:T(8,128)(2,1)S(1)}, bf16[2,144,128]{2,1,0:T(8,128)(2,1)S(1)}, u32[]{:S(2)}, u32[]{:S(2)}) collective-permute-start(bf16[2,144,128]{2,1,0:T(8,128)(2,1)S(1)} %get-tuple-element.24), channel_id=1, source_target_pairs={{0,2},{2,0},{4,6},{6,4},{1,3},{3,1},{5,7},{7,5},{8,10},{10,8},{12,... | collective-permute-start | bytes 221192 | tf_op jit(solution)/shard_map/ppermute | solution.py:285
  6.8 0.1 collective-permute-start.3
  7.0 2.3 %collective-permute-done.1.refs_0_ = bf16[2,144,128]{2,1,0:T(8,128)(2,1)S(1)} collective-permute-done((bf16[2,144,128]{2,1,0:T(8,128)(2,1)S(1)}, bf16[2,144,128]{2,1,0:T(8,128)(2,1)S(1)}, u32[]{:S(2)}, u32[]{:S(2)}) %collective-permute-start.1) | collective-permute-done | bytes 73760 | tf_op jit(solution)/shard_map/ppermute | solution.py:285
  9.3 1.6 %collective-permute-done.2.refs_1_ = bf16[2,144,128]{2,1,0:T(8,128)(2,1)S(1)} collective-permute-done((bf16[2,144,128]{2,1,0:T(8,128)(2,1)S(1)}, bf16[2,144,128]{2,1,0:T(8,128)(2,1)S(1)}, u32[]{:S(2)}, u32[]{:S(2)}) %collective-permute-start.2) | collective-permute-done | bytes 73760 | tf_op jit(solution)/shard_map/ppermute | solution.py:285
  10.8 0.3 %collective-permute-done.3.refs_2_ = bf16[2,144,128]{2,1,0:T(8,128)(2,1)S(1)} collective-permute-done((bf16[2,144,128]{2,1,0:T(8,128)(2,1)S(1)}, bf16[2,144,128]{2,1,0:T(8,128)(2,1)S(1)}, u32[]{:S(2)}, u32[]{:S(2)}) %collective-permute-start.3) | collective-permute-done | bytes 73760 | tf_op jit(solution)/shard_map/ppermute | solution.py:285
  11.2 1.6 %shard_map.93 = bf16[16,72,128]{2,1,0:T(8,128)(2,1)} custom-call(bf16[2,144,128]{2,1,0:T(8,128)(2,1)S(1)} %collective-permute-done.1.refs_0_, bf16[2,144,128]{2,1,0:T(8,128)(2,1)S(1)} %collective-permute-done.2.refs_1_, bf16[2,144,128]{2,1,0:T(8,128)(2,1)S(1)} %collective-permute-done.3.refs_2_, bf16[2,144,128]{2,1,0:T(8,128)(2,1)S(1)} %get-tuple-element.26.refs_3_, ...), custom_call_target="tpu_custom_call" | custom-call | tf_op jit(solution)/shard_map/pallas_call | solution.py:286
  12.8 0.0 copy-start.1
  12.8 5.3 %all-to-all-start = ((bf16[16,72,128]{2,1,0:T(8,128)(2,1)}), bf16[16,72,128]{2,1,0:T(8,128)(2,1)S(1)}, u32[]{:S(2)}, u32[]{:S(2)}) async-start(bf16[16,72,128]{2,1,0:T(8,128)(2,1)} %shard_map.93), calls=%async_computation | async-start | bytes 589824 | tf_op jit(solution)/shard_map/all_to_all | solution.py:309
  18.1 0.0 copy-start.2
  18.1 0.0 copy-start.3
  18.1 0.0 copy-done.1
  18.1 0.6 %copy-done.2 = f32[128]{0:T(128)S(1)} copy-done((f32[128]{0:T(128)S(1)}, f32[128]{0:T(128)}, u32[]{:S(2)}) %copy-start.2) | copy-done | bytes 536
  18.7 0.0 copy-done.3
  18.7 0.0 copy-start
  18.8 0.2 shard_map.94
  18.9 7.5 %all-to-all-done.total_ref = bf16[16,72,128]{2,1,0:T(8,128)(2,1)S(1)} async-done(((bf16[16,72,128]{2,1,0:T(8,128)(2,1)}), bf16[16,72,128]{2,1,0:T(8,128)(2,1)S(1)}, u32[]{:S(2)}, u32[]{:S(2)}) %all-to-all-start) | async-done | bytes 294944 | tf_op jit(solution)/shard_map/all_to_all | solution.py:309
  26.4 0.0 copy-done
  26.4 1.0 %shard_map.95 = bf16[12,48,128]{2,1,0:T(8,128)(2,1)} custom-call(bf16[16,72,128]{2,1,0:T(8,128)(2,1)S(1)} %all-to-all-done.total_ref, f32[576,128]{1,0:T(8,128)S(1)} %get-tuple-element.30.gate_ref, f32[128,1]{1,0:T(8,128)S(1)} %get-tuple-element.31.gain_ref, f32[128,1]{1,0:T(8,128)S(1)} %get-tuple-element.32.bias_ref, bf16[128,128]{1,0:T(8,128)(2,1)S(1)} %copy-done), custom_call_target="tpu_custom_call" | custom-call | tf_op jit(solution)/shard_map/pallas_call | solution.py:310
Async XLA Ops:
  0.0 2.2 %collective-permute-start = (bf16[12,48,128]{2,1,0:T(8,128)(2,1)}, bf16[12,48,128]{2,1,0:T(8,128)(2,1)S(1)}, u32[]{:S(2)}, u32[]{:S(2)}) collective-permute-start(bf16[12,48,128]{2,1,0:T(8,128)(2,1)} %pair_hbm.1), channel_id=1, source_target_pairs={{0,1},{1,0},{2,3},{3,2},{4,5},{5,4},{6,7},{7,6},{8,9},{9,8},{10,11... | collective-permute-start | bytes 442376 | tf_op jit(solution)/shard_map/ppermute | solution.py:250
  2.7 6.6 %collective-permute-start.1 = (bf16[2,144,128]{2,1,0:T(8,128)(2,1)S(1)}, bf16[2,144,128]{2,1,0:T(8,128)(2,1)S(1)}, u32[]{:S(2)}, u32[]{:S(2)}) collective-permute-start(bf16[2,144,128]{2,1,0:T(8,128)(2,1)S(1)} %get-tuple-element.23), channel_id=1, source_target_pairs={{0,6},{2,4},{4,2},{6,0},{1,7},{3,5},{5,3},{7,1},{8,14},{10,12},{12... | collective-permute-start | bytes 221192 | tf_op jit(solution)/shard_map/ppermute | solution.py:285
  6.3 4.5 %collective-permute-start.2 = (bf16[2,144,128]{2,1,0:T(8,128)(2,1)S(1)}, bf16[2,144,128]{2,1,0:T(8,128)(2,1)S(1)}, u32[]{:S(2)}, u32[]{:S(2)}) collective-permute-start(bf16[2,144,128]{2,1,0:T(8,128)(2,1)S(1)} %get-tuple-element.24), channel_id=1, source_target_pairs={{0,2},{2,0},{4,6},{6,4},{1,3},{3,1},{5,7},{7,5},{8,10},{10,8},{12,... | collective-permute-start | bytes 221192 | tf_op jit(solution)/shard_map/ppermute | solution.py:285
  6.8 4.4 %collective-permute-start.3 = (bf16[2,144,128]{2,1,0:T(8,128)(2,1)S(1)}, bf16[2,144,128]{2,1,0:T(8,128)(2,1)S(1)}, u32[]{:S(2)}, u32[]{:S(2)}) collective-permute-start(bf16[2,144,128]{2,1,0:T(8,128)(2,1)S(1)} %get-tuple-element.25), channel_id=1, source_target_pairs={{0,4},{2,6},{4,0},{6,2},{1,5},{3,7},{5,1},{7,3},{8,12},{10,14},{12... | collective-permute-start | bytes 221192 | tf_op jit(solution)/shard_map/ppermute | solution.py:285
  12.8 5.3 %copy-start.1 = (bf16[128,128]{1,0:T(8,128)(2,1)S(1)}, bf16[128,128]{1,0:T(8,128)(2,1)}, u32[]{:S(2)}) copy-start(bf16[128,128]{1,0:T(8,128)(2,1)} %w_ref.2) | copy-start | bytes 98308
  12.8 13.6 %all-to-all-start = ((bf16[16,72,128]{2,1,0:T(8,128)(2,1)}), bf16[16,72,128]{2,1,0:T(8,128)(2,1)S(1)}, u32[]{:S(2)}, u32[]{:S(2)}) async-start(bf16[16,72,128]{2,1,0:T(8,128)(2,1)} %shard_map.93), calls=%async_computation | async-start | bytes 589824 | tf_op jit(solution)/shard_map/all_to_all | solution.py:309
  18.1 0.7 %copy-start.2 = (f32[128]{0:T(128)S(1)}, f32[128]{0:T(128)}, u32[]{:S(2)}) copy-start(f32[128]{0:T(128)} %param.15) | copy-start | bytes 1540
  18.1 0.7 %copy-start.3 = (f32[128]{0:T(128)S(1)}, f32[128]{0:T(128)}, u32[]{:S(2)}) copy-start(f32[128]{0:T(128)} %param.16) | copy-start | bytes 1540
  18.7 7.7 %copy-start = (bf16[128,128]{1,0:T(8,128)(2,1)S(1)}, bf16[128,128]{1,0:T(8,128)(2,1)}, u32[]{:S(2)}) copy-start(bf16[128,128]{1,0:T(8,128)(2,1)} %w_ref.3) | copy-start | bytes 98308

commit v40 on v39

--- a/solution.py
+++ b/solution.py
@@ -235,10 +235,10 @@
     near = devices // halves
     quads = rows // halves
     far_order = []
-    for col in reversed(range(cols)):
-        ours = [quad * cols + col for quad in (range(quads) if col else [*range(1, quads), 0])]
-        behind = [near + quad * cols + col for quad in reversed(range(quads))]
-        far_order += behind[-1:] + ours + behind[:-1] if col else behind + ours
+    for n in range(quads):
+        far, other = [(quads - n) % quads, (n + 1) % quads], [quads - 1 - n, n]
+        spots = [near + far[0] * cols + 1, far[1] * cols, near + other[0] * cols, other[1] * cols + 1]
+        far_order += spots if n < quads - 1 else [spots[0], spots[3], spots[2], spots[1]]
     share = hidden // near
     tokens = row_count * col_count
     length = rows * row_count

time: 27.7 us -> 27.6 us (level)
  no operation moved by 1% of the time
where the time goes in v40:
time: 27.6 us; the launch traced here: 27.3 us
  waiting for transfers between devices  11.5 us (42%)
  starting transfers between devices  9.98 us (36%)
  Pallas kernels  5.05 us (18%)
  local copies, waits for them, and re-layouts  0.65 us (2%)
    all_to_all x1, waiting for transfers between devices, per_device(): lax.all_to_all(total, ('half', 'quad', 'col'), split_axis=0, concat_axis=...  7.3 us
    all_to_all x1, starting transfers between devices, per_device(): lax.all_to_all(total, ('half', 'quad', 'col'), split_axis=0, concat_axis=...  5.29 us
    ppermute x3, starting transfers between devices, per_device(): lax.ppermute(pieces[step], 'quad', [(i, i ^ step) for i in range(quads)])  4.24 us
    ppermute x3, waiting for transfers between devices, per_device(): lax.ppermute(pieces[step], 'quad', [(i, i ^ step) for i in range(quads)])  4.21 us
    pallas_call x1, Pallas kernels, per_device(): pl.pallas_call(functools.partial(own_kernel, quads, cols), out_shape=(jax...  1.71 us
    pallas_call x1, Pallas kernels, per_device(): pl.pallas_call(functools.partial(triangle_kernel, far_order, steps, cols,...  1.61 us
    pallas_call x1, Pallas kernels, per_device(): pl.pallas_call(functools.partial(output_kernel, far_order, near_order), o...  1.02 us
    unnamed x8, local copies, waits for them, and re-layouts  0.65 us
  transfers between devices with their start and end apart: 5, of which 4 were waited for; matrix products, arithmetic and copies ran while one was open for 0% of the time, Pallas kernels for 7%

profile of v40, /device:TPU:0, one launch (start us, length us, event | category | flops | bytes accessed | tf_op | source)
XLA Modules:
  0.0 27.3 jit_solution(1992783817071503245)
XLA Ops:
  0.0 0.5 %collective-permute-start = (bf16[12,48,128]{2,1,0:T(8,128)(2,1)}, bf16[12,48,128]{2,1,0:T(8,128)(2,1)S(1)}, u32[]{:S(2)}, u32[]{:S(2)}) collective-permute-start(bf16[12,48,128]{2,1,0:T(8,128)(2,1)} %pair_hbm.1), channel_id=1, source_target_pairs={{0,1},{1,0},{2,3},{3,2},{4,5},{5,4},{6,7},{7,6},{8,9},{9,8},{10,11... | collective-permute-start | bytes 442376 | tf_op jit(solution)/shard_map/ppermute | solution.py:250
  0.5 1.7 %shard_map.91 = (bf16[4,144,128]{2,1,0:T(8,128)(2,1)S(1)}, bf16[576,128]{1,0:T(8,128)(2,1)S(1)}, f32[8,384]{1,0:T(8,128)S(1)}, f32[96,1]{1,0:T(8,128)S(1)}, bf16...) custom-call(bf16[12,48,128]{2,1,0:T(8,128)(2,1)} %pair_hbm.1, f32[1,128]{1,0:T(1,128)} %bitcast.7, ...), custom_call_target="tpu_custom_call" | custom-call | flops 75497472 | bytes 1179648 | tf_op jit(solution)/shard_map/pallas_call | solution.py:252
  2.2 0.0 collective-permute-done.pair_ref
  2.2 0.5 %shard_map.92 = (bf16[2,144,128]{2,1,0:T(8,128)(2,1)S(1)}, bf16[2,144,128]{2,1,0:T(8,128)(2,1)S(1)}, bf16[2,144,128]{2,1,0:T(8,128)(2,1)S(1)}, bf16[2,144,128]{2,1,0:T(8,128)(2,1)S(1)}) custom-call(bf16[12,48,128]{2,1,0:T(8,128)(2,1)S(1)} %collective-permute-done.pair_ref, bf16[4,144,128]{2,1,0:T(8,128)(2,1)S(1)} %get-tuple-element.19.sides_ref, ...), custom_call_target="tpu_custom_call" | custom-call | flops 75497472 | bytes 1179648 | tf_op jit(solution)/shard_map/pallas_call | solution.py:275
  2.7 3.6 %collective-permute-start.1 = (bf16[2,144,128]{2,1,0:T(8,128)(2,1)S(1)}, bf16[2,144,128]{2,1,0:T(8,128)(2,1)S(1)}, u32[]{:S(2)}, u32[]{:S(2)}) collective-permute-start(bf16[2,144,128]{2,1,0:T(8,128)(2,1)S(1)} %get-tuple-element.23), channel_id=1, source_target_pairs={{0,6},{2,4},{4,2},{6,0},{1,7},{3,5},{5,3},{7,1},{8,14},{10,12},{12... | collective-permute-start | bytes 221192 | tf_op jit(solution)/shard_map/ppermute | solution.py:285
  6.3 0.5 %collective-permute-start.2 = (bf16[2,144,128]{2,1,0:T(8,128)(2,1)S(1)}, bf16[2,144,128]{2,1,0:T(8,128)(2,1)S(1)}, u32[]{:S(2)}, u32[]{:S(2)}) collective-permute-start(bf16[2,144,128]{2,1,0:T(8,128)(2,1)S(1)} %get-tuple-element.24), channel_id=1, source_target_pairs={{0,2},{2,0},{4,6},{6,4},{1,3},{3,1},{5,7},{7,5},{8,10},{10,8},{12,... | collective-permute-start | bytes 221192 | tf_op jit(solution)/shard_map/ppermute | solution.py:285
  6.8 0.1 collective-permute-start.3
  7.0 2.3 %collective-permute-done.1.refs_0_ = bf16[2,144,128]{2,1,0:T(8,128)(2,1)S(1)} collective-permute-done((bf16[2,144,128]{2,1,0:T(8,128)(2,1)S(1)}, bf16[2,144,128]{2,1,0:T(8,128)(2,1)S(1)}, u32[]{:S(2)}, u32[]{:S(2)}) %collective-permute-start.1) | collective-permute-done | bytes 73760 | tf_op jit(solution)/shard_map/ppermute | solution.py:285
  9.3 1.6 %collective-permute-done.2.refs_1_ = bf16[2,144,128]{2,1,0:T(8,128)(2,1)S(1)} collective-permute-done((bf16[2,144,128]{2,1,0:T(8,128)(2,1)S(1)}, bf16[2,144,128]{2,1,0:T(8,128)(2,1)S(1)}, u32[]{:S(2)}, u32[]{:S(2)}) %collective-permute-start.2) | collective-permute-done | bytes 73760 | tf_op jit(solution)/shard_map/ppermute | solution.py:285
  10.8 0.3 %collective-permute-done.3.refs_2_ = bf16[2,144,128]{2,1,0:T(8,128)(2,1)S(1)} collective-permute-done((bf16[2,144,128]{2,1,0:T(8,128)(2,1)S(1)}, bf16[2,144,128]{2,1,0:T(8,128)(2,1)S(1)}, u32[]{:S(2)}, u32[]{:S(2)}) %collective-permute-start.3) | collective-permute-done | bytes 73760 | tf_op jit(solution)/shard_map/ppermute | solution.py:285
  11.2 1.6 %shard_map.93 = bf16[16,72,128]{2,1,0:T(8,128)(2,1)} custom-call(bf16[2,144,128]{2,1,0:T(8,128)(2,1)S(1)} %collective-permute-done.1.refs_0_, bf16[2,144,128]{2,1,0:T(8,128)(2,1)S(1)} %collective-permute-done.2.refs_1_, bf16[2,144,128]{2,1,0:T(8,128)(2,1)S(1)} %collective-permute-done.3.refs_2_, bf16[2,144,128]{2,1,0:T(8,128)(2,1)S(1)} %get-tuple-element.26.refs_3_, ...), custom_call_target="tpu_custom_call" | custom-call | tf_op jit(solution)/shard_map/pallas_call | solution.py:286
  12.8 0.0 copy-start.1
  12.8 5.3 %all-to-all-start = ((bf16[16,72,128]{2,1,0:T(8,128)(2,1)}), bf16[16,72,128]{2,1,0:T(8,128)(2,1)S(1)}, u32[]{:S(2)}, u32[]{:S(2)}) async-start(bf16[16,72,128]{2,1,0:T(8,128)(2,1)} %shard_map.93), calls=%async_computation | async-start | bytes 589824 | tf_op jit(solution)/shard_map/all_to_all | solution.py:309
  18.1 0.0 copy-start.2
  18.1 0.0 copy-start.3
  18.1 0.0 copy-done.1
  18.1 0.6 %copy-done.2 = f32[128]{0:T(128)S(1)} copy-done((f32[128]{0:T(128)S(1)}, f32[128]{0:T(128)}, u32[]{:S(2)}) %copy-start.2) | copy-done | bytes 536
  18.7 0.0 copy-done.3
  18.7 0.0 copy-start
  18.8 0.2 shard_map.94
  18.9 7.3 %all-to-all-done.total_ref = bf16[16,72,128]{2,1,0:T(8,128)(2,1)S(1)} async-done(((bf16[16,72,128]{2,1,0:T(8,128)(2,1)}), bf16[16,72,128]{2,1,0:T(8,128)(2,1)S(1)}, u32[]{:S(2)}, u32[]{:S(2)}) %all-to-all-start) | async-done | bytes 294944 | tf_op jit(solution)/shard_map/all_to_all | solution.py:309
  26.2 0.0 copy-done
  26.3 1.0 %shard_map.95 = bf16[12,48,128]{2,1,0:T(8,128)(2,1)} custom-call(bf16[16,72,128]{2,1,0:T(8,128)(2,1)S(1)} %all-to-all-done.total_ref, f32[576,128]{1,0:T(8,128)S(1)} %get-tuple-element.30.gate_ref, f32[128,1]{1,0:T(8,128)S(1)} %get-tuple-element.31.gain_ref, f32[128,1]{1,0:T(8,128)S(1)} %get-tuple-element.32.bias_ref, bf16[128,128]{1,0:T(8,128)(2,1)S(1)} %copy-done), custom_call_target="tpu_custom_call" | custom-call | tf_op jit(solution)/shard_map/pallas_call | solution.py:310
Async XLA Ops:
  0.0 2.2 %collective-permute-start = (bf16[12,48,128]{2,1,0:T(8,128)(2,1)}, bf16[12,48,128]{2,1,0:T(8,128)(2,1)S(1)}, u32[]{:S(2)}, u32[]{:S(2)}) collective-permute-start(bf16[12,48,128]{2,1,0:T(8,128)(2,1)} %pair_hbm.1), channel_id=1, source_target_pairs={{0,1},{1,0},{2,3},{3,2},{4,5},{5,4},{6,7},{7,6},{8,9},{9,8},{10,11... | collective-permute-start | bytes 442376 | tf_op jit(solution)/shard_map/ppermute | solution.py:250
  2.7 6.6 %collective-permute-start.1 = (bf16[2,144,128]{2,1,0:T(8,128)(2,1)S(1)}, bf16[2,144,128]{2,1,0:T(8,128)(2,1)S(1)}, u32[]{:S(2)}, u32[]{:S(2)}) collective-permute-start(bf16[2,144,128]{2,1,0:T(8,128)(2,1)S(1)} %get-tuple-element.23), channel_id=1, source_target_pairs={{0,6},{2,4},{4,2},{6,0},{1,7},{3,5},{5,3},{7,1},{8,14},{10,12},{12... | collective-permute-start | bytes 221192 | tf_op jit(solution)/shard_map/ppermute | solution.py:285
  6.3 4.5 %collective-permute-start.2 = (bf16[2,144,128]{2,1,0:T(8,128)(2,1)S(1)}, bf16[2,144,128]{2,1,0:T(8,128)(2,1)S(1)}, u32[]{:S(2)}, u32[]{:S(2)}) collective-permute-start(bf16[2,144,128]{2,1,0:T(8,128)(2,1)S(1)} %get-tuple-element.24), channel_id=1, source_target_pairs={{0,2},{2,0},{4,6},{6,4},{1,3},{3,1},{5,7},{7,5},{8,10},{10,8},{12,... | collective-permute-start | bytes 221192 | tf_op jit(solution)/shard_map/ppermute | solution.py:285
  6.8 4.4 %collective-permute-start.3 = (bf16[2,144,128]{2,1,0:T(8,128)(2,1)S(1)}, bf16[2,144,128]{2,1,0:T(8,128)(2,1)S(1)}, u32[]{:S(2)}, u32[]{:S(2)}) collective-permute-start(bf16[2,144,128]{2,1,0:T(8,128)(2,1)S(1)} %get-tuple-element.25), channel_id=1, source_target_pairs={{0,4},{2,6},{4,0},{6,2},{1,5},{3,7},{5,1},{7,3},{8,12},{10,14},{12... | collective-permute-start | bytes 221192 | tf_op jit(solution)/shard_map/ppermute | solution.py:285
  12.8 5.3 %copy-start.1 = (bf16[128,128]{1,0:T(8,128)(2,1)S(1)}, bf16[128,128]{1,0:T(8,128)(2,1)}, u32[]{:S(2)}) copy-start(bf16[128,128]{1,0:T(8,128)(2,1)} %w_ref.2) | copy-start | bytes 98308
  12.8 13.5 %all-to-all-start = ((bf16[16,72,128]{2,1,0:T(8,128)(2,1)}), bf16[16,72,128]{2,1,0:T(8,128)(2,1)S(1)}, u32[]{:S(2)}, u32[]{:S(2)}) async-start(bf16[16,72,128]{2,1,0:T(8,128)(2,1)} %shard_map.93), calls=%async_computation | async-start | bytes 589824 | tf_op jit(solution)/shard_map/all_to_all | solution.py:309
  18.1 0.7 %copy-start.2 = (f32[128]{0:T(128)S(1)}, f32[128]{0:T(128)}, u32[]{:S(2)}) copy-start(f32[128]{0:T(128)} %param.15) | copy-start | bytes 1540
  18.1 0.7 %copy-start.3 = (f32[128]{0:T(128)S(1)}, f32[128]{0:T(128)}, u32[]{:S(2)}) copy-start(f32[128]{0:T(128)} %param.16) | copy-start | bytes 1540
  18.7 7.5 %copy-start = (bf16[128,128]{1,0:T(8,128)(2,1)S(1)}, bf16[128,128]{1,0:T(8,128)(2,1)}, u32[]{:S(2)}) copy-start(bf16[128,128]{1,0:T(8,128)(2,1)} %w_ref.3) | copy-start | bytes 98308

commit v41 on v31

--- a/solution.py
+++ b/solution.py
@@ -236,7 +236,7 @@
     quads = rows // halves
     far_order = []
     for col in reversed(range(cols)):
-        ahead = list(range(quads)) if col else list(range(1, quads)) + [0]
+        ahead = list(range(quads)) if col else list(reversed(range(quads)))
         behind = [0] + list(reversed(range(1, quads))) if col else list(reversed(range(quads)))
         for quad, other in zip(ahead, behind):
             far_order += [near + other * cols + col, quad * cols + col]

time: 26.8 us -> 26.8 us (level)
  no operation moved by 1% of the time
where the time goes in v41:
time: 26.8 us; the launch traced here: 26.5 us
  waiting for transfers between devices  10.7 us (40%)
  starting transfers between devices  9.98 us (37%)
  Pallas kernels  5.05 us (19%)
  local copies, waits for them, and re-layouts  0.65 us (2%)
    all_to_all x1, waiting for transfers between devices, per_device(): lax.all_to_all(total, ('half', 'quad', 'col'), split_axis=0, concat_axis=...  6.52 us
    all_to_all x1, starting transfers between devices, per_device(): lax.all_to_all(total, ('half', 'quad', 'col'), split_axis=0, concat_axis=...  5.29 us
    ppermute x3, starting transfers between devices, per_device(): lax.ppermute(pieces[step], 'quad', [(i, i ^ step) for i in range(quads)])  4.24 us
    ppermute x3, waiting for transfers between devices, per_device(): lax.ppermute(pieces[step], 'quad', [(i, i ^ step) for i in range(quads)])  4.21 us
    pallas_call x1, Pallas kernels, per_device(): pl.pallas_call(functools.partial(own_kernel, quads, cols), out_shape=(jax...  1.71 us
    pallas_call x1, Pallas kernels, per_device(): pl.pallas_call(functools.partial(triangle_kernel, far_order, steps, cols,...  1.61 us
    pallas_call x1, Pallas kernels, per_device(): pl.pallas_call(functools.partial(output_kernel, far_order, near_order), o...  1.02 us
    unnamed x8, local copies, waits for them, and re-layouts  0.65 us
  transfers between devices with their start and end apart: 5, of which 4 were waited for; matrix products, arithmetic and copies ran while one was open for 0% of the time, Pallas kernels for 7%

profile of v41, /device:TPU:0, one launch (start us, length us, event | category | flops | bytes accessed | tf_op | source)
XLA Modules:
  0.0 26.5 jit_solution(4628531458927907140)
XLA Ops:
  0.0 0.5 %collective-permute-start = (bf16[12,48,128]{2,1,0:T(8,128)(2,1)}, bf16[12,48,128]{2,1,0:T(8,128)(2,1)S(1)}, u32[]{:S(2)}, u32[]{:S(2)}) collective-permute-start(bf16[12,48,128]{2,1,0:T(8,128)(2,1)} %pair_hbm.1), channel_id=1, source_target_pairs={{0,1},{1,0},{2,3},{3,2},{4,5},{5,4},{6,7},{7,6},{8,9},{9,8},{10,11... | collective-permute-start | bytes 442376 | tf_op jit(solution)/shard_map/ppermute | solution.py:251
  0.5 1.7 %shard_map.91 = (bf16[4,144,128]{2,1,0:T(8,128)(2,1)S(1)}, bf16[576,128]{1,0:T(8,128)(2,1)S(1)}, f32[8,384]{1,0:T(8,128)S(1)}, f32[96,1]{1,0:T(8,128)S(1)}, bf16...) custom-call(bf16[12,48,128]{2,1,0:T(8,128)(2,1)} %pair_hbm.1, f32[1,128]{1,0:T(1,128)} %bitcast.7, ...), custom_call_target="tpu_custom_call" | custom-call | flops 75497472 | bytes 1179648 | tf_op jit(solution)/shard_map/pallas_call | solution.py:253
  2.2 0.0 collective-permute-done.pair_ref
  2.2 0.5 %shard_map.92 = (bf16[2,144,128]{2,1,0:T(8,128)(2,1)S(1)}, bf16[2,144,128]{2,1,0:T(8,128)(2,1)S(1)}, bf16[2,144,128]{2,1,0:T(8,128)(2,1)S(1)}, bf16[2,144,128]{2,1,0:T(8,128)(2,1)S(1)}) custom-call(bf16[12,48,128]{2,1,0:T(8,128)(2,1)S(1)} %collective-permute-done.pair_ref, bf16[4,144,128]{2,1,0:T(8,128)(2,1)S(1)} %get-tuple-element.19.sides_ref, ...), custom_call_target="tpu_custom_call" | custom-call | flops 75497472 | bytes 1179648 | tf_op jit(solution)/shard_map/pallas_call | solution.py:276
  2.7 3.6 %collective-permute-start.1 = (bf16[2,144,128]{2,1,0:T(8,128)(2,1)S(1)}, bf16[2,144,128]{2,1,0:T(8,128)(2,1)S(1)}, u32[]{:S(2)}, u32[]{:S(2)}) collective-permute-start(bf16[2,144,128]{2,1,0:T(8,128)(2,1)S(1)} %get-tuple-element.23), channel_id=1, source_target_pairs={{0,6},{2,4},{4,2},{6,0},{1,7},{3,5},{5,3},{7,1},{8,14},{10,12},{12... | collective-permute-start | bytes 221192 | tf_op jit(solution)/shard_map/ppermute | solution.py:286
  6.3 0.5 %collective-permute-start.2 = (bf16[2,144,128]{2,1,0:T(8,128)(2,1)S(1)}, bf16[2,144,128]{2,1,0:T(8,128)(2,1)S(1)}, u32[]{:S(2)}, u32[]{:S(2)}) collective-permute-start(bf16[2,144,128]{2,1,0:T(8,128)(2,1)S(1)} %get-tuple-element.24), channel_id=1, source_target_pairs={{0,2},{2,0},{4,6},{6,4},{1,3},{3,1},{5,7},{7,5},{8,10},{10,8},{12,... | collective-permute-start | bytes 221192 | tf_op jit(solution)/shard_map/ppermute | solution.py:286
  6.8 0.1 collective-permute-start.3
  7.0 2.3 %collective-permute-done.1.refs_0_ = bf16[2,144,128]{2,1,0:T(8,128)(2,1)S(1)} collective-permute-done((bf16[2,144,128]{2,1,0:T(8,128)(2,1)S(1)}, bf16[2,144,128]{2,1,0:T(8,128)(2,1)S(1)}, u32[]{:S(2)}, u32[]{:S(2)}) %collective-permute-start.1) | collective-permute-done | bytes 73760 | tf_op jit(solution)/shard_map/ppermute | solution.py:286
  9.3 1.6 %collective-permute-done.2.refs_1_ = bf16[2,144,128]{2,1,0:T(8,128)(2,1)S(1)} collective-permute-done((bf16[2,144,128]{2,1,0:T(8,128)(2,1)S(1)}, bf16[2,144,128]{2,1,0:T(8,128)(2,1)S(1)}, u32[]{:S(2)}, u32[]{:S(2)}) %collective-permute-start.2) | collective-permute-done | bytes 73760 | tf_op jit(solution)/shard_map/ppermute | solution.py:286
  10.8 0.3 %collective-permute-done.3.refs_2_ = bf16[2,144,128]{2,1,0:T(8,128)(2,1)S(1)} collective-permute-done((bf16[2,144,128]{2,1,0:T(8,128)(2,1)S(1)}, bf16[2,144,128]{2,1,0:T(8,128)(2,1)S(1)}, u32[]{:S(2)}, u32[]{:S(2)}) %collective-permute-start.3) | collective-permute-done | bytes 73760 | tf_op jit(solution)/shard_map/ppermute | solution.py:286
  11.2 1.6 %shard_map.93 = bf16[16,72,128]{2,1,0:T(8,128)(2,1)} custom-call(bf16[2,144,128]{2,1,0:T(8,128)(2,1)S(1)} %collective-permute-done.1.refs_0_, bf16[2,144,128]{2,1,0:T(8,128)(2,1)S(1)} %collective-permute-done.2.refs_1_, bf16[2,144,128]{2,1,0:T(8,128)(2,1)S(1)} %collective-permute-done.3.refs_2_, bf16[2,144,128]{2,1,0:T(8,128)(2,1)S(1)} %get-tuple-element.26.refs_3_, ...), custom_call_target="tpu_custom_call" | custom-call | tf_op jit(solution)/shard_map/pallas_call | solution.py:287
  12.8 0.0 copy-start.1
  12.8 5.3 %all-to-all-start = ((bf16[16,72,128]{2,1,0:T(8,128)(2,1)}), bf16[16,72,128]{2,1,0:T(8,128)(2,1)S(1)}, u32[]{:S(2)}, u32[]{:S(2)}) async-start(bf16[16,72,128]{2,1,0:T(8,128)(2,1)} %shard_map.93), calls=%async_computation | async-start | bytes 589824 | tf_op jit(solution)/shard_map/all_to_all | solution.py:310
  18.1 0.0 copy-start.2
  18.1 0.0 copy-start.3
  18.1 0.0 copy-done.1
  18.1 0.6 %copy-done.2 = f32[128]{0:T(128)S(1)} copy-done((f32[128]{0:T(128)S(1)}, f32[128]{0:T(128)}, u32[]{:S(2)}) %copy-start.2) | copy-done | bytes 536
  18.7 0.0 copy-done.3
  18.7 0.0 copy-start
  18.8 0.2 shard_map.94
  18.9 6.5 %all-to-all-done.total_ref = bf16[16,72,128]{2,1,0:T(8,128)(2,1)S(1)} async-done(((bf16[16,72,128]{2,1,0:T(8,128)(2,1)}), bf16[16,72,128]{2,1,0:T(8,128)(2,1)S(1)}, u32[]{:S(2)}, u32[]{:S(2)}) %all-to-all-start) | async-done | bytes 294944 | tf_op jit(solution)/shard_map/all_to_all | solution.py:310
  25.5 0.0 copy-done
  25.5 1.0 %shard_map.95 = bf16[12,48,128]{2,1,0:T(8,128)(2,1)} custom-call(bf16[16,72,128]{2,1,0:T(8,128)(2,1)S(1)} %all-to-all-done.total_ref, f32[576,128]{1,0:T(8,128)S(1)} %get-tuple-element.30.gate_ref, f32[128,1]{1,0:T(8,128)S(1)} %get-tuple-element.31.gain_ref, f32[128,1]{1,0:T(8,128)S(1)} %get-tuple-element.32.bias_ref, bf16[128,128]{1,0:T(8,128)(2,1)S(1)} %copy-done), custom_call_target="tpu_custom_call" | custom-call | tf_op jit(solution)/shard_map/pallas_call | solution.py:311
Async XLA Ops:
  0.0 2.2 %collective-permute-start = (bf16[12,48,128]{2,1,0:T(8,128)(2,1)}, bf16[12,48,128]{2,1,0:T(8,128)(2,1)S(1)}, u32[]{:S(2)}, u32[]{:S(2)}) collective-permute-start(bf16[12,48,128]{2,1,0:T(8,128)(2,1)} %pair_hbm.1), channel_id=1, source_target_pairs={{0,1},{1,0},{2,3},{3,2},{4,5},{5,4},{6,7},{7,6},{8,9},{9,8},{10,11... | collective-permute-start | bytes 442376 | tf_op jit(solution)/shard_map/ppermute | solution.py:251
  2.7 6.6 %collective-permute-start.1 = (bf16[2,144,128]{2,1,0:T(8,128)(2,1)S(1)}, bf16[2,144,128]{2,1,0:T(8,128)(2,1)S(1)}, u32[]{:S(2)}, u32[]{:S(2)}) collective-permute-start(bf16[2,144,128]{2,1,0:T(8,128)(2,1)S(1)} %get-tuple-element.23), channel_id=1, source_target_pairs={{0,6},{2,4},{4,2},{6,0},{1,7},{3,5},{5,3},{7,1},{8,14},{10,12},{12... | collective-permute-start | bytes 221192 | tf_op jit(solution)/shard_map/ppermute | solution.py:286
  6.3 4.5 %collective-permute-start.2 = (bf16[2,144,128]{2,1,0:T(8,128)(2,1)S(1)}, bf16[2,144,128]{2,1,0:T(8,128)(2,1)S(1)}, u32[]{:S(2)}, u32[]{:S(2)}) collective-permute-start(bf16[2,144,128]{2,1,0:T(8,128)(2,1)S(1)} %get-tuple-element.24), channel_id=1, source_target_pairs={{0,2},{2,0},{4,6},{6,4},{1,3},{3,1},{5,7},{7,5},{8,10},{10,8},{12,... | collective-permute-start | bytes 221192 | tf_op jit(solution)/shard_map/ppermute | solution.py:286
  6.8 4.4 %collective-permute-start.3 = (bf16[2,144,128]{2,1,0:T(8,128)(2,1)S(1)}, bf16[2,144,128]{2,1,0:T(8,128)(2,1)S(1)}, u32[]{:S(2)}, u32[]{:S(2)}) collective-permute-start(bf16[2,144,128]{2,1,0:T(8,128)(2,1)S(1)} %get-tuple-element.25), channel_id=1, source_target_pairs={{0,4},{2,6},{4,0},{6,2},{1,5},{3,7},{5,1},{7,3},{8,12},{10,14},{12... | collective-permute-start | bytes 221192 | tf_op jit(solution)/shard_map/ppermute | solution.py:286
  12.8 5.3 %copy-start.1 = (bf16[128,128]{1,0:T(8,128)(2,1)S(1)}, bf16[128,128]{1,0:T(8,128)(2,1)}, u32[]{:S(2)}) copy-start(bf16[128,128]{1,0:T(8,128)(2,1)} %w_ref.2) | copy-start | bytes 98308
  12.8 12.7 %all-to-all-start = ((bf16[16,72,128]{2,1,0:T(8,128)(2,1)}), bf16[16,72,128]{2,1,0:T(8,128)(2,1)S(1)}, u32[]{:S(2)}, u32[]{:S(2)}) async-start(bf16[16,72,128]{2,1,0:T(8,128)(2,1)} %shard_map.93), calls=%async_computation | async-start | bytes 589824 | tf_op jit(solution)/shard_map/all_to_all | solution.py:310
  18.1 0.7 %copy-start.2 = (f32[128]{0:T(128)S(1)}, f32[128]{0:T(128)}, u32[]{:S(2)}) copy-start(f32[128]{0:T(128)} %param.15) | copy-start | bytes 1540
  18.1 0.7 %copy-start.3 = (f32[128]{0:T(128)S(1)}, f32[128]{0:T(128)}, u32[]{:S(2)}) copy-start(f32[128]{0:T(128)} %param.16) | copy-start | bytes 1540
  18.7 6.7 %copy-start = (bf16[128,128]{1,0:T(8,128)(2,1)S(1)}, bf16[128,128]{1,0:T(8,128)(2,1)}, u32[]{:S(2)}) copy-start(bf16[128,128]{1,0:T(8,128)(2,1)} %w_ref.3) | copy-start | bytes 98308
